TPU v7x, 1024 devices: a whole 8x8x8 slice. The times are simulated.
1024 devices in a mesh: seq: 16 (over y_hi, x), dp: 64 (over z, y_lo, core).
Axes of the slice: x: 8, y: 8 (y_hi: 2, y_lo: 4; y = y_hi * 4 + y_lo), z: 8, core: 2. Of those that a mesh axis runs over, the one named last changes fastest.
Arguments:
- attn_out: bfloat16 [131072, 3072], P('dp', 'seq'), may hold values from -6 to 6
- cotangent: bfloat16 [131072, 3072], P(('seq', 'dp')), may hold values from -0.0625 to 0.0625
- gate: float32 [64, 3072], P('dp'), may hold values from -4 to 4
- weight: float32 [3072, 3072], P('dp', 'seq'), may hold values from -1.5 to 1.5
- exp_avg: float32 [3072, 3072], P('dp', 'seq'), may hold values from -6 to 6
- exp_avg_sq: float32 [3072, 3072], P('dp', 'seq'), may hold values from 0.25 to 4
- left_stats: float32 [3072, 768], P('dp', 'seq'), as said below
- right_stats: float32 [12288, 3072], P('dp', 'seq')
- left_basis: float32 [3072, 768], P('dp', 'seq'), may hold values from -0.875 to 0.875
- right_basis: float32 [12288, 3072], P('dp', 'seq'), may hold values from -0.4375 to 0.4375
Outputs:
- update: float32 [3072, 3072], P('dp', 'seq')
- new_weight: float32 [3072, 3072], P('dp', 'seq')
- new_exp_avg: float32 [3072, 3072], P('dp', 'seq')
- new_exp_avg_sq: float32 [3072, 3072], P('dp', 'seq')
- new_left_stats: float32 [3072, 768], P('dp', 'seq')
- new_right_stats: float32 [12288, 3072], P('dp', 'seq')
Inputs may be any that keep to these rules, and one draw needn't show every extreme that they name: Every 48 x 48 block of left_stats and 192 x 192 block of right_stats is symmetric.
All inputs are finite; a program needn't handle non-finite values.
Results may differ from a plain program's by a relative error of at most 0.0003.
Values may be sent and summed in bfloat16 or wider, within the bound.
No kernel may reach another device: no remote copies, remote signals or barrier semaphores. Data moves between devices by JAX's collectives and lax.ppermute only.
A program may use at most 64 MiB of HBM per device.

v0:
```python
import jax
import jax.numpy as jnp
from jax import lax
from jax.sharding import PartitionSpec as P

beta_one = 0.9
beta_two = 0.95
epsilon = 1e-08
learn_rate = 0.02
decay_rate = 0.1


def hi_dot(left_mat, right_mat):
    return jnp.dot(left_mat, right_mat, precision=lax.Precision.HIGHEST)


def local(
    attn_out,
    cotangent,
    gate,
    weight,
    exp_avg,
    exp_avg_sq,
    left_stats,
    right_stats,
    left_basis,
    right_basis,
):
    gate_row = gate[0]
    gathered = lax.all_gather(cotangent, "seq", axis=0, tiled=True)
    product = lax.dot_general(
        gathered, attn_out, (((0,), (0,)), ((), ())), preferred_element_type=jnp.float32
    )
    gradient = lax.psum_scatter(gate_row[:, None] * product, "dp", scatter_dimension=0, tiled=True)
    left_new = beta_two * left_stats + (1.0 - beta_two) * hi_dot(gradient, gradient.T)
    right_new = beta_two * right_stats + (1.0 - beta_two) * hi_dot(gradient.T, gradient)
    moment = beta_one * exp_avg + (1.0 - beta_one) * gradient

    def rotate_in(matrix):
        return hi_dot(hi_dot(left_basis.T, matrix), right_basis)

    rotated = rotate_in(gradient)
    second = beta_two * exp_avg_sq + (1.0 - beta_two) * rotated * rotated
    direction = rotate_in(moment) / (jnp.sqrt(second) + epsilon)
    update = hi_dot(hi_dot(left_basis, direction), right_basis.T)
    new_weight = weight * (1.0 - learn_rate * decay_rate) - learn_rate * update
    return (update, new_weight, moment, second, left_new, right_new)


def solution(mesh):
    in_specs = (
        P("dp", "seq"),
        P(("seq", "dp"), None),
        P("dp", None),
        P("dp", "seq"),
        P("dp", "seq"),
        P("dp", "seq"),
        P("dp", "seq"),
        P("dp", "seq"),
        P("dp", "seq"),
        P("dp", "seq"),
    )
    out_specs = (
        P("dp", "seq"),
        P("dp", "seq"),
        P("dp", "seq"),
        P("dp", "seq"),
        P("dp", "seq"),
        P("dp", "seq"),
    )
    return jax.shard_map(local, mesh=mesh, in_specs=in_specs, out_specs=out_specs, check_vma=False)
```

profile of v0, /device:TPU:1, one launch (start us, length us, event | category | flops | bytes accessed | tf_op | source)
XLA Modules:
  0.0 599.3 jit_solution(17417388123633883682)
XLA Ops:
  7.2 0.0 copy-start
  7.2 0.0 all-gather.2.cloned.1.call-start
  7.2 0.7 all-gather.2.cloned.1.call-update
  7.9 0.0 reduce-scatter.2.cloned.1.call-start
  8.0 286.4 %all-gather.2.cloned.1.call-done = bf16[2048,3072]{1,0:T(8,128)(2,1)} async-done(((bf16[128,3072]{1,0:T(8,128)(2,1)}), bf16[2048,3072]{1,0:T(8,128)(2,1)}) %all-gather.2.cloned.1.call-update) | async-done | bytes 12582928 | tf_op jit(solution)/shard_map/all_gather | solution.py:30
  294.4 0.0 copy-done
  294.4 0.0 copy-start.6
  294.4 0.0 copy-start.7
  294.4 0.0 copy-start.9
  294.4 0.0 copy-start.4
  294.4 10.2 %convolution_multiply_fusion = f32[3072,192]{1,0:T(8,128)} fusion(bf16[2048,3072]{1,0:T(8,128)(2,1)} %all-gather.2.cloned.1.call-done, bf16[2048,192]{0,1:T(8,128)(2,1)S(1)} %copy-done, f32[3072]{0:T(1024)} %bitcast.19), kind=kOutput, calls=%fused_computation | convolution fusion | flops 2416508928 | bytes 15740928 | tf_op jit(solution)/shard_map/dot_general | solution.py:31
  304.7 0.0 reduce-scatter.2.cloned.1.call-update
  304.7 279.8 %reduce-scatter.2.cloned.1.call-done = f32[48,192]{1,0:T(8,128)} async-done(((f32[3072,192]{1,0:T(8,128)}), f32[48,192]{1,0:T(8,128)}) %reduce-scatter.2.cloned.1.call-update) | async-done | bytes 36880 | tf_op jit(solution)/shard_map/reduce_scatter | solution.py:34
  584.5 0.0 copy-done.8
  584.5 0.8 multiply_add_fusion
  585.3 0.0 copy-done.2
  585.3 0.0 copy-start.5
  585.3 0.3 fusion.3
  585.7 1.1 fusion.4
  586.8 0.0 copy-done.1
  586.8 0.0 copy-done.6
  586.8 0.3 fusion.2
  587.2 0.0 copy-start.3
  587.2 0.3 convolution_divide_fusion
  587.5 0.3 fusion.5
  587.9 0.0 copy-done.7
  587.9 1.0 multiply_subtract_fusion
  588.9 0.0 copy-done.9
  588.9 1.7 fusion.1
  590.6 0.0 copy-done.4
  590.6 1.9 fusion
  592.5 0.0 copy-done.3
  (4 shorter events, 0.0 us)
Async XLA Ops:
  7.2 287.2 %copy-start = (bf16[2048,192]{0,1:T(8,128)(2,1)S(1)}, bf16[2048,192]{0,1:T(8,128)(2,1)}, u32[]{:S(2)}) copy-start(bf16[2048,192]{0,1:T(8,128)(2,1)} %param.10) | copy-start | bytes 2359300
  7.2 287.2 %all-gather.2.cloned.1.call-start = ((), (), s32[]{:S(2)}) async-start(), calls=%async_computation.1 | async-start | bytes 13369344 | tf_op jit(solution)/shard_map/all_gather | solution.py:30
  7.9 576.6 %reduce-scatter.2.cloned.1.call-start = ((), (), s32[]{:S(2)}) async-start(), calls=%async_computation.2 | async-start | bytes 3194880 | tf_op jit(solution)/shard_map/reduce_scatter | solution.py:34
  294.4 290.1 %copy-start.8 = (f32[48,192]{1,0:T(8,128)S(1)}, f32[48,192]{1,0:T(8,128)}, u32[]{:S(2)}) copy-start(f32[48,192]{1,0:T(8,128)} %param.14) | copy-start | bytes 110596
  294.4 290.9 %copy-start.2 = (f32[48,48]{1,0:T(8,128)S(1)}, f32[48,48]{1,0:T(8,128)}, u32[]{:S(2)}) copy-start(f32[48,48]{1,0:T(8,128)} %param.18) | copy-start | bytes 27652
  294.4 292.4 %copy-start.1 = (f32[192,192]{1,0:T(8,128)S(1)}, f32[192,192]{1,0:T(8,128)}, u32[]{:S(2)}) copy-start(f32[192,192]{1,0:T(8,128)} %param.19) | copy-start | bytes 442372
  294.4 292.4 %copy-start.6 = (f32[48,192]{1,0:T(8,128)S(1)}, f32[48,192]{1,0:T(8,128)}, u32[]{:S(2)}) copy-start(f32[48,192]{1,0:T(8,128)} %param.15) | copy-start | bytes 110596
  294.4 293.5 %copy-start.7 = (f32[48,192]{1,0:T(8,128)S(1)}, f32[48,192]{1,0:T(8,128)}, u32[]{:S(2)}) copy-start(f32[48,192]{1,0:T(8,128)} %param.13) | copy-start | bytes 110596
  294.4 294.5 %copy-start.9 = (f32[48,48]{1,0:T(8,128)S(1)}, f32[48,48]{1,0:T(8,128)}, u32[]{:S(2)}) copy-start(f32[48,48]{1,0:T(8,128)} %param.16) | copy-start | bytes 27652
  294.4 296.1 %copy-start.4 = (f32[192,192]{1,0:T(8,128)S(1)}, f32[192,192]{1,0:T(8,128)}, u32[]{:S(2)}) copy-start(f32[192,192]{1,0:T(8,128)} %param.17) | copy-start | bytes 442372
  585.3 7.1 %copy-start.5 = (f32[48,192]{1,0:T(8,128)}, f32[48,192]{1,0:T(8,128)S(1)}, u32[]{:S(2)}) copy-start(f32[48,192]{1,0:T(8,128)S(1)} %multiply_add_fusion) | copy-start | bytes 110596
  587.2 5.3 copy-start.3
Sparse Core Ops, SparseCore 0:
  12.4 281.9 all-gather.1
  304.8 279.6 reduce-scatter.1
where the time goes:
time: 605 us; the launch traced here: 599 us
  waiting for transfers between devices  567 us (94%)
  matrix products  17.3 us (3%)
  between operations  14.2 us (2%)
    all_gather x1, waiting for transfers between devices, local(): gathered = lax.all_gather(cotangent, 'seq', axis=0, tiled=True)  286 us
    reduce_scatter x1, waiting for transfers between devices, local(): lax.psum_scatter(gate_row[:, None] * product, 'dp', scatter_dimension=0,...  280 us
  transfers between devices with their start and end apart: 2, of which 2 were waited for; matrix products, arithmetic and copies ran while one was open for 0% of the time, Pallas kernels for 0%

commit v1 on v0

v1 whole, which is shorter than its diff:
```python
import jax
import jax.numpy as jnp
from jax import lax
from jax.sharding import Mesh, PartitionSpec as P

beta_one = 0.9
beta_two = 0.95
epsilon = 1e-08
learn_rate = 0.02
decay_rate = 0.1

D = 3072
LB = 48
HB = 192
NX = 8
NZ = 8
NY = 4
TOK = 1024
PIECES = 4
Z_PIECE = NZ // PIECES
WIDTH = D // PIECES
ROW = ("z", "yl", "c")
COL = ("yh", "x")


def hi_dot(left_mat, right_mat):
    return jnp.dot(left_mat, right_mat, precision=lax.Precision.HIGHEST)


def own_half(attn_out):
    yh = lax.axis_index("yh")
    keep = lax.dynamic_slice_in_dim(attn_out, yh * TOK, TOK, 0)
    send = lax.dynamic_slice_in_dim(attn_out, (1 - yh) * TOK, TOK, 0)
    came = lax.ppermute(send, "yh", [(0, 1), (1, 0)])
    first = yh == 0
    return jnp.where(first, keep, came), jnp.where(first, came, keep)


def piece_sum(gathered, halves, gate_rows):
    core = lax.axis_index("c")
    parts = []
    for half in halves:
        product = lax.dot_general(
            gathered, half, (((0,), (0,)), ((), ())), preferred_element_type=jnp.float32
        )
        product = gate_rows[:, None] * product
        parts.append(product.reshape(Z_PIECE, NY, 2, LB, HB).transpose(2, 1, 0, 3, 4))
    both = jnp.stack(parts, axis=1)
    mine = lax.dynamic_index_in_dim(both, core, 0, keepdims=False)
    other = lax.dynamic_index_in_dim(both, 1 - core, 0, keepdims=False)
    paired = mine + lax.ppermute(other, "c", [(0, 1), (1, 0)])
    paired = paired.reshape(2 * NY, Z_PIECE, LB, HB)
    return jnp.sum(lax.all_to_all(paired, ("yh", "yl"), 0, 0), axis=0)


def local(
    attn_out,
    cotangent,
    gate,
    weight,
    exp_avg,
    exp_avg_sq,
    left_stats,
    right_stats,
    left_basis,
    right_basis,
):
    gate_row = gate[0]
    spans = [slice(at * WIDTH, (at + 1) * WIDTH) for at in range(PIECES)]
    gathered = [lax.all_gather(cotangent[:, span], "x", axis=0, tiled=True) for span in spans]
    halves = own_half(attn_out)
    by_z = [piece_sum(got, halves, gate_row[span]) for got, span in zip(gathered, spans)]
    by_z = jnp.concatenate(by_z, axis=0)
    gradient = jnp.sum(lax.all_to_all(by_z, "z", 0, 0), axis=0)

    left_new = beta_two * left_stats + (1.0 - beta_two) * hi_dot(gradient, gradient.T)
    right_new = beta_two * right_stats + (1.0 - beta_two) * hi_dot(gradient.T, gradient)
    moment = beta_one * exp_avg + (1.0 - beta_one) * gradient

    def rotate_in(matrix):
        return hi_dot(hi_dot(left_basis.T, matrix), right_basis)

    rotated = rotate_in(gradient)
    second = beta_two * exp_avg_sq + (1.0 - beta_two) * rotated * rotated
    direction = rotate_in(moment) / (jnp.sqrt(second) + epsilon)
    update = hi_dot(hi_dot(left_basis, direction), right_basis.T)
    new_weight = weight * (1.0 - learn_rate * decay_rate) - learn_rate * update
    return (update, new_weight, moment, second, left_new, right_new)


def solution(mesh):
    fine = Mesh(mesh.devices.reshape(2, NX, NZ, NY, 2), ("yh", "x", "z", "yl", "c"))
    block = P(ROW, COL)
    in_specs = (block, P(COL + ROW, None), P(ROW, None)) + (block,) * 7
    return jax.shard_map(
        local, mesh=fine, in_specs=in_specs, out_specs=(block,) * 6, check_vma=False
    )
```

time: 605 us -> 324 us (0.54)
  waiting for transfers between devices: 567 us -> 189 us
  starting transfers between devices: 0.08 us -> 51.1 us
  blocking collectives: 0 us -> 18.7 us
  local copies, waits for them, and re-layouts: 0.05 us -> 17 us
  other arithmetic: 0.81 us -> 12.6 us
    reduce_scatter x1 -> x0, waiting for transfers between devices: 280 us -> none  [local(): lax.psum_scatter(gate_row[:, None] * product, 'dp', scatter_dimension=0,...]
    all_gather x1 -> x4, waiting for transfers between devices: 286 us -> 141 us  [local(): lax.all_gather(cotangent[:, span], 'x', axis=0, tiled=True)]
    all_to_all x0 -> x4, waiting for transfers between devices: none -> 36.8 us  [piece_sum(): return jnp.sum(lax.all_to_all(paired, ('yh', 'yl'), 0, 0), axis=0)]
    ppermute x0 -> x5, starting transfers between devices: none -> 30.8 us  [the longest x4 22 us: piece_sum(): paired = mine + lax.ppermute(other, 'c', [(0, 1), (1, 0)])]
    all_to_all x0 -> x4, starting transfers between devices: none -> 20.2 us  [piece_sum(): return jnp.sum(lax.all_to_all(paired, ('yh', 'yl'), 0, 0), axis=0)]
    all_to_all x0 -> x1, blocking collectives: none -> 18.7 us  [local(): gradient = jnp.sum(lax.all_to_all(by_z, 'z', 0, 0), axis=0)]
    mul x0 -> x8, local copies, waits for them, and re-layouts: none -> 11.7 us  [piece_sum(): product = gate_rows[:, None] * product]
    ppermute x0 -> x5, waiting for transfers between devices: none -> 10.4 us  [the longest x1 6.65 us: own_half(): came = lax.ppermute(send, 'yh', [(0, 1), (1, 0)])]
  transfers between devices with their start and end apart: 2 -> 13, of which waited for: 2 -> 10; matrix products, arithmetic and copies ran while one was open for 0% -> 12% of each run, Pallas kernels for 0% -> 0%
where the time goes in v1:
time: 324 us; the launch traced here: 320 us
  waiting for transfers between devices  189 us (58%)
  starting transfers between devices  51.1 us (16%)
  blocking collectives  18.7 us (6%)
  local copies, waits for them, and re-layouts  17 us (5%)
  matrix products  17 us (5%)
  between operations  14.2 us (4%)
  other arithmetic  12.6 us (4%)
    all_gather x4, waiting for transfers between devices, local(): lax.all_gather(cotangent[:, span], 'x', axis=0, tiled=True)  141 us
    all_to_all x4, waiting for transfers between devices, piece_sum(): return jnp.sum(lax.all_to_all(paired, ('yh', 'yl'), 0, 0), axis=0)  36.8 us
    ppermute x4, starting transfers between devices, piece_sum(): paired = mine + lax.ppermute(other, 'c', [(0, 1), (1, 0)])  22 us
    all_to_all x4, starting transfers between devices, piece_sum(): return jnp.sum(lax.all_to_all(paired, ('yh', 'yl'), 0, 0), axis=0)  20.2 us
    all_to_all x1, blocking collectives, local(): gradient = jnp.sum(lax.all_to_all(by_z, 'z', 0, 0), axis=0)  18.7 us
    dot_general x8, matrix products, piece_sum(): lax.dot_general(gathered, half, (((0,), (0,)), ((), ())), preferred_eleme...  13.1 us
    mul x8, local copies, waits for them, and re-layouts, piece_sum(): product = gate_rows[:, None] * product  11.7 us
    ppermute x1, starting transfers between devices, own_half(): came = lax.ppermute(send, 'yh', [(0, 1), (1, 0)])  8.74 us
  transfers between devices with their start and end apart: 13, of which 10 were waited for; matrix products, arithmetic and copies ran while one was open for 12% of the time, Pallas kernels for 0%

profile of v1, /device:TPU:1, one launch (start us, length us, event | category | flops | bytes accessed | tf_op | source)
XLA Modules:
  0.0 319.6 jit_solution(17075480748619982837)
XLA Ops:
  7.2 2.2 fusion.19
  11.1 8.7 %collective-permute-start = (bf16[1024,192]{0,1:T(8,128)(2,1)S(1)}, bf16[1024,192]{0,1:T(8,128)(2,1)S(1)}, u32[]{:S(2)}, u32[]{:S(2)}) collective-permute-start(bf16[1024,192]{0,1:T(8,128)(2,1)S(1)} %constant_dynamic-slice_fusion), channel_id=1, source_target_pairs={{0,512},{512,0},{1,513},{513,1},{2,514},{514,2},{3,515},{515,3},{4... | collective-permute-start | bytes 1179656 | tf_op jit(solution)/shard_map/ppermute | solution.py:34
  19.9 6.7 %collective-permute-done = bf16[1024,192]{0,1:T(8,128)(2,1)S(1)} collective-permute-done((bf16[1024,192]{0,1:T(8,128)(2,1)S(1)}, bf16[1024,192]{0,1:T(8,128)(2,1)S(1)}, u32[]{:S(2)}, u32[]{:S(2)}) %collective-permute-start) | collective-permute-done | bytes 393248 | tf_op jit(solution)/shard_map/ppermute | solution.py:34
  26.8 37.1 %all-gather.7.cloned.1.call-done = bf16[1024,768]{1,0:T(8,128)(2,1)} async-done(((bf16[128,768]{1,0:T(8,128)(2,1)}), bf16[1024,768]{1,0:T(8,128)(2,1)}) %all-gather.7.cloned.1.call-update) | async-done | bytes 1572880 | tf_op jit(solution)/shard_map/all_gather | solution.py:70
  63.8 2.0 fusion.5
  68.7 43.1 %all-gather.5.cloned.1.call-done = bf16[1024,768]{1,0:T(8,128)(2,1)} async-done(((bf16[128,768]{1,0:T(8,128)(2,1)}), bf16[1024,768]{1,0:T(8,128)(2,1)}) %all-gather.5.cloned.1.call-update) | async-done | bytes 1572880 | tf_op jit(solution)/shard_map/all_gather | solution.py:70
  111.8 2.0 fusion.7
  116.6 2.6 fusion.15
  119.2 6.7 %collective-permute-start.1 = (f32[2,4,2,48,192]{4,3,2,1,0:T(8,128)S(1)}, f32[2,4,2,48,192]{4,3,2,1,0:T(8,128)S(1)}, u32[]{:S(2)}, u32[]{:S(2)}) collective-permute-start(f32[2,4,2,48,192]{4,3,2,1,0:T(8,128)S(1)} %bitcast.122), channel_id=1, source_target_pairs={{0,1},{1,0},{2,3},{3,2},{4,5},{5,4},{6,7},{7,6},{8,9},{9,8},{10,11... | collective-permute-start | bytes 1769480 | tf_op jit(solution)/shard_map/ppermute | solution.py:51
  126.8 1.9 collective-permute-start.2
  128.7 30.4 %all-gather.9.cloned.1.call-done = bf16[1024,768]{1,0:T(8,128)(2,1)} async-done(((bf16[128,768]{1,0:T(8,128)(2,1)}), bf16[1024,768]{1,0:T(8,128)(2,1)}) %all-gather.9.cloned.1.call-update) | async-done | bytes 1572880 | tf_op jit(solution)/shard_map/all_gather | solution.py:70
  159.1 2.7 fusion.3
  162.7 2.2 bitcast_add_fusion.3
  165.0 6.6 %all-to-all-start = ((f32[8,2,48,192]{3,2,1,0:T(8,128)}), f32[8,2,48,192]{3,2,1,0:T(8,128)S(1)}, u32[]{:S(2)}, u32[]{:S(2)}) async-start(f32[8,2,48,192]{3,2,1,0:T(8,128)} %bitcast.112), calls=%async_computation | async-start | bytes 1572864 | tf_op jit(solution)/shard_map/all_to_all | solution.py:53
  172.8 2.3 copy.48
  176.3 30.0 %all-gather.11.cloned.1.call-done = bf16[1024,768]{1,0:T(8,128)(2,1)} async-done(((bf16[128,768]{1,0:T(8,128)(2,1)}), bf16[1024,768]{1,0:T(8,128)(2,1)}) %all-gather.11.cloned.1.call-update) | async-done | bytes 1572880 | tf_op jit(solution)/shard_map/all_gather | solution.py:70
  206.3 2.8 fusion.1
  209.1 2.2 copy.52
  212.7 2.3 copy.53
  215.0 2.2 bitcast_add_fusion.2
  217.1 6.5 %all-to-all-start.1 = ((f32[8,2,48,192]{3,2,1,0:T(8,128)}), f32[8,2,48,192]{3,2,1,0:T(8,128)S(1)}, u32[]{:S(2)}, u32[]{:S(2)}) async-start(f32[8,2,48,192]{3,2,1,0:T(8,128)} %bitcast.21), calls=%async_computation.1 | async-start | bytes 1572864 | tf_op jit(solution)/shard_map/all_to_all | solution.py:53
  223.7 3.1 fusion.11
  226.8 6.9 %collective-permute-start.3 = (f32[2,4,2,48,192]{4,3,2,1,0:T(8,128)S(1)}, f32[2,4,2,48,192]{4,3,2,1,0:T(8,128)S(1)}, u32[]{:S(2)}, u32[]{:S(2)}) collective-permute-start(f32[2,4,2,48,192]{4,3,2,1,0:T(8,128)S(1)} %bitcast.123), channel_id=1, source_target_pairs={{0,1},{1,0},{2,3},{3,2},{4,5},{5,4},{6,7},{7,6},{8,9},{9,8},{10,11... | collective-permute-start | bytes 1769480 | tf_op jit(solution)/shard_map/ppermute | solution.py:51
  233.7 1.9 collective-permute-done.3
  236.7 6.6 %all-to-all-done.1 = f32[8,2,48,192]{3,2,1,0:T(8,128)S(1)} async-done(((f32[8,2,48,192]{3,2,1,0:T(8,128)}), f32[8,2,48,192]{3,2,1,0:T(8,128)S(1)}, u32[]{:S(2)}, u32[]{:S(2)}) %all-to-all-start.1) | async-done | bytes 589856 | tf_op jit(solution)/shard_map/all_to_all | solution.py:53
  243.3 3.5 %all-to-all-start.2 = ((f32[8,2,48,192]{3,2,1,0:T(8,128)}), f32[8,2,48,192]{3,2,1,0:T(8,128)S(1)}, u32[]{:S(2)}, u32[]{:S(2)}) async-start(f32[8,2,48,192]{3,2,1,0:T(8,128)} %bitcast.32), calls=%async_computation.2 | async-start | bytes 1572864 | tf_op jit(solution)/shard_map/all_to_all | solution.py:53
  246.9 6.5 %collective-permute-start.4 = (f32[2,4,2,48,192]{4,3,2,1,0:T(8,128)S(1)}, f32[2,4,2,48,192]{4,3,2,1,0:T(8,128)S(1)}, u32[]{:S(2)}, u32[]{:S(2)}) collective-permute-start(f32[2,4,2,48,192]{4,3,2,1,0:T(8,128)S(1)} %bitcast.124), channel_id=1, source_target_pairs={{0,1},{1,0},{2,3},{3,2},{4,5},{5,4},{6,7},{7,6},{8,9},{9,8},{10,11... | collective-permute-start | bytes 1769480 | tf_op jit(solution)/shard_map/ppermute | solution.py:51
  253.4 1.9 collective-permute-done.4
  256.4 10.5 %all-to-all-done.2 = f32[8,2,48,192]{3,2,1,0:T(8,128)S(1)} async-done(((f32[8,2,48,192]{3,2,1,0:T(8,128)}), f32[8,2,48,192]{3,2,1,0:T(8,128)S(1)}, u32[]{:S(2)}, u32[]{:S(2)}) %all-to-all-start.2) | async-done | bytes 589856 | tf_op jit(solution)/shard_map/all_to_all | solution.py:53
  266.8 3.5 %all-to-all-start.3 = ((f32[8,2,48,192]{3,2,1,0:T(8,128)}), f32[8,2,48,192]{3,2,1,0:T(8,128)S(1)}, u32[]{:S(2)}, u32[]{:S(2)}) async-start(f32[8,2,48,192]{3,2,1,0:T(8,128)} %bitcast.113), calls=%async_computation.3 | async-start | bytes 1572864 | tf_op jit(solution)/shard_map/all_to_all | solution.py:53
  270.6 19.7 %all-to-all-done.3 = f32[8,2,48,192]{3,2,1,0:T(8,128)S(1)} async-done(((f32[8,2,48,192]{3,2,1,0:T(8,128)}), f32[8,2,48,192]{3,2,1,0:T(8,128)S(1)}, u32[]{:S(2)}, u32[]{:S(2)}) %all-to-all-start.3) | async-done | bytes 589856 | tf_op jit(solution)/shard_map/all_to_all | solution.py:53
  290.4 18.7 %all_to_all.25 = f32[8,48,192]{2,1,0:T(8,128)S(1)} all-to-all(f32[8,48,192]{2,1,0:T(8,128)S(1)} %pad_maximum_fusion), channel_id=1, replica_groups=mesh['yh'=2,'x'=8,'z'=8,'yl'=4,'c'=2] {'z'}, dimensions={0} | all-to-all | bytes 589824 | tf_op jit(solution)/shard_map/all_to_all | solution.py:74
  (84 shorter events, 19.6 us)
Async XLA Ops:
  7.2 302.5 %copy-start = (f32[192,192]{1,0:T(8,128)S(1)}, f32[192,192]{1,0:T(8,128)}, u32[]{:S(2)}) copy-start(f32[192,192]{1,0:T(8,128)} %param.19) | copy-start | bytes 442372
  7.2 3.8 %copy-start.9 = (bf16[2048,192]{0,1:T(8,128)(2,1)S(1)}, bf16[2048,192]{0,1:T(8,128)(2,1)}, u32[]{:S(2)}) copy-start(bf16[2048,192]{0,1:T(8,128)(2,1)} %param.10) | copy-start | bytes 2359300
  7.2 12.6 %copy-start.19 = (f32[1,3072]{1,0:T(1,128)S(1)}, f32[1,3072]{1,0:T(1,128)}, u32[]{:S(2)}) copy-start(f32[1,3072]{1,0:T(1,128)} %param.12) | copy-start | bytes 36868
  7.2 56.6 %all-gather.7.cloned.1.call-start = ((), (), s32[]{:S(2)}) async-start(), calls=%async_computation.6 | async-start | bytes 1769472 | tf_op jit(solution)/shard_map/all_gather | solution.py:70
  9.5 102.3 %all-gather.5.cloned.1.call-start = ((), (), s32[]{:S(2)}) async-start(), calls=%async_computation.5 | async-start | bytes 1769472 | tf_op jit(solution)/shard_map/all_gather | solution.py:70
  10.2 148.9 %all-gather.9.cloned.1.call-start = ((), (), s32[]{:S(2)}) async-start(), calls=%async_computation.7 | async-start | bytes 1769472 | tf_op jit(solution)/shard_map/all_gather | solution.py:70
  10.9 195.3 %all-gather.11.cloned.1.call-start = ((), (), s32[]{:S(2)}) async-start(), calls=%async_computation.8 | async-start | bytes 1769472 | tf_op jit(solution)/shard_map/all_gather | solution.py:70
  11.1 15.5 %collective-permute-start = (bf16[1024,192]{0,1:T(8,128)(2,1)S(1)}, bf16[1024,192]{0,1:T(8,128)(2,1)S(1)}, u32[]{:S(2)}, u32[]{:S(2)}) collective-permute-start(bf16[1024,192]{0,1:T(8,128)(2,1)S(1)} %constant_dynamic-slice_fusion), channel_id=1, source_target_pairs={{0,512},{512,0},{1,513},{513,1},{2,514},{514,2},{3,515},{515,3},{4... | collective-permute-start | bytes 1179656 | tf_op jit(solution)/shard_map/ppermute | solution.py:34
  63.8 3.2 copy-start.4
  111.8 3.2 copy-start.3
  115.4 1.1 copy-start.7
  119.2 42.6 %collective-permute-start.1 = (f32[2,4,2,48,192]{4,3,2,1,0:T(8,128)S(1)}, f32[2,4,2,48,192]{4,3,2,1,0:T(8,128)S(1)}, u32[]{:S(2)}, u32[]{:S(2)}) collective-permute-start(f32[2,4,2,48,192]{4,3,2,1,0:T(8,128)S(1)} %bitcast.122), channel_id=1, source_target_pairs={{0,1},{1,0},{2,3},{3,2},{4,5},{5,4},{6,7},{7,6},{8,9},{9,8},{10,11... | collective-permute-start | bytes 1769480 | tf_op jit(solution)/shard_map/ppermute | solution.py:51
  126.8 88.1 %collective-permute-start.2 = (f32[2,4,2,48,192]{4,3,2,1,0:T(8,128)}, f32[2,4,2,48,192]{4,3,2,1,0:T(8,128)}, u32[]{:S(2)}, u32[]{:S(2)}) collective-permute-start(f32[2,4,2,48,192]{4,3,2,1,0:T(8,128)} %bitcast.110), channel_id=1, source_target_pairs={{0,1},{1,0},{2,3},{3,2},{4,5},{5,4},{6,7},{7,6},{8,9},{9,8},{10,11... | collective-permute-start | bytes 1769480 | tf_op jit(solution)/shard_map/ppermute | solution.py:51
  162.7 8.8 %copy-start.1 = (bf16[1024,768]{1,0:T(8,128)(2,1)S(1)}, bf16[1024,768]{1,0:T(8,128)(2,1)}, u32[]{:S(2)}) copy-start(bf16[1024,768]{1,0:T(8,128)(2,1)} %all-gather.9.cloned.1.call-done) | copy-start | bytes 4718596
  165.0 52.2 %all-to-all-start = ((f32[8,2,48,192]{3,2,1,0:T(8,128)}), f32[8,2,48,192]{3,2,1,0:T(8,128)S(1)}, u32[]{:S(2)}, u32[]{:S(2)}) async-start(f32[8,2,48,192]{3,2,1,0:T(8,128)} %bitcast.112), calls=%async_computation | async-start | bytes 1572864 | tf_op jit(solution)/shard_map/all_to_all | solution.py:53
  172.8 2.3 copy-start.8
  206.3 5.1 %copy-start.2 = (bf16[1024,768]{1,0:T(8,128)(2,1)S(1)}, bf16[1024,768]{1,0:T(8,128)(2,1)}, u32[]{:S(2)}) copy-start(bf16[1024,768]{1,0:T(8,128)(2,1)} %all-gather.11.cloned.1.call-done) | copy-start | bytes 4718596
  212.7 2.3 copy-start.5
  217.1 26.2 %all-to-all-start.1 = ((f32[8,2,48,192]{3,2,1,0:T(8,128)}), f32[8,2,48,192]{3,2,1,0:T(8,128)S(1)}, u32[]{:S(2)}, u32[]{:S(2)}) async-start(f32[8,2,48,192]{3,2,1,0:T(8,128)} %bitcast.21), calls=%async_computation.1 | async-start | bytes 1572864 | tf_op jit(solution)/shard_map/all_to_all | solution.py:53
  226.8 8.8 %collective-permute-start.3 = (f32[2,4,2,48,192]{4,3,2,1,0:T(8,128)S(1)}, f32[2,4,2,48,192]{4,3,2,1,0:T(8,128)S(1)}, u32[]{:S(2)}, u32[]{:S(2)}) collective-permute-start(f32[2,4,2,48,192]{4,3,2,1,0:T(8,128)S(1)} %bitcast.123), channel_id=1, source_target_pairs={{0,1},{1,0},{2,3},{3,2},{4,5},{5,4},{6,7},{7,6},{8,9},{9,8},{10,11... | collective-permute-start | bytes 1769480 | tf_op jit(solution)/shard_map/ppermute | solution.py:51
  243.3 23.5 %all-to-all-start.2 = ((f32[8,2,48,192]{3,2,1,0:T(8,128)}), f32[8,2,48,192]{3,2,1,0:T(8,128)S(1)}, u32[]{:S(2)}, u32[]{:S(2)}) async-start(f32[8,2,48,192]{3,2,1,0:T(8,128)} %bitcast.32), calls=%async_computation.2 | async-start | bytes 1572864 | tf_op jit(solution)/shard_map/all_to_all | solution.py:53
  246.9 8.5 %copy-start.6 = (f32[1,2,4,2,48,192]{5,4,0,2,3,1:T(8,128)S(1)}, f32[1,2,4,2,48,192]{5,4,0,2,3,1:T(8,128)}, u32[]{:S(2)}) copy-start(f32[1,2,4,2,48,192]{5,4,0,2,3,1:T(8,128)} %get-tuple-element.16) | copy-start | bytes 1769476
  246.9 8.4 %collective-permute-start.4 = (f32[2,4,2,48,192]{4,3,2,1,0:T(8,128)S(1)}, f32[2,4,2,48,192]{4,3,2,1,0:T(8,128)S(1)}, u32[]{:S(2)}, u32[]{:S(2)}) collective-permute-start(f32[2,4,2,48,192]{4,3,2,1,0:T(8,128)S(1)} %bitcast.124), channel_id=1, source_target_pairs={{0,1},{1,0},{2,3},{3,2},{4,5},{5,4},{6,7},{7,6},{8,9},{9,8},{10,11... | collective-permute-start | bytes 1769480 | tf_op jit(solution)/shard_map/ppermute | solution.py:51
  266.8 23.5 %all-to-all-start.3 = ((f32[8,2,48,192]{3,2,1,0:T(8,128)}), f32[8,2,48,192]{3,2,1,0:T(8,128)S(1)}, u32[]{:S(2)}, u32[]{:S(2)}) async-start(f32[8,2,48,192]{3,2,1,0:T(8,128)} %bitcast.113), calls=%async_computation.3 | async-start | bytes 1572864 | tf_op jit(solution)/shard_map/all_to_all | solution.py:53
  270.6 38.6 %copy-start.11 = (f32[48,48]{1,0:T(8,128)S(1)}, f32[48,48]{1,0:T(8,128)}, u32[]{:S(2)}) copy-start(f32[48,48]{1,0:T(8,128)} %param.18) | copy-start | bytes 27652
  270.6 38.8 %copy-start.16 = (f32[48,192]{1,0:T(8,128)S(1)}, f32[48,192]{1,0:T(8,128)}, u32[]{:S(2)}) copy-start(f32[48,192]{1,0:T(8,128)} %param.14) | copy-start | bytes 110596
  270.6 39.1 %copy-start.17 = (f32[48,192]{1,0:T(8,128)S(1)}, f32[48,192]{1,0:T(8,128)}, u32[]{:S(2)}) copy-start(f32[48,192]{1,0:T(8,128)} %param.15) | copy-start | bytes 110596
  290.4 20.0 %copy-start.12 = (f32[192,192]{1,0:T(8,128)S(1)}, f32[192,192]{1,0:T(8,128)}, u32[]{:S(2)}) copy-start(f32[192,192]{1,0:T(8,128)} %param.17) | copy-start | bytes 442372
  290.4 21.0 %copy-start.18 = (f32[48,48]{1,0:T(8,128)S(1)}, f32[48,48]{1,0:T(8,128)}, u32[]{:S(2)}) copy-start(f32[48,48]{1,0:T(8,128)} %param.16) | copy-start | bytes 27652
  290.4 21.7 %copy-start.15 = (f32[48,192]{1,0:T(8,128)S(1)}, f32[48,192]{1,0:T(8,128)}, u32[]{:S(2)}) copy-start(f32[48,192]{1,0:T(8,128)} %param.13) | copy-start | bytes 110596
  309.4 3.7 %copy-start.13 = (f32[48,192]{1,0:T(8,128)}, f32[48,192]{1,0:T(8,128)S(1)}, u32[]{:S(2)}) copy-start(f32[48,192]{1,0:T(8,128)S(1)} %multiply_add_fusion) | copy-start | bytes 110596
  309.9 3.2 %copy-start.14 = (f32[48,192]{1,0:T(8,128)}, f32[48,192]{1,0:T(8,128)S(1)}, u32[]{:S(2)}) copy-start(f32[48,192]{1,0:T(8,128)S(1)} %fusion.18) | copy-start | bytes 110596
  (1 other events, 0.9 us)
Sparse Core Ops, SparseCore 0:
  10.7 53.0 all-gather.6
  67.1 44.6 all-gather.4
  114.4 44.6 all-gather.8
  161.6 44.6 all-gather.10

commit v2 on v1

v2 whole, which is shorter than its diff:
```python
import functools

import jax
import jax.numpy as jnp
from jax import lax
from jax.experimental import pallas as pl
from jax.experimental.pallas import tpu as pltpu
from jax.sharding import Mesh, PartitionSpec as P

beta_one = 0.9
beta_two = 0.95
epsilon = 1e-08
learn_rate = 0.02
decay_rate = 0.1

D = 3072
LB = 48
HB = 192
NX = 8
NZ = 8
NY = 4
CHUNK = 128
TOK = NX * CHUNK
FEAT = 2 * HB
GROUP = D // NZ
HALF = LB // 2
PACK = (LB * HB) // 128
PIECES = (2, 2, 2, 2)
ROW = ("z", "yl", "c")
COL = ("yh", "x")
Y = ("yh", "yl")
SWAP = [(0, 1), (1, 0)]
RING = [(2 * x + c, 2 * ((x + (1, -1)[c]) % NX) + c) for x in range(NX) for c in range(2)]


def product_kernel(
    place, att_own, att_oth, first, hop_one, hop_two, hop_three, last, gate_own, gate_oth, keep, send
):
    def term(att, at, block):
        columns = pl.ds(pl.multiple_of(place[1 + at] * CHUNK, CHUNK), CHUNK)
        return jnp.dot(att[:, columns], block, preferred_element_type=jnp.float32)

    own = term(att_own, 0, first[0]) + term(att_own, 4, last[...])
    oth = jnp.zeros_like(own)
    for at, hop in ((1, hop_one), (2, hop_two), (3, hop_three)):
        own += term(att_own, at, hop[0])
        oth += term(att_oth, at, hop[1])
    total = gate_own[...] * own + gate_oth[...] * oth
    packed = []
    for yh in range(2):
        at = yh * HB
        rest = total[at + 128 : at + HB]
        moved = pltpu.roll(rest, GROUP - HALF, 1)
        packed.append((total[at : at + 128].T, jnp.concatenate([rest, moved], axis=0).T))

    def store(ref, core):
        for yh in range(2):
            for yl in range(NY):
                at = (2 * yl + core) * LB
                ref[NY * yh + yl, 0, :LB] = packed[yh][0][at : at + LB]
                ref[NY * yh + yl, 0, LB:] = packed[yh][1][at : at + HALF]

    for core in range(2):

        @pl.when(place[0] == core)
        def _():
            store(keep, core)
            store(send, 1 - core)


def product(place, att_own, att_oth, blocks, gate_own, gate_oth):
    count = gate_own.shape[1] // GROUP
    whole = pl.BlockSpec((FEAT, TOK), lambda z: (0, 0))
    pair = pl.BlockSpec((2, CHUNK, GROUP), lambda z: (0, 0, z))
    row = pl.BlockSpec((1, GROUP), lambda z: (0, z))
    out = pl.BlockSpec((2 * NY, 1, PACK, 128), lambda z: (0, z, 0, 0))
    shape = jax.ShapeDtypeStruct((2 * NY, count, PACK, 128), jnp.float32)
    flops = 2 * 8 * CHUNK * FEAT * GROUP * count
    return pl.pallas_call(
        product_kernel,
        grid=(count,),
        in_specs=[pl.BlockSpec(memory_space=pltpu.SMEM), whole, whole, pair, pair, pair, pair]
        + [pl.BlockSpec((CHUNK, GROUP), lambda z: (0, z)), row, row],
        out_specs=[out, out],
        out_shape=[shape, shape],
        cost_estimate=pl.CostEstimate(flops=flops, bytes_accessed=6 << 20, transcendentals=0),
        compiler_params=pltpu.CompilerParams(vmem_limit_bytes=24 << 20),
        name="product",
    )(place, att_own, att_oth, *blocks, gate_own, gate_oth)


def update_kernel(
    parts,
    weight,
    exp_avg,
    exp_avg_sq,
    left_stats,
    right_stats,
    left_basis,
    right_basis,
    update,
    new_weight,
    moment_out,
    second_out,
    left_new,
    right_new,
):
    def dot(left, right, dims):
        return lax.dot_general(
            left,
            right,
            (dims, ((), ())),
            precision=lax.Precision.HIGHEST,
            preferred_element_type=jnp.float32,
        )

    plain, first, last = ((1,), (0,)), ((0,), (0,)), ((1,), (1,))
    packed = jnp.sum(parts[...], axis=0)
    rest = jnp.concatenate([packed[LB:, : HB - 128], packed[LB:, HB - 128 :]], axis=0)
    gradient = jnp.concatenate([packed[:LB], rest], axis=1)
    left_q, right_q = left_basis[...], right_basis[...]
    moment = beta_one * exp_avg[...] + (1.0 - beta_one) * gradient
    moment_out[...] = moment
    rotated = dot(dot(left_q, gradient, first), right_q, plain)
    second = beta_two * exp_avg_sq[...] + (1.0 - beta_two) * rotated * rotated
    second_out[...] = second
    turned = dot(dot(left_q, moment, first), right_q, plain)
    direction = turned / (jnp.sqrt(second) + epsilon)
    step = dot(dot(left_q, direction, plain), right_q, last)
    update[...] = step
    new_weight[...] = weight[...] * (1.0 - learn_rate * decay_rate) - learn_rate * step
    left_new[...] = beta_two * left_stats[...] + (1.0 - beta_two) * dot(gradient, gradient, last)
    right_new[...] = beta_two * right_stats[...] + (1.0 - beta_two) * dot(gradient, gradient, first)


def local(
    attn_out,
    cotangent,
    gate,
    weight,
    exp_avg,
    exp_avg_sq,
    left_stats,
    right_stats,
    left_basis,
    right_basis,
):
    yh, x, core = lax.axis_index("yh"), lax.axis_index("x"), lax.axis_index("c")
    step = 1 - 2 * core
    place = jnp.stack([core] + [lax.rem(x - step * hop + NX, NX) for hop in range(5)])

    spans, at = [], 0
    for count in PIECES:
        spans.append(slice(at, at + count * GROUP))
        at += count * GROUP
    rings = []
    for span in spans:
        own = cotangent[:, span]
        blocks = [jnp.stack([own, lax.ppermute(own, "c", SWAP)])]
        for _ in range(3):
            blocks.append(lax.ppermute(blocks[-1], ("x", "c"), RING))
        blocks.append(lax.ppermute(blocks[-1][0], ("x", "c"), RING))
        rings.append(blocks)

    features = attn_out.T
    kept = lax.dynamic_slice_in_dim(features, yh * TOK, TOK, 1)
    came = lax.ppermute(
        lax.dynamic_slice_in_dim(features, (1 - yh) * TOK, TOK, 1), "yh", SWAP
    )
    att_own = jnp.concatenate(
        [jnp.where(yh == 0, kept, came), jnp.where(yh == 0, came, kept)], axis=0
    )
    att_oth = lax.ppermute(att_own, "c", SWAP)
    gate_oth = lax.ppermute(gate, "c", SWAP)

    by_z = []
    for span, blocks in zip(spans, rings):
        keep, send = product(
            place, att_own, att_oth, blocks, gate[:, span], gate_oth[:, span]
        )
        paired = keep + lax.ppermute(send, "c", SWAP)
        by_z.append(jnp.sum(lax.all_to_all(paired, Y, 0, 0), axis=0))
    parts = lax.all_to_all(jnp.concatenate(by_z, axis=0), "z", 0, 0)

    block = jax.ShapeDtypeStruct((LB, HB), jnp.float32)
    return pl.pallas_call(
        update_kernel,
        out_shape=[block] * 4
        + [
            jax.ShapeDtypeStruct((LB, LB), jnp.float32),
            jax.ShapeDtypeStruct((HB, HB), jnp.float32),
        ],
        name="update",
    )(parts, weight, exp_avg, exp_avg_sq, left_stats, right_stats, left_basis, right_basis)


def solution(mesh):
    fine = Mesh(mesh.devices.reshape(2, NX, NZ, NY, 2), ("yh", "x", "z", "yl", "c"))
    block = P(ROW, COL)
    in_specs = (block, P(COL + ROW, None), P(ROW, None)) + (block,) * 7
    return jax.shard_map(
        local, mesh=fine, in_specs=in_specs, out_specs=(block,) * 6, check_vma=False
    )
```

time: 324 us -> 215 us (0.66)
  waiting for transfers between devices: 189 us -> 40.2 us
  starting transfers between devices: 51.1 us -> 113 us
  matrix products: 17 us -> 0 us
  Pallas kernels: 0 us -> 16.7 us
  between operations: 14.2 us -> 1.22 us
  local copies, waits for them, and re-layouts: 17 us -> 6.96 us
  blocking collectives: 18.7 us -> 27.8 us
  other arithmetic: 12.6 us -> 7.37 us
    all_gather x4 -> x0, waiting for transfers between devices: 141 us -> none  [local(): lax.all_gather(cotangent[:, span], 'x', axis=0, tiled=True)]
    ppermute x5 -> x27, starting transfers between devices: 30.8 us -> 90.1 us  [the longest x12 33.5 us: local(): blocks.append(lax.ppermute(blocks[-1], ('x', 'c'), RING))]
    all_to_all x4, waiting for transfers between devices: 36.8 us -> 17.7 us  [local(): by_z.append(jnp.sum(lax.all_to_all(paired, Y, 0, 0), axis=0))]
    dot_general x16 -> x0, matrix products: 17 us -> none  [the longest x8 13.1 us: piece_sum(): lax.dot_general(gathered, half, (((0,), (0,)), ((), ())), preferred_eleme...]
    pallas_call x0 -> x5, Pallas kernels: none -> 16.7 us  [the longest x4 13.5 us: product(): pl.pallas_call(product_kernel, grid=(count,), in_specs=[pl.BlockSpec(memo...]
    ppermute x5 -> x27, waiting for transfers between devices: 10.4 us -> 22.5 us  [the longest x4 9.51 us: local(): blocks.append(lax.ppermute(blocks[-1][0], ('x', 'c'), RING))]
    mul x8 -> x0, local copies, waits for them, and re-layouts: 11.7 us -> none  [piece_sum(): product = gate_rows[:, None] * product]
    all_to_all x1, blocking collectives: 18.7 us -> 27.8 us  [local(): parts = lax.all_to_all(jnp.concatenate(by_z, axis=0), 'z', 0, 0)]
  transfers between devices with their start and end apart: 13 -> 31, of which waited for: 10 -> 9; matrix products, arithmetic and copies ran while one was open for 12% -> 5% of each run, Pallas kernels for 0% -> 6%
where the time goes in v2:
time: 215 us; the launch traced here: 214 us
  starting transfers between devices  113 us (53%)
  waiting for transfers between devices  40.2 us (19%)
  blocking collectives  27.8 us (13%)
  Pallas kernels  16.7 us (8%)
  other arithmetic  7.37 us (3%)
  local copies, waits for them, and re-layouts  6.96 us (3%)
    ppermute x12, starting transfers between devices, local(): blocks.append(lax.ppermute(blocks[-1], ('x', 'c'), RING))  33.5 us
    all_to_all x1, blocking collectives, local(): parts = lax.all_to_all(jnp.concatenate(by_z, axis=0), 'z', 0, 0)  27.8 us
    all_to_all x4, starting transfers between devices, local(): by_z.append(jnp.sum(lax.all_to_all(paired, Y, 0, 0), axis=0))  23.2 us
    ppermute x4, starting transfers between devices, local(): blocks = [jnp.stack([own, lax.ppermute(own, 'c', SWAP)])]  22.3 us
    ppermute x4, starting transfers between devices, local(): paired = keep + lax.ppermute(send, 'c', SWAP)  18.6 us
    all_to_all x4, waiting for transfers between devices, local(): by_z.append(jnp.sum(lax.all_to_all(paired, Y, 0, 0), axis=0))  17.7 us
    pallas_call x4, Pallas kernels, product(): pl.pallas_call(product_kernel, grid=(count,), in_specs=[pl.BlockSpec(memo...  13.5 us
    ppermute x4, waiting for transfers between devices, local(): blocks.append(lax.ppermute(blocks[-1][0], ('x', 'c'), RING))  9.51 us
  transfers between devices with their start and end apart: 31, of which 9 were waited for; matrix products, arithmetic and copies ran while one was open for 5% of the time, Pallas kernels for 6%

profile of v2, /device:TPU:1, one launch (start us, length us, event | category | flops | bytes accessed | tf_op | source)
XLA Modules:
  0.0 213.5 jit_solution(10394473324083499921)
XLA Ops:
  0.6 2.1 slice_bitcast_fusion.7
  2.8 16.2 %collective-permute-start.2 = (bf16[128,768]{1,0:T(8,128)(2,1)S(1)}, bf16[128,768]{1,0:T(8,128)(2,1)S(1)}, u32[]{:S(2)}, u32[]{:S(2)}) collective-permute-start(bf16[128,768]{1,0:T(8,128)(2,1)S(1)} %get-tuple-element.29), channel_id=1, source_target_pairs={{0,1},{1,0},{2,3},{3,2},{4,5},{5,4},{6,7},{7,6},{8,9},{9,8},{10,11... | collective-permute-start | bytes 589832 | tf_op jit(solution)/shard_map/ppermute | solution.py:159
  24.1 2.3 %collective-permute-start.9 = (bf16[128,768]{1,0:T(8,128)(2,1)S(1)}, bf16[128,768]{1,0:T(8,128)(2,1)S(1)}, u32[]{:S(2)}, u32[]{:S(2)}) collective-permute-start(bf16[128,768]{1,0:T(8,128)(2,1)S(1)} %get-tuple-element.28), channel_id=1, source_target_pairs={{0,1},{1,0},{2,3},{3,2},{4,5},{5,4},{6,7},{7,6},{8,9},{9,8},{10,11... | collective-permute-start | bytes 589832 | tf_op jit(solution)/shard_map/ppermute | solution.py:159
  26.4 2.5 %collective-permute-done.3.hop_one = bf16[2,128,768]{2,1,0:T(8,128)(2,1)S(1)} collective-permute-done((bf16[2,128,768]{2,1,0:T(8,128)(2,1)S(1)}, bf16[2,128,768]{2,1,0:T(8,128)(2,1)S(1)}, u32[]{:S(2)}, u32[]{:S(2)}) %collective-permute-start.3) | collective-permute-done | bytes 393248 | tf_op jit(solution)/shard_map/ppermute | solution.py:161
  28.8 2.8 %collective-permute-start.4 = (bf16[2,128,768]{2,1,0:T(8,128)(2,1)S(1)}, bf16[2,128,768]{2,1,0:T(8,128)(2,1)}, u32[]{:S(2)}, u32[]{:S(2)}) collective-permute-start(bf16[2,128,768]{2,1,0:T(8,128)(2,1)S(1)} %collective-permute-done.3.hop_one), channel_id=1, source_target_pairs={{0,64},{1,449},{64,128},{65,1},{128,192},{129,65},{192,256},{193,1... | collective-permute-start | bytes 1179656 | tf_op jit(solution)/shard_map/ppermute | solution.py:161
  33.7 7.8 %collective-permute-done = bf16[192,1024]{1,0:T(8,128)(2,1)S(1)} collective-permute-done((bf16[192,1024]{1,0:T(8,128)(2,1)S(1)}, bf16[192,1024]{1,0:T(8,128)(2,1)S(1)}, u32[]{:S(2)}, u32[]{:S(2)}) %collective-permute-start) | collective-permute-done | bytes 393248 | tf_op jit(solution)/shard_map/ppermute | solution.py:167
  43.7 2.4 %collective-permute-start.1 = (bf16[384,1024]{1,0:T(8,128)(2,1)S(1)}, bf16[384,1024]{1,0:T(8,128)(2,1)S(1)}, u32[]{:S(2)}, u32[]{:S(2)}) collective-permute-start(bf16[384,1024]{1,0:T(8,128)(2,1)S(1)} %pad_maximum_fusion.att_own), channel_id=1, source_target_pairs={{0,1},{1,0},{2,3},{3,2},{4,5},{5,4},{6,7},{7,6},{8,9},{9,8},{10,11... | collective-permute-start | bytes 2359304 | tf_op jit(solution)/shard_map/ppermute | solution.py:173
  49.5 4.8 %collective-permute-start.11 = (bf16[2,128,768]{2,1,0:T(8,128)(2,1)S(1)}, bf16[2,128,768]{2,1,0:T(8,128)(2,1)}, u32[]{:S(2)}, u32[]{:S(2)}) collective-permute-start(bf16[2,128,768]{2,1,0:T(8,128)(2,1)S(1)} %collective-permute-done.10.hop_one), channel_id=1, source_target_pairs={{0,64},{1,449},{64,128},{65,1},{128,192},{129,65},{192,256},{193,1... | collective-permute-start | bytes 1179656 | tf_op jit(solution)/shard_map/ppermute | solution.py:161
  57.6 3.5 %collective-permute-done.6.last = bf16[128,768]{1,0:T(8,128)(2,1)S(1)} collective-permute-done((bf16[128,768]{1,0:T(8,128)(2,1)S(1)}, bf16[128,768]{1,0:T(8,128)(2,1)S(1)}, u32[]{:S(2)}, u32[]{:S(2)}) %collective-permute-start.6) | collective-permute-done | bytes 196640 | tf_op jit(solution)/shard_map/ppermute | solution.py:162
  61.2 3.4 %product.4 = (f32[8,2,72,128]{3,2,1,0:T(8,128)S(1)}, f32[8,2,72,128]{3,2,1,0:T(8,128)S(1)}) custom-call(s32[6]{0:T(128)S(1)} %stack.63.place, bf16[384,1024]{1,0:T(8,128)(2,1)S(1)} %pad_maximum_fusion.att_own, bf16[384,1024]{1,0:T(8,128)(2,1)S(1)} %collective-permute-done.1.att_oth, bf16[2,128,768]{2,1,0:T(8,128)(2,1)S(1)} %pad_maximum_fusion.1.first, ...), custom_call_target="tpu_custom_call" | custom-call | flops 603979776 | bytes 6291456 | tf_op jit(solution)/shard_map/product/pallas_call | solution.py:79
  64.6 3.7 %collective-permute-start.8 = (f32[8,2,72,128]{3,2,1,0:T(8,128)S(1)}, f32[8,2,72,128]{3,2,1,0:T(8,128)S(1)}, u32[]{:S(2)}, u32[]{:S(2)}) collective-permute-start(f32[8,2,72,128]{3,2,1,0:T(8,128)S(1)} %get-tuple-element.15), channel_id=1, source_target_pairs={{0,1},{1,0},{2,3},{3,2},{4,5},{5,4},{6,7},{7,6},{8,9},{9,8},{10,11... | collective-permute-start | bytes 1769480 | tf_op jit(solution)/shard_map/ppermute | solution.py:181
  70.3 3.7 %collective-permute-start.12 = (bf16[2,128,768]{2,1,0:T(8,128)(2,1)}, bf16[2,128,768]{2,1,0:T(8,128)(2,1)S(1)}, u32[]{:S(2)}, u32[]{:S(2)}) collective-permute-start(bf16[2,128,768]{2,1,0:T(8,128)(2,1)} %collective-permute-done.11.hop_two), channel_id=1, source_target_pairs={{0,64},{1,449},{64,128},{65,1},{128,192},{129,65},{192,256},{193,1... | collective-permute-start | bytes 1179656 | tf_op jit(solution)/shard_map/ppermute | solution.py:161
  76.9 4.2 %all-to-all-start = ((f32[8,2,72,128]{3,2,1,0:T(8,128)}), f32[8,2,72,128]{3,2,1,0:T(8,128)}, u32[]{:S(2)}, u32[]{:S(2)}) async-start(f32[8,2,72,128]{3,2,1,0:T(8,128)} %add.40), calls=%async_computation | async-start | bytes 1179648 | tf_op jit(solution)/shard_map/all_to_all | solution.py:182
  81.2 2.8 %collective-permute-start.13 = (bf16[128,768]{1,0:T(8,128)(2,1)S(1)}, bf16[128,768]{1,0:T(8,128)(2,1)S(1)}, u32[]{:S(2)}, u32[]{:S(2)}) collective-permute-start(bf16[128,768]{1,0:T(8,128)(2,1)S(1)} %slice_bitcast_fusion.2), channel_id=1, source_target_pairs={{0,64},{1,449},{64,128},{65,1},{128,192},{129,65},{192,256},{193,1... | collective-permute-start | bytes 589832 | tf_op jit(solution)/shard_map/ppermute | solution.py:162
  84.0 4.2 %collective-permute-start.17 = (bf16[2,128,768]{2,1,0:T(8,128)(2,1)S(1)}, bf16[2,128,768]{2,1,0:T(8,128)(2,1)}, u32[]{:S(2)}, u32[]{:S(2)}) collective-permute-start(bf16[2,128,768]{2,1,0:T(8,128)(2,1)S(1)} %collective-permute-done.16.hop_one), channel_id=1, source_target_pairs={{0,64},{1,449},{64,128},{65,1},{128,192},{129,65},{192,256},{193,1... | collective-permute-start | bytes 1179656 | tf_op jit(solution)/shard_map/ppermute | solution.py:161
  89.6 3.4 %product.5 = (f32[8,2,72,128]{3,2,1,0:T(8,128)S(1)}, f32[8,2,72,128]{3,2,1,0:T(8,128)S(1)}) custom-call(s32[6]{0:T(128)S(1)} %stack.63.place, bf16[384,1024]{1,0:T(8,128)(2,1)S(1)} %pad_maximum_fusion.att_own, bf16[384,1024]{1,0:T(8,128)(2,1)S(1)} %collective-permute-done.1.att_oth, bf16[2,128,768]{2,1,0:T(8,128)(2,1)S(1)} %pad_maximum_fusion.2.first, ...), custom_call_target="tpu_custom_call" | custom-call | flops 603979776 | bytes 6291456 | tf_op jit(solution)/shard_map/product/pallas_call | solution.py:79
  93.0 4.4 %collective-permute-start.14 = (f32[8,2,72,128]{3,2,1,0:T(8,128)S(1)}, f32[8,2,72,128]{3,2,1,0:T(8,128)S(1)}, u32[]{:S(2)}, u32[]{:S(2)}) collective-permute-start(f32[8,2,72,128]{3,2,1,0:T(8,128)S(1)} %get-tuple-element.17), channel_id=1, source_target_pairs={{0,1},{1,0},{2,3},{3,2},{4,5},{5,4},{6,7},{7,6},{8,9},{9,8},{10,11... | collective-permute-start | bytes 1769480 | tf_op jit(solution)/shard_map/ppermute | solution.py:181
  99.3 2.2 %collective-permute-start.18 = (bf16[2,128,768]{2,1,0:T(8,128)(2,1)}, bf16[2,128,768]{2,1,0:T(8,128)(2,1)S(1)}, u32[]{:S(2)}, u32[]{:S(2)}) collective-permute-start(bf16[2,128,768]{2,1,0:T(8,128)(2,1)} %collective-permute-done.17.hop_two), channel_id=1, source_target_pairs={{0,64},{1,449},{64,128},{65,1},{128,192},{129,65},{192,256},{193,1... | collective-permute-start | bytes 1179656 | tf_op jit(solution)/shard_map/ppermute | solution.py:161
  101.6 3.1 %collective-permute-start.22 = (bf16[2,128,768]{2,1,0:T(8,128)(2,1)S(1)}, bf16[2,128,768]{2,1,0:T(8,128)(2,1)S(1)}, u32[]{:S(2)}, u32[]{:S(2)}) collective-permute-start(bf16[2,128,768]{2,1,0:T(8,128)(2,1)S(1)} %pad_maximum_fusion.4.first), channel_id=1, source_target_pairs={{0,64},{1,449},{64,128},{65,1},{128,192},{129,65},{192,256},{193,1... | collective-permute-start | bytes 1179656 | tf_op jit(solution)/shard_map/ppermute | solution.py:161
  105.6 6.8 %all-to-all-start.1 = ((f32[8,2,72,128]{3,2,1,0:T(8,128)}), f32[8,2,72,128]{3,2,1,0:T(8,128)}, u32[]{:S(2)}, u32[]{:S(2)}) async-start(f32[8,2,72,128]{3,2,1,0:T(8,128)} %add.41), calls=%async_computation.1 | async-start | bytes 1179648 | tf_op jit(solution)/shard_map/all_to_all | solution.py:182
  112.4 2.4 %collective-permute-start.19 = (bf16[128,768]{1,0:T(8,128)(2,1)S(1)}, bf16[128,768]{1,0:T(8,128)(2,1)S(1)}, u32[]{:S(2)}, u32[]{:S(2)}) collective-permute-start(bf16[128,768]{1,0:T(8,128)(2,1)S(1)} %slice_bitcast_fusion.1), channel_id=1, source_target_pairs={{0,64},{1,449},{64,128},{65,1},{128,192},{129,65},{192,256},{193,1... | collective-permute-start | bytes 589832 | tf_op jit(solution)/shard_map/ppermute | solution.py:162
  114.9 3.1 %collective-permute-start.23 = (bf16[2,128,768]{2,1,0:T(8,128)(2,1)S(1)}, bf16[2,128,768]{2,1,0:T(8,128)(2,1)}, u32[]{:S(2)}, u32[]{:S(2)}) collective-permute-start(bf16[2,128,768]{2,1,0:T(8,128)(2,1)S(1)} %collective-permute-done.22.hop_one), channel_id=1, source_target_pairs={{0,64},{1,449},{64,128},{65,1},{128,192},{129,65},{192,256},{193,1... | collective-permute-start | bytes 1179656 | tf_op jit(solution)/shard_map/ppermute | solution.py:161
  119.9 3.3 %product.6 = (f32[8,2,72,128]{3,2,1,0:T(8,128)S(1)}, f32[8,2,72,128]{3,2,1,0:T(8,128)S(1)}) custom-call(s32[6]{0:T(128)S(1)} %stack.63.place, bf16[384,1024]{1,0:T(8,128)(2,1)S(1)} %pad_maximum_fusion.att_own, bf16[384,1024]{1,0:T(8,128)(2,1)S(1)} %collective-permute-done.1.att_oth, bf16[2,128,768]{2,1,0:T(8,128)(2,1)S(1)} %pad_maximum_fusion.3.first, ...), custom_call_target="tpu_custom_call" | custom-call | flops 603979776 | bytes 6291456 | tf_op jit(solution)/shard_map/product/pallas_call | solution.py:79
  123.2 5.3 %collective-permute-start.20 = (f32[8,2,72,128]{3,2,1,0:T(8,128)S(1)}, f32[8,2,72,128]{3,2,1,0:T(8,128)S(1)}, u32[]{:S(2)}, u32[]{:S(2)}) collective-permute-start(f32[8,2,72,128]{3,2,1,0:T(8,128)S(1)} %get-tuple-element.19), channel_id=1, source_target_pairs={{0,1},{1,0},{2,3},{3,2},{4,5},{5,4},{6,7},{7,6},{8,9},{9,8},{10,11... | collective-permute-start | bytes 1769480 | tf_op jit(solution)/shard_map/ppermute | solution.py:181
  131.4 6.9 %all-to-all-start.2 = ((f32[8,2,72,128]{3,2,1,0:T(8,128)}), f32[8,2,72,128]{3,2,1,0:T(8,128)}, u32[]{:S(2)}, u32[]{:S(2)}) async-start(f32[8,2,72,128]{3,2,1,0:T(8,128)} %add.42), calls=%async_computation.2 | async-start | bytes 1179648 | tf_op jit(solution)/shard_map/all_to_all | solution.py:182
  140.5 4.7 %collective-permute-done.25.last = bf16[128,768]{1,0:T(8,128)(2,1)S(1)} collective-permute-done((bf16[128,768]{1,0:T(8,128)(2,1)S(1)}, bf16[128,768]{1,0:T(8,128)(2,1)S(1)}, u32[]{:S(2)}, u32[]{:S(2)}) %collective-permute-start.25) | collective-permute-done | bytes 196640 | tf_op jit(solution)/shard_map/ppermute | solution.py:162
  145.2 3.3 %product.7 = (f32[8,2,72,128]{3,2,1,0:T(8,128)S(1)}, f32[8,2,72,128]{3,2,1,0:T(8,128)S(1)}) custom-call(s32[6]{0:T(128)S(1)} %stack.63.place, bf16[384,1024]{1,0:T(8,128)(2,1)S(1)} %pad_maximum_fusion.att_own, bf16[384,1024]{1,0:T(8,128)(2,1)S(1)} %collective-permute-done.1.att_oth, bf16[2,128,768]{2,1,0:T(8,128)(2,1)S(1)} %pad_maximum_fusion.4.first, ...), custom_call_target="tpu_custom_call" | custom-call | flops 603979776 | bytes 6291456 | tf_op jit(solution)/shard_map/product/pallas_call | solution.py:79
  148.5 5.2 %collective-permute-start.26 = (f32[8,2,72,128]{3,2,1,0:T(8,128)S(1)}, f32[8,2,72,128]{3,2,1,0:T(8,128)S(1)}, u32[]{:S(2)}, u32[]{:S(2)}) collective-permute-start(f32[8,2,72,128]{3,2,1,0:T(8,128)S(1)} %get-tuple-element.21), channel_id=1, source_target_pairs={{0,1},{1,0},{2,3},{3,2},{4,5},{5,4},{6,7},{7,6},{8,9},{9,8},{10,11... | collective-permute-start | bytes 1769480 | tf_op jit(solution)/shard_map/ppermute | solution.py:181
  157.9 5.2 %all-to-all-start.3 = ((f32[8,2,72,128]{3,2,1,0:T(8,128)}), f32[8,2,72,128]{3,2,1,0:T(8,128)S(1)}, u32[]{:S(2)}, u32[]{:S(2)}) async-start(f32[8,2,72,128]{3,2,1,0:T(8,128)} %add.43), calls=%async_computation.3 | async-start | bytes 1179648 | tf_op jit(solution)/shard_map/all_to_all | solution.py:182
  166.4 16.0 %all-to-all-done.3 = f32[8,2,72,128]{3,2,1,0:T(8,128)S(1)} async-done(((f32[8,2,72,128]{3,2,1,0:T(8,128)}), f32[8,2,72,128]{3,2,1,0:T(8,128)S(1)}, u32[]{:S(2)}, u32[]{:S(2)}) %all-to-all-start.3) | async-done | bytes 589856 | tf_op jit(solution)/shard_map/all_to_all | solution.py:182
  182.5 27.8 %all_to_all.25.parts = f32[8,72,128]{2,1,0:T(8,128)} all-to-all(f32[8,72,128]{2,1,0:T(8,128)S(1)} %pad_maximum_fusion.5), channel_id=1, replica_groups=mesh['yh'=2,'x'=8,'z'=8,'yl'=4,'c'=2] {'z'}, dimensions={0} | all-to-all | bytes 589824 | tf_op jit(solution)/shard_map/all_to_all | solution.py:183
  210.4 3.2 %update.1 = (f32[48,192]{1,0:T(8,128)}, f32[48,192]{1,0:T(8,128)}, f32[48,192]{1,0:T(8,128)}, f32[48,192]{1,0:T(8,128)}, f32[48,48]{1,0:T(8,128)}, /*index=5*/f32[192,192]{1,0:T(8,128)}) custom-call(f32[8,72,128]{2,1,0:T(8,128)} %all_to_all.25.parts, f32[48,192]{1,0:T(8,128)} %weight.1, f32[48,192]{1,0:T(8,128)} %exp_avg.1, f32[48,192]{1,0:T(8,128)} %exp_avg_sq.1, ...), custom_call_target="tpu_custom_call" | custom-call | tf_op jit(solution)/shard_map/update/pallas_call | solution.py:186
  (78 shorter events, 39.3 us)
Async XLA Ops:
  2.8 17.2 %collective-permute-start.2 = (bf16[128,768]{1,0:T(8,128)(2,1)S(1)}, bf16[128,768]{1,0:T(8,128)(2,1)S(1)}, u32[]{:S(2)}, u32[]{:S(2)}) collective-permute-start(bf16[128,768]{1,0:T(8,128)(2,1)S(1)} %get-tuple-element.29), channel_id=1, source_target_pairs={{0,1},{1,0},{2,3},{3,2},{4,5},{5,4},{6,7},{7,6},{8,9},{9,8},{10,11... | collective-permute-start | bytes 589832 | tf_op jit(solution)/shard_map/ppermute | solution.py:159
  20.0 8.8 %collective-permute-start.3 = (bf16[2,128,768]{2,1,0:T(8,128)(2,1)S(1)}, bf16[2,128,768]{2,1,0:T(8,128)(2,1)S(1)}, u32[]{:S(2)}, u32[]{:S(2)}) collective-permute-start(bf16[2,128,768]{2,1,0:T(8,128)(2,1)S(1)} %pad_maximum_fusion.1.first), channel_id=1, source_target_pairs={{0,64},{1,449},{64,128},{65,1},{128,192},{129,65},{192,256},{193,1... | collective-permute-start | bytes 1179656 | tf_op jit(solution)/shard_map/ppermute | solution.py:161
  22.0 19.5 %copy-start.6 = (bf16[2048,192]{0,1:T(8,128)(2,1)S(1)}, bf16[2048,192]{0,1:T(8,128)(2,1)}, u32[]{:S(2)}) copy-start(bf16[2048,192]{0,1:T(8,128)(2,1)} %param.10) | copy-start | bytes 2359300
  22.0 19.4 %collective-permute-start = (bf16[192,1024]{1,0:T(8,128)(2,1)S(1)}, bf16[192,1024]{1,0:T(8,128)(2,1)S(1)}, u32[]{:S(2)}, u32[]{:S(2)}) collective-permute-start(bf16[192,1024]{1,0:T(8,128)(2,1)S(1)} %dynamic-slice_bitcast_fusion), channel_id=1, source_target_pairs={{0,512},{512,0},{1,513},{513,1},{2,514},{514,2},{3,515},{515,3},{4... | collective-permute-start | bytes 1179656 | tf_op jit(solution)/shard_map/ppermute | solution.py:167
  24.1 7.6 %collective-permute-start.9 = (bf16[128,768]{1,0:T(8,128)(2,1)S(1)}, bf16[128,768]{1,0:T(8,128)(2,1)S(1)}, u32[]{:S(2)}, u32[]{:S(2)}) collective-permute-start(bf16[128,768]{1,0:T(8,128)(2,1)S(1)} %get-tuple-element.28), channel_id=1, source_target_pairs={{0,1},{1,0},{2,3},{3,2},{4,5},{5,4},{6,7},{7,6},{8,9},{9,8},{10,11... | collective-permute-start | bytes 589832 | tf_op jit(solution)/shard_map/ppermute | solution.py:159
  28.8 12.9 %collective-permute-start.4 = (bf16[2,128,768]{2,1,0:T(8,128)(2,1)S(1)}, bf16[2,128,768]{2,1,0:T(8,128)(2,1)}, u32[]{:S(2)}, u32[]{:S(2)}) collective-permute-start(bf16[2,128,768]{2,1,0:T(8,128)(2,1)S(1)} %collective-permute-done.3.hop_one), channel_id=1, source_target_pairs={{0,64},{1,449},{64,128},{65,1},{128,192},{129,65},{192,256},{193,1... | collective-permute-start | bytes 1179656 | tf_op jit(solution)/shard_map/ppermute | solution.py:161
  31.7 17.8 %collective-permute-start.10 = (bf16[2,128,768]{2,1,0:T(8,128)(2,1)S(1)}, bf16[2,128,768]{2,1,0:T(8,128)(2,1)S(1)}, u32[]{:S(2)}, u32[]{:S(2)}) collective-permute-start(bf16[2,128,768]{2,1,0:T(8,128)(2,1)S(1)} %pad_maximum_fusion.2.first), channel_id=1, source_target_pairs={{0,64},{1,449},{64,128},{65,1},{128,192},{129,65},{192,256},{193,1... | collective-permute-start | bytes 1179656 | tf_op jit(solution)/shard_map/ppermute | solution.py:161
  41.7 12.6 %collective-permute-start.5 = (bf16[2,128,768]{2,1,0:T(8,128)(2,1)}, bf16[2,128,768]{2,1,0:T(8,128)(2,1)S(1)}, u32[]{:S(2)}, u32[]{:S(2)}) collective-permute-start(bf16[2,128,768]{2,1,0:T(8,128)(2,1)} %collective-permute-done.4.hop_two), channel_id=1, source_target_pairs={{0,64},{1,449},{64,128},{65,1},{128,192},{129,65},{192,256},{193,1... | collective-permute-start | bytes 1179656 | tf_op jit(solution)/shard_map/ppermute | solution.py:161
  43.7 13.9 %collective-permute-start.1 = (bf16[384,1024]{1,0:T(8,128)(2,1)S(1)}, bf16[384,1024]{1,0:T(8,128)(2,1)S(1)}, u32[]{:S(2)}, u32[]{:S(2)}) collective-permute-start(bf16[384,1024]{1,0:T(8,128)(2,1)S(1)} %pad_maximum_fusion.att_own), channel_id=1, source_target_pairs={{0,1},{1,0},{2,3},{3,2},{4,5},{5,4},{6,7},{7,6},{8,9},{9,8},{10,11... | collective-permute-start | bytes 2359304 | tf_op jit(solution)/shard_map/ppermute | solution.py:173
  46.2 10.2 %collective-permute-start.7 = (f32[1,3072]{1,0:T(1,128)}, f32[1,3072]{1,0:T(1,128)}, u32[]{:S(2)}, u32[]{:S(2)}) collective-permute-start(f32[1,3072]{1,0:T(1,128)} %param.12), channel_id=1, source_target_pairs={{0,1},{1,0},{2,3},{3,2},{4,5},{5,4},{6,7},{7,6},{8,9},{9,8},{10,11... | collective-permute-start | bytes 36872 | tf_op jit(solution)/shard_map/ppermute | solution.py:174
  49.5 20.8 %collective-permute-start.11 = (bf16[2,128,768]{2,1,0:T(8,128)(2,1)S(1)}, bf16[2,128,768]{2,1,0:T(8,128)(2,1)}, u32[]{:S(2)}, u32[]{:S(2)}) collective-permute-start(bf16[2,128,768]{2,1,0:T(8,128)(2,1)S(1)} %collective-permute-done.10.hop_one), channel_id=1, source_target_pairs={{0,64},{1,449},{64,128},{65,1},{128,192},{129,65},{192,256},{193,1... | collective-permute-start | bytes 1179656 | tf_op jit(solution)/shard_map/ppermute | solution.py:161
  54.4 6.8 %collective-permute-start.6 = (bf16[128,768]{1,0:T(8,128)(2,1)S(1)}, bf16[128,768]{1,0:T(8,128)(2,1)S(1)}, u32[]{:S(2)}, u32[]{:S(2)}) collective-permute-start(bf16[128,768]{1,0:T(8,128)(2,1)S(1)} %slice_bitcast_fusion.3), channel_id=1, source_target_pairs={{0,64},{1,449},{64,128},{65,1},{128,192},{129,65},{192,256},{193,1... | collective-permute-start | bytes 589832 | tf_op jit(solution)/shard_map/ppermute | solution.py:162
  64.6 11.4 %collective-permute-start.8 = (f32[8,2,72,128]{3,2,1,0:T(8,128)S(1)}, f32[8,2,72,128]{3,2,1,0:T(8,128)S(1)}, u32[]{:S(2)}, u32[]{:S(2)}) collective-permute-start(f32[8,2,72,128]{3,2,1,0:T(8,128)S(1)} %get-tuple-element.15), channel_id=1, source_target_pairs={{0,1},{1,0},{2,3},{3,2},{4,5},{5,4},{6,7},{7,6},{8,9},{9,8},{10,11... | collective-permute-start | bytes 1769480 | tf_op jit(solution)/shard_map/ppermute | solution.py:181
  68.3 5.7 %collective-permute-start.15 = (bf16[128,768]{1,0:T(8,128)(2,1)S(1)}, bf16[128,768]{1,0:T(8,128)(2,1)S(1)}, u32[]{:S(2)}, u32[]{:S(2)}) collective-permute-start(bf16[128,768]{1,0:T(8,128)(2,1)S(1)} %copy-done.8), channel_id=1, source_target_pairs={{0,1},{1,0},{2,3},{3,2},{4,5},{5,4},{6,7},{7,6},{8,9},{9,8},{10,11... | collective-permute-start | bytes 589832 | tf_op jit(solution)/shard_map/ppermute | solution.py:159
  70.3 10.9 %collective-permute-start.12 = (bf16[2,128,768]{2,1,0:T(8,128)(2,1)}, bf16[2,128,768]{2,1,0:T(8,128)(2,1)S(1)}, u32[]{:S(2)}, u32[]{:S(2)}) collective-permute-start(bf16[2,128,768]{2,1,0:T(8,128)(2,1)} %collective-permute-done.11.hop_two), channel_id=1, source_target_pairs={{0,64},{1,449},{64,128},{65,1},{128,192},{129,65},{192,256},{193,1... | collective-permute-start | bytes 1179656 | tf_op jit(solution)/shard_map/ppermute | solution.py:161
  74.1 9.9 %collective-permute-start.16 = (bf16[2,128,768]{2,1,0:T(8,128)(2,1)S(1)}, bf16[2,128,768]{2,1,0:T(8,128)(2,1)S(1)}, u32[]{:S(2)}, u32[]{:S(2)}) collective-permute-start(bf16[2,128,768]{2,1,0:T(8,128)(2,1)S(1)} %pad_maximum_fusion.3.first), channel_id=1, source_target_pairs={{0,64},{1,449},{64,128},{65,1},{128,192},{129,65},{192,256},{193,1... | collective-permute-start | bytes 1179656 | tf_op jit(solution)/shard_map/ppermute | solution.py:161
  76.9 28.6 %all-to-all-start = ((f32[8,2,72,128]{3,2,1,0:T(8,128)}), f32[8,2,72,128]{3,2,1,0:T(8,128)}, u32[]{:S(2)}, u32[]{:S(2)}) async-start(f32[8,2,72,128]{3,2,1,0:T(8,128)} %add.40), calls=%async_computation | async-start | bytes 1179648 | tf_op jit(solution)/shard_map/all_to_all | solution.py:182
  81.2 7.0 %collective-permute-start.13 = (bf16[128,768]{1,0:T(8,128)(2,1)S(1)}, bf16[128,768]{1,0:T(8,128)(2,1)S(1)}, u32[]{:S(2)}, u32[]{:S(2)}) collective-permute-start(bf16[128,768]{1,0:T(8,128)(2,1)S(1)} %slice_bitcast_fusion.2), channel_id=1, source_target_pairs={{0,64},{1,449},{64,128},{65,1},{128,192},{129,65},{192,256},{193,1... | collective-permute-start | bytes 589832 | tf_op jit(solution)/shard_map/ppermute | solution.py:162
  84.0 15.3 %collective-permute-start.17 = (bf16[2,128,768]{2,1,0:T(8,128)(2,1)S(1)}, bf16[2,128,768]{2,1,0:T(8,128)(2,1)}, u32[]{:S(2)}, u32[]{:S(2)}) collective-permute-start(bf16[2,128,768]{2,1,0:T(8,128)(2,1)S(1)} %collective-permute-done.16.hop_one), channel_id=1, source_target_pairs={{0,64},{1,449},{64,128},{65,1},{128,192},{129,65},{192,256},{193,1... | collective-permute-start | bytes 1179656 | tf_op jit(solution)/shard_map/ppermute | solution.py:161
  93.0 11.7 %collective-permute-start.14 = (f32[8,2,72,128]{3,2,1,0:T(8,128)S(1)}, f32[8,2,72,128]{3,2,1,0:T(8,128)S(1)}, u32[]{:S(2)}, u32[]{:S(2)}) collective-permute-start(f32[8,2,72,128]{3,2,1,0:T(8,128)S(1)} %get-tuple-element.17), channel_id=1, source_target_pairs={{0,1},{1,0},{2,3},{3,2},{4,5},{5,4},{6,7},{7,6},{8,9},{9,8},{10,11... | collective-permute-start | bytes 1769480 | tf_op jit(solution)/shard_map/ppermute | solution.py:181
  97.4 4.2 %collective-permute-start.21 = (bf16[128,768]{1,0:T(8,128)(2,1)S(1)}, bf16[128,768]{1,0:T(8,128)(2,1)S(1)}, u32[]{:S(2)}, u32[]{:S(2)}) collective-permute-start(bf16[128,768]{1,0:T(8,128)(2,1)S(1)} %copy-done.7), channel_id=1, source_target_pairs={{0,1},{1,0},{2,3},{3,2},{4,5},{5,4},{6,7},{7,6},{8,9},{9,8},{10,11... | collective-permute-start | bytes 589832 | tf_op jit(solution)/shard_map/ppermute | solution.py:159
  99.3 13.1 %collective-permute-start.18 = (bf16[2,128,768]{2,1,0:T(8,128)(2,1)}, bf16[2,128,768]{2,1,0:T(8,128)(2,1)S(1)}, u32[]{:S(2)}, u32[]{:S(2)}) collective-permute-start(bf16[2,128,768]{2,1,0:T(8,128)(2,1)} %collective-permute-done.17.hop_two), channel_id=1, source_target_pairs={{0,64},{1,449},{64,128},{65,1},{128,192},{129,65},{192,256},{193,1... | collective-permute-start | bytes 1179656 | tf_op jit(solution)/shard_map/ppermute | solution.py:161
  101.6 13.3 %collective-permute-start.22 = (bf16[2,128,768]{2,1,0:T(8,128)(2,1)S(1)}, bf16[2,128,768]{2,1,0:T(8,128)(2,1)S(1)}, u32[]{:S(2)}, u32[]{:S(2)}) collective-permute-start(bf16[2,128,768]{2,1,0:T(8,128)(2,1)S(1)} %pad_maximum_fusion.4.first), channel_id=1, source_target_pairs={{0,64},{1,449},{64,128},{65,1},{128,192},{129,65},{192,256},{193,1... | collective-permute-start | bytes 1179656 | tf_op jit(solution)/shard_map/ppermute | solution.py:161
  105.6 25.8 %all-to-all-start.1 = ((f32[8,2,72,128]{3,2,1,0:T(8,128)}), f32[8,2,72,128]{3,2,1,0:T(8,128)}, u32[]{:S(2)}, u32[]{:S(2)}) async-start(f32[8,2,72,128]{3,2,1,0:T(8,128)} %add.41), calls=%async_computation.1 | async-start | bytes 1179648 | tf_op jit(solution)/shard_map/all_to_all | solution.py:182
  112.4 6.8 %collective-permute-start.19 = (bf16[128,768]{1,0:T(8,128)(2,1)S(1)}, bf16[128,768]{1,0:T(8,128)(2,1)S(1)}, u32[]{:S(2)}, u32[]{:S(2)}) collective-permute-start(bf16[128,768]{1,0:T(8,128)(2,1)S(1)} %slice_bitcast_fusion.1), channel_id=1, source_target_pairs={{0,64},{1,449},{64,128},{65,1},{128,192},{129,65},{192,256},{193,1... | collective-permute-start | bytes 589832 | tf_op jit(solution)/shard_map/ppermute | solution.py:162
  114.9 13.7 %collective-permute-start.23 = (bf16[2,128,768]{2,1,0:T(8,128)(2,1)S(1)}, bf16[2,128,768]{2,1,0:T(8,128)(2,1)}, u32[]{:S(2)}, u32[]{:S(2)}) collective-permute-start(bf16[2,128,768]{2,1,0:T(8,128)(2,1)S(1)} %collective-permute-done.22.hop_one), channel_id=1, source_target_pairs={{0,64},{1,449},{64,128},{65,1},{128,192},{129,65},{192,256},{193,1... | collective-permute-start | bytes 1179656 | tf_op jit(solution)/shard_map/ppermute | solution.py:161
  123.2 7.3 %collective-permute-start.20 = (f32[8,2,72,128]{3,2,1,0:T(8,128)S(1)}, f32[8,2,72,128]{3,2,1,0:T(8,128)S(1)}, u32[]{:S(2)}, u32[]{:S(2)}) collective-permute-start(f32[8,2,72,128]{3,2,1,0:T(8,128)S(1)} %get-tuple-element.19), channel_id=1, source_target_pairs={{0,1},{1,0},{2,3},{3,2},{4,5},{5,4},{6,7},{7,6},{8,9},{9,8},{10,11... | collective-permute-start | bytes 1769480 | tf_op jit(solution)/shard_map/ppermute | solution.py:181
  128.6 9.8 %collective-permute-start.24 = (bf16[2,128,768]{2,1,0:T(8,128)(2,1)}, bf16[2,128,768]{2,1,0:T(8,128)(2,1)S(1)}, u32[]{:S(2)}, u32[]{:S(2)}) collective-permute-start(bf16[2,128,768]{2,1,0:T(8,128)(2,1)} %collective-permute-done.23.hop_two), channel_id=1, source_target_pairs={{0,64},{1,449},{64,128},{65,1},{128,192},{129,65},{192,256},{193,1... | collective-permute-start | bytes 1179656 | tf_op jit(solution)/shard_map/ppermute | solution.py:161
  131.4 26.5 %all-to-all-start.2 = ((f32[8,2,72,128]{3,2,1,0:T(8,128)}), f32[8,2,72,128]{3,2,1,0:T(8,128)}, u32[]{:S(2)}, u32[]{:S(2)}) async-start(f32[8,2,72,128]{3,2,1,0:T(8,128)} %add.42), calls=%async_computation.2 | async-start | bytes 1179648 | tf_op jit(solution)/shard_map/all_to_all | solution.py:182
  138.4 6.8 %collective-permute-start.25 = (bf16[128,768]{1,0:T(8,128)(2,1)S(1)}, bf16[128,768]{1,0:T(8,128)(2,1)S(1)}, u32[]{:S(2)}, u32[]{:S(2)}) collective-permute-start(bf16[128,768]{1,0:T(8,128)(2,1)S(1)} %slice_bitcast_fusion), channel_id=1, source_target_pairs={{0,64},{1,449},{64,128},{65,1},{128,192},{129,65},{192,256},{193,1... | collective-permute-start | bytes 589832 | tf_op jit(solution)/shard_map/ppermute | solution.py:162
  148.5 6.8 %collective-permute-start.26 = (f32[8,2,72,128]{3,2,1,0:T(8,128)S(1)}, f32[8,2,72,128]{3,2,1,0:T(8,128)S(1)}, u32[]{:S(2)}, u32[]{:S(2)}) collective-permute-start(f32[8,2,72,128]{3,2,1,0:T(8,128)S(1)} %get-tuple-element.21), channel_id=1, source_target_pairs={{0,1},{1,0},{2,3},{3,2},{4,5},{5,4},{6,7},{7,6},{8,9},{9,8},{10,11... | collective-permute-start | bytes 1769480 | tf_op jit(solution)/shard_map/ppermute | solution.py:181
  157.9 24.6 %all-to-all-start.3 = ((f32[8,2,72,128]{3,2,1,0:T(8,128)}), f32[8,2,72,128]{3,2,1,0:T(8,128)S(1)}, u32[]{:S(2)}, u32[]{:S(2)}) async-start(f32[8,2,72,128]{3,2,1,0:T(8,128)} %add.43), calls=%async_computation.3 | async-start | bytes 1179648 | tf_op jit(solution)/shard_map/all_to_all | solution.py:182
  (8 other events, 61.1 us)

commit v3 on v2

--- a/solution.py
+++ b/solution.py
@@ -17,35 +17,82 @@
 LB = 48
 HB = 192
 NX = 8
-NZ = 8
+NZH = 4
 NY = 4
 CHUNK = 128
 TOK = NX * CHUNK
 FEAT = 2 * HB
-GROUP = D // NZ
+GROUP = D // 8
 HALF = LB // 2
 PACK = (LB * HB) // 128
-PIECES = (2, 2, 2, 2)
-ROW = ("z", "yl", "c")
+PIECES = ((0, 1), (2, 3))
+ROW = ("zh", "zl", "yl", "c")
 COL = ("yh", "x")
 Y = ("yh", "yl")
 SWAP = [(0, 1), (1, 0)]
-RING = [(2 * x + c, 2 * ((x + (1, -1)[c]) % NX) + c) for x in range(NX) for c in range(2)]
+
+
+def at_ring(x, zl, c):
+    return (x % NX) * 4 + 2 * zl + c
+
+
+def ring(other_z, other_core):
+    pairs = []
+    for x in range(NX):
+        for zl in range(2):
+            for c in range(2):
+                to_z, to_c = zl ^ other_z, c ^ other_core
+                pairs.append((at_ring(x, zl, c), at_ring(x + 1 - 2 * to_c, to_z, to_c)))
+    return pairs
+
+
+def hop(block, other_z=0, other_core=0):
+    return lax.ppermute(block, ("x", "zl", "c"), ring(other_z, other_core))
+
+
+def split_kernel(place, cotangent, mine_one, mine_two, other_one, other_two, other_all):
+    for zh in range(NZH):
+        span = slice((zh % 2) * GROUP, (zh % 2 + 1) * GROUP)
+        for parity, ref in ((place[6], (mine_one, mine_two)), (1 - place[6], (other_one, other_two))):
+            start = pl.multiple_of((2 * zh + parity) * GROUP, GROUP)
+            ref[zh // 2][:, span] = cotangent[:, pl.ds(start, GROUP)]
+        start = pl.multiple_of((2 * zh + 1 - place[6]) * GROUP, GROUP)
+        other_all[:, zh * GROUP : (zh + 1) * GROUP] = cotangent[:, pl.ds(start, GROUP)]
+
+
+def split(place, cotangent):
+    half = jax.ShapeDtypeStruct((CHUNK, 2 * GROUP), cotangent.dtype)
+    return pl.pallas_call(
+        split_kernel,
+        in_specs=[pl.BlockSpec(memory_space=pltpu.SMEM), pl.BlockSpec((CHUNK, D), lambda: (0, 0))],
+        out_shape=[half] * 4 + [jax.ShapeDtypeStruct((CHUNK, 4 * GROUP), cotangent.dtype)],
+        name="split",
+    )(place, cotangent)
 
 
 def product_kernel(
-    place, att_own, att_oth, first, hop_one, hop_two, hop_three, last, gate_own, gate_oth, keep, send
+    place, att_same, att_cross, own, beside, hop_one, hop_two, hop_three, last, gates, keep, send
 ):
-    def term(att, at, block):
-        columns = pl.ds(pl.multiple_of(place[1 + at] * CHUNK, CHUNK), CHUNK)
-        return jnp.dot(att[:, columns], block, preferred_element_type=jnp.float32)
-
-    own = term(att_own, 0, first[0]) + term(att_own, 4, last[...])
-    oth = jnp.zeros_like(own)
-    for at, hop in ((1, hop_one), (2, hop_two), (3, hop_three)):
-        own += term(att_own, at, hop[0])
-        oth += term(att_oth, at, hop[1])
-    total = gate_own[...] * own + gate_oth[...] * oth
+    def att(which, *hops):
+        ref = (att_same, att_cross)[which // 2]
+        parts = []
+        for at in hops:
+            columns = pl.ds(pl.multiple_of(place[1 + at] * CHUNK, CHUNK), CHUNK)
+            parts.append(ref[which % 2, :, columns])
+        return parts[0] if len(parts) == 1 else jnp.concatenate(parts, axis=1)
+
+    def dot(left, *blocks):
+        right = blocks[0] if len(blocks) == 1 else jnp.concatenate(blocks, axis=0)
+        return jnp.dot(left, right, preferred_element_type=jnp.float32)
+
+    total = jnp.zeros((FEAT, GROUP), jnp.float32)
+    for which in range(4):
+        clip = dot(att(which, 1, 2), hop_one[which], hop_two[which])
+        clip += dot(att(which, 3), hop_three[which])
+        if which < 2:
+            near = (own, beside)[which][...]
+            clip += dot(att(which, 0, 4), near, last[which])
+        total += gates[pl.ds(place[7 + which], 1), :] * clip
     packed = []
     for yh in range(2):
         at = yh * HB
@@ -68,25 +115,27 @@
             store(send, 1 - core)
 
 
-def product(place, att_own, att_oth, blocks, gate_own, gate_oth):
-    count = gate_own.shape[1] // GROUP
-    whole = pl.BlockSpec((FEAT, TOK), lambda z: (0, 0))
+def product(place, att_same, att_cross, own, beside, blocks, gates):
+    count = own.shape[1] // GROUP
+    attn = pl.BlockSpec((2, FEAT, TOK), lambda z: (0, 0, 0))
+    plain = pl.BlockSpec((CHUNK, GROUP), lambda z: (0, z))
+    four = pl.BlockSpec((4, CHUNK, GROUP), lambda z: (0, 0, z))
     pair = pl.BlockSpec((2, CHUNK, GROUP), lambda z: (0, 0, z))
-    row = pl.BlockSpec((1, GROUP), lambda z: (0, z))
+    rows = pl.BlockSpec((4, GROUP), lambda z: (0, z))
     out = pl.BlockSpec((2 * NY, 1, PACK, 128), lambda z: (0, z, 0, 0))
     shape = jax.ShapeDtypeStruct((2 * NY, count, PACK, 128), jnp.float32)
-    flops = 2 * 8 * CHUNK * FEAT * GROUP * count
+    flops = 2 * 16 * CHUNK * FEAT * GROUP * count
     return pl.pallas_call(
         product_kernel,
         grid=(count,),
-        in_specs=[pl.BlockSpec(memory_space=pltpu.SMEM), whole, whole, pair, pair, pair, pair]
-        + [pl.BlockSpec((CHUNK, GROUP), lambda z: (0, z)), row, row],
+        in_specs=[pl.BlockSpec(memory_space=pltpu.SMEM), attn, attn, plain, plain]
+        + [four, four, four, pair, rows],
         out_specs=[out, out],
         out_shape=[shape, shape],
-        cost_estimate=pl.CostEstimate(flops=flops, bytes_accessed=6 << 20, transcendentals=0),
-        compiler_params=pltpu.CompilerParams(vmem_limit_bytes=24 << 20),
+        cost_estimate=pl.CostEstimate(flops=flops, bytes_accessed=8 << 20, transcendentals=0),
+        compiler_params=pltpu.CompilerParams(vmem_limit_bytes=32 << 20),
         name="product",
-    )(place, att_own, att_oth, *blocks, gate_own, gate_oth)
+    )(place, att_same, att_cross, own, beside, *blocks, gates)
 
 
 def update_kernel(
@@ -145,22 +194,23 @@
     left_basis,
     right_basis,
 ):
-    yh, x, core = lax.axis_index("yh"), lax.axis_index("x"), lax.axis_index("c")
+    yh, x, zl, core = (lax.axis_index(name) for name in ("yh", "x", "zl", "c"))
     step = 1 - 2 * core
-    place = jnp.stack([core] + [lax.rem(x - step * hop + NX, NX) for hop in range(5)])
-
-    spans, at = [], 0
-    for count in PIECES:
-        spans.append(slice(at, at + count * GROUP))
-        at += count * GROUP
+    clips = [2 * z + c for c in (core, 1 - core) for z in (zl, 1 - zl)]
+    place = [core] + [lax.rem(x - step * hops + NX, NX) for hops in range(5)] + [zl] + clips
+    place = jnp.stack(place)
+
+    mine_one, mine_two, other_one, other_two, other_all = split(place, cotangent)
     rings = []
-    for span in spans:
-        own = cotangent[:, span]
-        blocks = [jnp.stack([own, lax.ppermute(own, "c", SWAP)])]
-        for _ in range(3):
-            blocks.append(lax.ppermute(blocks[-1], ("x", "c"), RING))
-        blocks.append(lax.ppermute(blocks[-1][0], ("x", "c"), RING))
+    for mine, other in ((mine_one, other_one), (mine_two, other_two)):
+        blocks = [
+            jnp.stack([hop(mine), hop(other, 1, 0), hop(mine, 0, 1), hop(other, 1, 1)])
+        ]
+        blocks.append(hop(blocks[-1]))
+        blocks.append(hop(blocks[-1]))
+        blocks.append(hop(blocks[-1][:2]))
         rings.append(blocks)
+    beside = lax.ppermute(other_all, "zl", SWAP)
 
     features = attn_out.T
     kept = lax.dynamic_slice_in_dim(features, yh * TOK, TOK, 1)
@@ -170,17 +220,22 @@
     att_own = jnp.concatenate(
         [jnp.where(yh == 0, kept, came), jnp.where(yh == 0, came, kept)], axis=0
     )
-    att_oth = lax.ppermute(att_own, "c", SWAP)
-    gate_oth = lax.ppermute(gate, "c", SWAP)
+    att_same = jnp.stack([att_own, lax.ppermute(att_own, "zl", SWAP)])
+    att_cross = lax.ppermute(att_same, "c", SWAP)
+    gates = lax.all_gather(gate, ("zl", "c"), axis=0, tiled=True)
 
     by_z = []
-    for span, blocks in zip(spans, rings):
+    for at, (zhs, mine, blocks) in enumerate(zip(PIECES, (mine_one, mine_two), rings)):
+        groups = [
+            lax.dynamic_slice_in_dim(gates, (2 * zh + zl) * GROUP, GROUP, 1) for zh in zhs
+        ]
+        near = beside[:, 2 * at * GROUP : 2 * (at + 1) * GROUP]
         keep, send = product(
-            place, att_own, att_oth, blocks, gate[:, span], gate_oth[:, span]
+            place, att_same, att_cross, mine, near, blocks, jnp.concatenate(groups, axis=1)
         )
         paired = keep + lax.ppermute(send, "c", SWAP)
         by_z.append(jnp.sum(lax.all_to_all(paired, Y, 0, 0), axis=0))
-    parts = lax.all_to_all(jnp.concatenate(by_z, axis=0), "z", 0, 0)
+    parts = lax.all_to_all(jnp.concatenate(by_z, axis=0), "zh", 0, 0)
 
     block = jax.ShapeDtypeStruct((LB, HB), jnp.float32)
     return pl.pallas_call(
@@ -195,7 +250,8 @@
 
 
 def solution(mesh):
-    fine = Mesh(mesh.devices.reshape(2, NX, NZ, NY, 2), ("yh", "x", "z", "yl", "c"))
+    axes = ("yh", "x", "zh", "zl", "yl", "c")
+    fine = Mesh(mesh.devices.reshape(2, NX, NZH, 2, NY, 2), axes)
     block = P(ROW, COL)
     in_specs = (block, P(COL + ROW, None), P(ROW, None)) + (block,) * 7
     return jax.shard_map(

time: 215 us -> 215 us (level)
  starting transfers between devices: 113 us -> 98.1 us
  waiting for transfers between devices: 40.2 us -> 53 us
  blocking collectives: 27.8 us -> 32.4 us
  Pallas kernels: 16.7 us -> 13.9 us
    all_to_all x4 -> x2, starting transfers between devices: 23.2 us -> 10.8 us  [local(): by_z.append(jnp.sum(lax.all_to_all(paired, Y, 0, 0), axis=0))]
    ppermute x4 -> x2, starting transfers between devices: 18.6 us -> 7.41 us  [local(): paired = keep + lax.ppermute(send, 'c', SWAP)]
    all_gather x0 -> x1, blocking collectives: none -> 10.5 us  [local(): gates = lax.all_gather(gate, ('zl', 'c'), axis=0, tiled=True)]
    all_to_all x4 -> x2, waiting for transfers between devices: 17.7 us -> 25.8 us  [local(): by_z.append(jnp.sum(lax.all_to_all(paired, Y, 0, 0), axis=0))]
    ppermute x1, starting transfers between devices: 2.05 us -> 8.74 us  [local(): lax.ppermute(lax.dynamic_slice_in_dim(features, (1 - yh) * TOK, TOK, 1),...]
    all_to_all x1, blocking collectives: 27.8 us -> 21.9 us  [local(): parts = lax.all_to_all(jnp.concatenate(by_z, axis=0), 'zh', 0, 0)]
    ppermute x22 -> x17, waiting for transfers between devices: 13.1 us -> 19 us  [the longest x14 19 us: hop(): return lax.ppermute(block, ('x', 'zl', 'c'), ring(other_z, other_core))]
    pallas_call x4 -> x2, Pallas kernels: 13.5 us -> 8.43 us  [product(): pl.pallas_call(product_kernel, grid=(count,), in_specs=[pl.BlockSpec(memo...]
  transfers between devices with their start and end apart: 31 -> 22, of which waited for: 9 -> 10; matrix products, arithmetic and copies ran while one was open for 5% -> 4% of each run, Pallas kernels for 6% -> 5%
where the time goes in v3:
time: 215 us; the launch traced here: 213 us
  starting transfers between devices  98.1 us (46%)
  waiting for transfers between devices  53 us (25%)
  blocking collectives  32.4 us (15%)
  Pallas kernels  13.9 us (6%)
  local copies, waits for them, and re-layouts  8.76 us (4%)
  other arithmetic  5.55 us (3%)
    ppermute x14, starting transfers between devices, hop(): return lax.ppermute(block, ('x', 'zl', 'c'), ring(other_z, other_core))  57.2 us
    all_to_all x2, waiting for transfers between devices, local(): by_z.append(jnp.sum(lax.all_to_all(paired, Y, 0, 0), axis=0))  25.8 us
    all_to_all x1, blocking collectives, local(): parts = lax.all_to_all(jnp.concatenate(by_z, axis=0), 'zh', 0, 0)  21.9 us
    ppermute x14, waiting for transfers between devices, hop(): return lax.ppermute(block, ('x', 'zl', 'c'), ring(other_z, other_core))  19 us
    all_to_all x2, starting transfers between devices, local(): by_z.append(jnp.sum(lax.all_to_all(paired, Y, 0, 0), axis=0))  10.8 us
    all_gather x1, blocking collectives, local(): gates = lax.all_gather(gate, ('zl', 'c'), axis=0, tiled=True)  10.5 us
    ppermute x1, starting transfers between devices, local(): att_same = jnp.stack([att_own, lax.ppermute(att_own, 'zl', SWAP)])  10.1 us
    ppermute x1, starting transfers between devices, local(): lax.ppermute(lax.dynamic_slice_in_dim(features, (1 - yh) * TOK, TOK, 1),...  8.74 us
  transfers between devices with their start and end apart: 22, of which 10 were waited for; matrix products, arithmetic and copies ran while one was open for 4% of the time, Pallas kernels for 5%

profile of v3, /device:TPU:1, one launch (start us, length us, event | category | flops | bytes accessed | tf_op | source)
XLA Modules:
  0.0 212.8 jit_solution(3693138947407320699)
XLA Ops:
  1.7 8.7 %collective-permute-start = (bf16[192,1024]{1,0:T(8,128)(2,1)S(1)}, bf16[192,1024]{1,0:T(8,128)(2,1)S(1)}, u32[]{:S(2)}, u32[]{:S(2)}) collective-permute-start(bf16[192,1024]{1,0:T(8,128)(2,1)S(1)} %dynamic-slice_bitcast_fusion), channel_id=1, source_target_pairs={{0,512},{512,0},{1,513},{513,1},{2,514},{514,2},{3,515},{515,3},{4... | collective-permute-start | bytes 1179656 | tf_op jit(solution)/shard_map/ppermute | solution.py:217
  10.4 6.6 %collective-permute-done = bf16[192,1024]{1,0:T(8,128)(2,1)S(1)} collective-permute-done((bf16[192,1024]{1,0:T(8,128)(2,1)S(1)}, bf16[192,1024]{1,0:T(8,128)(2,1)S(1)}, u32[]{:S(2)}, u32[]{:S(2)}) %collective-permute-start) | collective-permute-done | bytes 393248 | tf_op jit(solution)/shard_map/ppermute | solution.py:217
  18.4 10.1 %collective-permute-start.1 = (bf16[384,1024]{1,0:T(8,128)(2,1)S(1)}, bf16[384,1024]{1,0:T(8,128)(2,1)S(1)}, u32[]{:S(2)}, u32[]{:S(2)}) collective-permute-start(bf16[384,1024]{1,0:T(8,128)(2,1)S(1)} %get-tuple-element.27), channel_id=1, source_target_pairs={{0,8},{8,0},{1,9},{9,1},{2,10},{10,2},{3,11},{11,3},{4,12},{12,4},... | collective-permute-start | bytes 2359304 | tf_op jit(solution)/shard_map/ppermute | solution.py:223
  29.2 2.3 %split.1 = (bf16[128,768]{1,0:T(8,128)(2,1)}, bf16[128,768]{1,0:T(8,128)(2,1)}, bf16[128,768]{1,0:T(8,128)(2,1)}, bf16[128,768]{1,0:T(8,128)(2,1)}, bf16[128,1536]{1,0:T(8,128)(2,1)}) custom-call(s32[11]{0:T(128)} %stack.86.place, bf16[128,3072]{1,0:T(8,128)(2,1)} %cotangent.1), custom_call_target="tpu_custom_call" | custom-call | tf_op jit(solution)/shard_map/split/pallas_call | solution.py:65
  31.5 4.5 %collective-permute-start.4 = (bf16[128,768]{1,0:T(8,128)(2,1)}, bf16[128,768]{1,0:T(8,128)(2,1)S(1)}, u32[]{:S(2)}, u32[]{:S(2)}) collective-permute-start(bf16[128,768]{1,0:T(8,128)(2,1)} %get-tuple-element.15.own), channel_id=1, source_target_pairs={{0,64},{1,449},{8,72},{9,457},{64,128},{65,1},{72,136},{73,9},{128... | collective-permute-start | bytes 589832 | tf_op jit(solution)/shard_map/ppermute | solution.py:50
  36.0 2.8 %collective-permute-start.5 = (bf16[128,768]{1,0:T(8,128)(2,1)}, bf16[128,768]{1,0:T(8,128)(2,1)S(1)}, u32[]{:S(2)}, u32[]{:S(2)}) collective-permute-start(bf16[128,768]{1,0:T(8,128)(2,1)} %get-tuple-element.17), channel_id=1, source_target_pairs={{0,72},{1,457},{8,64},{9,449},{64,136},{65,9},{72,128},{73,1},{128... | collective-permute-start | bytes 589832 | tf_op jit(solution)/shard_map/ppermute | solution.py:50
  38.8 3.6 %collective-permute-start.6 = (bf16[128,768]{1,0:T(8,128)(2,1)}, bf16[128,768]{1,0:T(8,128)(2,1)S(1)}, u32[]{:S(2)}, u32[]{:S(2)}) collective-permute-start(bf16[128,768]{1,0:T(8,128)(2,1)} %get-tuple-element.15.own), channel_id=1, source_target_pairs={{0,449},{1,64},{8,457},{9,72},{64,1},{65,128},{72,9},{73,136},{128... | collective-permute-start | bytes 589832 | tf_op jit(solution)/shard_map/ppermute | solution.py:50
  42.4 3.4 %collective-permute-start.7 = (bf16[128,768]{1,0:T(8,128)(2,1)}, bf16[128,768]{1,0:T(8,128)(2,1)S(1)}, u32[]{:S(2)}, u32[]{:S(2)}) collective-permute-start(bf16[128,768]{1,0:T(8,128)(2,1)} %get-tuple-element.17), channel_id=1, source_target_pairs={{0,457},{1,72},{8,449},{9,64},{64,9},{65,136},{72,1},{73,128},{128... | collective-permute-start | bytes 589832 | tf_op jit(solution)/shard_map/ppermute | solution.py:50
  47.5 5.2 %collective-permute-done.7 = bf16[128,768]{1,0:T(8,128)(2,1)S(1)} collective-permute-done((bf16[128,768]{1,0:T(8,128)(2,1)}, bf16[128,768]{1,0:T(8,128)(2,1)S(1)}, u32[]{:S(2)}, u32[]{:S(2)}) %collective-permute-start.7) | collective-permute-done | bytes 196640 | tf_op jit(solution)/shard_map/ppermute | solution.py:50
  52.8 7.1 %collective-permute-start.8 = (bf16[4,128,768]{2,1,0:T(8,128)(2,1)S(1)}, bf16[4,128,768]{2,1,0:T(8,128)(2,1)}, u32[]{:S(2)}, u32[]{:S(2)}) collective-permute-start(bf16[4,128,768]{2,1,0:T(8,128)(2,1)S(1)} %pad_maximum_fusion.2.hop_one), channel_id=1, source_target_pairs={{0,64},{1,449},{8,72},{9,457},{64,128},{65,1},{72,136},{73,9},{128... | collective-permute-start | bytes 2359304 | tf_op jit(solution)/shard_map/ppermute | solution.py:50
  62.1 4.1 %collective-permute-start.12 = (bf16[128,768]{1,0:T(8,128)(2,1)S(1)}, bf16[128,768]{1,0:T(8,128)(2,1)S(1)}, u32[]{:S(2)}, u32[]{:S(2)}) collective-permute-start(bf16[128,768]{1,0:T(8,128)(2,1)S(1)} %copy-done.4), channel_id=1, source_target_pairs={{0,64},{1,449},{8,72},{9,457},{64,128},{65,1},{72,136},{73,9},{128... | collective-permute-start | bytes 589832 | tf_op jit(solution)/shard_map/ppermute | solution.py:50
  66.2 2.6 %collective-permute-done.8.hop_two = bf16[4,128,768]{2,1,0:T(8,128)(2,1)} collective-permute-done((bf16[4,128,768]{2,1,0:T(8,128)(2,1)S(1)}, bf16[4,128,768]{2,1,0:T(8,128)(2,1)}, u32[]{:S(2)}, u32[]{:S(2)}) %collective-permute-start.8) | collective-permute-done | bytes 786464 | tf_op jit(solution)/shard_map/ppermute | solution.py:50
  68.8 5.1 %collective-permute-start.9 = (bf16[4,128,768]{2,1,0:T(8,128)(2,1)}, bf16[4,128,768]{2,1,0:T(8,128)(2,1)}, u32[]{:S(2)}, u32[]{:S(2)}) collective-permute-start(bf16[4,128,768]{2,1,0:T(8,128)(2,1)} %collective-permute-done.8.hop_two), channel_id=1, source_target_pairs={{0,64},{1,449},{8,72},{9,457},{64,128},{65,1},{72,136},{73,9},{128... | collective-permute-start | bytes 2359304 | tf_op jit(solution)/shard_map/ppermute | solution.py:50
  73.9 1.9 collective-permute-start.14
  75.9 4.8 %collective-permute-start.13 = (bf16[128,768]{1,0:T(8,128)(2,1)S(1)}, bf16[128,768]{1,0:T(8,128)(2,1)S(1)}, u32[]{:S(2)}, u32[]{:S(2)}) collective-permute-start(bf16[128,768]{1,0:T(8,128)(2,1)S(1)} %copy-done.8), channel_id=1, source_target_pairs={{0,72},{1,457},{8,64},{9,449},{64,136},{65,9},{72,128},{73,1},{128... | collective-permute-start | bytes 589832 | tf_op jit(solution)/shard_map/ppermute | solution.py:50
  80.7 2.2 %collective-permute-start.15 = (bf16[128,768]{1,0:T(8,128)(2,1)S(1)}, bf16[128,768]{1,0:T(8,128)(2,1)S(1)}, u32[]{:S(2)}, u32[]{:S(2)}) collective-permute-start(bf16[128,768]{1,0:T(8,128)(2,1)S(1)} %copy-done.8), channel_id=1, source_target_pairs={{0,457},{1,72},{8,449},{9,64},{64,9},{65,136},{72,1},{73,128},{128... | collective-permute-start | bytes 589832 | tf_op jit(solution)/shard_map/ppermute | solution.py:50
  82.9 7.2 %collective-permute-done.13 = bf16[128,768]{1,0:T(8,128)(2,1)S(1)} collective-permute-done((bf16[128,768]{1,0:T(8,128)(2,1)S(1)}, bf16[128,768]{1,0:T(8,128)(2,1)S(1)}, u32[]{:S(2)}, u32[]{:S(2)}) %collective-permute-start.13) | collective-permute-done | bytes 196640 | tf_op jit(solution)/shard_map/ppermute | solution.py:50
  91.6 7.8 %collective-permute-start.16 = (bf16[4,128,768]{2,1,0:T(8,128)(2,1)}, bf16[4,128,768]{2,1,0:T(8,128)(2,1)}, u32[]{:S(2)}, u32[]{:S(2)}) collective-permute-start(bf16[4,128,768]{2,1,0:T(8,128)(2,1)} %pad_maximum_fusion.3.hop_one), channel_id=1, source_target_pairs={{0,64},{1,449},{8,72},{9,457},{64,128},{65,1},{72,136},{73,9},{128... | collective-permute-start | bytes 2359304 | tf_op jit(solution)/shard_map/ppermute | solution.py:50
  99.4 1.9 collective-permute-start.3
  101.3 10.5 %all-gather = f32[4,1,3072]{2,1,0:T(1,128)S(1)} all-gather(f32[1,1,3072]{2,1,0:T(1,128)S(1)} %bitcast.45), channel_id=1, replica_groups=mesh['yh'=2,'x'=8,'zh'=4,'zl'=2,'yl'=4,'c'=2] {'zl','c'}, dimensions={0}, use_global_device_ids=true | all-gather | bytes 61440 | tf_op jit(solution)/shard_map/all_gather | solution.py:225
  113.5 4.0 %collective-permute-start.10 = (bf16[2,128,768]{2,1,0:T(8,128)(2,1)S(1)}, bf16[2,128,768]{2,1,0:T(8,128)(2,1)S(1)}, u32[]{:S(2)}, u32[]{:S(2)}) collective-permute-start(bf16[2,128,768]{2,1,0:T(8,128)(2,1)S(1)} %slice.17), channel_id=1, source_target_pairs={{0,64},{1,449},{8,72},{9,457},{64,128},{65,1},{72,136},{73,9},{128... | collective-permute-start | bytes 1179656 | tf_op jit(solution)/shard_map/ppermute | solution.py:50
  123.3 4.2 %product.2 = (f32[8,2,72,128]{3,2,1,0:T(8,128)S(1)}, f32[8,2,72,128]{3,2,1,0:T(8,128)S(1)}) custom-call(s32[11]{0:T(128)S(1)} %copy-done.6, bf16[2,384,1024]{2,1,0:T(8,128)(2,1)S(1)} %pad_maximum_fusion.att_same, bf16[2,384,1024]{2,1,0:T(8,128)(2,1)S(1)} %collective-permute-done.2.att_cross, bf16[128,768]{1,0:T(8,128)(2,1)S(1)} %copy-done.5, ...), custom_call_target="tpu_custom_call" | custom-call | flops 1207959552 | bytes 8388608 | tf_op jit(solution)/shard_map/product/pallas_call | solution.py:128
  127.5 4.3 %collective-permute-start.11 = (f32[8,2,72,128]{3,2,1,0:T(8,128)S(1)}, f32[8,2,72,128]{3,2,1,0:T(8,128)S(1)}, u32[]{:S(2)}, u32[]{:S(2)}) collective-permute-start(f32[8,2,72,128]{3,2,1,0:T(8,128)S(1)} %get-tuple-element.19), channel_id=1, source_target_pairs={{0,1},{1,0},{2,3},{3,2},{4,5},{5,4},{6,7},{7,6},{8,9},{9,8},{10,11... | collective-permute-start | bytes 1769480 | tf_op jit(solution)/shard_map/ppermute | solution.py:236
  133.4 3.9 %collective-permute-start.18 = (bf16[2,128,768]{2,1,0:T(8,128)(2,1)}, bf16[2,128,768]{2,1,0:T(8,128)(2,1)}, u32[]{:S(2)}, u32[]{:S(2)}) collective-permute-start(bf16[2,128,768]{2,1,0:T(8,128)(2,1)} %slice.19), channel_id=1, source_target_pairs={{0,64},{1,449},{8,72},{9,457},{64,128},{65,1},{72,136},{73,9},{128... | collective-permute-start | bytes 1179656 | tf_op jit(solution)/shard_map/ppermute | solution.py:50
  138.2 7.3 %all-to-all-start = ((f32[8,2,72,128]{3,2,1,0:T(8,128)}), f32[8,2,72,128]{3,2,1,0:T(8,128)}, u32[]{:S(2)}, u32[]{:S(2)}) async-start(f32[8,2,72,128]{3,2,1,0:T(8,128)} %add.71), calls=%async_computation | async-start | bytes 1179648 | tf_op jit(solution)/shard_map/all_to_all | solution.py:237
  147.4 4.2 %product.3 = (f32[8,2,72,128]{3,2,1,0:T(8,128)S(1)}, f32[8,2,72,128]{3,2,1,0:T(8,128)S(1)}) custom-call(s32[11]{0:T(128)S(1)} %copy-done.6, bf16[2,384,1024]{2,1,0:T(8,128)(2,1)S(1)} %pad_maximum_fusion.att_same, bf16[2,384,1024]{2,1,0:T(8,128)(2,1)S(1)} %collective-permute-done.2.att_cross, bf16[128,768]{1,0:T(8,128)(2,1)S(1)} %copy-done.4, ...), custom_call_target="tpu_custom_call" | custom-call | flops 1207959552 | bytes 8388608 | tf_op jit(solution)/shard_map/product/pallas_call | solution.py:128
  151.6 3.2 %collective-permute-start.19 = (f32[8,2,72,128]{3,2,1,0:T(8,128)S(1)}, f32[8,2,72,128]{3,2,1,0:T(8,128)S(1)}, u32[]{:S(2)}, u32[]{:S(2)}) collective-permute-start(f32[8,2,72,128]{3,2,1,0:T(8,128)S(1)} %get-tuple-element.23), channel_id=1, source_target_pairs={{0,1},{1,0},{2,3},{3,2},{4,5},{5,4},{6,7},{7,6},{8,9},{9,8},{10,11... | collective-permute-start | bytes 1769480 | tf_op jit(solution)/shard_map/ppermute | solution.py:236
  157.2 7.6 %all-to-all-done = f32[8,2,72,128]{3,2,1,0:T(8,128)} async-done(((f32[8,2,72,128]{3,2,1,0:T(8,128)}), f32[8,2,72,128]{3,2,1,0:T(8,128)}, u32[]{:S(2)}, u32[]{:S(2)}) %all-to-all-start) | async-done | bytes 589856 | tf_op jit(solution)/shard_map/all_to_all | solution.py:237
  164.9 3.5 %all-to-all-start.1 = ((f32[8,2,72,128]{3,2,1,0:T(8,128)}), f32[8,2,72,128]{3,2,1,0:T(8,128)S(1)}, u32[]{:S(2)}, u32[]{:S(2)}) async-start(f32[8,2,72,128]{3,2,1,0:T(8,128)} %add.75), calls=%async_computation.1 | async-start | bytes 1179648 | tf_op jit(solution)/shard_map/all_to_all | solution.py:237
  169.5 18.2 %all-to-all-done.1 = f32[8,2,72,128]{3,2,1,0:T(8,128)S(1)} async-done(((f32[8,2,72,128]{3,2,1,0:T(8,128)}), f32[8,2,72,128]{3,2,1,0:T(8,128)S(1)}, u32[]{:S(2)}, u32[]{:S(2)}) %all-to-all-start.1) | async-done | bytes 589856 | tf_op jit(solution)/shard_map/all_to_all | solution.py:237
  187.7 21.9 %all_to_all.15.parts = f32[4,72,128]{2,1,0:T(8,128)} all-to-all(f32[4,72,128]{2,1,0:T(8,128)S(1)} %pad_maximum_fusion.4), channel_id=1, replica_groups=mesh['yh'=2,'x'=8,'zh'=4,'zl'=2,'yl'=4,'c'=2] {'zh'}, dimensions={0} | all-to-all | bytes 294912 | tf_op jit(solution)/shard_map/all_to_all | solution.py:238
  209.6 3.2 %update.1 = (f32[48,192]{1,0:T(8,128)}, f32[48,192]{1,0:T(8,128)}, f32[48,192]{1,0:T(8,128)}, f32[48,192]{1,0:T(8,128)}, f32[48,48]{1,0:T(8,128)}, /*index=5*/f32[192,192]{1,0:T(8,128)}) custom-call(f32[4,72,128]{2,1,0:T(8,128)} %all_to_all.15.parts, f32[48,192]{1,0:T(8,128)} %weight.1, f32[48,192]{1,0:T(8,128)} %exp_avg.1, f32[48,192]{1,0:T(8,128)} %exp_avg_sq.1, ...), custom_call_target="tpu_custom_call" | custom-call | tf_op jit(solution)/shard_map/update/pallas_call | solution.py:241
  (56 shorter events, 23.7 us)
Async XLA Ops:
  1.7 15.4 %collective-permute-start = (bf16[192,1024]{1,0:T(8,128)(2,1)S(1)}, bf16[192,1024]{1,0:T(8,128)(2,1)S(1)}, u32[]{:S(2)}, u32[]{:S(2)}) collective-permute-start(bf16[192,1024]{1,0:T(8,128)(2,1)S(1)} %dynamic-slice_bitcast_fusion), channel_id=1, source_target_pairs={{0,512},{512,0},{1,513},{513,1},{2,514},{514,2},{3,515},{515,3},{4... | collective-permute-start | bytes 1179656 | tf_op jit(solution)/shard_map/ppermute | solution.py:217
  18.4 41.5 %collective-permute-start.1 = (bf16[384,1024]{1,0:T(8,128)(2,1)S(1)}, bf16[384,1024]{1,0:T(8,128)(2,1)S(1)}, u32[]{:S(2)}, u32[]{:S(2)}) collective-permute-start(bf16[384,1024]{1,0:T(8,128)(2,1)S(1)} %get-tuple-element.27), channel_id=1, source_target_pairs={{0,8},{8,0},{1,9},{9,1},{2,10},{10,2},{3,11},{11,3},{4,12},{12,4},... | collective-permute-start | bytes 2359304 | tf_op jit(solution)/shard_map/ppermute | solution.py:223
  31.5 14.3 %collective-permute-start.4 = (bf16[128,768]{1,0:T(8,128)(2,1)}, bf16[128,768]{1,0:T(8,128)(2,1)S(1)}, u32[]{:S(2)}, u32[]{:S(2)}) collective-permute-start(bf16[128,768]{1,0:T(8,128)(2,1)} %get-tuple-element.15.own), channel_id=1, source_target_pairs={{0,64},{1,449},{8,72},{9,457},{64,128},{65,1},{72,136},{73,9},{128... | collective-permute-start | bytes 589832 | tf_op jit(solution)/shard_map/ppermute | solution.py:50
  36.0 9.8 %collective-permute-start.5 = (bf16[128,768]{1,0:T(8,128)(2,1)}, bf16[128,768]{1,0:T(8,128)(2,1)S(1)}, u32[]{:S(2)}, u32[]{:S(2)}) collective-permute-start(bf16[128,768]{1,0:T(8,128)(2,1)} %get-tuple-element.17), channel_id=1, source_target_pairs={{0,72},{1,457},{8,64},{9,449},{64,136},{65,9},{72,128},{73,1},{128... | collective-permute-start | bytes 589832 | tf_op jit(solution)/shard_map/ppermute | solution.py:50
  38.8 8.7 %collective-permute-start.6 = (bf16[128,768]{1,0:T(8,128)(2,1)}, bf16[128,768]{1,0:T(8,128)(2,1)S(1)}, u32[]{:S(2)}, u32[]{:S(2)}) collective-permute-start(bf16[128,768]{1,0:T(8,128)(2,1)} %get-tuple-element.15.own), channel_id=1, source_target_pairs={{0,449},{1,64},{8,457},{9,72},{64,1},{65,128},{72,9},{73,136},{128... | collective-permute-start | bytes 589832 | tf_op jit(solution)/shard_map/ppermute | solution.py:50
  42.4 10.3 %collective-permute-start.7 = (bf16[128,768]{1,0:T(8,128)(2,1)}, bf16[128,768]{1,0:T(8,128)(2,1)S(1)}, u32[]{:S(2)}, u32[]{:S(2)}) collective-permute-start(bf16[128,768]{1,0:T(8,128)(2,1)} %get-tuple-element.17), channel_id=1, source_target_pairs={{0,457},{1,72},{8,449},{9,64},{64,9},{65,136},{72,1},{73,128},{128... | collective-permute-start | bytes 589832 | tf_op jit(solution)/shard_map/ppermute | solution.py:50
  52.8 7.3 %copy-start = (bf16[4,128,768]{2,1,0:T(8,128)(2,1)}, bf16[4,128,768]{2,1,0:T(8,128)(2,1)S(1)}, u32[]{:S(2)}) copy-start(bf16[4,128,768]{2,1,0:T(8,128)(2,1)S(1)} %pad_maximum_fusion.2.hop_one) | copy-start | bytes 2359300
  52.8 16.0 %collective-permute-start.8 = (bf16[4,128,768]{2,1,0:T(8,128)(2,1)S(1)}, bf16[4,128,768]{2,1,0:T(8,128)(2,1)}, u32[]{:S(2)}, u32[]{:S(2)}) collective-permute-start(bf16[4,128,768]{2,1,0:T(8,128)(2,1)S(1)} %pad_maximum_fusion.2.hop_one), channel_id=1, source_target_pairs={{0,64},{1,449},{8,72},{9,457},{64,128},{65,1},{72,136},{73,9},{128... | collective-permute-start | bytes 2359304 | tf_op jit(solution)/shard_map/ppermute | solution.py:50
  59.9 2.1 copy-start.4
  59.9 15.9 %copy-start.8 = (bf16[128,768]{1,0:T(8,128)(2,1)S(1)}, bf16[128,768]{1,0:T(8,128)(2,1)}, u32[]{:S(2)}) copy-start(bf16[128,768]{1,0:T(8,128)(2,1)} %get-tuple-element.21) | copy-start | bytes 589828
  60.1 41.2 %copy-start.7 = (f32[1,3072]{1,0:T(1,128)S(1)}, f32[1,3072]{1,0:T(1,128)}, u32[]{:S(2)}) copy-start(f32[1,3072]{1,0:T(1,128)} %param.12) | copy-start | bytes 36868
  60.1 62.2 %collective-permute-start.2 = (bf16[2,384,1024]{2,1,0:T(8,128)(2,1)S(1)}, bf16[2,384,1024]{2,1,0:T(8,128)(2,1)S(1)}, u32[]{:S(2)}, u32[]{:S(2)}) collective-permute-start(bf16[2,384,1024]{2,1,0:T(8,128)(2,1)S(1)} %pad_maximum_fusion.att_same), channel_id=1, source_target_pairs={{0,1},{1,0},{2,3},{3,2},{4,5},{5,4},{6,7},{7,6},{8,9},{9,8},{10,11... | collective-permute-start | bytes 4718600 | tf_op jit(solution)/shard_map/ppermute | solution.py:224
  62.1 18.7 %collective-permute-start.12 = (bf16[128,768]{1,0:T(8,128)(2,1)S(1)}, bf16[128,768]{1,0:T(8,128)(2,1)S(1)}, u32[]{:S(2)}, u32[]{:S(2)}) collective-permute-start(bf16[128,768]{1,0:T(8,128)(2,1)S(1)} %copy-done.4), channel_id=1, source_target_pairs={{0,64},{1,449},{8,72},{9,457},{64,128},{65,1},{72,136},{73,9},{128... | collective-permute-start | bytes 589832 | tf_op jit(solution)/shard_map/ppermute | solution.py:50
  68.8 43.7 %collective-permute-start.9 = (bf16[4,128,768]{2,1,0:T(8,128)(2,1)}, bf16[4,128,768]{2,1,0:T(8,128)(2,1)}, u32[]{:S(2)}, u32[]{:S(2)}) collective-permute-start(bf16[4,128,768]{2,1,0:T(8,128)(2,1)} %collective-permute-done.8.hop_two), channel_id=1, source_target_pairs={{0,64},{1,449},{8,72},{9,457},{64,128},{65,1},{72,136},{73,9},{128... | collective-permute-start | bytes 2359304 | tf_op jit(solution)/shard_map/ppermute | solution.py:50
  73.9 16.2 %collective-permute-start.14 = (bf16[128,768]{1,0:T(8,128)(2,1)S(1)}, bf16[128,768]{1,0:T(8,128)(2,1)S(1)}, u32[]{:S(2)}, u32[]{:S(2)}) collective-permute-start(bf16[128,768]{1,0:T(8,128)(2,1)S(1)} %copy-done.4), channel_id=1, source_target_pairs={{0,449},{1,64},{8,457},{9,72},{64,1},{65,128},{72,9},{73,136},{128... | collective-permute-start | bytes 589832 | tf_op jit(solution)/shard_map/ppermute | solution.py:50
  75.9 14.2 %collective-permute-start.13 = (bf16[128,768]{1,0:T(8,128)(2,1)S(1)}, bf16[128,768]{1,0:T(8,128)(2,1)S(1)}, u32[]{:S(2)}, u32[]{:S(2)}) collective-permute-start(bf16[128,768]{1,0:T(8,128)(2,1)S(1)} %copy-done.8), channel_id=1, source_target_pairs={{0,72},{1,457},{8,64},{9,449},{64,136},{65,9},{72,128},{73,1},{128... | collective-permute-start | bytes 589832 | tf_op jit(solution)/shard_map/ppermute | solution.py:50
  80.7 9.8 %collective-permute-start.15 = (bf16[128,768]{1,0:T(8,128)(2,1)S(1)}, bf16[128,768]{1,0:T(8,128)(2,1)S(1)}, u32[]{:S(2)}, u32[]{:S(2)}) collective-permute-start(bf16[128,768]{1,0:T(8,128)(2,1)S(1)} %copy-done.8), channel_id=1, source_target_pairs={{0,457},{1,72},{8,449},{9,64},{64,9},{65,136},{72,1},{73,128},{128... | collective-permute-start | bytes 589832 | tf_op jit(solution)/shard_map/ppermute | solution.py:50
  90.6 31.7 %copy-start.6 = (s32[11]{0:T(128)S(1)}, s32[11]{0:T(128)}, u32[]{:S(2)}) copy-start(s32[11]{0:T(128)} %stack.86.place) | copy-start | bytes 136
  91.6 26.0 %collective-permute-start.16 = (bf16[4,128,768]{2,1,0:T(8,128)(2,1)}, bf16[4,128,768]{2,1,0:T(8,128)(2,1)}, u32[]{:S(2)}, u32[]{:S(2)}) collective-permute-start(bf16[4,128,768]{2,1,0:T(8,128)(2,1)} %pad_maximum_fusion.3.hop_one), channel_id=1, source_target_pairs={{0,64},{1,449},{8,72},{9,457},{64,128},{65,1},{72,136},{73,9},{128... | collective-permute-start | bytes 2359304 | tf_op jit(solution)/shard_map/ppermute | solution.py:50
  99.4 20.1 %collective-permute-start.3 = (bf16[128,1536]{1,0:T(8,128)(2,1)}, bf16[128,1536]{1,0:T(8,128)(2,1)}, u32[]{:S(2)}, u32[]{:S(2)}) collective-permute-start(bf16[128,1536]{1,0:T(8,128)(2,1)} %get-tuple-element.16), channel_id=1, source_target_pairs={{0,8},{8,0},{1,9},{9,1},{2,10},{10,2},{3,11},{11,3},{4,12},{12,4},... | collective-permute-start | bytes 1179656 | tf_op jit(solution)/shard_map/ppermute | solution.py:213
  101.3 21.0 %copy-start.1 = (bf16[4,128,768]{2,1,0:T(8,128)(2,1)S(1)}, bf16[4,128,768]{2,1,0:T(8,128)(2,1)}, u32[]{:S(2)}) copy-start(bf16[4,128,768]{2,1,0:T(8,128)(2,1)} %copy-done) | copy-start | bytes 2359300
  113.5 8.8 %collective-permute-start.10 = (bf16[2,128,768]{2,1,0:T(8,128)(2,1)S(1)}, bf16[2,128,768]{2,1,0:T(8,128)(2,1)S(1)}, u32[]{:S(2)}, u32[]{:S(2)}) collective-permute-start(bf16[2,128,768]{2,1,0:T(8,128)(2,1)S(1)} %slice.17), channel_id=1, source_target_pairs={{0,64},{1,449},{8,72},{9,457},{64,128},{65,1},{72,136},{73,9},{128... | collective-permute-start | bytes 1179656 | tf_op jit(solution)/shard_map/ppermute | solution.py:50
  117.6 14.2 %collective-permute-start.17 = (bf16[4,128,768]{2,1,0:T(8,128)(2,1)}, bf16[4,128,768]{2,1,0:T(8,128)(2,1)S(1)}, u32[]{:S(2)}, u32[]{:S(2)}) collective-permute-start(bf16[4,128,768]{2,1,0:T(8,128)(2,1)} %collective-permute-done.16.hop_two), channel_id=1, source_target_pairs={{0,64},{1,449},{8,72},{9,457},{64,128},{65,1},{72,136},{73,9},{128... | collective-permute-start | bytes 2359304 | tf_op jit(solution)/shard_map/ppermute | solution.py:50
  122.3 0.9 copy-start.5
  127.5 9.8 %collective-permute-start.11 = (f32[8,2,72,128]{3,2,1,0:T(8,128)S(1)}, f32[8,2,72,128]{3,2,1,0:T(8,128)S(1)}, u32[]{:S(2)}, u32[]{:S(2)}) collective-permute-start(f32[8,2,72,128]{3,2,1,0:T(8,128)S(1)} %get-tuple-element.19), channel_id=1, source_target_pairs={{0,1},{1,0},{2,3},{3,2},{4,5},{5,4},{6,7},{7,6},{8,9},{9,8},{10,11... | collective-permute-start | bytes 1769480 | tf_op jit(solution)/shard_map/ppermute | solution.py:236
  132.5 0.9 copy-start.2
  133.4 12.8 %collective-permute-start.18 = (bf16[2,128,768]{2,1,0:T(8,128)(2,1)}, bf16[2,128,768]{2,1,0:T(8,128)(2,1)}, u32[]{:S(2)}, u32[]{:S(2)}) collective-permute-start(bf16[2,128,768]{2,1,0:T(8,128)(2,1)} %slice.19), channel_id=1, source_target_pairs={{0,64},{1,449},{8,72},{9,457},{64,128},{65,1},{72,136},{73,9},{128... | collective-permute-start | bytes 1179656 | tf_op jit(solution)/shard_map/ppermute | solution.py:50
  138.2 26.6 %all-to-all-start = ((f32[8,2,72,128]{3,2,1,0:T(8,128)}), f32[8,2,72,128]{3,2,1,0:T(8,128)}, u32[]{:S(2)}, u32[]{:S(2)}) async-start(f32[8,2,72,128]{3,2,1,0:T(8,128)} %add.71), calls=%async_computation | async-start | bytes 1179648 | tf_op jit(solution)/shard_map/all_to_all | solution.py:237
  146.2 1.1 copy-start.3
  151.6 4.8 %collective-permute-start.19 = (f32[8,2,72,128]{3,2,1,0:T(8,128)S(1)}, f32[8,2,72,128]{3,2,1,0:T(8,128)S(1)}, u32[]{:S(2)}, u32[]{:S(2)}) collective-permute-start(f32[8,2,72,128]{3,2,1,0:T(8,128)S(1)} %get-tuple-element.23), channel_id=1, source_target_pairs={{0,1},{1,0},{2,3},{3,2},{4,5},{5,4},{6,7},{7,6},{8,9},{9,8},{10,11... | collective-permute-start | bytes 1769480 | tf_op jit(solution)/shard_map/ppermute | solution.py:236
  164.9 22.8 %all-to-all-start.1 = ((f32[8,2,72,128]{3,2,1,0:T(8,128)}), f32[8,2,72,128]{3,2,1,0:T(8,128)S(1)}, u32[]{:S(2)}, u32[]{:S(2)}) async-start(f32[8,2,72,128]{3,2,1,0:T(8,128)} %add.75), calls=%async_computation.1 | async-start | bytes 1179648 | tf_op jit(solution)/shard_map/all_to_all | solution.py:237

commit v4 on v3

--- a/solution.py
+++ b/solution.py
@@ -25,7 +25,6 @@
 GROUP = D // 8
 HALF = LB // 2
 PACK = (LB * HB) // 128
-PIECES = ((0, 1), (2, 3))
 ROW = ("zh", "zl", "yl", "c")
 COL = ("yh", "x")
 Y = ("yh", "yl")
@@ -50,6 +49,10 @@
     return lax.ppermute(block, ("x", "zl", "c"), ring(other_z, other_core))
 
 
+def after(value, *others):
+    return lax.optimization_barrier((value, *others))[0]
+
+
 def split_kernel(place, cotangent, mine_one, mine_two, other_one, other_two, other_all):
     for zh in range(NZH):
         span = slice((zh % 2) * GROUP, (zh % 2 + 1) * GROUP)
@@ -70,29 +73,84 @@
     )(place, cotangent)
 
 
+def features_kernel(place, kept, came, gate, own, cross):
+    for top, bottom, yh in ((kept, came, 0), (came, kept, 1)):
+
+        @pl.when(place[9] == yh)
+        def _():
+            for ref, hops, sign in ((own, range(5), 1), (cross, range(1, 4), -1)):
+                for at, count in enumerate(hops):
+                    start = pl.multiple_of(place[1 + (sign * count) % NX] * CHUNK, CHUNK)
+                    here = slice(at * CHUNK, (at + 1) * CHUNK)
+                    ref[:HB, here] = top[:, pl.ds(start, CHUNK)]
+                    ref[HB:FEAT, here] = bottom[:, pl.ds(start, CHUNK)]
+
+    rest = gate[...]
+    rows = []
+    for _ in range(3):
+        part = rest.astype(jnp.bfloat16)
+        rest = rest - part.astype(jnp.float32)
+        rows.append(part)
+    rows = jnp.concatenate(rows + [jnp.zeros_like(rows[0])], axis=0)
+    for ref in (own, cross):
+        ref[FEAT:, :GROUP] = rows
+        if ref.shape[1] > GROUP:
+            ref[FEAT:, GROUP:] = jnp.zeros((32, ref.shape[1] - GROUP), jnp.bfloat16)
+
+
+def features_of(place, kept, came, gate):
+    def shape(hops):
+        return jax.ShapeDtypeStruct((FEAT + 32, hops * CHUNK), jnp.bfloat16)
+
+    def whole(array):
+        return pl.BlockSpec(array.shape, lambda: (0, 0))
+
+    return pl.pallas_call(
+        features_kernel,
+        in_specs=[pl.BlockSpec(memory_space=pltpu.SMEM), whole(kept), whole(came), whole(gate)],
+        out_shape=[shape(5), shape(3)],
+        name="features",
+    )(place, kept, came, gate)
+
+
 def product_kernel(
-    place, att_same, att_cross, own, beside, hop_one, hop_two, hop_three, last, gates, keep, send
+    piece,
+    place,
+    att_own,
+    att_beside,
+    att_cross,
+    att_across,
+    own,
+    beside,
+    hop_one,
+    hop_two,
+    hop_three,
+    last,
+    keep,
+    send,
 ):
-    def att(which, *hops):
-        ref = (att_same, att_cross)[which // 2]
-        parts = []
-        for at in hops:
-            columns = pl.ds(pl.multiple_of(place[1 + at] * CHUNK, CHUNK), CHUNK)
-            parts.append(ref[which % 2, :, columns])
-        return parts[0] if len(parts) == 1 else jnp.concatenate(parts, axis=1)
+    group = 2 * (2 * piece + pl.program_id(0)) + place[6]
 
     def dot(left, *blocks):
         right = blocks[0] if len(blocks) == 1 else jnp.concatenate(blocks, axis=0)
         return jnp.dot(left, right, preferred_element_type=jnp.float32)
 
     total = jnp.zeros((FEAT, GROUP), jnp.float32)
-    for which in range(4):
-        clip = dot(att(which, 1, 2), hop_one[which], hop_two[which])
-        clip += dot(att(which, 3), hop_three[which])
+    for which, att in enumerate((att_own, att_beside, att_cross, att_across)):
+        one, two, three = hop_one[which], hop_two[which], hop_three[which]
         if which < 2:
             near = (own, beside)[which][...]
-            clip += dot(att(which, 0, 4), near, last[which])
-        total += gates[pl.ds(place[7 + which], 1), :] * clip
+            clip = dot(att[:FEAT, : 2 * CHUNK], near, one)
+            clip += dot(att[:FEAT, 2 * CHUNK : 4 * CHUNK], two, three)
+            clip += dot(att[:FEAT, 4 * CHUNK :], last[which])
+        else:
+            clip = dot(att[:FEAT, : 2 * CHUNK], one, two)
+            clip += dot(att[:FEAT, 2 * CHUNK :], three)
+        parts = att[FEAT:, :GROUP].astype(jnp.float32)
+        rows = lax.broadcasted_iota(jnp.int32, parts.shape, 0)
+        mine = (rows & 7 == group) & (rows < 24)
+        gate = jnp.sum(jnp.where(mine, parts, 0.0), axis=0, keepdims=True)
+        total += gate * clip
     packed = []
     for yh in range(2):
         at = yh * HB
@@ -115,27 +173,28 @@
             store(send, 1 - core)
 
 
-def product(place, att_same, att_cross, own, beside, blocks, gates):
+def product(piece, place, atts, own, beside, blocks):
     count = own.shape[1] // GROUP
-    attn = pl.BlockSpec((2, FEAT, TOK), lambda z: (0, 0, 0))
+    attn = [pl.BlockSpec(att.shape, lambda z: (0, 0)) for att in atts]
     plain = pl.BlockSpec((CHUNK, GROUP), lambda z: (0, z))
+    near = pl.BlockSpec((CHUNK, GROUP), lambda z: (0, 2 * piece + z))
     four = pl.BlockSpec((4, CHUNK, GROUP), lambda z: (0, 0, z))
     pair = pl.BlockSpec((2, CHUNK, GROUP), lambda z: (0, 0, z))
-    rows = pl.BlockSpec((4, GROUP), lambda z: (0, z))
     out = pl.BlockSpec((2 * NY, 1, PACK, 128), lambda z: (0, z, 0, 0))
     shape = jax.ShapeDtypeStruct((2 * NY, count, PACK, 128), jnp.float32)
     flops = 2 * 16 * CHUNK * FEAT * GROUP * count
     return pl.pallas_call(
-        product_kernel,
+        functools.partial(product_kernel, piece),
         grid=(count,),
-        in_specs=[pl.BlockSpec(memory_space=pltpu.SMEM), attn, attn, plain, plain]
-        + [four, four, four, pair, rows],
+        in_specs=[pl.BlockSpec(memory_space=pltpu.SMEM)]
+        + attn
+        + [plain, near, four, four, four, pair],
         out_specs=[out, out],
         out_shape=[shape, shape],
         cost_estimate=pl.CostEstimate(flops=flops, bytes_accessed=8 << 20, transcendentals=0),
         compiler_params=pltpu.CompilerParams(vmem_limit_bytes=32 << 20),
         name="product",
-    )(place, att_same, att_cross, own, beside, *blocks, gates)
+    )(place, *atts, own, beside, *blocks)
 
 
 def update_kernel(
@@ -196,43 +255,46 @@
 ):
     yh, x, zl, core = (lax.axis_index(name) for name in ("yh", "x", "zl", "c"))
     step = 1 - 2 * core
-    clips = [2 * z + c for c in (core, 1 - core) for z in (zl, 1 - zl)]
-    place = [core] + [lax.rem(x - step * hops + NX, NX) for hops in range(5)] + [zl] + clips
-    place = jnp.stack(place)
+    sources = [lax.rem(x - step * count + 2 * NX, NX) for count in range(NX)]
+    place = jnp.stack([core] + sources[:5] + [zl])
 
     mine_one, mine_two, other_one, other_two, other_all = split(place, cotangent)
-    rings = []
-    for mine, other in ((mine_one, other_one), (mine_two, other_two)):
-        blocks = [
-            jnp.stack([hop(mine), hop(other, 1, 0), hop(mine, 0, 1), hop(other, 1, 1)])
-        ]
-        blocks.append(hop(blocks[-1]))
-        blocks.append(hop(blocks[-1]))
-        blocks.append(hop(blocks[-1][:2]))
-        rings.append(blocks)
-    beside = lax.ppermute(other_all, "zl", SWAP)
+
+    def first_hop(mine, other):
+        return [hop(mine), hop(other, 1, 0), hop(mine, 0, 1), hop(other, 1, 1)]
+
+    parts_one = first_hop(mine_one, other_one)
+    parts_two = first_hop(after(mine_two, parts_one[0]), after(other_two, parts_one[0]))
+    first_one = jnp.stack(parts_one)
+    first_two = jnp.stack(parts_two)
 
     features = attn_out.T
     kept = lax.dynamic_slice_in_dim(features, yh * TOK, TOK, 1)
-    came = lax.ppermute(
-        lax.dynamic_slice_in_dim(features, (1 - yh) * TOK, TOK, 1), "yh", SWAP
+    away = lax.dynamic_slice_in_dim(features, (1 - yh) * TOK, TOK, 1)
+    came = after(lax.ppermute(after(away, parts_one[0]), "yh", SWAP), first_two)
+    att_own, att_swap = features_of(jnp.stack([core] + sources + [yh]), kept, came, gate.reshape(8, GROUP))
+    atts = (
+        att_own,
+        lax.ppermute(att_own, "zl", SWAP),
+        lax.ppermute(att_swap, "c", SWAP),
+        lax.ppermute(att_swap, ("zl", "c"), [(0, 3), (1, 2), (2, 1), (3, 0)]),
     )
-    att_own = jnp.concatenate(
-        [jnp.where(yh == 0, kept, came), jnp.where(yh == 0, came, kept)], axis=0
+
+    second_one = hop(first_one)
+    second_two = hop(first_two)
+    third_one = hop(after(second_one, first_two, att_own))
+    third_two = hop(second_two)
+    last_one = hop(after(third_one, second_two)[:2])
+    last_two = hop(third_two[:2])
+    beside = lax.ppermute(after(other_all, second_two), "zl", SWAP)
+    rings = (
+        (mine_one, (first_one, second_one, third_one, last_one)),
+        (mine_two, (first_two, second_two, third_two, last_two)),
     )
-    att_same = jnp.stack([att_own, lax.ppermute(att_own, "zl", SWAP)])
-    att_cross = lax.ppermute(att_same, "c", SWAP)
-    gates = lax.all_gather(gate, ("zl", "c"), axis=0, tiled=True)
 
     by_z = []
-    for at, (zhs, mine, blocks) in enumerate(zip(PIECES, (mine_one, mine_two), rings)):
-        groups = [
-            lax.dynamic_slice_in_dim(gates, (2 * zh + zl) * GROUP, GROUP, 1) for zh in zhs
-        ]
-        near = beside[:, 2 * at * GROUP : 2 * (at + 1) * GROUP]
-        keep, send = product(
-            place, att_same, att_cross, mine, near, blocks, jnp.concatenate(groups, axis=1)
-        )
+    for at, (mine, blocks) in enumerate(rings):
+        keep, send = product(at, place, atts, mine, beside, blocks)
         paired = keep + lax.ppermute(send, "c", SWAP)
         by_z.append(jnp.sum(lax.all_to_all(paired, Y, 0, 0), axis=0))
     parts = lax.all_to_all(jnp.concatenate(by_z, axis=0), "zh", 0, 0)

time: 215 us -> 185 us (0.86)
  waiting for transfers between devices: 53 us -> 38.2 us
  blocking collectives: 32.4 us -> 19.1 us
    ppermute x14, waiting for transfers between devices: 19 us -> 5.99 us  [hop(): return lax.ppermute(block, ('x', 'zl', 'c'), ring(other_z, other_core))]
    all_gather x1 -> x0, blocking collectives: 10.5 us -> none  [local(): gates = lax.all_gather(gate, ('zl', 'c'), axis=0, tiled=True)]
    ppermute x14, starting transfers between devices: 57.2 us -> 66.4 us  [hop(): return lax.ppermute(block, ('x', 'zl', 'c'), ring(other_z, other_core))]
    ppermute x4 -> x5, starting transfers between devices: 22.7 us -> 14.1 us  [the longest x1 4.88 us: local(): lax.ppermute(att_swap, ('zl', 'c'), [(0, 3), (1, 2), (2, 1), (3, 0)])]
    all_to_all x1, blocking collectives: 21.9 us -> 19.1 us  [local(): parts = lax.all_to_all(jnp.concatenate(by_z, axis=0), 'zh', 0, 0)]
    pallas_call x2 -> x3, Pallas kernels: 8.43 us -> 10.1 us  [the longest x2 7.83 us: product(): pl.pallas_call(functools.partial(product_kernel, piece), grid=(count,), i...]
    ppermute x4 -> x5, waiting for transfers between devices: 6.62 us -> 5.5 us  [the longest x1 5.13 us: local(): lax.ppermute(att_swap, ('zl', 'c'), [(0, 3), (1, 2), (2, 1), (3, 0)])]
    unnamed x20 -> x33, local copies, waits for them, and re-layouts: 3.67 us -> 4.73 us
  transfers between devices with their start and end apart: 22 -> 23, of which waited for: 10 -> 8; matrix products, arithmetic and copies ran while one was open for 4% -> 4% of each run, Pallas kernels for 5% -> 6%
where the time goes in v4:
time: 185 us; the launch traced here: 184 us
  starting transfers between devices  96.6 us (52%)
  waiting for transfers between devices  38.2 us (21%)
  blocking collectives  19.1 us (10%)
  Pallas kernels  15.5 us (8%)
  local copies, waits for them, and re-layouts  8.19 us (4%)
  other arithmetic  4.81 us (3%)
    ppermute x14, starting transfers between devices, hop(): return lax.ppermute(block, ('x', 'zl', 'c'), ring(other_z, other_core))  66.4 us
    all_to_all x2, waiting for transfers between devices, local(): by_z.append(jnp.sum(lax.all_to_all(paired, Y, 0, 0), axis=0))  25.1 us
    all_to_all x1, blocking collectives, local(): parts = lax.all_to_all(jnp.concatenate(by_z, axis=0), 'zh', 0, 0)  19.1 us
    all_to_all x2, starting transfers between devices, local(): by_z.append(jnp.sum(lax.all_to_all(paired, Y, 0, 0), axis=0))  9.3 us
    pallas_call x2, Pallas kernels, product(): pl.pallas_call(functools.partial(product_kernel, piece), grid=(count,), i...  7.83 us
    ppermute x2, starting transfers between devices, local(): paired = keep + lax.ppermute(send, 'c', SWAP)  6.81 us
    ppermute x14, waiting for transfers between devices, hop(): return lax.ppermute(block, ('x', 'zl', 'c'), ring(other_z, other_core))  5.99 us
    ppermute x1, waiting for transfers between devices, local(): lax.ppermute(att_swap, ('zl', 'c'), [(0, 3), (1, 2), (2, 1), (3, 0)])  5.13 us
  transfers between devices with their start and end apart: 23, of which 8 were waited for; matrix products, arithmetic and copies ran while one was open for 4% of the time, Pallas kernels for 6%

profile of v4, /device:TPU:1, one launch (start us, length us, event | category | flops | bytes accessed | tf_op | source)
XLA Modules:
  0.0 183.5 jit_solution(6899153791301319435)
XLA Ops:
  1.3 2.2 %split.1 = (bf16[128,768]{1,0:T(8,128)(2,1)}, bf16[128,768]{1,0:T(8,128)(2,1)}, bf16[128,768]{1,0:T(8,128)(2,1)}, bf16[128,768]{1,0:T(8,128)(2,1)}, bf16[128,1536]{1,0:T(8,128)(2,1)}) custom-call(s32[7]{0:T(128)} %stack.82.place, bf16[128,3072]{1,0:T(8,128)(2,1)} %cotangent.1), custom_call_target="tpu_custom_call" | custom-call | tf_op jit(solution)/shard_map/split/pallas_call | solution.py:68
  3.5 5.3 %collective-permute-start = (bf16[128,768]{1,0:T(8,128)(2,1)}, bf16[128,768]{1,0:T(8,128)(2,1)S(1)}, u32[]{:S(2)}, u32[]{:S(2)}) collective-permute-start(bf16[128,768]{1,0:T(8,128)(2,1)} %get-tuple-element.24.own), channel_id=1, source_target_pairs={{0,64},{1,449},{8,72},{9,457},{64,128},{65,1},{72,136},{73,9},{128... | collective-permute-start | bytes 589832 | tf_op jit(solution)/shard_map/ppermute | solution.py:49
  8.9 5.3 %collective-permute-start.13 = (bf16[128,768]{1,0:T(8,128)(2,1)}, bf16[128,768]{1,0:T(8,128)(2,1)S(1)}, u32[]{:S(2)}, u32[]{:S(2)}) collective-permute-start(bf16[128,768]{1,0:T(8,128)(2,1)} %get-tuple-element.35), channel_id=1, source_target_pairs={{0,457},{1,72},{8,449},{9,64},{64,9},{65,136},{72,1},{73,128},{128... | collective-permute-start | bytes 589832 | tf_op jit(solution)/shard_map/ppermute | solution.py:49
  14.2 3.0 %collective-permute-start.12 = (bf16[128,768]{1,0:T(8,128)(2,1)}, bf16[128,768]{1,0:T(8,128)(2,1)S(1)}, u32[]{:S(2)}, u32[]{:S(2)}) collective-permute-start(bf16[128,768]{1,0:T(8,128)(2,1)} %get-tuple-element.24.own), channel_id=1, source_target_pairs={{0,449},{1,64},{8,457},{9,72},{64,1},{65,128},{72,9},{73,136},{128... | collective-permute-start | bytes 589832 | tf_op jit(solution)/shard_map/ppermute | solution.py:49
  17.1 11.7 %collective-permute-start.11 = (bf16[128,768]{1,0:T(8,128)(2,1)}, bf16[128,768]{1,0:T(8,128)(2,1)S(1)}, u32[]{:S(2)}, u32[]{:S(2)}) collective-permute-start(bf16[128,768]{1,0:T(8,128)(2,1)} %get-tuple-element.35), channel_id=1, source_target_pairs={{0,72},{1,457},{8,64},{9,449},{64,136},{65,9},{72,128},{73,1},{128... | collective-permute-start | bytes 589832 | tf_op jit(solution)/shard_map/ppermute | solution.py:49
  28.8 2.9 %collective-permute-done.11 = bf16[128,768]{1,0:T(8,128)(2,1)S(1)} collective-permute-done((bf16[128,768]{1,0:T(8,128)(2,1)}, bf16[128,768]{1,0:T(8,128)(2,1)S(1)}, u32[]{:S(2)}, u32[]{:S(2)}) %collective-permute-start.11) | collective-permute-done | bytes 196640 | tf_op jit(solution)/shard_map/ppermute | solution.py:49
  31.8 6.8 %collective-permute-start.14 = (bf16[4,128,768]{2,1,0:T(8,128)(2,1)S(1)}, bf16[4,128,768]{2,1,0:T(8,128)(2,1)S(1)}, u32[]{:S(2)}, u32[]{:S(2)}) collective-permute-start(bf16[4,128,768]{2,1,0:T(8,128)(2,1)S(1)} %pad_maximum_fusion.1.hop_one), channel_id=1, source_target_pairs={{0,64},{1,449},{8,72},{9,457},{64,128},{65,1},{72,136},{73,9},{128... | collective-permute-start | bytes 2359304 | tf_op jit(solution)/shard_map/ppermute | solution.py:49
  38.6 1.9 %collective-permute-start.5 = (bf16[128,768]{1,0:T(8,128)(2,1)}, bf16[128,768]{1,0:T(8,128)(2,1)S(1)}, u32[]{:S(2)}, u32[]{:S(2)}) collective-permute-start(bf16[128,768]{1,0:T(8,128)(2,1)} %get-tuple-element.29), channel_id=1, source_target_pairs={{0,457},{1,72},{8,449},{9,64},{64,9},{65,136},{72,1},{73,128},{128... | collective-permute-start | bytes 589832 | tf_op jit(solution)/shard_map/ppermute | solution.py:49
  43.4 3.9 %collective-permute-start.3 = (bf16[128,768]{1,0:T(8,128)(2,1)}, bf16[128,768]{1,0:T(8,128)(2,1)S(1)}, u32[]{:S(2)}, u32[]{:S(2)}) collective-permute-start(bf16[128,768]{1,0:T(8,128)(2,1)} %get-tuple-element.29), channel_id=1, source_target_pairs={{0,72},{1,457},{8,64},{9,449},{64,136},{65,9},{72,128},{73,1},{128... | collective-permute-start | bytes 589832 | tf_op jit(solution)/shard_map/ppermute | solution.py:49
  47.3 1.9 %collective-permute-start.4 = (bf16[128,768]{1,0:T(8,128)(2,1)S(1)}, bf16[128,768]{1,0:T(8,128)(2,1)}, u32[]{:S(2)}, u32[]{:S(2)}) collective-permute-start(bf16[128,768]{1,0:T(8,128)(2,1)S(1)} %copy-done.9), channel_id=1, source_target_pairs={{0,449},{1,64},{8,457},{9,72},{64,1},{65,128},{72,9},{73,136},{128... | collective-permute-start | bytes 589832 | tf_op jit(solution)/shard_map/ppermute | solution.py:49
  49.3 5.5 %collective-permute-start.2 = (bf16[128,768]{1,0:T(8,128)(2,1)S(1)}, bf16[128,768]{1,0:T(8,128)(2,1)}, u32[]{:S(2)}, u32[]{:S(2)}) collective-permute-start(bf16[128,768]{1,0:T(8,128)(2,1)S(1)} %copy-done.9), channel_id=1, source_target_pairs={{0,64},{1,449},{8,72},{9,457},{64,128},{65,1},{72,136},{73,9},{128... | collective-permute-start | bytes 589832 | tf_op jit(solution)/shard_map/ppermute | solution.py:49
  58.5 5.3 %collective-permute-start.9 = (bf16[4,128,768]{2,1,0:T(8,128)(2,1)S(1)}, bf16[4,128,768]{2,1,0:T(8,128)(2,1)}, u32[]{:S(2)}, u32[]{:S(2)}) collective-permute-start(bf16[4,128,768]{2,1,0:T(8,128)(2,1)S(1)} %pad_maximum_fusion.hop_one), channel_id=1, source_target_pairs={{0,64},{1,449},{8,72},{9,457},{64,128},{65,1},{72,136},{73,9},{128... | collective-permute-start | bytes 2359304 | tf_op jit(solution)/shard_map/ppermute | solution.py:49
  64.9 2.3 %features.1 = (bf16[416,640]{1,0:T(8,128)(2,1)}, bf16[416,384]{1,0:T(8,128)(2,1)}) custom-call(s32[10]{0:T(128)} %stack.87.place, bf16[192,1024]{1,0:T(8,128)(2,1)} %get-tuple-element.43.kept, bf16[192,1024]{1,0:T(8,128)(2,1)} %copy-done.14, f32[8,384]{1,0:T(8,128)} %reshape.15.gate), custom_call_target="tpu_custom_call" | custom-call | tf_op jit(solution)/shard_map/features/pallas_call | solution.py:108
  67.2 3.7 %collective-permute-start.15 = (bf16[4,128,768]{2,1,0:T(8,128)(2,1)S(1)}, bf16[4,128,768]{2,1,0:T(8,128)(2,1)S(1)}, u32[]{:S(2)}, u32[]{:S(2)}) collective-permute-start(bf16[4,128,768]{2,1,0:T(8,128)(2,1)S(1)} %collective-permute-done.14.hop_two), channel_id=1, source_target_pairs={{0,64},{1,449},{8,72},{9,457},{64,128},{65,1},{72,136},{73,9},{128... | collective-permute-start | bytes 2359304 | tf_op jit(solution)/shard_map/ppermute | solution.py:49
  70.8 2.4 %collective-permute-start.6 = (bf16[416,640]{1,0:T(8,128)(2,1)}, bf16[416,640]{1,0:T(8,128)(2,1)S(1)}, u32[]{:S(2)}, u32[]{:S(2)}) collective-permute-start(bf16[416,640]{1,0:T(8,128)(2,1)} %get-tuple-element.31.att_own), channel_id=1, source_target_pairs={{0,8},{8,0},{1,9},{9,1},{2,10},{10,2},{3,11},{11,3},{4,12},{12,4},... | collective-permute-start | bytes 1597448 | tf_op jit(solution)/shard_map/ppermute | solution.py:278
  75.2 3.0 %collective-permute-start.10 = (bf16[128,1536]{1,0:T(8,128)(2,1)}, bf16[128,1536]{1,0:T(8,128)(2,1)S(1)}, u32[]{:S(2)}, u32[]{:S(2)}) collective-permute-start(bf16[128,1536]{1,0:T(8,128)(2,1)} %get-tuple-element.34), channel_id=1, source_target_pairs={{0,8},{8,0},{1,9},{9,1},{2,10},{10,2},{3,11},{11,3},{4,12},{12,4},... | collective-permute-start | bytes 1179656 | tf_op jit(solution)/shard_map/ppermute | solution.py:289
  78.2 2.9 %collective-permute-done.15.hop_three = bf16[4,128,768]{2,1,0:T(8,128)(2,1)S(1)} collective-permute-done((bf16[4,128,768]{2,1,0:T(8,128)(2,1)S(1)}, bf16[4,128,768]{2,1,0:T(8,128)(2,1)S(1)}, u32[]{:S(2)}, u32[]{:S(2)}) %collective-permute-start.15) | collective-permute-done | bytes 786464 | tf_op jit(solution)/shard_map/ppermute | solution.py:49
  81.1 5.0 %collective-permute-start.16 = (bf16[2,128,768]{2,1,0:T(8,128)(2,1)S(1)}, bf16[2,128,768]{2,1,0:T(8,128)(2,1)S(1)}, u32[]{:S(2)}, u32[]{:S(2)}) collective-permute-start(bf16[2,128,768]{2,1,0:T(8,128)(2,1)S(1)} %slice.6), channel_id=1, source_target_pairs={{0,64},{1,449},{8,72},{9,457},{64,128},{65,1},{72,136},{73,9},{128... | collective-permute-start | bytes 1179656 | tf_op jit(solution)/shard_map/ppermute | solution.py:49
  86.2 4.9 %collective-permute-start.8 = (bf16[416,384]{1,0:T(8,128)(2,1)}, bf16[416,384]{1,0:T(8,128)(2,1)S(1)}, u32[]{:S(2)}, u32[]{:S(2)}) collective-permute-start(bf16[416,384]{1,0:T(8,128)(2,1)} %get-tuple-element.32), channel_id=1, source_target_pairs={{0,9},{1,8},{8,1},{9,0},{2,11},{3,10},{10,3},{11,2},{4,13},{5,12},... | collective-permute-start | bytes 958472 | tf_op jit(solution)/shard_map/ppermute | solution.py:280
  91.1 4.9 %collective-permute-start.18 = (bf16[4,128,768]{2,1,0:T(8,128)(2,1)}, bf16[4,128,768]{2,1,0:T(8,128)(2,1)S(1)}, u32[]{:S(2)}, u32[]{:S(2)}) collective-permute-start(bf16[4,128,768]{2,1,0:T(8,128)(2,1)} %collective-permute-done.9.hop_two), channel_id=1, source_target_pairs={{0,64},{1,449},{8,72},{9,457},{64,128},{65,1},{72,136},{73,9},{128... | collective-permute-start | bytes 2359304 | tf_op jit(solution)/shard_map/ppermute | solution.py:49
  95.9 5.1 %collective-permute-done.8.att_across = bf16[416,384]{1,0:T(8,128)(2,1)S(1)} collective-permute-done((bf16[416,384]{1,0:T(8,128)(2,1)}, bf16[416,384]{1,0:T(8,128)(2,1)S(1)}, u32[]{:S(2)}, u32[]{:S(2)}) %collective-permute-start.8) | collective-permute-done | bytes 319520 | tf_op jit(solution)/shard_map/ppermute | solution.py:280
  102.5 3.7 %product.2 = (f32[8,2,72,128]{3,2,1,0:T(8,128)S(1)}, f32[8,2,72,128]{3,2,1,0:T(8,128)S(1)}) custom-call(s32[7]{0:T(128)S(1)} %copy-done.12, bf16[416,640]{1,0:T(8,128)(2,1)S(1)} %copy-done, bf16[416,640]{1,0:T(8,128)(2,1)S(1)} %collective-permute-done.6.att_beside, bf16[416,384]{1,0:T(8,128)(2,1)S(1)} %collective-permute-done.7.att_cross, ...), custom_call_target="tpu_custom_call" | custom-call | flops 1207959552 | bytes 8388608 | tf_op jit(solution)/shard_map/product/pallas_call | solution.py:186
  106.2 2.9 %collective-permute-start.17 = (f32[8,2,72,128]{3,2,1,0:T(8,128)S(1)}, f32[8,2,72,128]{3,2,1,0:T(8,128)S(1)}, u32[]{:S(2)}, u32[]{:S(2)}) collective-permute-start(f32[8,2,72,128]{3,2,1,0:T(8,128)S(1)} %get-tuple-element.39), channel_id=1, source_target_pairs={{0,1},{1,0},{2,3},{3,2},{4,5},{5,4},{6,7},{7,6},{8,9},{9,8},{10,11... | collective-permute-start | bytes 1769480 | tf_op jit(solution)/shard_map/ppermute | solution.py:298
  109.9 2.2 %collective-permute-start.19 = (bf16[2,128,768]{2,1,0:T(8,128)(2,1)}, bf16[2,128,768]{2,1,0:T(8,128)(2,1)}, u32[]{:S(2)}, u32[]{:S(2)}) collective-permute-start(bf16[2,128,768]{2,1,0:T(8,128)(2,1)} %slice.8), channel_id=1, source_target_pairs={{0,64},{1,449},{8,72},{9,457},{64,128},{65,1},{72,136},{73,9},{128... | collective-permute-start | bytes 1179656 | tf_op jit(solution)/shard_map/ppermute | solution.py:49
  113.0 5.8 %all-to-all-start = ((f32[8,2,72,128]{3,2,1,0:T(8,128)}), f32[8,2,72,128]{3,2,1,0:T(8,128)}, u32[]{:S(2)}, u32[]{:S(2)}) async-start(f32[8,2,72,128]{3,2,1,0:T(8,128)} %add.46), calls=%async_computation | async-start | bytes 1179648 | tf_op jit(solution)/shard_map/all_to_all | solution.py:299
  120.9 4.1 %product.3 = (f32[8,2,72,128]{3,2,1,0:T(8,128)S(1)}, f32[8,2,72,128]{3,2,1,0:T(8,128)S(1)}) custom-call(s32[7]{0:T(128)S(1)} %copy-done.12, bf16[416,640]{1,0:T(8,128)(2,1)S(1)} %copy-done, bf16[416,640]{1,0:T(8,128)(2,1)S(1)} %collective-permute-done.6.att_beside, bf16[416,384]{1,0:T(8,128)(2,1)S(1)} %copy-done.4, bf16[416,384]{1,0:T(8,128)(2,1)S(1)} %copy-done.6, ...), custom_call_target="tpu_custom_call" | custom-call | flops 1207959552 | bytes 8388608 | tf_op jit(solution)/shard_map/product/pallas_call | solution.py:186
  125.0 3.9 %collective-permute-start.20 = (f32[8,2,72,128]{3,2,1,0:T(8,128)S(1)}, f32[8,2,72,128]{3,2,1,0:T(8,128)S(1)}, u32[]{:S(2)}, u32[]{:S(2)}) collective-permute-start(f32[8,2,72,128]{3,2,1,0:T(8,128)S(1)} %get-tuple-element.41), channel_id=1, source_target_pairs={{0,1},{1,0},{2,3},{3,2},{4,5},{5,4},{6,7},{7,6},{8,9},{9,8},{10,11... | collective-permute-start | bytes 1769480 | tf_op jit(solution)/shard_map/ppermute | solution.py:298
  131.5 6.9 %all-to-all-done = f32[8,2,72,128]{3,2,1,0:T(8,128)} async-done(((f32[8,2,72,128]{3,2,1,0:T(8,128)}), f32[8,2,72,128]{3,2,1,0:T(8,128)}, u32[]{:S(2)}, u32[]{:S(2)}) %all-to-all-start) | async-done | bytes 589856 | tf_op jit(solution)/shard_map/all_to_all | solution.py:299
  138.4 3.5 %all-to-all-start.1 = ((f32[8,2,72,128]{3,2,1,0:T(8,128)}), f32[8,2,72,128]{3,2,1,0:T(8,128)S(1)}, u32[]{:S(2)}, u32[]{:S(2)}) async-start(f32[8,2,72,128]{3,2,1,0:T(8,128)} %add.47), calls=%async_computation.1 | async-start | bytes 1179648 | tf_op jit(solution)/shard_map/all_to_all | solution.py:299
  143.0 18.2 %all-to-all-done.1 = f32[8,2,72,128]{3,2,1,0:T(8,128)S(1)} async-done(((f32[8,2,72,128]{3,2,1,0:T(8,128)}), f32[8,2,72,128]{3,2,1,0:T(8,128)S(1)}, u32[]{:S(2)}, u32[]{:S(2)}) %all-to-all-start.1) | async-done | bytes 589856 | tf_op jit(solution)/shard_map/all_to_all | solution.py:299
  161.3 19.1 %all_to_all.15.parts = f32[4,72,128]{2,1,0:T(8,128)} all-to-all(f32[4,72,128]{2,1,0:T(8,128)S(1)} %pad_maximum_fusion.2), channel_id=1, replica_groups=mesh['yh'=2,'x'=8,'zh'=4,'zl'=2,'yl'=4,'c'=2] {'zh'}, dimensions={0} | all-to-all | bytes 294912 | tf_op jit(solution)/shard_map/all_to_all | solution.py:300
  180.4 3.2 %update.1 = (f32[48,192]{1,0:T(8,128)}, f32[48,192]{1,0:T(8,128)}, f32[48,192]{1,0:T(8,128)}, f32[48,192]{1,0:T(8,128)}, f32[48,48]{1,0:T(8,128)}, /*index=5*/f32[192,192]{1,0:T(8,128)}) custom-call(f32[4,72,128]{2,1,0:T(8,128)} %all_to_all.15.parts, f32[48,192]{1,0:T(8,128)} %weight.1, f32[48,192]{1,0:T(8,128)} %exp_avg.1, f32[48,192]{1,0:T(8,128)} %exp_avg_sq.1, ...), custom_call_target="tpu_custom_call" | custom-call | tf_op jit(solution)/shard_map/update/pallas_call | solution.py:303
  (67 shorter events, 19.0 us)
Async XLA Ops:
  3.5 25.3 %collective-permute-start = (bf16[128,768]{1,0:T(8,128)(2,1)}, bf16[128,768]{1,0:T(8,128)(2,1)S(1)}, u32[]{:S(2)}, u32[]{:S(2)}) collective-permute-start(bf16[128,768]{1,0:T(8,128)(2,1)} %get-tuple-element.24.own), channel_id=1, source_target_pairs={{0,64},{1,449},{8,72},{9,457},{64,128},{65,1},{72,136},{73,9},{128... | collective-permute-start | bytes 589832 | tf_op jit(solution)/shard_map/ppermute | solution.py:49
  8.9 20.0 %collective-permute-start.13 = (bf16[128,768]{1,0:T(8,128)(2,1)}, bf16[128,768]{1,0:T(8,128)(2,1)S(1)}, u32[]{:S(2)}, u32[]{:S(2)}) collective-permute-start(bf16[128,768]{1,0:T(8,128)(2,1)} %get-tuple-element.35), channel_id=1, source_target_pairs={{0,457},{1,72},{8,449},{9,64},{64,9},{65,136},{72,1},{73,128},{128... | collective-permute-start | bytes 589832 | tf_op jit(solution)/shard_map/ppermute | solution.py:49
  14.2 14.7 %collective-permute-start.12 = (bf16[128,768]{1,0:T(8,128)(2,1)}, bf16[128,768]{1,0:T(8,128)(2,1)S(1)}, u32[]{:S(2)}, u32[]{:S(2)}) collective-permute-start(bf16[128,768]{1,0:T(8,128)(2,1)} %get-tuple-element.24.own), channel_id=1, source_target_pairs={{0,449},{1,64},{8,457},{9,72},{64,1},{65,128},{72,9},{73,136},{128... | collective-permute-start | bytes 589832 | tf_op jit(solution)/shard_map/ppermute | solution.py:49
  17.1 14.6 %collective-permute-start.11 = (bf16[128,768]{1,0:T(8,128)(2,1)}, bf16[128,768]{1,0:T(8,128)(2,1)S(1)}, u32[]{:S(2)}, u32[]{:S(2)}) collective-permute-start(bf16[128,768]{1,0:T(8,128)(2,1)} %get-tuple-element.35), channel_id=1, source_target_pairs={{0,72},{1,457},{8,64},{9,449},{64,136},{65,9},{72,128},{73,1},{128... | collective-permute-start | bytes 589832 | tf_op jit(solution)/shard_map/ppermute | solution.py:49
  31.7 8.9 %copy-start.13 = (bf16[2048,192]{0,1:T(8,128)(2,1)S(1)}, bf16[2048,192]{0,1:T(8,128)(2,1)}, u32[]{:S(2)}) copy-start(bf16[2048,192]{0,1:T(8,128)(2,1)} %param.10) | copy-start | bytes 2359300
  31.8 35.3 %collective-permute-start.14 = (bf16[4,128,768]{2,1,0:T(8,128)(2,1)S(1)}, bf16[4,128,768]{2,1,0:T(8,128)(2,1)S(1)}, u32[]{:S(2)}, u32[]{:S(2)}) collective-permute-start(bf16[4,128,768]{2,1,0:T(8,128)(2,1)S(1)} %pad_maximum_fusion.1.hop_one), channel_id=1, source_target_pairs={{0,64},{1,449},{8,72},{9,457},{64,128},{65,1},{72,136},{73,9},{128... | collective-permute-start | bytes 2359304 | tf_op jit(solution)/shard_map/ppermute | solution.py:49
  38.6 10.6 %collective-permute-start.5 = (bf16[128,768]{1,0:T(8,128)(2,1)}, bf16[128,768]{1,0:T(8,128)(2,1)S(1)}, u32[]{:S(2)}, u32[]{:S(2)}) collective-permute-start(bf16[128,768]{1,0:T(8,128)(2,1)} %get-tuple-element.29), channel_id=1, source_target_pairs={{0,457},{1,72},{8,449},{9,64},{64,9},{65,136},{72,1},{73,128},{128... | collective-permute-start | bytes 589832 | tf_op jit(solution)/shard_map/ppermute | solution.py:49
  40.6 6.7 %copy-start.9 = (bf16[128,768]{1,0:T(8,128)(2,1)S(1)}, bf16[128,768]{1,0:T(8,128)(2,1)}, u32[]{:S(2)}) copy-start(bf16[128,768]{1,0:T(8,128)(2,1)} %get-tuple-element.27.own) | copy-start | bytes 589828
  41.4 22.7 %collective-permute-start.1 = (bf16[192,1024]{1,0:T(8,128)(2,1)S(1)}, bf16[192,1024]{1,0:T(8,128)(2,1)S(1)}, u32[]{:S(2)}, u32[]{:S(2)}) collective-permute-start(bf16[192,1024]{1,0:T(8,128)(2,1)S(1)} %get-tuple-element.25), channel_id=1, source_target_pairs={{0,512},{512,0},{1,513},{513,1},{2,514},{514,2},{3,515},{515,3},{4... | collective-permute-start | bytes 1179656 | tf_op jit(solution)/shard_map/ppermute | solution.py:274
  43.4 14.0 %collective-permute-start.3 = (bf16[128,768]{1,0:T(8,128)(2,1)}, bf16[128,768]{1,0:T(8,128)(2,1)S(1)}, u32[]{:S(2)}, u32[]{:S(2)}) collective-permute-start(bf16[128,768]{1,0:T(8,128)(2,1)} %get-tuple-element.29), channel_id=1, source_target_pairs={{0,72},{1,457},{8,64},{9,449},{64,136},{65,9},{72,128},{73,1},{128... | collective-permute-start | bytes 589832 | tf_op jit(solution)/shard_map/ppermute | solution.py:49
  47.3 10.0 %collective-permute-start.4 = (bf16[128,768]{1,0:T(8,128)(2,1)S(1)}, bf16[128,768]{1,0:T(8,128)(2,1)}, u32[]{:S(2)}, u32[]{:S(2)}) collective-permute-start(bf16[128,768]{1,0:T(8,128)(2,1)S(1)} %copy-done.9), channel_id=1, source_target_pairs={{0,449},{1,64},{8,457},{9,72},{64,1},{65,128},{72,9},{73,136},{128... | collective-permute-start | bytes 589832 | tf_op jit(solution)/shard_map/ppermute | solution.py:49
  49.3 8.1 %collective-permute-start.2 = (bf16[128,768]{1,0:T(8,128)(2,1)S(1)}, bf16[128,768]{1,0:T(8,128)(2,1)}, u32[]{:S(2)}, u32[]{:S(2)}) collective-permute-start(bf16[128,768]{1,0:T(8,128)(2,1)S(1)} %copy-done.9), channel_id=1, source_target_pairs={{0,64},{1,449},{8,72},{9,457},{64,128},{65,1},{72,136},{73,9},{128... | collective-permute-start | bytes 589832 | tf_op jit(solution)/shard_map/ppermute | solution.py:49
  58.5 16.8 %collective-permute-start.9 = (bf16[4,128,768]{2,1,0:T(8,128)(2,1)S(1)}, bf16[4,128,768]{2,1,0:T(8,128)(2,1)}, u32[]{:S(2)}, u32[]{:S(2)}) collective-permute-start(bf16[4,128,768]{2,1,0:T(8,128)(2,1)S(1)} %pad_maximum_fusion.hop_one), channel_id=1, source_target_pairs={{0,64},{1,449},{8,72},{9,457},{64,128},{65,1},{72,136},{73,9},{128... | collective-permute-start | bytes 2359304 | tf_op jit(solution)/shard_map/ppermute | solution.py:49
  67.2 33.9 %copy-start = (bf16[416,640]{1,0:T(8,128)(2,1)S(1)}, bf16[416,640]{1,0:T(8,128)(2,1)}, u32[]{:S(2)}) copy-start(bf16[416,640]{1,0:T(8,128)(2,1)} %get-tuple-element.31.att_own) | copy-start | bytes 1597444
  67.2 23.9 %copy-start.7 = (bf16[4,128,768]{2,1,0:T(8,128)(2,1)}, bf16[4,128,768]{2,1,0:T(8,128)(2,1)S(1)}, u32[]{:S(2)}) copy-start(bf16[4,128,768]{2,1,0:T(8,128)(2,1)S(1)} %collective-permute-done.14.hop_two) | copy-start | bytes 2359300
  67.2 13.9 %collective-permute-start.15 = (bf16[4,128,768]{2,1,0:T(8,128)(2,1)S(1)}, bf16[4,128,768]{2,1,0:T(8,128)(2,1)S(1)}, u32[]{:S(2)}, u32[]{:S(2)}) collective-permute-start(bf16[4,128,768]{2,1,0:T(8,128)(2,1)S(1)} %collective-permute-done.14.hop_two), channel_id=1, source_target_pairs={{0,64},{1,449},{8,72},{9,457},{64,128},{65,1},{72,136},{73,9},{128... | collective-permute-start | bytes 2359304 | tf_op jit(solution)/shard_map/ppermute | solution.py:49
  70.8 30.2 %collective-permute-start.6 = (bf16[416,640]{1,0:T(8,128)(2,1)}, bf16[416,640]{1,0:T(8,128)(2,1)S(1)}, u32[]{:S(2)}, u32[]{:S(2)}) collective-permute-start(bf16[416,640]{1,0:T(8,128)(2,1)} %get-tuple-element.31.att_own), channel_id=1, source_target_pairs={{0,8},{8,0},{1,9},{9,1},{2,10},{10,2},{3,11},{11,3},{4,12},{12,4},... | collective-permute-start | bytes 1597448 | tf_op jit(solution)/shard_map/ppermute | solution.py:278
  73.3 17.8 %collective-permute-start.7 = (bf16[416,384]{1,0:T(8,128)(2,1)}, bf16[416,384]{1,0:T(8,128)(2,1)S(1)}, u32[]{:S(2)}, u32[]{:S(2)}) collective-permute-start(bf16[416,384]{1,0:T(8,128)(2,1)} %get-tuple-element.32), channel_id=1, source_target_pairs={{0,1},{1,0},{2,3},{3,2},{4,5},{5,4},{6,7},{7,6},{8,9},{9,8},{10,11... | collective-permute-start | bytes 958472 | tf_op jit(solution)/shard_map/ppermute | solution.py:279
  75.2 25.9 %copy-start.11 = (bf16[128,768]{1,0:T(8,128)(2,1)S(1)}, bf16[128,768]{1,0:T(8,128)(2,1)}, u32[]{:S(2)}) copy-start(bf16[128,768]{1,0:T(8,128)(2,1)} %get-tuple-element.24.own) | copy-start | bytes 589828
  75.2 25.9 %copy-start.12 = (s32[7]{0:T(128)S(1)}, s32[7]{0:T(128)}, u32[]{:S(2)}) copy-start(s32[7]{0:T(128)} %stack.82.place) | copy-start | bytes 88
  75.2 25.8 %collective-permute-start.10 = (bf16[128,1536]{1,0:T(8,128)(2,1)}, bf16[128,1536]{1,0:T(8,128)(2,1)S(1)}, u32[]{:S(2)}, u32[]{:S(2)}) collective-permute-start(bf16[128,1536]{1,0:T(8,128)(2,1)} %get-tuple-element.34), channel_id=1, source_target_pairs={{0,8},{8,0},{1,9},{9,1},{2,10},{10,2},{3,11},{11,3},{4,12},{12,4},... | collective-permute-start | bytes 1179656 | tf_op jit(solution)/shard_map/ppermute | solution.py:289
  81.1 20.0 %collective-permute-start.16 = (bf16[2,128,768]{2,1,0:T(8,128)(2,1)S(1)}, bf16[2,128,768]{2,1,0:T(8,128)(2,1)S(1)}, u32[]{:S(2)}, u32[]{:S(2)}) collective-permute-start(bf16[2,128,768]{2,1,0:T(8,128)(2,1)S(1)} %slice.6), channel_id=1, source_target_pairs={{0,64},{1,449},{8,72},{9,457},{64,128},{65,1},{72,136},{73,9},{128... | collective-permute-start | bytes 1179656 | tf_op jit(solution)/shard_map/ppermute | solution.py:49
  86.2 14.9 %collective-permute-start.8 = (bf16[416,384]{1,0:T(8,128)(2,1)}, bf16[416,384]{1,0:T(8,128)(2,1)S(1)}, u32[]{:S(2)}, u32[]{:S(2)}) collective-permute-start(bf16[416,384]{1,0:T(8,128)(2,1)} %get-tuple-element.32), channel_id=1, source_target_pairs={{0,9},{1,8},{8,1},{9,0},{2,11},{3,10},{10,3},{11,2},{4,13},{5,12},... | collective-permute-start | bytes 958472 | tf_op jit(solution)/shard_map/ppermute | solution.py:280
  91.1 15.1 %copy-start.3 = (bf16[416,384]{1,0:T(8,128)(2,1)}, bf16[416,384]{1,0:T(8,128)(2,1)S(1)}, u32[]{:S(2)}) copy-start(bf16[416,384]{1,0:T(8,128)(2,1)S(1)} %collective-permute-done.7.att_cross) | copy-start | bytes 958468
  91.1 18.0 %collective-permute-start.18 = (bf16[4,128,768]{2,1,0:T(8,128)(2,1)}, bf16[4,128,768]{2,1,0:T(8,128)(2,1)S(1)}, u32[]{:S(2)}, u32[]{:S(2)}) collective-permute-start(bf16[4,128,768]{2,1,0:T(8,128)(2,1)} %collective-permute-done.9.hop_two), channel_id=1, source_target_pairs={{0,64},{1,449},{8,72},{9,457},{64,128},{65,1},{72,136},{73,9},{128... | collective-permute-start | bytes 2359304 | tf_op jit(solution)/shard_map/ppermute | solution.py:49
  106.2 5.9 %collective-permute-start.17 = (f32[8,2,72,128]{3,2,1,0:T(8,128)S(1)}, f32[8,2,72,128]{3,2,1,0:T(8,128)S(1)}, u32[]{:S(2)}, u32[]{:S(2)}) collective-permute-start(f32[8,2,72,128]{3,2,1,0:T(8,128)S(1)} %get-tuple-element.39), channel_id=1, source_target_pairs={{0,1},{1,0},{2,3},{3,2},{4,5},{5,4},{6,7},{7,6},{8,9},{9,8},{10,11... | collective-permute-start | bytes 1769480 | tf_op jit(solution)/shard_map/ppermute | solution.py:298
  109.9 9.1 %collective-permute-start.19 = (bf16[2,128,768]{2,1,0:T(8,128)(2,1)}, bf16[2,128,768]{2,1,0:T(8,128)(2,1)}, u32[]{:S(2)}, u32[]{:S(2)}) collective-permute-start(bf16[2,128,768]{2,1,0:T(8,128)(2,1)} %slice.8), channel_id=1, source_target_pairs={{0,64},{1,449},{8,72},{9,457},{64,128},{65,1},{72,136},{73,9},{128... | collective-permute-start | bytes 1179656 | tf_op jit(solution)/shard_map/ppermute | solution.py:49
  113.0 6.0 %copy-start.2 = (bf16[128,1536]{1,0:T(8,128)(2,1)S(1)}, bf16[128,1536]{1,0:T(8,128)(2,1)}, u32[]{:S(2)}) copy-start(bf16[128,1536]{1,0:T(8,128)(2,1)} %copy-done.1) | copy-start | bytes 1179652
  113.0 6.0 %copy-start.4 = (bf16[416,384]{1,0:T(8,128)(2,1)S(1)}, bf16[416,384]{1,0:T(8,128)(2,1)}, u32[]{:S(2)}) copy-start(bf16[416,384]{1,0:T(8,128)(2,1)} %copy-done.3) | copy-start | bytes 958468
  113.0 25.3 %all-to-all-start = ((f32[8,2,72,128]{3,2,1,0:T(8,128)}), f32[8,2,72,128]{3,2,1,0:T(8,128)}, u32[]{:S(2)}, u32[]{:S(2)}) async-start(f32[8,2,72,128]{3,2,1,0:T(8,128)} %add.46), calls=%async_computation | async-start | bytes 1179648 | tf_op jit(solution)/shard_map/all_to_all | solution.py:299
  125.0 5.6 %collective-permute-start.20 = (f32[8,2,72,128]{3,2,1,0:T(8,128)S(1)}, f32[8,2,72,128]{3,2,1,0:T(8,128)S(1)}, u32[]{:S(2)}, u32[]{:S(2)}) collective-permute-start(f32[8,2,72,128]{3,2,1,0:T(8,128)S(1)} %get-tuple-element.41), channel_id=1, source_target_pairs={{0,1},{1,0},{2,3},{3,2},{4,5},{5,4},{6,7},{7,6},{8,9},{9,8},{10,11... | collective-permute-start | bytes 1769480 | tf_op jit(solution)/shard_map/ppermute | solution.py:298
  138.4 22.9 %all-to-all-start.1 = ((f32[8,2,72,128]{3,2,1,0:T(8,128)}), f32[8,2,72,128]{3,2,1,0:T(8,128)S(1)}, u32[]{:S(2)}, u32[]{:S(2)}) async-start(f32[8,2,72,128]{3,2,1,0:T(8,128)} %add.47), calls=%async_computation.1 | async-start | bytes 1179648 | tf_op jit(solution)/shard_map/all_to_all | solution.py:299
  (7 other events, 15.0 us)

commit v5 on v4

--- a/solution.py
+++ b/solution.py
@@ -53,22 +53,20 @@
     return lax.optimization_barrier((value, *others))[0]
 
 
-def split_kernel(place, cotangent, mine_one, mine_two, other_one, other_two, other_all):
+def split_kernel(place, cotangent, mine, other):
     for zh in range(NZH):
-        span = slice((zh % 2) * GROUP, (zh % 2 + 1) * GROUP)
-        for parity, ref in ((place[6], (mine_one, mine_two)), (1 - place[6], (other_one, other_two))):
+        for parity, ref in ((place[10], mine), (1 - place[10], other)):
             start = pl.multiple_of((2 * zh + parity) * GROUP, GROUP)
-            ref[zh // 2][:, span] = cotangent[:, pl.ds(start, GROUP)]
-        start = pl.multiple_of((2 * zh + 1 - place[6]) * GROUP, GROUP)
-        other_all[:, zh * GROUP : (zh + 1) * GROUP] = cotangent[:, pl.ds(start, GROUP)]
+            at = (zh % 2) * GROUP
+            ref[zh // 2, :, at : at + GROUP] = cotangent[:, pl.ds(start, GROUP)]
 
 
 def split(place, cotangent):
-    half = jax.ShapeDtypeStruct((CHUNK, 2 * GROUP), cotangent.dtype)
+    half = jax.ShapeDtypeStruct((2, CHUNK, D // 4), cotangent.dtype)
     return pl.pallas_call(
         split_kernel,
         in_specs=[pl.BlockSpec(memory_space=pltpu.SMEM), pl.BlockSpec((CHUNK, D), lambda: (0, 0))],
-        out_shape=[half] * 4 + [jax.ShapeDtypeStruct((CHUNK, 4 * GROUP), cotangent.dtype)],
+        out_shape=[half] * 2,
         name="split",
     )(place, cotangent)
 
@@ -85,7 +83,7 @@
                     ref[:HB, here] = top[:, pl.ds(start, CHUNK)]
                     ref[HB:FEAT, here] = bottom[:, pl.ds(start, CHUNK)]
 
-    rest = gate[...]
+    rest = jnp.concatenate([gate[:, z * GROUP : (z + 1) * GROUP] for z in range(8)], axis=0)
     rows = []
     for _ in range(3):
         part = rest.astype(jnp.bfloat16)
@@ -129,7 +127,7 @@
     keep,
     send,
 ):
-    group = 2 * (2 * piece + pl.program_id(0)) + place[6]
+    group = 2 * (2 * piece + pl.program_id(0)) + place[10]
 
     def dot(left, *blocks):
         right = blocks[0] if len(blocks) == 1 else jnp.concatenate(blocks, axis=0)
@@ -139,7 +137,7 @@
     for which, att in enumerate((att_own, att_beside, att_cross, att_across)):
         one, two, three = hop_one[which], hop_two[which], hop_three[which]
         if which < 2:
-            near = (own, beside)[which][...]
+            near = (own, beside)[which][0]
             clip = dot(att[:FEAT, : 2 * CHUNK], near, one)
             clip += dot(att[:FEAT, 2 * CHUNK : 4 * CHUNK], two, three)
             clip += dot(att[:FEAT, 4 * CHUNK :], last[which])
@@ -174,10 +172,9 @@
 
 
 def product(piece, place, atts, own, beside, blocks):
-    count = own.shape[1] // GROUP
+    count = blocks[0].shape[2] // GROUP
     attn = [pl.BlockSpec(att.shape, lambda z: (0, 0)) for att in atts]
-    plain = pl.BlockSpec((CHUNK, GROUP), lambda z: (0, z))
-    near = pl.BlockSpec((CHUNK, GROUP), lambda z: (0, 2 * piece + z))
+    near = pl.BlockSpec((1, CHUNK, GROUP), lambda z: (piece, 0, z))
     four = pl.BlockSpec((4, CHUNK, GROUP), lambda z: (0, 0, z))
     pair = pl.BlockSpec((2, CHUNK, GROUP), lambda z: (0, 0, z))
     out = pl.BlockSpec((2 * NY, 1, PACK, 128), lambda z: (0, z, 0, 0))
@@ -188,7 +185,7 @@
         grid=(count,),
         in_specs=[pl.BlockSpec(memory_space=pltpu.SMEM)]
         + attn
-        + [plain, near, four, four, four, pair],
+        + [near, near, four, four, four, pair],
         out_specs=[out, out],
         out_shape=[shape, shape],
         cost_estimate=pl.CostEstimate(flops=flops, bytes_accessed=8 << 20, transcendentals=0),
@@ -256,23 +253,21 @@
     yh, x, zl, core = (lax.axis_index(name) for name in ("yh", "x", "zl", "c"))
     step = 1 - 2 * core
     sources = [lax.rem(x - step * count + 2 * NX, NX) for count in range(NX)]
-    place = jnp.stack([core] + sources[:5] + [zl])
-
-    mine_one, mine_two, other_one, other_two, other_all = split(place, cotangent)
-
-    def first_hop(mine, other):
-        return [hop(mine), hop(other, 1, 0), hop(mine, 0, 1), hop(other, 1, 1)]
-
-    parts_one = first_hop(mine_one, other_one)
-    parts_two = first_hop(after(mine_two, parts_one[0]), after(other_two, parts_one[0]))
-    first_one = jnp.stack(parts_one)
-    first_two = jnp.stack(parts_two)
+    place = jnp.stack([core] + sources + [yh, zl])
 
     features = attn_out.T
     kept = lax.dynamic_slice_in_dim(features, yh * TOK, TOK, 1)
     away = lax.dynamic_slice_in_dim(features, (1 - yh) * TOK, TOK, 1)
-    came = after(lax.ppermute(after(away, parts_one[0]), "yh", SWAP), first_two)
-    att_own, att_swap = features_of(jnp.stack([core] + sources + [yh]), kept, came, gate.reshape(8, GROUP))
+    came = lax.ppermute(away, "yh", SWAP)
+
+    mine, other = split(place, cotangent)
+    parts = [hop(mine), hop(other, 1, 0), hop(mine, 0, 1), hop(other, 1, 1)]
+    first_one = jnp.stack([part[0] for part in parts])
+    first_two = jnp.stack([part[1] for part in parts])
+    second_one = hop(after(first_one, came))
+    second_two = hop(after(first_two, came))
+
+    att_own, att_swap = features_of(place, kept, after(came, first_two), gate)
     atts = (
         att_own,
         lax.ppermute(att_own, "zl", SWAP),
@@ -280,20 +275,18 @@
         lax.ppermute(att_swap, ("zl", "c"), [(0, 3), (1, 2), (2, 1), (3, 0)]),
     )
 
-    second_one = hop(first_one)
-    second_two = hop(first_two)
-    third_one = hop(after(second_one, first_two, att_own))
+    third_one = hop(after(second_one, att_own))
     third_two = hop(second_two)
     last_one = hop(after(third_one, second_two)[:2])
     last_two = hop(third_two[:2])
-    beside = lax.ppermute(after(other_all, second_two), "zl", SWAP)
+    beside = lax.ppermute(after(other, second_one), "zl", SWAP)
     rings = (
-        (mine_one, (first_one, second_one, third_one, last_one)),
-        (mine_two, (first_two, second_two, third_two, last_two)),
+        (first_one, second_one, third_one, last_one),
+        (first_two, second_two, third_two, last_two),
     )
 
     by_z = []
-    for at, (mine, blocks) in enumerate(rings):
+    for at, blocks in enumerate(rings):
         keep, send = product(at, place, atts, mine, beside, blocks)
         paired = keep + lax.ppermute(send, "c", SWAP)
         by_z.append(jnp.sum(lax.all_to_all(paired, Y, 0, 0), axis=0))

time: 185 us -> 185 us (level)
  waiting for transfers between devices: 38.2 us -> 66.1 us
  starting transfers between devices: 96.6 us -> 71.6 us
    ppermute x14 -> x10, starting transfers between devices: 66.4 us -> 42.7 us  [hop(): return lax.ppermute(block, ('x', 'zl', 'c'), ring(other_z, other_core))]
    ppermute x2, waiting for transfers between devices: 0.36 us -> 15 us  [the longest x1 11.8 us: local(): came = lax.ppermute(away, 'yh', SWAP)]
    ppermute x14 -> x10, waiting for transfers between devices: 5.99 us -> 19.3 us  [hop(): return lax.ppermute(block, ('x', 'zl', 'c'), ring(other_z, other_core))]
    ppermute x1, starting transfers between devices: 4.88 us -> 1.95 us  [local(): lax.ppermute(att_swap, ('zl', 'c'), [(0, 3), (1, 2), (2, 1), (3, 0)])]
    ppermute x1, starting transfers between devices: 2.44 us -> 4.93 us  [local(): lax.ppermute(att_own, 'zl', SWAP)]
    all_to_all x2, waiting for transfers between devices: 25.1 us -> 23.2 us  [local(): by_z.append(jnp.sum(lax.all_to_all(paired, Y, 0, 0), axis=0))]
    unnamed x33 -> x28, local copies, waits for them, and re-layouts: 4.73 us -> 4.24 us
  transfers between devices with their start and end apart: 23 -> 19, of which waited for: 8 -> 12; matrix products, arithmetic and copies ran while one was open for 4% -> 3% of each run, Pallas kernels for 6% -> 6%
where the time goes in v5:
time: 185 us; the launch traced here: 184 us
  starting transfers between devices  71.6 us (39%)
  waiting for transfers between devices  66.1 us (36%)
  blocking collectives  19.4 us (10%)
  Pallas kernels  15.8 us (9%)
  local copies, waits for them, and re-layouts  6.59 us (4%)
  other arithmetic  3.09 us (2%)
    ppermute x10, starting transfers between devices, hop(): return lax.ppermute(block, ('x', 'zl', 'c'), ring(other_z, other_core))  42.7 us
    all_to_all x2, waiting for transfers between devices, local(): by_z.append(jnp.sum(lax.all_to_all(paired, Y, 0, 0), axis=0))  23.2 us
    all_to_all x1, blocking collectives, local(): parts = lax.all_to_all(jnp.concatenate(by_z, axis=0), 'zh', 0, 0)  19.4 us
    ppermute x10, waiting for transfers between devices, hop(): return lax.ppermute(block, ('x', 'zl', 'c'), ring(other_z, other_core))  19.3 us
    ppermute x1, waiting for transfers between devices, local(): came = lax.ppermute(away, 'yh', SWAP)  11.8 us
    pallas_call x2, Pallas kernels, product(): pl.pallas_call(functools.partial(product_kernel, piece), grid=(count,), i...  8.21 us
    all_to_all x2, starting transfers between devices, local(): by_z.append(jnp.sum(lax.all_to_all(paired, Y, 0, 0), axis=0))  7.86 us
    ppermute x1, waiting for transfers between devices, local(): lax.ppermute(att_swap, ('zl', 'c'), [(0, 3), (1, 2), (2, 1), (3, 0)])  6.93 us
  transfers between devices with their start and end apart: 19, of which 12 were waited for; matrix products, arithmetic and copies ran while one was open for 3% of the time, Pallas kernels for 6%

profile of v5, /device:TPU:1, one launch (start us, length us, event | category | flops | bytes accessed | tf_op | source)
XLA Modules:
  0.0 183.5 jit_solution(3801317863069814534)
XLA Ops:
  1.3 2.1 %split.1 = (bf16[2,128,768]{2,1,0:T(8,128)(2,1)}, bf16[2,128,768]{2,1,0:T(8,128)(2,1)}) custom-call(s32[11]{0:T(128)} %stack.53.place, bf16[128,3072]{1,0:T(8,128)(2,1)} %cotangent.1), custom_call_target="tpu_custom_call" | custom-call | tf_op jit(solution)/shard_map/split/pallas_call | solution.py:66
  3.4 7.2 %collective-permute-start.4 = (bf16[2,128,768]{2,1,0:T(8,128)(2,1)}, bf16[2,128,768]{2,1,0:T(8,128)(2,1)S(1)}, u32[]{:S(2)}, u32[]{:S(2)}) collective-permute-start(bf16[2,128,768]{2,1,0:T(8,128)(2,1)} %get-tuple-element.26), channel_id=1, source_target_pairs={{0,457},{1,72},{8,449},{9,64},{64,9},{65,136},{72,1},{73,128},{128... | collective-permute-start | bytes 1179656 | tf_op jit(solution)/shard_map/ppermute | solution.py:49
  10.6 14.2 %collective-permute-start.2 = (bf16[2,128,768]{2,1,0:T(8,128)(2,1)}, bf16[2,128,768]{2,1,0:T(8,128)(2,1)S(1)}, u32[]{:S(2)}, u32[]{:S(2)}) collective-permute-start(bf16[2,128,768]{2,1,0:T(8,128)(2,1)} %get-tuple-element.26), channel_id=1, source_target_pairs={{0,72},{1,457},{8,64},{9,449},{64,136},{65,9},{72,128},{73,1},{128... | collective-permute-start | bytes 1179656 | tf_op jit(solution)/shard_map/ppermute | solution.py:49
  24.8 1.9 %collective-permute-start.3 = (bf16[2,128,768]{2,1,0:T(8,128)(2,1)}, bf16[2,128,768]{2,1,0:T(8,128)(2,1)S(1)}, u32[]{:S(2)}, u32[]{:S(2)}) collective-permute-start(bf16[2,128,768]{2,1,0:T(8,128)(2,1)} %get-tuple-element.20.own), channel_id=1, source_target_pairs={{0,449},{1,64},{8,457},{9,72},{64,1},{65,128},{72,9},{73,136},{128... | collective-permute-start | bytes 1179656 | tf_op jit(solution)/shard_map/ppermute | solution.py:49
  31.5 2.6 %collective-permute-done.2 = bf16[2,128,768]{2,1,0:T(8,128)(2,1)S(1)} collective-permute-done((bf16[2,128,768]{2,1,0:T(8,128)(2,1)}, bf16[2,128,768]{2,1,0:T(8,128)(2,1)S(1)}, u32[]{:S(2)}, u32[]{:S(2)}) %collective-permute-start.2) | collective-permute-done | bytes 393248 | tf_op jit(solution)/shard_map/ppermute | solution.py:49
  34.1 2.8 %collective-permute-done.3 = bf16[2,128,768]{2,1,0:T(8,128)(2,1)S(1)} collective-permute-done((bf16[2,128,768]{2,1,0:T(8,128)(2,1)}, bf16[2,128,768]{2,1,0:T(8,128)(2,1)S(1)}, u32[]{:S(2)}, u32[]{:S(2)}) %collective-permute-start.3) | collective-permute-done | bytes 393248 | tf_op jit(solution)/shard_map/ppermute | solution.py:49
  38.5 11.8 %collective-permute-done.came = bf16[192,1024]{1,0:T(8,128)(2,1)S(1)} collective-permute-done((bf16[192,1024]{1,0:T(8,128)(2,1)S(1)}, bf16[192,1024]{1,0:T(8,128)(2,1)S(1)}, u32[]{:S(2)}, u32[]{:S(2)}) %collective-permute-start) | collective-permute-done | bytes 393248 | tf_op jit(solution)/shard_map/ppermute | solution.py:261
  50.3 2.3 %collective-permute-start.11 = (bf16[4,128,768]{2,1,0:T(8,128)(2,1)S(1)}, bf16[4,128,768]{2,1,0:T(8,128)(2,1)}, u32[]{:S(2)}, u32[]{:S(2)}) collective-permute-start(bf16[4,128,768]{2,1,0:T(8,128)(2,1)S(1)} %pad_maximum_fusion.hop_one), channel_id=1, source_target_pairs={{0,64},{1,449},{8,72},{9,457},{64,128},{65,1},{72,136},{73,9},{128... | collective-permute-start | bytes 2359304 | tf_op jit(solution)/shard_map/ppermute | solution.py:49
  52.7 1.9 %collective-permute-start.8 = (bf16[4,128,768]{2,1,0:T(8,128)(2,1)S(1)}, bf16[4,128,768]{2,1,0:T(8,128)(2,1)}, u32[]{:S(2)}, u32[]{:S(2)}) collective-permute-start(bf16[4,128,768]{2,1,0:T(8,128)(2,1)S(1)} %pad_maximum_fusion.1.hop_one), channel_id=1, source_target_pairs={{0,64},{1,449},{8,72},{9,457},{64,128},{65,1},{72,136},{73,9},{128... | collective-permute-start | bytes 2359304 | tf_op jit(solution)/shard_map/ppermute | solution.py:49
  54.6 8.8 %collective-permute-done.11.hop_two = bf16[4,128,768]{2,1,0:T(8,128)(2,1)} collective-permute-done((bf16[4,128,768]{2,1,0:T(8,128)(2,1)S(1)}, bf16[4,128,768]{2,1,0:T(8,128)(2,1)}, u32[]{:S(2)}, u32[]{:S(2)}) %collective-permute-start.11) | collective-permute-done | bytes 786464 | tf_op jit(solution)/shard_map/ppermute | solution.py:49
  63.4 3.2 %collective-permute-start.14 = (bf16[4,128,768]{2,1,0:T(8,128)(2,1)}, bf16[4,128,768]{2,1,0:T(8,128)(2,1)S(1)}, u32[]{:S(2)}, u32[]{:S(2)}) collective-permute-start(bf16[4,128,768]{2,1,0:T(8,128)(2,1)} %collective-permute-done.11.hop_two), channel_id=1, source_target_pairs={{0,64},{1,449},{8,72},{9,457},{64,128},{65,1},{72,136},{73,9},{128... | collective-permute-start | bytes 2359304 | tf_op jit(solution)/shard_map/ppermute | solution.py:49
  66.6 2.3 %features.1 = (bf16[416,640]{1,0:T(8,128)(2,1)}, bf16[416,384]{1,0:T(8,128)(2,1)}) custom-call(s32[11]{0:T(128)} %stack.53.place, bf16[192,1024]{1,0:T(8,128)(2,1)} %get-tuple-element.35.kept, bf16[192,1024]{1,0:T(8,128)(2,1)} %copy-done.13, f32[1,3072]{1,0:T(1,128)} %gate.1), custom_call_target="tpu_custom_call" | custom-call | tf_op jit(solution)/shard_map/features/pallas_call | solution.py:106
  68.9 4.9 %collective-permute-start.5 = (bf16[416,640]{1,0:T(8,128)(2,1)}, bf16[416,640]{1,0:T(8,128)(2,1)S(1)}, u32[]{:S(2)}, u32[]{:S(2)}) collective-permute-start(bf16[416,640]{1,0:T(8,128)(2,1)} %get-tuple-element.23.att_own), channel_id=1, source_target_pairs={{0,8},{8,0},{1,9},{9,1},{2,10},{10,2},{3,11},{11,3},{4,12},{12,4},... | collective-permute-start | bytes 1597448 | tf_op jit(solution)/shard_map/ppermute | solution.py:273
  73.8 2.0 %collective-permute-start.7 = (bf16[416,384]{1,0:T(8,128)(2,1)}, bf16[416,384]{1,0:T(8,128)(2,1)S(1)}, u32[]{:S(2)}, u32[]{:S(2)}) collective-permute-start(bf16[416,384]{1,0:T(8,128)(2,1)} %get-tuple-element.24), channel_id=1, source_target_pairs={{0,9},{1,8},{8,1},{9,0},{2,11},{3,10},{10,3},{11,2},{4,13},{5,12},... | collective-permute-start | bytes 958472 | tf_op jit(solution)/shard_map/ppermute | solution.py:275
  75.8 2.6 %collective-permute-start.9 = (bf16[2,128,768]{2,1,0:T(8,128)(2,1)}, bf16[2,128,768]{2,1,0:T(8,128)(2,1)S(1)}, u32[]{:S(2)}, u32[]{:S(2)}) collective-permute-start(bf16[2,128,768]{2,1,0:T(8,128)(2,1)} %get-tuple-element.26), channel_id=1, source_target_pairs={{0,8},{8,0},{1,9},{9,1},{2,10},{10,2},{3,11},{11,3},{4,12},{12,4},... | collective-permute-start | bytes 1179656 | tf_op jit(solution)/shard_map/ppermute | solution.py:282
  80.2 3.2 %collective-permute-start.15 = (bf16[2,128,768]{2,1,0:T(8,128)(2,1)S(1)}, bf16[2,128,768]{2,1,0:T(8,128)(2,1)S(1)}, u32[]{:S(2)}, u32[]{:S(2)}) collective-permute-start(bf16[2,128,768]{2,1,0:T(8,128)(2,1)S(1)} %slice.48), channel_id=1, source_target_pairs={{0,64},{1,449},{8,72},{9,457},{64,128},{65,1},{72,136},{73,9},{128... | collective-permute-start | bytes 1179656 | tf_op jit(solution)/shard_map/ppermute | solution.py:49
  83.4 3.2 %collective-permute-start.6 = (bf16[416,384]{1,0:T(8,128)(2,1)}, bf16[416,384]{1,0:T(8,128)(2,1)S(1)}, u32[]{:S(2)}, u32[]{:S(2)}) collective-permute-start(bf16[416,384]{1,0:T(8,128)(2,1)} %get-tuple-element.24), channel_id=1, source_target_pairs={{0,1},{1,0},{2,3},{3,2},{4,5},{5,4},{6,7},{7,6},{8,9},{9,8},{10,11... | collective-permute-start | bytes 958472 | tf_op jit(solution)/shard_map/ppermute | solution.py:274
  86.6 6.9 %collective-permute-done.7.att_across = bf16[416,384]{1,0:T(8,128)(2,1)S(1)} collective-permute-done((bf16[416,384]{1,0:T(8,128)(2,1)}, bf16[416,384]{1,0:T(8,128)(2,1)S(1)}, u32[]{:S(2)}, u32[]{:S(2)}) %collective-permute-start.7) | collective-permute-done | bytes 319520 | tf_op jit(solution)/shard_map/ppermute | solution.py:275
  93.5 4.9 %collective-permute-start.10 = (bf16[4,128,768]{2,1,0:T(8,128)(2,1)}, bf16[4,128,768]{2,1,0:T(8,128)(2,1)S(1)}, u32[]{:S(2)}, u32[]{:S(2)}) collective-permute-start(bf16[4,128,768]{2,1,0:T(8,128)(2,1)} %collective-permute-done.8.hop_two), channel_id=1, source_target_pairs={{0,64},{1,449},{8,72},{9,457},{64,128},{65,1},{72,136},{73,9},{128... | collective-permute-start | bytes 2359304 | tf_op jit(solution)/shard_map/ppermute | solution.py:49
  98.5 3.2 %collective-permute-done.9.beside = bf16[2,128,768]{2,1,0:T(8,128)(2,1)S(1)} collective-permute-done((bf16[2,128,768]{2,1,0:T(8,128)(2,1)}, bf16[2,128,768]{2,1,0:T(8,128)(2,1)S(1)}, u32[]{:S(2)}, u32[]{:S(2)}) %collective-permute-start.9) | collective-permute-done | bytes 393248 | tf_op jit(solution)/shard_map/ppermute | solution.py:282
  103.9 4.1 %product.3 = (f32[8,2,72,128]{3,2,1,0:T(8,128)S(1)}, f32[8,2,72,128]{3,2,1,0:T(8,128)S(1)}) custom-call(s32[11]{0:T(128)S(1)} %copy-done.11, bf16[416,640]{1,0:T(8,128)(2,1)S(1)} %copy-done, bf16[416,640]{1,0:T(8,128)(2,1)S(1)} %collective-permute-done.5.att_beside, bf16[416,384]{1,0:T(8,128)(2,1)S(1)} %collective-permute-done.6.att_cross, ...), custom_call_target="tpu_custom_call" | custom-call | flops 1207959552 | bytes 8388608 | tf_op jit(solution)/shard_map/product/pallas_call | solution.py:183
  108.0 2.6 %collective-permute-start.16 = (f32[8,2,72,128]{3,2,1,0:T(8,128)S(1)}, f32[8,2,72,128]{3,2,1,0:T(8,128)S(1)}, u32[]{:S(2)}, u32[]{:S(2)}) collective-permute-start(f32[8,2,72,128]{3,2,1,0:T(8,128)S(1)} %get-tuple-element.33), channel_id=1, source_target_pairs={{0,1},{1,0},{2,3},{3,2},{4,5},{5,4},{6,7},{7,6},{8,9},{9,8},{10,11... | collective-permute-start | bytes 1769480 | tf_op jit(solution)/shard_map/ppermute | solution.py:291
  111.4 1.9 %collective-permute-start.12 = (bf16[2,128,768]{2,1,0:T(8,128)(2,1)}, bf16[2,128,768]{2,1,0:T(8,128)(2,1)}, u32[]{:S(2)}, u32[]{:S(2)}) collective-permute-start(bf16[2,128,768]{2,1,0:T(8,128)(2,1)} %slice.38), channel_id=1, source_target_pairs={{0,64},{1,449},{8,72},{9,457},{64,128},{65,1},{72,136},{73,9},{128... | collective-permute-start | bytes 1179656 | tf_op jit(solution)/shard_map/ppermute | solution.py:49
  114.3 4.3 %all-to-all-start.1 = ((f32[8,2,72,128]{3,2,1,0:T(8,128)}), f32[8,2,72,128]{3,2,1,0:T(8,128)}, u32[]{:S(2)}, u32[]{:S(2)}) async-start(f32[8,2,72,128]{3,2,1,0:T(8,128)} %add.47), calls=%async_computation.1 | async-start | bytes 1179648 | tf_op jit(solution)/shard_map/all_to_all | solution.py:292
  118.6 1.9 %collective-permute-done.12.last = bf16[2,128,768]{2,1,0:T(8,128)(2,1)} collective-permute-done((bf16[2,128,768]{2,1,0:T(8,128)(2,1)}, bf16[2,128,768]{2,1,0:T(8,128)(2,1)}, u32[]{:S(2)}, u32[]{:S(2)}) %collective-permute-start.12) | collective-permute-done | bytes 393248 | tf_op jit(solution)/shard_map/ppermute | solution.py:49
  122.5 4.1 %product.2 = (f32[8,2,72,128]{3,2,1,0:T(8,128)S(1)}, f32[8,2,72,128]{3,2,1,0:T(8,128)S(1)}) custom-call(s32[11]{0:T(128)S(1)} %copy-done.11, bf16[416,640]{1,0:T(8,128)(2,1)S(1)} %copy-done, bf16[416,640]{1,0:T(8,128)(2,1)S(1)} %collective-permute-done.5.att_beside, bf16[416,384]{1,0:T(8,128)(2,1)S(1)} %copy-done.10, bf16[416,384]{1,0:T(8,128)(2,1)S(1)} %copy-done.8, ...), custom_call_target="tpu_custom_call" | custom-call | flops 1207959552 | bytes 8388608 | tf_op jit(solution)/shard_map/product/pallas_call | solution.py:183
  126.6 3.9 %collective-permute-start.13 = (f32[8,2,72,128]{3,2,1,0:T(8,128)S(1)}, f32[8,2,72,128]{3,2,1,0:T(8,128)S(1)}, u32[]{:S(2)}, u32[]{:S(2)}) collective-permute-start(f32[8,2,72,128]{3,2,1,0:T(8,128)S(1)} %get-tuple-element.31), channel_id=1, source_target_pairs={{0,1},{1,0},{2,3},{3,2},{4,5},{5,4},{6,7},{7,6},{8,9},{9,8},{10,11... | collective-permute-start | bytes 1769480 | tf_op jit(solution)/shard_map/ppermute | solution.py:291
  133.0 5.0 %all-to-all-done.1 = f32[8,2,72,128]{3,2,1,0:T(8,128)} async-done(((f32[8,2,72,128]{3,2,1,0:T(8,128)}), f32[8,2,72,128]{3,2,1,0:T(8,128)}, u32[]{:S(2)}, u32[]{:S(2)}) %all-to-all-start.1) | async-done | bytes 589856 | tf_op jit(solution)/shard_map/all_to_all | solution.py:292
  138.0 3.5 %all-to-all-start = ((f32[8,2,72,128]{3,2,1,0:T(8,128)}), f32[8,2,72,128]{3,2,1,0:T(8,128)S(1)}, u32[]{:S(2)}, u32[]{:S(2)}) async-start(f32[8,2,72,128]{3,2,1,0:T(8,128)} %add.46), calls=%async_computation | async-start | bytes 1179648 | tf_op jit(solution)/shard_map/all_to_all | solution.py:292
  142.7 18.2 %all-to-all-done = f32[8,2,72,128]{3,2,1,0:T(8,128)S(1)} async-done(((f32[8,2,72,128]{3,2,1,0:T(8,128)}), f32[8,2,72,128]{3,2,1,0:T(8,128)S(1)}, u32[]{:S(2)}, u32[]{:S(2)}) %all-to-all-start) | async-done | bytes 589856 | tf_op jit(solution)/shard_map/all_to_all | solution.py:292
  161.0 19.4 %all_to_all.15.parts = f32[4,72,128]{2,1,0:T(8,128)} all-to-all(f32[4,72,128]{2,1,0:T(8,128)S(1)} %pad_maximum_fusion.2), channel_id=1, replica_groups=mesh['yh'=2,'x'=8,'zh'=4,'zl'=2,'yl'=4,'c'=2] {'zh'}, dimensions={0} | all-to-all | bytes 294912 | tf_op jit(solution)/shard_map/all_to_all | solution.py:293
  180.4 3.2 %update.1 = (f32[48,192]{1,0:T(8,128)}, f32[48,192]{1,0:T(8,128)}, f32[48,192]{1,0:T(8,128)}, f32[48,192]{1,0:T(8,128)}, f32[48,48]{1,0:T(8,128)}, /*index=5*/f32[192,192]{1,0:T(8,128)}) custom-call(f32[4,72,128]{2,1,0:T(8,128)} %all_to_all.15.parts, f32[48,192]{1,0:T(8,128)} %weight.1, f32[48,192]{1,0:T(8,128)} %exp_avg.1, f32[48,192]{1,0:T(8,128)} %exp_avg_sq.1, ...), custom_call_target="tpu_custom_call" | custom-call | tf_op jit(solution)/shard_map/update/pallas_call | solution.py:296
  (55 shorter events, 18.3 us)
Async XLA Ops:
  0.6 28.1 %copy-start.12 = (bf16[2048,192]{0,1:T(8,128)(2,1)S(1)}, bf16[2048,192]{0,1:T(8,128)(2,1)}, u32[]{:S(2)}) copy-start(bf16[2048,192]{0,1:T(8,128)(2,1)} %param.10) | copy-start | bytes 2359300
  3.4 28.0 %collective-permute-start.4 = (bf16[2,128,768]{2,1,0:T(8,128)(2,1)}, bf16[2,128,768]{2,1,0:T(8,128)(2,1)S(1)}, u32[]{:S(2)}, u32[]{:S(2)}) collective-permute-start(bf16[2,128,768]{2,1,0:T(8,128)(2,1)} %get-tuple-element.26), channel_id=1, source_target_pairs={{0,457},{1,72},{8,449},{9,64},{64,9},{65,136},{72,1},{73,128},{128... | collective-permute-start | bytes 1179656 | tf_op jit(solution)/shard_map/ppermute | solution.py:49
  10.6 23.5 %collective-permute-start.2 = (bf16[2,128,768]{2,1,0:T(8,128)(2,1)}, bf16[2,128,768]{2,1,0:T(8,128)(2,1)S(1)}, u32[]{:S(2)}, u32[]{:S(2)}) collective-permute-start(bf16[2,128,768]{2,1,0:T(8,128)(2,1)} %get-tuple-element.26), channel_id=1, source_target_pairs={{0,72},{1,457},{8,64},{9,449},{64,136},{65,9},{72,128},{73,1},{128... | collective-permute-start | bytes 1179656 | tf_op jit(solution)/shard_map/ppermute | solution.py:49
  24.8 12.1 %collective-permute-start.3 = (bf16[2,128,768]{2,1,0:T(8,128)(2,1)}, bf16[2,128,768]{2,1,0:T(8,128)(2,1)S(1)}, u32[]{:S(2)}, u32[]{:S(2)}) collective-permute-start(bf16[2,128,768]{2,1,0:T(8,128)(2,1)} %get-tuple-element.20.own), channel_id=1, source_target_pairs={{0,449},{1,64},{8,457},{9,72},{64,1},{65,128},{72,9},{73,136},{128... | collective-permute-start | bytes 1179656 | tf_op jit(solution)/shard_map/ppermute | solution.py:49
  26.7 11.6 %collective-permute-start.1 = (bf16[2,128,768]{2,1,0:T(8,128)(2,1)}, bf16[2,128,768]{2,1,0:T(8,128)(2,1)S(1)}, u32[]{:S(2)}, u32[]{:S(2)}) collective-permute-start(bf16[2,128,768]{2,1,0:T(8,128)(2,1)} %get-tuple-element.20.own), channel_id=1, source_target_pairs={{0,64},{1,449},{8,72},{9,457},{64,128},{65,1},{72,136},{73,9},{128... | collective-permute-start | bytes 1179656 | tf_op jit(solution)/shard_map/ppermute | solution.py:49
  29.5 20.8 %collective-permute-start = (bf16[192,1024]{1,0:T(8,128)(2,1)S(1)}, bf16[192,1024]{1,0:T(8,128)(2,1)S(1)}, u32[]{:S(2)}, u32[]{:S(2)}) collective-permute-start(bf16[192,1024]{1,0:T(8,128)(2,1)S(1)} %get-tuple-element.34), channel_id=1, source_target_pairs={{0,512},{512,0},{1,513},{513,1},{2,514},{514,2},{3,515},{515,3},{4... | collective-permute-start | bytes 1179656 | tf_op jit(solution)/shard_map/ppermute | solution.py:261
  50.3 2.4 %copy-start.13 = (bf16[192,1024]{1,0:T(8,128)(2,1)}, bf16[192,1024]{1,0:T(8,128)(2,1)S(1)}, u32[]{:S(2)}) copy-start(bf16[192,1024]{1,0:T(8,128)(2,1)S(1)} %collective-permute-done.came) | copy-start | bytes 1179652
  50.3 13.1 %collective-permute-start.11 = (bf16[4,128,768]{2,1,0:T(8,128)(2,1)S(1)}, bf16[4,128,768]{2,1,0:T(8,128)(2,1)}, u32[]{:S(2)}, u32[]{:S(2)}) collective-permute-start(bf16[4,128,768]{2,1,0:T(8,128)(2,1)S(1)} %pad_maximum_fusion.hop_one), channel_id=1, source_target_pairs={{0,64},{1,449},{8,72},{9,457},{64,128},{65,1},{72,136},{73,9},{128... | collective-permute-start | bytes 2359304 | tf_op jit(solution)/shard_map/ppermute | solution.py:49
  52.7 23.1 %collective-permute-start.8 = (bf16[4,128,768]{2,1,0:T(8,128)(2,1)S(1)}, bf16[4,128,768]{2,1,0:T(8,128)(2,1)}, u32[]{:S(2)}, u32[]{:S(2)}) collective-permute-start(bf16[4,128,768]{2,1,0:T(8,128)(2,1)S(1)} %pad_maximum_fusion.1.hop_one), channel_id=1, source_target_pairs={{0,64},{1,449},{8,72},{9,457},{64,128},{65,1},{72,136},{73,9},{128... | collective-permute-start | bytes 2359304 | tf_op jit(solution)/shard_map/ppermute | solution.py:49
  63.4 16.7 %collective-permute-start.14 = (bf16[4,128,768]{2,1,0:T(8,128)(2,1)}, bf16[4,128,768]{2,1,0:T(8,128)(2,1)S(1)}, u32[]{:S(2)}, u32[]{:S(2)}) collective-permute-start(bf16[4,128,768]{2,1,0:T(8,128)(2,1)} %collective-permute-done.11.hop_two), channel_id=1, source_target_pairs={{0,64},{1,449},{8,72},{9,457},{64,128},{65,1},{72,136},{73,9},{128... | collective-permute-start | bytes 2359304 | tf_op jit(solution)/shard_map/ppermute | solution.py:49
  68.9 32.8 %copy-start = (bf16[416,640]{1,0:T(8,128)(2,1)S(1)}, bf16[416,640]{1,0:T(8,128)(2,1)}, u32[]{:S(2)}) copy-start(bf16[416,640]{1,0:T(8,128)(2,1)} %get-tuple-element.23.att_own) | copy-start | bytes 1597444
  68.9 29.6 %collective-permute-start.5 = (bf16[416,640]{1,0:T(8,128)(2,1)}, bf16[416,640]{1,0:T(8,128)(2,1)S(1)}, u32[]{:S(2)}, u32[]{:S(2)}) collective-permute-start(bf16[416,640]{1,0:T(8,128)(2,1)} %get-tuple-element.23.att_own), channel_id=1, source_target_pairs={{0,8},{8,0},{1,9},{9,1},{2,10},{10,2},{3,11},{11,3},{4,12},{12,4},... | collective-permute-start | bytes 1597448 | tf_op jit(solution)/shard_map/ppermute | solution.py:273
  73.8 27.8 %copy-start.11 = (s32[11]{0:T(128)S(1)}, s32[11]{0:T(128)}, u32[]{:S(2)}) copy-start(s32[11]{0:T(128)} %stack.53.place) | copy-start | bytes 136
  73.8 19.7 %collective-permute-start.7 = (bf16[416,384]{1,0:T(8,128)(2,1)}, bf16[416,384]{1,0:T(8,128)(2,1)S(1)}, u32[]{:S(2)}, u32[]{:S(2)}) collective-permute-start(bf16[416,384]{1,0:T(8,128)(2,1)} %get-tuple-element.24), channel_id=1, source_target_pairs={{0,9},{1,8},{8,1},{9,0},{2,11},{3,10},{10,3},{11,2},{4,13},{5,12},... | collective-permute-start | bytes 958472 | tf_op jit(solution)/shard_map/ppermute | solution.py:275
  75.8 25.8 %collective-permute-start.9 = (bf16[2,128,768]{2,1,0:T(8,128)(2,1)}, bf16[2,128,768]{2,1,0:T(8,128)(2,1)S(1)}, u32[]{:S(2)}, u32[]{:S(2)}) collective-permute-start(bf16[2,128,768]{2,1,0:T(8,128)(2,1)} %get-tuple-element.26), channel_id=1, source_target_pairs={{0,8},{8,0},{1,9},{9,1},{2,10},{10,2},{3,11},{11,3},{4,12},{12,4},... | collective-permute-start | bytes 1179656 | tf_op jit(solution)/shard_map/ppermute | solution.py:282
  80.1 6.4 %copy-start.1 = (bf16[4,128,768]{2,1,0:T(8,128)(2,1)}, bf16[4,128,768]{2,1,0:T(8,128)(2,1)S(1)}, u32[]{:S(2)}) copy-start(bf16[4,128,768]{2,1,0:T(8,128)(2,1)S(1)} %collective-permute-done.14.hop_three) | copy-start | bytes 2359300
  80.2 21.5 %collective-permute-start.15 = (bf16[2,128,768]{2,1,0:T(8,128)(2,1)S(1)}, bf16[2,128,768]{2,1,0:T(8,128)(2,1)S(1)}, u32[]{:S(2)}, u32[]{:S(2)}) collective-permute-start(bf16[2,128,768]{2,1,0:T(8,128)(2,1)S(1)} %slice.48), channel_id=1, source_target_pairs={{0,64},{1,449},{8,72},{9,457},{64,128},{65,1},{72,136},{73,9},{128... | collective-permute-start | bytes 1179656 | tf_op jit(solution)/shard_map/ppermute | solution.py:49
  83.4 15.1 %collective-permute-start.6 = (bf16[416,384]{1,0:T(8,128)(2,1)}, bf16[416,384]{1,0:T(8,128)(2,1)S(1)}, u32[]{:S(2)}, u32[]{:S(2)}) collective-permute-start(bf16[416,384]{1,0:T(8,128)(2,1)} %get-tuple-element.24), channel_id=1, source_target_pairs={{0,1},{1,0},{2,3},{3,2},{4,5},{5,4},{6,7},{7,6},{8,9},{9,8},{10,11... | collective-permute-start | bytes 958472 | tf_op jit(solution)/shard_map/ppermute | solution.py:274
  93.5 14.5 %copy-start.7 = (bf16[416,384]{1,0:T(8,128)(2,1)}, bf16[416,384]{1,0:T(8,128)(2,1)S(1)}, u32[]{:S(2)}) copy-start(bf16[416,384]{1,0:T(8,128)(2,1)S(1)} %collective-permute-done.7.att_across) | copy-start | bytes 958468
  93.5 17.1 %collective-permute-start.10 = (bf16[4,128,768]{2,1,0:T(8,128)(2,1)}, bf16[4,128,768]{2,1,0:T(8,128)(2,1)S(1)}, u32[]{:S(2)}, u32[]{:S(2)}) collective-permute-start(bf16[4,128,768]{2,1,0:T(8,128)(2,1)} %collective-permute-done.8.hop_two), channel_id=1, source_target_pairs={{0,64},{1,449},{8,72},{9,457},{64,128},{65,1},{72,136},{73,9},{128... | collective-permute-start | bytes 2359304 | tf_op jit(solution)/shard_map/ppermute | solution.py:49
  98.4 9.6 %copy-start.9 = (bf16[416,384]{1,0:T(8,128)(2,1)}, bf16[416,384]{1,0:T(8,128)(2,1)S(1)}, u32[]{:S(2)}) copy-start(bf16[416,384]{1,0:T(8,128)(2,1)S(1)} %collective-permute-done.6.att_cross) | copy-start | bytes 958468
  101.6 6.4 %copy-start.5 = (bf16[2,128,768]{2,1,0:T(8,128)(2,1)}, bf16[2,128,768]{2,1,0:T(8,128)(2,1)S(1)}, u32[]{:S(2)}) copy-start(bf16[2,128,768]{2,1,0:T(8,128)(2,1)S(1)} %collective-permute-done.9.beside) | copy-start | bytes 1179652
  101.7 1.3 copy-start.2
  102.9 1.0 copy-start.3
  108.0 5.3 %collective-permute-start.16 = (f32[8,2,72,128]{3,2,1,0:T(8,128)S(1)}, f32[8,2,72,128]{3,2,1,0:T(8,128)S(1)}, u32[]{:S(2)}, u32[]{:S(2)}) collective-permute-start(f32[8,2,72,128]{3,2,1,0:T(8,128)S(1)} %get-tuple-element.33), channel_id=1, source_target_pairs={{0,1},{1,0},{2,3},{3,2},{4,5},{5,4},{6,7},{7,6},{8,9},{9,8},{10,11... | collective-permute-start | bytes 1769480 | tf_op jit(solution)/shard_map/ppermute | solution.py:291
  111.4 9.1 %collective-permute-start.12 = (bf16[2,128,768]{2,1,0:T(8,128)(2,1)}, bf16[2,128,768]{2,1,0:T(8,128)(2,1)}, u32[]{:S(2)}, u32[]{:S(2)}) collective-permute-start(bf16[2,128,768]{2,1,0:T(8,128)(2,1)} %slice.38), channel_id=1, source_target_pairs={{0,64},{1,449},{8,72},{9,457},{64,128},{65,1},{72,136},{73,9},{128... | collective-permute-start | bytes 1179656 | tf_op jit(solution)/shard_map/ppermute | solution.py:49
  114.3 6.3 %copy-start.4 = (bf16[2,128,768]{2,1,0:T(8,128)(2,1)S(1)}, bf16[2,128,768]{2,1,0:T(8,128)(2,1)}, u32[]{:S(2)}) copy-start(bf16[2,128,768]{2,1,0:T(8,128)(2,1)} %get-tuple-element.20.own) | copy-start | bytes 1179652
  114.3 6.3 %copy-start.6 = (bf16[2,128,768]{2,1,0:T(8,128)(2,1)S(1)}, bf16[2,128,768]{2,1,0:T(8,128)(2,1)}, u32[]{:S(2)}) copy-start(bf16[2,128,768]{2,1,0:T(8,128)(2,1)} %copy-done.5) | copy-start | bytes 1179652
  114.3 23.8 %all-to-all-start.1 = ((f32[8,2,72,128]{3,2,1,0:T(8,128)}), f32[8,2,72,128]{3,2,1,0:T(8,128)}, u32[]{:S(2)}, u32[]{:S(2)}) async-start(f32[8,2,72,128]{3,2,1,0:T(8,128)} %add.47), calls=%async_computation.1 | async-start | bytes 1179648 | tf_op jit(solution)/shard_map/all_to_all | solution.py:292
  120.5 1.0 copy-start.8
  126.6 5.6 %collective-permute-start.13 = (f32[8,2,72,128]{3,2,1,0:T(8,128)S(1)}, f32[8,2,72,128]{3,2,1,0:T(8,128)S(1)}, u32[]{:S(2)}, u32[]{:S(2)}) collective-permute-start(f32[8,2,72,128]{3,2,1,0:T(8,128)S(1)} %get-tuple-element.31), channel_id=1, source_target_pairs={{0,1},{1,0},{2,3},{3,2},{4,5},{5,4},{6,7},{7,6},{8,9},{9,8},{10,11... | collective-permute-start | bytes 1769480 | tf_op jit(solution)/shard_map/ppermute | solution.py:291
  138.0 22.9 %all-to-all-start = ((f32[8,2,72,128]{3,2,1,0:T(8,128)}), f32[8,2,72,128]{3,2,1,0:T(8,128)S(1)}, u32[]{:S(2)}, u32[]{:S(2)}) async-start(f32[8,2,72,128]{3,2,1,0:T(8,128)} %add.46), calls=%async_computation | async-start | bytes 1179648 | tf_op jit(solution)/shard_map/all_to_all | solution.py:292
  (1 other events, 1.0 us)

commit v6 on v5

--- a/solution.py
+++ b/solution.py
@@ -262,10 +262,11 @@
 
     mine, other = split(place, cotangent)
     parts = [hop(mine), hop(other, 1, 0), hop(mine, 0, 1), hop(other, 1, 1)]
+    parts = [after(part, came) for part in parts]
     first_one = jnp.stack([part[0] for part in parts])
     first_two = jnp.stack([part[1] for part in parts])
-    second_one = hop(after(first_one, came))
-    second_two = hop(after(first_two, came))
+    second_one = hop(first_one)
+    second_two = hop(first_two)
 
     att_own, att_swap = features_of(place, kept, after(came, first_two), gate)
     atts = (
@@ -275,11 +276,11 @@
         lax.ppermute(att_swap, ("zl", "c"), [(0, 3), (1, 2), (2, 1), (3, 0)]),
     )
 
-    third_one = hop(after(second_one, att_own))
-    third_two = hop(second_two)
-    last_one = hop(after(third_one, second_two)[:2])
+    beside = lax.ppermute(after(other, first_two), "zl", SWAP)
+    third_one = hop(after(second_one, first_two, att_own))
+    third_two = hop(after(second_two, third_one, atts[1]))
+    last_one = after(hop(after(third_one, second_two, beside)[:2]), third_two)
     last_two = hop(third_two[:2])
-    beside = lax.ppermute(after(other, second_one), "zl", SWAP)
     rings = (
         (first_one, second_one, third_one, last_one),
         (first_two, second_two, third_two, last_two),

time: 185 us -> 187 us (1.011)
  waiting for transfers between devices: 66.1 us -> 61.3 us
  starting transfers between devices: 71.6 us -> 74.6 us
  local copies, waits for them, and re-layouts: 6.59 us -> 8.52 us
    ppermute x1, waiting for transfers between devices: 11.8 us -> 0.01 us  [local(): came = lax.ppermute(away, 'yh', SWAP)]
    ppermute x1, waiting for transfers between devices: 0.01 us -> 9.04 us  [local(): lax.ppermute(att_own, 'zl', SWAP)]
    ppermute x1, starting transfers between devices: 1.91 us -> 8.73 us  [local(): came = lax.ppermute(away, 'yh', SWAP)]
    ppermute x10, starting transfers between devices: 42.7 us -> 38.3 us  [hop(): return lax.ppermute(block, ('x', 'zl', 'c'), ring(other_z, other_core))]
    ppermute x1, waiting for transfers between devices: 6.93 us -> 3.56 us  [local(): lax.ppermute(att_swap, ('zl', 'c'), [(0, 3), (1, 2), (2, 1), (3, 0)])]
    ppermute x1, starting transfers between devices: 4.93 us -> 1.92 us  [local(): lax.ppermute(att_own, 'zl', SWAP)]
    ppermute x1, waiting for transfers between devices: 3.17 us -> 5.61 us  [local(): beside = lax.ppermute(after(other, first_two), 'zl', SWAP)]
    ppermute x1, starting transfers between devices: 1.95 us -> 4.08 us  [local(): lax.ppermute(att_swap, ('zl', 'c'), [(0, 3), (1, 2), (2, 1), (3, 0)])]
  transfers between devices with their start and end apart: 19 -> 19, of which waited for: 12 -> 11; matrix products, arithmetic and copies ran while one was open for 3% -> 2% of each run, Pallas kernels for 6% -> 5%
where the time goes in v6:
time: 187 us; the launch traced here: 185 us
  starting transfers between devices  74.6 us (40%)
  waiting for transfers between devices  61.3 us (33%)
  blocking collectives  20.6 us (11%)
  Pallas kernels  15.8 us (8%)
  local copies, waits for them, and re-layouts  8.52 us (5%)
  other arithmetic  3.13 us (2%)
    ppermute x10, starting transfers between devices, hop(): return lax.ppermute(block, ('x', 'zl', 'c'), ring(other_z, other_core))  38.3 us
    all_to_all x2, waiting for transfers between devices, local(): by_z.append(jnp.sum(lax.all_to_all(paired, Y, 0, 0), axis=0))  24.2 us
    all_to_all x1, blocking collectives, local(): parts = lax.all_to_all(jnp.concatenate(by_z, axis=0), 'zh', 0, 0)  20.6 us
    ppermute x10, waiting for transfers between devices, hop(): return lax.ppermute(block, ('x', 'zl', 'c'), ring(other_z, other_core))  17.2 us
    ppermute x1, waiting for transfers between devices, local(): lax.ppermute(att_own, 'zl', SWAP)  9.04 us
    all_to_all x2, starting transfers between devices, local(): by_z.append(jnp.sum(lax.all_to_all(paired, Y, 0, 0), axis=0))  9.03 us
    ppermute x1, starting transfers between devices, local(): came = lax.ppermute(away, 'yh', SWAP)  8.73 us
    pallas_call x2, Pallas kernels, product(): pl.pallas_call(functools.partial(product_kernel, piece), grid=(count,), i...  8.23 us
  transfers between devices with their start and end apart: 19, of which 11 were waited for; matrix products, arithmetic and copies ran while one was open for 2% of the time, Pallas kernels for 5%

profile of v6, /device:TPU:1, one launch (start us, length us, event | category | flops | bytes accessed | tf_op | source)
XLA Modules:
  0.0 184.9 jit_solution(2866479851499961461)
XLA Ops:
  2.6 8.7 %collective-permute-start = (bf16[192,1024]{1,0:T(8,128)(2,1)S(1)}, bf16[192,1024]{1,0:T(8,128)(2,1)S(1)}, u32[]{:S(2)}, u32[]{:S(2)}) collective-permute-start(bf16[192,1024]{1,0:T(8,128)(2,1)S(1)} %get-tuple-element.42), channel_id=1, source_target_pairs={{0,512},{512,0},{1,513},{513,1},{2,514},{514,2},{3,515},{515,3},{4... | collective-permute-start | bytes 1179656 | tf_op jit(solution)/shard_map/ppermute | solution.py:261
  11.9 2.1 %split.1 = (bf16[2,128,768]{2,1,0:T(8,128)(2,1)}, bf16[2,128,768]{2,1,0:T(8,128)(2,1)}) custom-call(s32[11]{0:T(128)} %stack.53.place, bf16[128,3072]{1,0:T(8,128)(2,1)} %cotangent.1), custom_call_target="tpu_custom_call" | custom-call | tf_op jit(solution)/shard_map/split/pallas_call | solution.py:66
  14.0 6.7 %collective-permute-start.4 = (bf16[2,128,768]{2,1,0:T(8,128)(2,1)}, bf16[2,128,768]{2,1,0:T(8,128)(2,1)S(1)}, u32[]{:S(2)}, u32[]{:S(2)}) collective-permute-start(bf16[2,128,768]{2,1,0:T(8,128)(2,1)} %get-tuple-element.33), channel_id=1, source_target_pairs={{0,457},{1,72},{8,449},{9,64},{64,9},{65,136},{72,1},{73,128},{128... | collective-permute-start | bytes 1179656 | tf_op jit(solution)/shard_map/ppermute | solution.py:49
  20.7 7.9 %collective-permute-start.2 = (bf16[2,128,768]{2,1,0:T(8,128)(2,1)}, bf16[2,128,768]{2,1,0:T(8,128)(2,1)S(1)}, u32[]{:S(2)}, u32[]{:S(2)}) collective-permute-start(bf16[2,128,768]{2,1,0:T(8,128)(2,1)} %get-tuple-element.33), channel_id=1, source_target_pairs={{0,72},{1,457},{8,64},{9,449},{64,136},{65,9},{72,128},{73,1},{128... | collective-permute-start | bytes 1179656 | tf_op jit(solution)/shard_map/ppermute | solution.py:49
  28.7 1.9 %collective-permute-start.3 = (bf16[2,128,768]{2,1,0:T(8,128)(2,1)}, bf16[2,128,768]{2,1,0:T(8,128)(2,1)S(1)}, u32[]{:S(2)}, u32[]{:S(2)}) collective-permute-start(bf16[2,128,768]{2,1,0:T(8,128)(2,1)} %get-tuple-element.24.own), channel_id=1, source_target_pairs={{0,449},{1,64},{8,457},{9,72},{64,1},{65,128},{72,9},{73,136},{128... | collective-permute-start | bytes 1179656 | tf_op jit(solution)/shard_map/ppermute | solution.py:49
  30.6 1.9 %collective-permute-start.1 = (bf16[2,128,768]{2,1,0:T(8,128)(2,1)}, bf16[2,128,768]{2,1,0:T(8,128)(2,1)S(1)}, u32[]{:S(2)}, u32[]{:S(2)}) collective-permute-start(bf16[2,128,768]{2,1,0:T(8,128)(2,1)} %get-tuple-element.24.own), channel_id=1, source_target_pairs={{0,64},{1,449},{8,72},{9,457},{64,128},{65,1},{72,136},{73,9},{128... | collective-permute-start | bytes 1179656 | tf_op jit(solution)/shard_map/ppermute | solution.py:49
  32.5 5.7 %collective-permute-done.2 = bf16[2,128,768]{2,1,0:T(8,128)(2,1)S(1)} collective-permute-done((bf16[2,128,768]{2,1,0:T(8,128)(2,1)}, bf16[2,128,768]{2,1,0:T(8,128)(2,1)S(1)}, u32[]{:S(2)}, u32[]{:S(2)}) %collective-permute-start.2) | collective-permute-done | bytes 393248 | tf_op jit(solution)/shard_map/ppermute | solution.py:49
  38.3 4.8 %collective-permute-done.3 = bf16[2,128,768]{2,1,0:T(8,128)(2,1)S(1)} collective-permute-done((bf16[2,128,768]{2,1,0:T(8,128)(2,1)}, bf16[2,128,768]{2,1,0:T(8,128)(2,1)S(1)}, u32[]{:S(2)}, u32[]{:S(2)}) %collective-permute-start.3) | collective-permute-done | bytes 393248 | tf_op jit(solution)/shard_map/ppermute | solution.py:49
  45.0 3.6 %collective-permute-start.9 = (bf16[4,128,768]{2,1,0:T(8,128)(2,1)S(1)}, bf16[4,128,768]{2,1,0:T(8,128)(2,1)}, u32[]{:S(2)}, u32[]{:S(2)}) collective-permute-start(bf16[4,128,768]{2,1,0:T(8,128)(2,1)S(1)} %pad_maximum_fusion.1.hop_one), channel_id=1, source_target_pairs={{0,64},{1,449},{8,72},{9,457},{64,128},{65,1},{72,136},{73,9},{128... | collective-permute-start | bytes 2359304 | tf_op jit(solution)/shard_map/ppermute | solution.py:49
  48.7 4.0 %collective-permute-start.11 = (bf16[4,128,768]{2,1,0:T(8,128)(2,1)S(1)}, bf16[4,128,768]{2,1,0:T(8,128)(2,1)S(1)}, u32[]{:S(2)}, u32[]{:S(2)}) collective-permute-start(bf16[4,128,768]{2,1,0:T(8,128)(2,1)S(1)} %pad_maximum_fusion.hop_one), channel_id=1, source_target_pairs={{0,64},{1,449},{8,72},{9,457},{64,128},{65,1},{72,136},{73,9},{128... | collective-permute-start | bytes 2359304 | tf_op jit(solution)/shard_map/ppermute | solution.py:49
  52.7 2.3 %features.1 = (bf16[416,640]{1,0:T(8,128)(2,1)}, bf16[416,384]{1,0:T(8,128)(2,1)}) custom-call(s32[11]{0:T(128)} %stack.53.place, bf16[192,1024]{1,0:T(8,128)(2,1)} %get-tuple-element.43.kept, bf16[192,1024]{1,0:T(8,128)(2,1)} %copy-done.12, f32[1,3072]{1,0:T(1,128)} %gate.1), custom_call_target="tpu_custom_call" | custom-call | tf_op jit(solution)/shard_map/features/pallas_call | solution.py:106
  55.0 3.2 %collective-permute-done.9.hop_two = bf16[4,128,768]{2,1,0:T(8,128)(2,1)} collective-permute-done((bf16[4,128,768]{2,1,0:T(8,128)(2,1)S(1)}, bf16[4,128,768]{2,1,0:T(8,128)(2,1)}, u32[]{:S(2)}, u32[]{:S(2)}) %collective-permute-start.9) | collective-permute-done | bytes 786464 | tf_op jit(solution)/shard_map/ppermute | solution.py:49
  58.1 4.5 %collective-permute-start.10 = (bf16[4,128,768]{2,1,0:T(8,128)(2,1)}, bf16[4,128,768]{2,1,0:T(8,128)(2,1)S(1)}, u32[]{:S(2)}, u32[]{:S(2)}) collective-permute-start(bf16[4,128,768]{2,1,0:T(8,128)(2,1)} %collective-permute-done.9.hop_two), channel_id=1, source_target_pairs={{0,64},{1,449},{8,72},{9,457},{64,128},{65,1},{72,136},{73,9},{128... | collective-permute-start | bytes 2359304 | tf_op jit(solution)/shard_map/ppermute | solution.py:49
  62.6 1.9 %collective-permute-start.5 = (bf16[416,640]{1,0:T(8,128)(2,1)}, bf16[416,640]{1,0:T(8,128)(2,1)S(1)}, u32[]{:S(2)}, u32[]{:S(2)}) collective-permute-start(bf16[416,640]{1,0:T(8,128)(2,1)} %get-tuple-element.31.att_own), channel_id=1, source_target_pairs={{0,8},{8,0},{1,9},{9,1},{2,10},{10,2},{3,11},{11,3},{4,12},{12,4},... | collective-permute-start | bytes 1597448 | tf_op jit(solution)/shard_map/ppermute | solution.py:274
  64.5 3.4 %collective-permute-start.8 = (bf16[2,128,768]{2,1,0:T(8,128)(2,1)}, bf16[2,128,768]{2,1,0:T(8,128)(2,1)S(1)}, u32[]{:S(2)}, u32[]{:S(2)}) collective-permute-start(bf16[2,128,768]{2,1,0:T(8,128)(2,1)} %get-tuple-element.33), channel_id=1, source_target_pairs={{0,8},{8,0},{1,9},{9,1},{2,10},{10,2},{3,11},{11,3},{4,12},{12,4},... | collective-permute-start | bytes 1179656 | tf_op jit(solution)/shard_map/ppermute | solution.py:279
  67.9 9.0 %collective-permute-done.5.att_beside = bf16[416,640]{1,0:T(8,128)(2,1)S(1)} collective-permute-done((bf16[416,640]{1,0:T(8,128)(2,1)}, bf16[416,640]{1,0:T(8,128)(2,1)S(1)}, u32[]{:S(2)}, u32[]{:S(2)}) %collective-permute-start.5) | collective-permute-done | bytes 532512 | tf_op jit(solution)/shard_map/ppermute | solution.py:274
  79.8 5.6 %collective-permute-done.8.beside = bf16[2,128,768]{2,1,0:T(8,128)(2,1)S(1)} collective-permute-done((bf16[2,128,768]{2,1,0:T(8,128)(2,1)}, bf16[2,128,768]{2,1,0:T(8,128)(2,1)S(1)}, u32[]{:S(2)}, u32[]{:S(2)}) %collective-permute-start.8) | collective-permute-done | bytes 393248 | tf_op jit(solution)/shard_map/ppermute | solution.py:279
  85.4 1.9 %collective-permute-start.12 = (bf16[2,128,768]{2,1,0:T(8,128)(2,1)S(1)}, bf16[2,128,768]{2,1,0:T(8,128)(2,1)S(1)}, u32[]{:S(2)}, u32[]{:S(2)}) collective-permute-start(bf16[2,128,768]{2,1,0:T(8,128)(2,1)S(1)} %slice.38), channel_id=1, source_target_pairs={{0,64},{1,449},{8,72},{9,457},{64,128},{65,1},{72,136},{73,9},{128... | collective-permute-start | bytes 1179656 | tf_op jit(solution)/shard_map/ppermute | solution.py:49
  87.4 4.1 %collective-permute-start.7 = (bf16[416,384]{1,0:T(8,128)(2,1)}, bf16[416,384]{1,0:T(8,128)(2,1)S(1)}, u32[]{:S(2)}, u32[]{:S(2)}) collective-permute-start(bf16[416,384]{1,0:T(8,128)(2,1)} %get-tuple-element.32), channel_id=1, source_target_pairs={{0,9},{1,8},{8,1},{9,0},{2,11},{3,10},{10,3},{11,2},{4,13},{5,12},... | collective-permute-start | bytes 958472 | tf_op jit(solution)/shard_map/ppermute | solution.py:276
  91.4 2.0 %collective-permute-start.6 = (bf16[416,384]{1,0:T(8,128)(2,1)}, bf16[416,384]{1,0:T(8,128)(2,1)S(1)}, u32[]{:S(2)}, u32[]{:S(2)}) collective-permute-start(bf16[416,384]{1,0:T(8,128)(2,1)} %get-tuple-element.32), channel_id=1, source_target_pairs={{0,1},{1,0},{2,3},{3,2},{4,5},{5,4},{6,7},{7,6},{8,9},{9,8},{10,11... | collective-permute-start | bytes 958472 | tf_op jit(solution)/shard_map/ppermute | solution.py:275
  95.3 3.6 %collective-permute-done.7.att_across = bf16[416,384]{1,0:T(8,128)(2,1)S(1)} collective-permute-done((bf16[416,384]{1,0:T(8,128)(2,1)}, bf16[416,384]{1,0:T(8,128)(2,1)S(1)}, u32[]{:S(2)}, u32[]{:S(2)}) %collective-permute-start.7) | collective-permute-done | bytes 319520 | tf_op jit(solution)/shard_map/ppermute | solution.py:276
  100.0 4.1 %product.2 = (f32[8,2,72,128]{3,2,1,0:T(8,128)S(1)}, f32[8,2,72,128]{3,2,1,0:T(8,128)S(1)}) custom-call(s32[11]{0:T(128)S(1)} %copy-done.11, bf16[416,640]{1,0:T(8,128)(2,1)S(1)} %copy-done, bf16[416,640]{1,0:T(8,128)(2,1)S(1)} %collective-permute-done.5.att_beside, bf16[416,384]{1,0:T(8,128)(2,1)S(1)} %collective-permute-done.6.att_cross, ...), custom_call_target="tpu_custom_call" | custom-call | flops 1207959552 | bytes 8388608 | tf_op jit(solution)/shard_map/product/pallas_call | solution.py:183
  104.2 4.5 %collective-permute-start.14 = (f32[8,2,72,128]{3,2,1,0:T(8,128)S(1)}, f32[8,2,72,128]{3,2,1,0:T(8,128)S(1)}, u32[]{:S(2)}, u32[]{:S(2)}) collective-permute-start(f32[8,2,72,128]{3,2,1,0:T(8,128)S(1)} %get-tuple-element.39), channel_id=1, source_target_pairs={{0,1},{1,0},{2,3},{3,2},{4,5},{5,4},{6,7},{7,6},{8,9},{9,8},{10,11... | collective-permute-start | bytes 1769480 | tf_op jit(solution)/shard_map/ppermute | solution.py:292
  109.5 4.0 %collective-permute-start.15 = (bf16[2,128,768]{2,1,0:T(8,128)(2,1)}, bf16[2,128,768]{2,1,0:T(8,128)(2,1)}, u32[]{:S(2)}, u32[]{:S(2)}) collective-permute-start(bf16[2,128,768]{2,1,0:T(8,128)(2,1)} %slice.40), channel_id=1, source_target_pairs={{0,64},{1,449},{8,72},{9,457},{64,128},{65,1},{72,136},{73,9},{128... | collective-permute-start | bytes 1179656 | tf_op jit(solution)/shard_map/ppermute | solution.py:49
  114.4 5.5 %all-to-all-start = ((f32[8,2,72,128]{3,2,1,0:T(8,128)}), f32[8,2,72,128]{3,2,1,0:T(8,128)}, u32[]{:S(2)}, u32[]{:S(2)}) async-start(f32[8,2,72,128]{3,2,1,0:T(8,128)} %add.46), calls=%async_computation | async-start | bytes 1179648 | tf_op jit(solution)/shard_map/all_to_all | solution.py:293
  123.0 4.1 %product.3 = (f32[8,2,72,128]{3,2,1,0:T(8,128)S(1)}, f32[8,2,72,128]{3,2,1,0:T(8,128)S(1)}) custom-call(s32[11]{0:T(128)S(1)} %copy-done.11, bf16[416,640]{1,0:T(8,128)(2,1)S(1)} %copy-done, bf16[416,640]{1,0:T(8,128)(2,1)S(1)} %collective-permute-done.5.att_beside, bf16[416,384]{1,0:T(8,128)(2,1)S(1)} %copy-done.8, bf16[416,384]{1,0:T(8,128)(2,1)S(1)} %copy-done.6, ...), custom_call_target="tpu_custom_call" | custom-call | flops 1207959552 | bytes 8388608 | tf_op jit(solution)/shard_map/product/pallas_call | solution.py:183
  127.1 2.6 %collective-permute-start.16 = (f32[8,2,72,128]{3,2,1,0:T(8,128)S(1)}, f32[8,2,72,128]{3,2,1,0:T(8,128)S(1)}, u32[]{:S(2)}, u32[]{:S(2)}) collective-permute-start(f32[8,2,72,128]{3,2,1,0:T(8,128)S(1)} %get-tuple-element.41), channel_id=1, source_target_pairs={{0,1},{1,0},{2,3},{3,2},{4,5},{5,4},{6,7},{7,6},{8,9},{9,8},{10,11... | collective-permute-start | bytes 1769480 | tf_op jit(solution)/shard_map/ppermute | solution.py:292
  132.2 6.0 %all-to-all-done = f32[8,2,72,128]{3,2,1,0:T(8,128)} async-done(((f32[8,2,72,128]{3,2,1,0:T(8,128)}), f32[8,2,72,128]{3,2,1,0:T(8,128)}, u32[]{:S(2)}, u32[]{:S(2)}) %all-to-all-start) | async-done | bytes 589856 | tf_op jit(solution)/shard_map/all_to_all | solution.py:293
  138.2 3.5 %all-to-all-start.1 = ((f32[8,2,72,128]{3,2,1,0:T(8,128)}), f32[8,2,72,128]{3,2,1,0:T(8,128)S(1)}, u32[]{:S(2)}, u32[]{:S(2)}) async-start(f32[8,2,72,128]{3,2,1,0:T(8,128)} %add.47), calls=%async_computation.1 | async-start | bytes 1179648 | tf_op jit(solution)/shard_map/all_to_all | solution.py:293
  142.8 18.2 %all-to-all-done.1 = f32[8,2,72,128]{3,2,1,0:T(8,128)S(1)} async-done(((f32[8,2,72,128]{3,2,1,0:T(8,128)}), f32[8,2,72,128]{3,2,1,0:T(8,128)S(1)}, u32[]{:S(2)}, u32[]{:S(2)}) %all-to-all-start.1) | async-done | bytes 589856 | tf_op jit(solution)/shard_map/all_to_all | solution.py:293
  161.1 20.6 %all_to_all.15.parts = f32[4,72,128]{2,1,0:T(8,128)} all-to-all(f32[4,72,128]{2,1,0:T(8,128)S(1)} %pad_maximum_fusion.2), channel_id=1, replica_groups=mesh['yh'=2,'x'=8,'zh'=4,'zl'=2,'yl'=4,'c'=2] {'zh'}, dimensions={0} | all-to-all | bytes 294912 | tf_op jit(solution)/shard_map/all_to_all | solution.py:294
  181.7 3.2 %update.1 = (f32[48,192]{1,0:T(8,128)}, f32[48,192]{1,0:T(8,128)}, f32[48,192]{1,0:T(8,128)}, f32[48,192]{1,0:T(8,128)}, f32[48,48]{1,0:T(8,128)}, /*index=5*/f32[192,192]{1,0:T(8,128)}) custom-call(f32[4,72,128]{2,1,0:T(8,128)} %all_to_all.15.parts, f32[48,192]{1,0:T(8,128)} %weight.1, f32[48,192]{1,0:T(8,128)} %exp_avg.1, f32[48,192]{1,0:T(8,128)} %exp_avg_sq.1, ...), custom_call_target="tpu_custom_call" | custom-call | tf_op jit(solution)/shard_map/update/pallas_call | solution.py:297
  (51 shorter events, 18.7 us)
Async XLA Ops:
  2.6 30.0 %collective-permute-start = (bf16[192,1024]{1,0:T(8,128)(2,1)S(1)}, bf16[192,1024]{1,0:T(8,128)(2,1)S(1)}, u32[]{:S(2)}, u32[]{:S(2)}) collective-permute-start(bf16[192,1024]{1,0:T(8,128)(2,1)S(1)} %get-tuple-element.42), channel_id=1, source_target_pairs={{0,512},{512,0},{1,513},{513,1},{2,514},{514,2},{3,515},{515,3},{4... | collective-permute-start | bytes 1179656 | tf_op jit(solution)/shard_map/ppermute | solution.py:261
  14.0 18.5 %collective-permute-start.4 = (bf16[2,128,768]{2,1,0:T(8,128)(2,1)}, bf16[2,128,768]{2,1,0:T(8,128)(2,1)S(1)}, u32[]{:S(2)}, u32[]{:S(2)}) collective-permute-start(bf16[2,128,768]{2,1,0:T(8,128)(2,1)} %get-tuple-element.33), channel_id=1, source_target_pairs={{0,457},{1,72},{8,449},{9,64},{64,9},{65,136},{72,1},{73,128},{128... | collective-permute-start | bytes 1179656 | tf_op jit(solution)/shard_map/ppermute | solution.py:49
  20.7 17.6 %collective-permute-start.2 = (bf16[2,128,768]{2,1,0:T(8,128)(2,1)}, bf16[2,128,768]{2,1,0:T(8,128)(2,1)S(1)}, u32[]{:S(2)}, u32[]{:S(2)}) collective-permute-start(bf16[2,128,768]{2,1,0:T(8,128)(2,1)} %get-tuple-element.33), channel_id=1, source_target_pairs={{0,72},{1,457},{8,64},{9,449},{64,136},{65,9},{72,128},{73,1},{128... | collective-permute-start | bytes 1179656 | tf_op jit(solution)/shard_map/ppermute | solution.py:49
  28.7 14.4 %collective-permute-start.3 = (bf16[2,128,768]{2,1,0:T(8,128)(2,1)}, bf16[2,128,768]{2,1,0:T(8,128)(2,1)S(1)}, u32[]{:S(2)}, u32[]{:S(2)}) collective-permute-start(bf16[2,128,768]{2,1,0:T(8,128)(2,1)} %get-tuple-element.24.own), channel_id=1, source_target_pairs={{0,449},{1,64},{8,457},{9,72},{64,1},{65,128},{72,9},{73,136},{128... | collective-permute-start | bytes 1179656 | tf_op jit(solution)/shard_map/ppermute | solution.py:49
  30.6 14.2 %collective-permute-start.1 = (bf16[2,128,768]{2,1,0:T(8,128)(2,1)}, bf16[2,128,768]{2,1,0:T(8,128)(2,1)S(1)}, u32[]{:S(2)}, u32[]{:S(2)}) collective-permute-start(bf16[2,128,768]{2,1,0:T(8,128)(2,1)} %get-tuple-element.24.own), channel_id=1, source_target_pairs={{0,64},{1,449},{8,72},{9,457},{64,128},{65,1},{72,136},{73,9},{128... | collective-permute-start | bytes 1179656 | tf_op jit(solution)/shard_map/ppermute | solution.py:49
  32.5 12.3 %copy-start.12 = (bf16[192,1024]{1,0:T(8,128)(2,1)}, bf16[192,1024]{1,0:T(8,128)(2,1)S(1)}, u32[]{:S(2)}) copy-start(bf16[192,1024]{1,0:T(8,128)(2,1)S(1)} %collective-permute-done.came) | copy-start | bytes 1179652
  45.0 13.1 %collective-permute-start.9 = (bf16[4,128,768]{2,1,0:T(8,128)(2,1)S(1)}, bf16[4,128,768]{2,1,0:T(8,128)(2,1)}, u32[]{:S(2)}, u32[]{:S(2)}) collective-permute-start(bf16[4,128,768]{2,1,0:T(8,128)(2,1)S(1)} %pad_maximum_fusion.1.hop_one), channel_id=1, source_target_pairs={{0,64},{1,449},{8,72},{9,457},{64,128},{65,1},{72,136},{73,9},{128... | collective-permute-start | bytes 2359304 | tf_op jit(solution)/shard_map/ppermute | solution.py:49
  48.7 28.3 %collective-permute-start.11 = (bf16[4,128,768]{2,1,0:T(8,128)(2,1)S(1)}, bf16[4,128,768]{2,1,0:T(8,128)(2,1)S(1)}, u32[]{:S(2)}, u32[]{:S(2)}) collective-permute-start(bf16[4,128,768]{2,1,0:T(8,128)(2,1)S(1)} %pad_maximum_fusion.hop_one), channel_id=1, source_target_pairs={{0,64},{1,449},{8,72},{9,457},{64,128},{65,1},{72,136},{73,9},{128... | collective-permute-start | bytes 2359304 | tf_op jit(solution)/shard_map/ppermute | solution.py:49
  55.0 43.9 %copy-start = (bf16[416,640]{1,0:T(8,128)(2,1)S(1)}, bf16[416,640]{1,0:T(8,128)(2,1)}, u32[]{:S(2)}) copy-start(bf16[416,640]{1,0:T(8,128)(2,1)} %get-tuple-element.31.att_own) | copy-start | bytes 1597444
  58.1 19.7 %collective-permute-start.10 = (bf16[4,128,768]{2,1,0:T(8,128)(2,1)}, bf16[4,128,768]{2,1,0:T(8,128)(2,1)S(1)}, u32[]{:S(2)}, u32[]{:S(2)}) collective-permute-start(bf16[4,128,768]{2,1,0:T(8,128)(2,1)} %collective-permute-done.9.hop_two), channel_id=1, source_target_pairs={{0,64},{1,449},{8,72},{9,457},{64,128},{65,1},{72,136},{73,9},{128... | collective-permute-start | bytes 2359304 | tf_op jit(solution)/shard_map/ppermute | solution.py:49
  62.6 14.3 %collective-permute-start.5 = (bf16[416,640]{1,0:T(8,128)(2,1)}, bf16[416,640]{1,0:T(8,128)(2,1)S(1)}, u32[]{:S(2)}, u32[]{:S(2)}) collective-permute-start(bf16[416,640]{1,0:T(8,128)(2,1)} %get-tuple-element.31.att_own), channel_id=1, source_target_pairs={{0,8},{8,0},{1,9},{9,1},{2,10},{10,2},{3,11},{11,3},{4,12},{12,4},... | collective-permute-start | bytes 1597448 | tf_op jit(solution)/shard_map/ppermute | solution.py:274
  64.5 20.8 %collective-permute-start.8 = (bf16[2,128,768]{2,1,0:T(8,128)(2,1)}, bf16[2,128,768]{2,1,0:T(8,128)(2,1)S(1)}, u32[]{:S(2)}, u32[]{:S(2)}) collective-permute-start(bf16[2,128,768]{2,1,0:T(8,128)(2,1)} %get-tuple-element.33), channel_id=1, source_target_pairs={{0,8},{8,0},{1,9},{9,1},{2,10},{10,2},{3,11},{11,3},{4,12},{12,4},... | collective-permute-start | bytes 1179656 | tf_op jit(solution)/shard_map/ppermute | solution.py:279
  77.0 0.9 copy-start.9
  77.9 17.4 %collective-permute-start.13 = (bf16[4,128,768]{2,1,0:T(8,128)(2,1)}, bf16[4,128,768]{2,1,0:T(8,128)(2,1)S(1)}, u32[]{:S(2)}, u32[]{:S(2)}) collective-permute-start(bf16[4,128,768]{2,1,0:T(8,128)(2,1)} %copy-done.9), channel_id=1, source_target_pairs={{0,64},{1,449},{8,72},{9,457},{64,128},{65,1},{72,136},{73,9},{128... | collective-permute-start | bytes 2359304 | tf_op jit(solution)/shard_map/ppermute | solution.py:49
  85.4 13.5 %copy-start.3 = (bf16[2,128,768]{2,1,0:T(8,128)(2,1)}, bf16[2,128,768]{2,1,0:T(8,128)(2,1)S(1)}, u32[]{:S(2)}) copy-start(bf16[2,128,768]{2,1,0:T(8,128)(2,1)S(1)} %collective-permute-done.8.beside) | copy-start | bytes 1179652
  85.4 13.5 %copy-start.11 = (s32[11]{0:T(128)S(1)}, s32[11]{0:T(128)}, u32[]{:S(2)}) copy-start(s32[11]{0:T(128)} %stack.53.place) | copy-start | bytes 136
  85.4 9.9 %collective-permute-start.12 = (bf16[2,128,768]{2,1,0:T(8,128)(2,1)S(1)}, bf16[2,128,768]{2,1,0:T(8,128)(2,1)S(1)}, u32[]{:S(2)}, u32[]{:S(2)}) collective-permute-start(bf16[2,128,768]{2,1,0:T(8,128)(2,1)S(1)} %slice.38), channel_id=1, source_target_pairs={{0,64},{1,449},{8,72},{9,457},{64,128},{65,1},{72,136},{73,9},{128... | collective-permute-start | bytes 1179656 | tf_op jit(solution)/shard_map/ppermute | solution.py:49
  87.4 11.5 %collective-permute-start.7 = (bf16[416,384]{1,0:T(8,128)(2,1)}, bf16[416,384]{1,0:T(8,128)(2,1)S(1)}, u32[]{:S(2)}, u32[]{:S(2)}) collective-permute-start(bf16[416,384]{1,0:T(8,128)(2,1)} %get-tuple-element.32), channel_id=1, source_target_pairs={{0,9},{1,8},{8,1},{9,0},{2,11},{3,10},{10,3},{11,2},{4,13},{5,12},... | collective-permute-start | bytes 958472 | tf_op jit(solution)/shard_map/ppermute | solution.py:276
  91.4 7.4 %collective-permute-start.6 = (bf16[416,384]{1,0:T(8,128)(2,1)}, bf16[416,384]{1,0:T(8,128)(2,1)S(1)}, u32[]{:S(2)}, u32[]{:S(2)}) collective-permute-start(bf16[416,384]{1,0:T(8,128)(2,1)} %get-tuple-element.32), channel_id=1, source_target_pairs={{0,1},{1,0},{2,3},{3,2},{4,5},{5,4},{6,7},{7,6},{8,9},{9,8},{10,11... | collective-permute-start | bytes 958472 | tf_op jit(solution)/shard_map/ppermute | solution.py:275
  98.9 5.3 %copy-start.5 = (bf16[416,384]{1,0:T(8,128)(2,1)}, bf16[416,384]{1,0:T(8,128)(2,1)S(1)}, u32[]{:S(2)}) copy-start(bf16[416,384]{1,0:T(8,128)(2,1)S(1)} %collective-permute-done.7.att_across) | copy-start | bytes 958468
  98.9 1.1 copy-start.1
  100.0 4.2 %copy-start.7 = (bf16[416,384]{1,0:T(8,128)(2,1)}, bf16[416,384]{1,0:T(8,128)(2,1)S(1)}, u32[]{:S(2)}) copy-start(bf16[416,384]{1,0:T(8,128)(2,1)S(1)} %collective-permute-done.6.att_cross) | copy-start | bytes 958468
  104.2 9.3 %collective-permute-start.14 = (f32[8,2,72,128]{3,2,1,0:T(8,128)S(1)}, f32[8,2,72,128]{3,2,1,0:T(8,128)S(1)}, u32[]{:S(2)}, u32[]{:S(2)}) collective-permute-start(f32[8,2,72,128]{3,2,1,0:T(8,128)S(1)} %get-tuple-element.39), channel_id=1, source_target_pairs={{0,1},{1,0},{2,3},{3,2},{4,5},{5,4},{6,7},{7,6},{8,9},{9,8},{10,11... | collective-permute-start | bytes 1769480 | tf_op jit(solution)/shard_map/ppermute | solution.py:292
  109.5 10.4 %collective-permute-start.15 = (bf16[2,128,768]{2,1,0:T(8,128)(2,1)}, bf16[2,128,768]{2,1,0:T(8,128)(2,1)}, u32[]{:S(2)}, u32[]{:S(2)}) collective-permute-start(bf16[2,128,768]{2,1,0:T(8,128)(2,1)} %slice.40), channel_id=1, source_target_pairs={{0,64},{1,449},{8,72},{9,457},{64,128},{65,1},{72,136},{73,9},{128... | collective-permute-start | bytes 1179656 | tf_op jit(solution)/shard_map/ppermute | solution.py:49
  114.4 5.5 %copy-start.2 = (bf16[2,128,768]{2,1,0:T(8,128)(2,1)S(1)}, bf16[2,128,768]{2,1,0:T(8,128)(2,1)}, u32[]{:S(2)}) copy-start(bf16[2,128,768]{2,1,0:T(8,128)(2,1)} %get-tuple-element.24.own) | copy-start | bytes 1179652
  114.4 5.5 %copy-start.4 = (bf16[2,128,768]{2,1,0:T(8,128)(2,1)S(1)}, bf16[2,128,768]{2,1,0:T(8,128)(2,1)}, u32[]{:S(2)}) copy-start(bf16[2,128,768]{2,1,0:T(8,128)(2,1)} %copy-done.3) | copy-start | bytes 1179652
  114.4 23.8 %all-to-all-start = ((f32[8,2,72,128]{3,2,1,0:T(8,128)}), f32[8,2,72,128]{3,2,1,0:T(8,128)}, u32[]{:S(2)}, u32[]{:S(2)}) async-start(f32[8,2,72,128]{3,2,1,0:T(8,128)} %add.46), calls=%async_computation | async-start | bytes 1179648 | tf_op jit(solution)/shard_map/all_to_all | solution.py:293
  119.9 1.0 copy-start.6
  120.9 1.0 copy-start.8
  121.8 1.1 copy-start.10
  127.1 4.3 %collective-permute-start.16 = (f32[8,2,72,128]{3,2,1,0:T(8,128)S(1)}, f32[8,2,72,128]{3,2,1,0:T(8,128)S(1)}, u32[]{:S(2)}, u32[]{:S(2)}) collective-permute-start(f32[8,2,72,128]{3,2,1,0:T(8,128)S(1)} %get-tuple-element.41), channel_id=1, source_target_pairs={{0,1},{1,0},{2,3},{3,2},{4,5},{5,4},{6,7},{7,6},{8,9},{9,8},{10,11... | collective-permute-start | bytes 1769480 | tf_op jit(solution)/shard_map/ppermute | solution.py:292
  138.2 22.9 %all-to-all-start.1 = ((f32[8,2,72,128]{3,2,1,0:T(8,128)}), f32[8,2,72,128]{3,2,1,0:T(8,128)S(1)}, u32[]{:S(2)}, u32[]{:S(2)}) async-start(f32[8,2,72,128]{3,2,1,0:T(8,128)} %add.47), calls=%async_computation.1 | async-start | bytes 1179648 | tf_op jit(solution)/shard_map/all_to_all | solution.py:293

commit v7 on v6

--- a/solution.py
+++ b/solution.py
@@ -31,42 +31,37 @@
 SWAP = [(0, 1), (1, 0)]
 
 
-def at_ring(x, zl, c):
-    return (x % NX) * 4 + 2 * zl + c
-
-
-def ring(other_z, other_core):
+def ring(other_core):
     pairs = []
     for x in range(NX):
-        for zl in range(2):
-            for c in range(2):
-                to_z, to_c = zl ^ other_z, c ^ other_core
-                pairs.append((at_ring(x, zl, c), at_ring(x + 1 - 2 * to_c, to_z, to_c)))
+        for c in range(2):
+            to = c ^ other_core
+            pairs.append((2 * x + c, 2 * ((x + 1 - 2 * to) % NX) + to))
     return pairs
 
 
-def hop(block, other_z=0, other_core=0):
-    return lax.ppermute(block, ("x", "zl", "c"), ring(other_z, other_core))
+def hop(block, other_core=0):
+    return lax.ppermute(block, ("x", "c"), ring(other_core))
 
 
 def after(value, *others):
     return lax.optimization_barrier((value, *others))[0]
 
 
-def split_kernel(place, cotangent, mine, other):
-    for zh in range(NZH):
-        for parity, ref in ((place[10], mine), (1 - place[10], other)):
+def split_kernel(place, cotangent, mine_one, mine_two, other_one, other_two):
+    for parity, refs in ((place[10], (mine_one, mine_two)), (1 - place[10], (other_one, other_two))):
+        for zh in range(NZH):
             start = pl.multiple_of((2 * zh + parity) * GROUP, GROUP)
             at = (zh % 2) * GROUP
-            ref[zh // 2, :, at : at + GROUP] = cotangent[:, pl.ds(start, GROUP)]
+            refs[zh // 2][:, at : at + GROUP] = cotangent[:, pl.ds(start, GROUP)]
 
 
 def split(place, cotangent):
-    half = jax.ShapeDtypeStruct((2, CHUNK, D // 4), cotangent.dtype)
+    piece = jax.ShapeDtypeStruct((CHUNK, D // 4), cotangent.dtype)
     return pl.pallas_call(
         split_kernel,
         in_specs=[pl.BlockSpec(memory_space=pltpu.SMEM), pl.BlockSpec((CHUNK, D), lambda: (0, 0))],
-        out_shape=[half] * 2,
+        out_shape=[piece] * 4,
         name="split",
     )(place, cotangent)
 
@@ -118,8 +113,7 @@
     att_beside,
     att_cross,
     att_across,
-    own,
-    beside,
+    local_pair,
     hop_one,
     hop_two,
     hop_three,
@@ -137,8 +131,7 @@
     for which, att in enumerate((att_own, att_beside, att_cross, att_across)):
         one, two, three = hop_one[which], hop_two[which], hop_three[which]
         if which < 2:
-            near = (own, beside)[which][0]
-            clip = dot(att[:FEAT, : 2 * CHUNK], near, one)
+            clip = dot(att[:FEAT, : 2 * CHUNK], local_pair[which], one)
             clip += dot(att[:FEAT, 2 * CHUNK : 4 * CHUNK], two, three)
             clip += dot(att[:FEAT, 4 * CHUNK :], last[which])
         else:
@@ -171,10 +164,9 @@
             store(send, 1 - core)
 
 
-def product(piece, place, atts, own, beside, blocks):
+def product(piece, place, atts, blocks):
     count = blocks[0].shape[2] // GROUP
     attn = [pl.BlockSpec(att.shape, lambda z: (0, 0)) for att in atts]
-    near = pl.BlockSpec((1, CHUNK, GROUP), lambda z: (piece, 0, z))
     four = pl.BlockSpec((4, CHUNK, GROUP), lambda z: (0, 0, z))
     pair = pl.BlockSpec((2, CHUNK, GROUP), lambda z: (0, 0, z))
     out = pl.BlockSpec((2 * NY, 1, PACK, 128), lambda z: (0, z, 0, 0))
@@ -185,13 +177,13 @@
         grid=(count,),
         in_specs=[pl.BlockSpec(memory_space=pltpu.SMEM)]
         + attn
-        + [near, near, four, four, four, pair],
+        + [pair, four, four, four, pair],
         out_specs=[out, out],
         out_shape=[shape, shape],
         cost_estimate=pl.CostEstimate(flops=flops, bytes_accessed=8 << 20, transcendentals=0),
         compiler_params=pltpu.CompilerParams(vmem_limit_bytes=32 << 20),
         name="product",
-    )(place, *atts, own, beside, *blocks)
+    )(place, *atts, *blocks)
 
 
 def update_kernel(
@@ -260,35 +252,32 @@
     away = lax.dynamic_slice_in_dim(features, (1 - yh) * TOK, TOK, 1)
     came = lax.ppermute(away, "yh", SWAP)
 
-    mine, other = split(place, cotangent)
-    parts = [hop(mine), hop(other, 1, 0), hop(mine, 0, 1), hop(other, 1, 1)]
-    parts = [after(part, came) for part in parts]
-    first_one = jnp.stack([part[0] for part in parts])
-    first_two = jnp.stack([part[1] for part in parts])
+    mine_one, mine_two, other_one, other_two = split(place, cotangent)
+    pair_one = jnp.stack([mine_one, lax.ppermute(other_one, "zl", SWAP)])
+    pair_two = jnp.stack([mine_two, lax.ppermute(other_two, "zl", SWAP)])
+    first_one = jnp.concatenate([after(hop(pair_one), came), hop(pair_one, 1)])
+
+    att_own, att_swap = features_of(place, kept, after(came, first_one), gate)
+    first_two = jnp.concatenate([after(hop(pair_two), att_own), hop(pair_two, 1)])
+    att_beside = lax.ppermute(att_own, "zl", SWAP)
+    att_across = lax.ppermute(att_swap, ("zl", "c"), [(0, 3), (1, 2), (2, 1), (3, 0)])
+    att_cross = lax.ppermute(after(att_swap, att_beside, att_across), "c", SWAP)
+    atts = att_own, att_beside, att_cross, att_across
+
     second_one = hop(first_one)
     second_two = hop(first_two)
-
-    att_own, att_swap = features_of(place, kept, after(came, first_two), gate)
-    atts = (
-        att_own,
-        lax.ppermute(att_own, "zl", SWAP),
-        lax.ppermute(att_swap, "c", SWAP),
-        lax.ppermute(att_swap, ("zl", "c"), [(0, 3), (1, 2), (2, 1), (3, 0)]),
-    )
-
-    beside = lax.ppermute(after(other, first_two), "zl", SWAP)
-    third_one = hop(after(second_one, first_two, att_own))
-    third_two = hop(after(second_two, third_one, atts[1]))
-    last_one = after(hop(after(third_one, second_two, beside)[:2]), third_two)
+    third_one = hop(after(second_one, first_two))
+    third_two = hop(after(second_two, third_one))
+    last_one = after(hop(after(third_one, second_two)[:2]), third_two)
     last_two = hop(third_two[:2])
     rings = (
-        (first_one, second_one, third_one, last_one),
-        (first_two, second_two, third_two, last_two),
+        (pair_one, first_one, second_one, third_one, last_one),
+        (pair_two, first_two, second_two, third_two, last_two),
     )
 
     by_z = []
     for at, blocks in enumerate(rings):
-        keep, send = product(at, place, atts, mine, beside, blocks)
+        keep, send = product(at, place, atts, blocks)
         paired = keep + lax.ppermute(send, "c", SWAP)
         by_z.append(jnp.sum(lax.all_to_all(paired, Y, 0, 0), axis=0))
     parts = lax.all_to_all(jnp.concatenate(by_z, axis=0), "zh", 0, 0)

time: 187 us -> 192 us (1.027)
  starting transfers between devices: 74.6 us -> 82.5 us
  waiting for transfers between devices: 61.3 us -> 58.6 us
    ppermute x13 -> x14, starting transfers between devices: 45.6 us -> 51.7 us  [the longest x10 39 us: hop(): return lax.ppermute(block, ('x', 'c'), ring(other_core))]
    ppermute x13 -> x14, waiting for transfers between devices: 31.9 us -> 29.4 us  [the longest x10 28.2 us: hop(): return lax.ppermute(block, ('x', 'c'), ring(other_core))]
    unnamed x26 -> x42, local copies, waits for them, and re-layouts: 5.08 us -> 4.96 us
  transfers between devices with their start and end apart: 19 -> 20, of which waited for: 11 -> 11; matrix products, arithmetic and copies ran while one was open for 2% -> 3% of each run, Pallas kernels for 5% -> 3%
where the time goes in v7:
time: 192 us; the launch traced here: 189 us
  starting transfers between devices  82.5 us (43%)
  waiting for transfers between devices  58.6 us (31%)
  blocking collectives  20.3 us (11%)
  Pallas kernels  15.3 us (8%)
  local copies, waits for them, and re-layouts  8.29 us (4%)
  other arithmetic  3.01 us (2%)
    ppermute x10, starting transfers between devices, hop(): return lax.ppermute(block, ('x', 'c'), ring(other_core))  39 us
    ppermute x10, waiting for transfers between devices, hop(): return lax.ppermute(block, ('x', 'c'), ring(other_core))  28.2 us
    all_to_all x2, waiting for transfers between devices, local(): by_z.append(jnp.sum(lax.all_to_all(paired, Y, 0, 0), axis=0))  23.6 us
    all_to_all x1, blocking collectives, local(): parts = lax.all_to_all(jnp.concatenate(by_z, axis=0), 'zh', 0, 0)  20.3 us
    ppermute x2, starting transfers between devices, local(): paired = keep + lax.ppermute(send, 'c', SWAP)  9.08 us
    all_to_all x2, starting transfers between devices, local(): by_z.append(jnp.sum(lax.all_to_all(paired, Y, 0, 0), axis=0))  8.19 us
    ppermute x1, starting transfers between devices, local(): came = lax.ppermute(away, 'yh', SWAP)  7.9 us
    pallas_call x2, Pallas kernels, product(): pl.pallas_call(functools.partial(product_kernel, piece), grid=(count,), i...  7.78 us
  transfers between devices with their start and end apart: 20, of which 11 were waited for; matrix products, arithmetic and copies ran while one was open for 3% of the time, Pallas kernels for 3%

profile of v7, /device:TPU:1, one launch (start us, length us, event | category | flops | bytes accessed | tf_op | source)
XLA Modules:
  0.0 189.1 jit_solution(18281073313665369136)
XLA Ops:
  1.2 2.1 %split.1 = (bf16[128,768]{1,0:T(8,128)(2,1)}, bf16[128,768]{1,0:T(8,128)(2,1)}, bf16[128,768]{1,0:T(8,128)(2,1)}, bf16[128,768]{1,0:T(8,128)(2,1)}) custom-call(s32[11]{0:T(128)} %stack.65.place, bf16[128,3072]{1,0:T(8,128)(2,1)} %cotangent.1), custom_call_target="tpu_custom_call" | custom-call | tf_op jit(solution)/shard_map/split/pallas_call | solution.py:61
  3.3 5.7 %collective-permute-start.1 = (bf16[128,768]{1,0:T(8,128)(2,1)}, bf16[128,768]{1,0:T(8,128)(2,1)S(1)}, u32[]{:S(2)}, u32[]{:S(2)}) collective-permute-start(bf16[128,768]{1,0:T(8,128)(2,1)} %get-tuple-element.25), channel_id=1, source_target_pairs={{0,8},{8,0},{1,9},{9,1},{2,10},{10,2},{3,11},{11,3},{4,12},{12,4},... | collective-permute-start | bytes 589832 | tf_op jit(solution)/shard_map/ppermute | solution.py:256
  9.9 7.9 %collective-permute-start = (bf16[192,1024]{1,0:T(8,128)(2,1)S(1)}, bf16[192,1024]{1,0:T(8,128)(2,1)S(1)}, u32[]{:S(2)}, u32[]{:S(2)}) collective-permute-start(bf16[192,1024]{1,0:T(8,128)(2,1)S(1)} %get-tuple-element.42), channel_id=1, source_target_pairs={{0,512},{512,0},{1,513},{513,1},{2,514},{514,2},{3,515},{515,3},{4... | collective-permute-start | bytes 1179656 | tf_op jit(solution)/shard_map/ppermute | solution.py:253
  17.9 4.6 %collective-permute-start.2 = (bf16[2,128,768]{2,1,0:T(8,128)(2,1)S(1)}, bf16[2,128,768]{2,1,0:T(8,128)(2,1)S(1)}, u32[]{:S(2)}, u32[]{:S(2)}) collective-permute-start(bf16[2,128,768]{2,1,0:T(8,128)(2,1)S(1)} %pad_maximum_fusion.local_pair), channel_id=1, source_target_pairs={{0,64},{1,449},{64,128},{65,1},{128,192},{129,65},{192,256},{193,1... | collective-permute-start | bytes 1179656 | tf_op jit(solution)/shard_map/ppermute | solution.py:44
  22.6 3.1 %collective-permute-start.3 = (bf16[2,128,768]{2,1,0:T(8,128)(2,1)S(1)}, bf16[2,128,768]{2,1,0:T(8,128)(2,1)S(1)}, u32[]{:S(2)}, u32[]{:S(2)}) collective-permute-start(bf16[2,128,768]{2,1,0:T(8,128)(2,1)S(1)} %pad_maximum_fusion.local_pair), channel_id=1, source_target_pairs={{0,449},{1,64},{64,1},{65,128},{128,65},{129,192},{192,129},{193,2... | collective-permute-start | bytes 1179656 | tf_op jit(solution)/shard_map/ppermute | solution.py:44
  25.7 1.9 %collective-permute-start.8 = (bf16[128,768]{1,0:T(8,128)(2,1)S(1)}, bf16[128,768]{1,0:T(8,128)(2,1)S(1)}, u32[]{:S(2)}, u32[]{:S(2)}) collective-permute-start(bf16[128,768]{1,0:T(8,128)(2,1)S(1)} %copy-done.19), channel_id=1, source_target_pairs={{0,8},{8,0},{1,9},{9,1},{2,10},{10,2},{3,11},{11,3},{4,12},{12,4},... | collective-permute-start | bytes 589832 | tf_op jit(solution)/shard_map/ppermute | solution.py:257
  29.8 2.9 %collective-permute-done.3 = bf16[2,128,768]{2,1,0:T(8,128)(2,1)S(1)} collective-permute-done((bf16[2,128,768]{2,1,0:T(8,128)(2,1)S(1)}, bf16[2,128,768]{2,1,0:T(8,128)(2,1)S(1)}, u32[]{:S(2)}, u32[]{:S(2)}) %collective-permute-start.3) | collective-permute-done | bytes 393248 | tf_op jit(solution)/shard_map/ppermute | solution.py:44
  32.7 8.6 %collective-permute-start.7 = (bf16[4,128,768]{2,1,0:T(8,128)(2,1)S(1)}, bf16[4,128,768]{2,1,0:T(8,128)(2,1)S(1)}, u32[]{:S(2)}, u32[]{:S(2)}) collective-permute-start(bf16[4,128,768]{2,1,0:T(8,128)(2,1)S(1)} %constant_dynamic-update-slice_fusion.hop_one), channel_id=1, source_target_pairs={{0,64},{1,449},{64,128},{65,1},{128,192},{129,65},{192,256},{193,1... | collective-permute-start | bytes 2359304 | tf_op jit(solution)/shard_map/ppermute | solution.py:44
  41.4 1.9 %collective-permute-start.9 = (bf16[2,128,768]{2,1,0:T(8,128)(2,1)S(1)}, bf16[2,128,768]{2,1,0:T(8,128)(2,1)S(1)}, u32[]{:S(2)}, u32[]{:S(2)}) collective-permute-start(bf16[2,128,768]{2,1,0:T(8,128)(2,1)S(1)} %pad_maximum_fusion.1.local_pair), channel_id=1, source_target_pairs={{0,64},{1,449},{64,128},{65,1},{128,192},{129,65},{192,256},{193,1... | collective-permute-start | bytes 1179656 | tf_op jit(solution)/shard_map/ppermute | solution.py:44
  43.4 1.9 %collective-permute-start.10 = (bf16[2,128,768]{2,1,0:T(8,128)(2,1)S(1)}, bf16[2,128,768]{2,1,0:T(8,128)(2,1)}, u32[]{:S(2)}, u32[]{:S(2)}) collective-permute-start(bf16[2,128,768]{2,1,0:T(8,128)(2,1)S(1)} %pad_maximum_fusion.1.local_pair), channel_id=1, source_target_pairs={{0,449},{1,64},{64,1},{65,128},{128,65},{129,192},{192,129},{193,2... | collective-permute-start | bytes 1179656 | tf_op jit(solution)/shard_map/ppermute | solution.py:44
  45.3 2.3 %features.1 = (bf16[416,640]{1,0:T(8,128)(2,1)}, bf16[416,384]{1,0:T(8,128)(2,1)}) custom-call(s32[11]{0:T(128)} %stack.65.place, bf16[192,1024]{1,0:T(8,128)(2,1)} %get-tuple-element.43.kept, bf16[192,1024]{1,0:T(8,128)(2,1)} %copy-done.15, f32[1,3072]{1,0:T(1,128)} %gate.1), custom_call_target="tpu_custom_call" | custom-call | tf_op jit(solution)/shard_map/features/pallas_call | solution.py:101
  47.6 11.1 %collective-permute-done.9 = bf16[2,128,768]{2,1,0:T(8,128)(2,1)S(1)} collective-permute-done((bf16[2,128,768]{2,1,0:T(8,128)(2,1)S(1)}, bf16[2,128,768]{2,1,0:T(8,128)(2,1)S(1)}, u32[]{:S(2)}, u32[]{:S(2)}) %collective-permute-start.9) | collective-permute-done | bytes 393248 | tf_op jit(solution)/shard_map/ppermute | solution.py:44
  59.8 5.0 %collective-permute-start.12 = (bf16[4,128,768]{2,1,0:T(8,128)(2,1)S(1)}, bf16[4,128,768]{2,1,0:T(8,128)(2,1)S(1)}, u32[]{:S(2)}, u32[]{:S(2)}) collective-permute-start(bf16[4,128,768]{2,1,0:T(8,128)(2,1)S(1)} %constant_dynamic-update-slice_fusion.2.hop_one), channel_id=1, source_target_pairs={{0,64},{1,449},{64,128},{65,1},{128,192},{129,65},{192,256},{193,1... | collective-permute-start | bytes 2359304 | tf_op jit(solution)/shard_map/ppermute | solution.py:44
  64.9 1.9 %collective-permute-start.11 = (bf16[4,128,768]{2,1,0:T(8,128)(2,1)S(1)}, bf16[4,128,768]{2,1,0:T(8,128)(2,1)S(1)}, u32[]{:S(2)}, u32[]{:S(2)}) collective-permute-start(bf16[4,128,768]{2,1,0:T(8,128)(2,1)S(1)} %collective-permute-done.7.hop_two), channel_id=1, source_target_pairs={{0,64},{1,449},{64,128},{65,1},{128,192},{129,65},{192,256},{193,1... | collective-permute-start | bytes 2359304 | tf_op jit(solution)/shard_map/ppermute | solution.py:44
  69.6 4.2 %collective-permute-done.12.hop_two = bf16[4,128,768]{2,1,0:T(8,128)(2,1)S(1)} collective-permute-done((bf16[4,128,768]{2,1,0:T(8,128)(2,1)S(1)}, bf16[4,128,768]{2,1,0:T(8,128)(2,1)S(1)}, u32[]{:S(2)}, u32[]{:S(2)}) %collective-permute-start.12) | collective-permute-done | bytes 786464 | tf_op jit(solution)/shard_map/ppermute | solution.py:44
  73.8 8.4 %collective-permute-done.11.hop_three = bf16[4,128,768]{2,1,0:T(8,128)(2,1)S(1)} collective-permute-done((bf16[4,128,768]{2,1,0:T(8,128)(2,1)S(1)}, bf16[4,128,768]{2,1,0:T(8,128)(2,1)S(1)}, u32[]{:S(2)}, u32[]{:S(2)}) %collective-permute-start.11) | collective-permute-done | bytes 786464 | tf_op jit(solution)/shard_map/ppermute | solution.py:44
  82.2 5.0 %collective-permute-start.14 = (bf16[4,128,768]{2,1,0:T(8,128)(2,1)S(1)}, bf16[4,128,768]{2,1,0:T(8,128)(2,1)S(1)}, u32[]{:S(2)}, u32[]{:S(2)}) collective-permute-start(bf16[4,128,768]{2,1,0:T(8,128)(2,1)S(1)} %collective-permute-done.12.hop_two), channel_id=1, source_target_pairs={{0,64},{1,449},{64,128},{65,1},{128,192},{129,65},{192,256},{193,1... | collective-permute-start | bytes 2359304 | tf_op jit(solution)/shard_map/ppermute | solution.py:44
  87.3 5.6 %collective-permute-start.5 = (bf16[416,384]{1,0:T(8,128)(2,1)S(1)}, bf16[416,384]{1,0:T(8,128)(2,1)S(1)}, u32[]{:S(2)}, u32[]{:S(2)}) collective-permute-start(bf16[416,384]{1,0:T(8,128)(2,1)S(1)} %copy-done.18), channel_id=1, source_target_pairs={{0,9},{1,8},{8,1},{9,0},{2,11},{3,10},{10,3},{11,2},{4,13},{5,12},... | collective-permute-start | bytes 958472 | tf_op jit(solution)/shard_map/ppermute | solution.py:263
  92.9 4.9 %collective-permute-start.13 = (bf16[2,128,768]{2,1,0:T(8,128)(2,1)S(1)}, bf16[2,128,768]{2,1,0:T(8,128)(2,1)S(1)}, u32[]{:S(2)}, u32[]{:S(2)}) collective-permute-start(bf16[2,128,768]{2,1,0:T(8,128)(2,1)S(1)} %slice.6), channel_id=1, source_target_pairs={{0,64},{1,449},{64,128},{65,1},{128,192},{129,65},{192,256},{193,1... | collective-permute-start | bytes 1179656 | tf_op jit(solution)/shard_map/ppermute | solution.py:44
  97.8 2.6 %collective-permute-done.5.att_across = bf16[416,384]{1,0:T(8,128)(2,1)S(1)} collective-permute-done((bf16[416,384]{1,0:T(8,128)(2,1)S(1)}, bf16[416,384]{1,0:T(8,128)(2,1)S(1)}, u32[]{:S(2)}, u32[]{:S(2)}) %collective-permute-start.5) | collective-permute-done | bytes 319520 | tf_op jit(solution)/shard_map/ppermute | solution.py:263
  100.4 3.2 %collective-permute-start.6 = (bf16[416,384]{1,0:T(8,128)(2,1)S(1)}, bf16[416,384]{1,0:T(8,128)(2,1)S(1)}, u32[]{:S(2)}, u32[]{:S(2)}) collective-permute-start(bf16[416,384]{1,0:T(8,128)(2,1)S(1)} %copy-done.18), channel_id=1, source_target_pairs={{0,1},{1,0},{2,3},{3,2},{4,5},{5,4},{6,7},{7,6},{8,9},{9,8},{10,11... | collective-permute-start | bytes 958472 | tf_op jit(solution)/shard_map/ppermute | solution.py:264
  105.9 3.7 %product.2 = (f32[8,2,72,128]{3,2,1,0:T(8,128)S(1)}, f32[8,2,72,128]{3,2,1,0:T(8,128)S(1)}) custom-call(s32[11]{0:T(128)S(1)} %copy-done.13, bf16[416,640]{1,0:T(8,128)(2,1)S(1)} %copy-done, bf16[416,640]{1,0:T(8,128)(2,1)S(1)} %collective-permute-done.4.att_beside, bf16[416,384]{1,0:T(8,128)(2,1)S(1)} %collective-permute-done.6.att_cross, ...), custom_call_target="tpu_custom_call" | custom-call | flops 1207959552 | bytes 8388608 | tf_op jit(solution)/shard_map/product/pallas_call | solution.py:175
  109.7 5.1 %collective-permute-start.15 = (f32[8,2,72,128]{3,2,1,0:T(8,128)S(1)}, f32[8,2,72,128]{3,2,1,0:T(8,128)S(1)}, u32[]{:S(2)}, u32[]{:S(2)}) collective-permute-start(f32[8,2,72,128]{3,2,1,0:T(8,128)S(1)} %get-tuple-element.39), channel_id=1, source_target_pairs={{0,1},{1,0},{2,3},{3,2},{4,5},{5,4},{6,7},{7,6},{8,9},{9,8},{10,11... | collective-permute-start | bytes 1769480 | tf_op jit(solution)/shard_map/ppermute | solution.py:281
  115.6 1.9 %collective-permute-start.16 = (bf16[2,128,768]{2,1,0:T(8,128)(2,1)}, bf16[2,128,768]{2,1,0:T(8,128)(2,1)}, u32[]{:S(2)}, u32[]{:S(2)}) collective-permute-start(bf16[2,128,768]{2,1,0:T(8,128)(2,1)} %slice.8), channel_id=1, source_target_pairs={{0,64},{1,449},{64,128},{65,1},{128,192},{129,65},{192,256},{193,1... | collective-permute-start | bytes 1179656 | tf_op jit(solution)/shard_map/ppermute | solution.py:44
  118.5 4.6 %all-to-all-start = ((f32[8,2,72,128]{3,2,1,0:T(8,128)}), f32[8,2,72,128]{3,2,1,0:T(8,128)}, u32[]{:S(2)}, u32[]{:S(2)}) async-start(f32[8,2,72,128]{3,2,1,0:T(8,128)} %add.46), calls=%async_computation | async-start | bytes 1179648 | tf_op jit(solution)/shard_map/all_to_all | solution.py:282
  126.9 4.1 %product.3 = (f32[8,2,72,128]{3,2,1,0:T(8,128)S(1)}, f32[8,2,72,128]{3,2,1,0:T(8,128)S(1)}) custom-call(s32[11]{0:T(128)S(1)} %copy-done.13, bf16[416,640]{1,0:T(8,128)(2,1)S(1)} %copy-done, bf16[416,640]{1,0:T(8,128)(2,1)S(1)} %collective-permute-done.4.att_beside, bf16[416,384]{1,0:T(8,128)(2,1)S(1)} %copy-done.8, bf16[416,384]{1,0:T(8,128)(2,1)S(1)} %copy-done.6, ...), custom_call_target="tpu_custom_call" | custom-call | flops 1207959552 | bytes 8388608 | tf_op jit(solution)/shard_map/product/pallas_call | solution.py:175
  130.9 3.9 %collective-permute-start.17 = (f32[8,2,72,128]{3,2,1,0:T(8,128)S(1)}, f32[8,2,72,128]{3,2,1,0:T(8,128)S(1)}, u32[]{:S(2)}, u32[]{:S(2)}) collective-permute-start(f32[8,2,72,128]{3,2,1,0:T(8,128)S(1)} %get-tuple-element.41), channel_id=1, source_target_pairs={{0,1},{1,0},{2,3},{3,2},{4,5},{5,4},{6,7},{7,6},{8,9},{9,8},{10,11... | collective-permute-start | bytes 1769480 | tf_op jit(solution)/shard_map/ppermute | solution.py:281
  137.4 5.4 %all-to-all-done = f32[8,2,72,128]{3,2,1,0:T(8,128)} async-done(((f32[8,2,72,128]{3,2,1,0:T(8,128)}), f32[8,2,72,128]{3,2,1,0:T(8,128)}, u32[]{:S(2)}, u32[]{:S(2)}) %all-to-all-start) | async-done | bytes 589856 | tf_op jit(solution)/shard_map/all_to_all | solution.py:282
  142.7 3.5 %all-to-all-start.1 = ((f32[8,2,72,128]{3,2,1,0:T(8,128)}), f32[8,2,72,128]{3,2,1,0:T(8,128)S(1)}, u32[]{:S(2)}, u32[]{:S(2)}) async-start(f32[8,2,72,128]{3,2,1,0:T(8,128)} %add.47), calls=%async_computation.1 | async-start | bytes 1179648 | tf_op jit(solution)/shard_map/all_to_all | solution.py:282
  147.4 18.2 %all-to-all-done.1 = f32[8,2,72,128]{3,2,1,0:T(8,128)S(1)} async-done(((f32[8,2,72,128]{3,2,1,0:T(8,128)}), f32[8,2,72,128]{3,2,1,0:T(8,128)S(1)}, u32[]{:S(2)}, u32[]{:S(2)}) %all-to-all-start.1) | async-done | bytes 589856 | tf_op jit(solution)/shard_map/all_to_all | solution.py:282
  165.7 20.3 %all_to_all.15.parts = f32[4,72,128]{2,1,0:T(8,128)} all-to-all(f32[4,72,128]{2,1,0:T(8,128)S(1)} %pad_maximum_fusion.2), channel_id=1, replica_groups=mesh['yh'=2,'x'=8,'zh'=4,'zl'=2,'yl'=4,'c'=2] {'zh'}, dimensions={0} | all-to-all | bytes 294912 | tf_op jit(solution)/shard_map/all_to_all | solution.py:283
  186.0 3.2 %update.1 = (f32[48,192]{1,0:T(8,128)}, f32[48,192]{1,0:T(8,128)}, f32[48,192]{1,0:T(8,128)}, f32[48,192]{1,0:T(8,128)}, f32[48,48]{1,0:T(8,128)}, /*index=5*/f32[192,192]{1,0:T(8,128)}) custom-call(f32[4,72,128]{2,1,0:T(8,128)} %all_to_all.15.parts, f32[48,192]{1,0:T(8,128)} %weight.1, f32[48,192]{1,0:T(8,128)} %exp_avg.1, f32[48,192]{1,0:T(8,128)} %exp_avg_sq.1, ...), custom_call_target="tpu_custom_call" | custom-call | tf_op jit(solution)/shard_map/update/pallas_call | solution.py:286
  (69 shorter events, 19.0 us)
Async XLA Ops:
  0.6 8.5 %copy-start.14 = (bf16[2048,192]{0,1:T(8,128)(2,1)S(1)}, bf16[2048,192]{0,1:T(8,128)(2,1)}, u32[]{:S(2)}) copy-start(bf16[2048,192]{0,1:T(8,128)(2,1)} %param.10) | copy-start | bytes 2359300
  3.3 14.5 %collective-permute-start.1 = (bf16[128,768]{1,0:T(8,128)(2,1)}, bf16[128,768]{1,0:T(8,128)(2,1)S(1)}, u32[]{:S(2)}, u32[]{:S(2)}) collective-permute-start(bf16[128,768]{1,0:T(8,128)(2,1)} %get-tuple-element.25), channel_id=1, source_target_pairs={{0,8},{8,0},{1,9},{9,1},{2,10},{10,2},{3,11},{11,3},{4,12},{12,4},... | collective-permute-start | bytes 589832 | tf_op jit(solution)/shard_map/ppermute | solution.py:256
  9.1 8.8 %copy-start.17 = (bf16[128,768]{1,0:T(8,128)(2,1)S(1)}, bf16[128,768]{1,0:T(8,128)(2,1)}, u32[]{:S(2)}) copy-start(bf16[128,768]{1,0:T(8,128)(2,1)} %get-tuple-element.24) | copy-start | bytes 589828
  9.9 19.1 %collective-permute-start = (bf16[192,1024]{1,0:T(8,128)(2,1)S(1)}, bf16[192,1024]{1,0:T(8,128)(2,1)S(1)}, u32[]{:S(2)}, u32[]{:S(2)}) collective-permute-start(bf16[192,1024]{1,0:T(8,128)(2,1)S(1)} %get-tuple-element.42), channel_id=1, source_target_pairs={{0,512},{512,0},{1,513},{513,1},{2,514},{514,2},{3,515},{515,3},{4... | collective-permute-start | bytes 1179656 | tf_op jit(solution)/shard_map/ppermute | solution.py:253
  17.9 7.9 %copy-start.19 = (bf16[128,768]{1,0:T(8,128)(2,1)S(1)}, bf16[128,768]{1,0:T(8,128)(2,1)}, u32[]{:S(2)}) copy-start(bf16[128,768]{1,0:T(8,128)(2,1)} %get-tuple-element.32) | copy-start | bytes 589828
  17.9 11.2 %copy-start.1 = (bf16[2,128,768]{2,1,0:T(8,128)(2,1)}, bf16[2,128,768]{2,1,0:T(8,128)(2,1)S(1)}, u32[]{:S(2)}) copy-start(bf16[2,128,768]{2,1,0:T(8,128)(2,1)S(1)} %pad_maximum_fusion.local_pair) | copy-start | bytes 1179652
  17.9 11.1 %collective-permute-start.2 = (bf16[2,128,768]{2,1,0:T(8,128)(2,1)S(1)}, bf16[2,128,768]{2,1,0:T(8,128)(2,1)S(1)}, u32[]{:S(2)}, u32[]{:S(2)}) collective-permute-start(bf16[2,128,768]{2,1,0:T(8,128)(2,1)S(1)} %pad_maximum_fusion.local_pair), channel_id=1, source_target_pairs={{0,64},{1,449},{64,128},{65,1},{128,192},{129,65},{192,256},{193,1... | collective-permute-start | bytes 1179656 | tf_op jit(solution)/shard_map/ppermute | solution.py:44
  22.6 10.1 %collective-permute-start.3 = (bf16[2,128,768]{2,1,0:T(8,128)(2,1)S(1)}, bf16[2,128,768]{2,1,0:T(8,128)(2,1)S(1)}, u32[]{:S(2)}, u32[]{:S(2)}) collective-permute-start(bf16[2,128,768]{2,1,0:T(8,128)(2,1)S(1)} %pad_maximum_fusion.local_pair), channel_id=1, source_target_pairs={{0,449},{1,64},{64,1},{65,128},{128,65},{129,192},{192,129},{193,2... | collective-permute-start | bytes 1179656 | tf_op jit(solution)/shard_map/ppermute | solution.py:44
  25.7 15.6 %collective-permute-start.8 = (bf16[128,768]{1,0:T(8,128)(2,1)S(1)}, bf16[128,768]{1,0:T(8,128)(2,1)S(1)}, u32[]{:S(2)}, u32[]{:S(2)}) collective-permute-start(bf16[128,768]{1,0:T(8,128)(2,1)S(1)} %copy-done.19), channel_id=1, source_target_pairs={{0,8},{8,0},{1,9},{9,1},{2,10},{10,2},{3,11},{11,3},{4,12},{12,4},... | collective-permute-start | bytes 589832 | tf_op jit(solution)/shard_map/ppermute | solution.py:257
  29.8 11.6 %copy-start.16 = (bf16[128,768]{1,0:T(8,128)(2,1)S(1)}, bf16[128,768]{1,0:T(8,128)(2,1)}, u32[]{:S(2)}) copy-start(bf16[128,768]{1,0:T(8,128)(2,1)} %get-tuple-element.31) | copy-start | bytes 589828
  32.7 32.1 %collective-permute-start.7 = (bf16[4,128,768]{2,1,0:T(8,128)(2,1)S(1)}, bf16[4,128,768]{2,1,0:T(8,128)(2,1)S(1)}, u32[]{:S(2)}, u32[]{:S(2)}) collective-permute-start(bf16[4,128,768]{2,1,0:T(8,128)(2,1)S(1)} %constant_dynamic-update-slice_fusion.hop_one), channel_id=1, source_target_pairs={{0,64},{1,449},{64,128},{65,1},{128,192},{129,65},{192,256},{193,1... | collective-permute-start | bytes 2359304 | tf_op jit(solution)/shard_map/ppermute | solution.py:44
  41.4 17.3 %collective-permute-start.9 = (bf16[2,128,768]{2,1,0:T(8,128)(2,1)S(1)}, bf16[2,128,768]{2,1,0:T(8,128)(2,1)S(1)}, u32[]{:S(2)}, u32[]{:S(2)}) collective-permute-start(bf16[2,128,768]{2,1,0:T(8,128)(2,1)S(1)} %pad_maximum_fusion.1.local_pair), channel_id=1, source_target_pairs={{0,64},{1,449},{64,128},{65,1},{128,192},{129,65},{192,256},{193,1... | collective-permute-start | bytes 1179656 | tf_op jit(solution)/shard_map/ppermute | solution.py:44
  43.4 15.4 %collective-permute-start.10 = (bf16[2,128,768]{2,1,0:T(8,128)(2,1)S(1)}, bf16[2,128,768]{2,1,0:T(8,128)(2,1)}, u32[]{:S(2)}, u32[]{:S(2)}) collective-permute-start(bf16[2,128,768]{2,1,0:T(8,128)(2,1)S(1)} %pad_maximum_fusion.1.local_pair), channel_id=1, source_target_pairs={{0,449},{1,64},{64,1},{65,128},{128,65},{129,192},{192,129},{193,2... | collective-permute-start | bytes 1179656 | tf_op jit(solution)/shard_map/ppermute | solution.py:44
  58.7 28.5 %copy-start.18 = (bf16[416,384]{1,0:T(8,128)(2,1)S(1)}, bf16[416,384]{1,0:T(8,128)(2,1)}, u32[]{:S(2)}) copy-start(bf16[416,384]{1,0:T(8,128)(2,1)} %get-tuple-element.30) | copy-start | bytes 958468
  58.7 9.0 %copy-start = (bf16[416,640]{1,0:T(8,128)(2,1)S(1)}, bf16[416,640]{1,0:T(8,128)(2,1)}, u32[]{:S(2)}) copy-start(bf16[416,640]{1,0:T(8,128)(2,1)} %get-tuple-element.28.att_own) | copy-start | bytes 1597444
  59.8 13.9 %collective-permute-start.12 = (bf16[4,128,768]{2,1,0:T(8,128)(2,1)S(1)}, bf16[4,128,768]{2,1,0:T(8,128)(2,1)S(1)}, u32[]{:S(2)}, u32[]{:S(2)}) collective-permute-start(bf16[4,128,768]{2,1,0:T(8,128)(2,1)S(1)} %constant_dynamic-update-slice_fusion.2.hop_one), channel_id=1, source_target_pairs={{0,64},{1,449},{64,128},{65,1},{128,192},{129,65},{192,256},{193,1... | collective-permute-start | bytes 2359304 | tf_op jit(solution)/shard_map/ppermute | solution.py:44
  64.9 17.3 %collective-permute-start.11 = (bf16[4,128,768]{2,1,0:T(8,128)(2,1)S(1)}, bf16[4,128,768]{2,1,0:T(8,128)(2,1)S(1)}, u32[]{:S(2)}, u32[]{:S(2)}) collective-permute-start(bf16[4,128,768]{2,1,0:T(8,128)(2,1)S(1)} %collective-permute-done.7.hop_two), channel_id=1, source_target_pairs={{0,64},{1,449},{64,128},{65,1},{128,192},{129,65},{192,256},{193,1... | collective-permute-start | bytes 2359304 | tf_op jit(solution)/shard_map/ppermute | solution.py:44
  67.7 32.7 %collective-permute-start.4 = (bf16[416,640]{1,0:T(8,128)(2,1)S(1)}, bf16[416,640]{1,0:T(8,128)(2,1)S(1)}, u32[]{:S(2)}, u32[]{:S(2)}) collective-permute-start(bf16[416,640]{1,0:T(8,128)(2,1)S(1)} %copy-done), channel_id=1, source_target_pairs={{0,8},{8,0},{1,9},{9,1},{2,10},{10,2},{3,11},{11,3},{4,12},{12,4},... | collective-permute-start | bytes 1597448 | tf_op jit(solution)/shard_map/ppermute | solution.py:262
  73.8 29.8 %copy-start.11 = (bf16[4,128,768]{2,1,0:T(8,128)(2,1)}, bf16[4,128,768]{2,1,0:T(8,128)(2,1)S(1)}, u32[]{:S(2)}) copy-start(bf16[4,128,768]{2,1,0:T(8,128)(2,1)S(1)} %collective-permute-done.12.hop_two) | copy-start | bytes 2359300
  82.2 21.4 %collective-permute-start.14 = (bf16[4,128,768]{2,1,0:T(8,128)(2,1)S(1)}, bf16[4,128,768]{2,1,0:T(8,128)(2,1)S(1)}, u32[]{:S(2)}, u32[]{:S(2)}) collective-permute-start(bf16[4,128,768]{2,1,0:T(8,128)(2,1)S(1)} %collective-permute-done.12.hop_two), channel_id=1, source_target_pairs={{0,64},{1,449},{64,128},{65,1},{128,192},{129,65},{192,256},{193,1... | collective-permute-start | bytes 2359304 | tf_op jit(solution)/shard_map/ppermute | solution.py:44
  87.2 17.6 %copy-start.2 = (bf16[2,128,768]{2,1,0:T(8,128)(2,1)S(1)}, bf16[2,128,768]{2,1,0:T(8,128)(2,1)}, u32[]{:S(2)}) copy-start(bf16[2,128,768]{2,1,0:T(8,128)(2,1)} %copy-done.1) | copy-start | bytes 1179652
  87.3 17.5 %copy-start.13 = (s32[11]{0:T(128)S(1)}, s32[11]{0:T(128)}, u32[]{:S(2)}) copy-start(s32[11]{0:T(128)} %stack.65.place) | copy-start | bytes 136
  87.3 13.1 %collective-permute-start.5 = (bf16[416,384]{1,0:T(8,128)(2,1)S(1)}, bf16[416,384]{1,0:T(8,128)(2,1)S(1)}, u32[]{:S(2)}, u32[]{:S(2)}) collective-permute-start(bf16[416,384]{1,0:T(8,128)(2,1)S(1)} %copy-done.18), channel_id=1, source_target_pairs={{0,9},{1,8},{8,1},{9,0},{2,11},{3,10},{10,3},{11,2},{4,13},{5,12},... | collective-permute-start | bytes 958472 | tf_op jit(solution)/shard_map/ppermute | solution.py:263
  92.9 10.6 %collective-permute-start.13 = (bf16[2,128,768]{2,1,0:T(8,128)(2,1)S(1)}, bf16[2,128,768]{2,1,0:T(8,128)(2,1)S(1)}, u32[]{:S(2)}, u32[]{:S(2)}) collective-permute-start(bf16[2,128,768]{2,1,0:T(8,128)(2,1)S(1)} %slice.6), channel_id=1, source_target_pairs={{0,64},{1,449},{64,128},{65,1},{128,192},{129,65},{192,256},{193,1... | collective-permute-start | bytes 1179656 | tf_op jit(solution)/shard_map/ppermute | solution.py:44
  100.4 9.3 %copy-start.5 = (bf16[416,384]{1,0:T(8,128)(2,1)}, bf16[416,384]{1,0:T(8,128)(2,1)S(1)}, u32[]{:S(2)}) copy-start(bf16[416,384]{1,0:T(8,128)(2,1)S(1)} %collective-permute-done.5.att_across) | copy-start | bytes 958468
  100.4 4.4 %collective-permute-start.6 = (bf16[416,384]{1,0:T(8,128)(2,1)S(1)}, bf16[416,384]{1,0:T(8,128)(2,1)S(1)}, u32[]{:S(2)}, u32[]{:S(2)}) collective-permute-start(bf16[416,384]{1,0:T(8,128)(2,1)S(1)} %copy-done.18), channel_id=1, source_target_pairs={{0,1},{1,0},{2,3},{3,2},{4,5},{5,4},{6,7},{7,6},{8,9},{9,8},{10,11... | collective-permute-start | bytes 958472 | tf_op jit(solution)/shard_map/ppermute | solution.py:264
  109.7 7.9 %collective-permute-start.15 = (f32[8,2,72,128]{3,2,1,0:T(8,128)S(1)}, f32[8,2,72,128]{3,2,1,0:T(8,128)S(1)}, u32[]{:S(2)}, u32[]{:S(2)}) collective-permute-start(f32[8,2,72,128]{3,2,1,0:T(8,128)S(1)} %get-tuple-element.39), channel_id=1, source_target_pairs={{0,1},{1,0},{2,3},{3,2},{4,5},{5,4},{6,7},{7,6},{8,9},{9,8},{10,11... | collective-permute-start | bytes 1769480 | tf_op jit(solution)/shard_map/ppermute | solution.py:281
  115.6 9.1 %collective-permute-start.16 = (bf16[2,128,768]{2,1,0:T(8,128)(2,1)}, bf16[2,128,768]{2,1,0:T(8,128)(2,1)}, u32[]{:S(2)}, u32[]{:S(2)}) collective-permute-start(bf16[2,128,768]{2,1,0:T(8,128)(2,1)} %slice.8), channel_id=1, source_target_pairs={{0,64},{1,449},{64,128},{65,1},{128,192},{129,65},{192,256},{193,1... | collective-permute-start | bytes 1179656 | tf_op jit(solution)/shard_map/ppermute | solution.py:44
  118.5 6.3 %copy-start.6 = (bf16[416,384]{1,0:T(8,128)(2,1)S(1)}, bf16[416,384]{1,0:T(8,128)(2,1)}, u32[]{:S(2)}) copy-start(bf16[416,384]{1,0:T(8,128)(2,1)} %copy-done.5) | copy-start | bytes 958468
  118.5 24.3 %all-to-all-start = ((f32[8,2,72,128]{3,2,1,0:T(8,128)}), f32[8,2,72,128]{3,2,1,0:T(8,128)}, u32[]{:S(2)}, u32[]{:S(2)}) async-start(f32[8,2,72,128]{3,2,1,0:T(8,128)} %add.46), calls=%async_computation | async-start | bytes 1179648 | tf_op jit(solution)/shard_map/all_to_all | solution.py:282
  130.9 5.6 %collective-permute-start.17 = (f32[8,2,72,128]{3,2,1,0:T(8,128)S(1)}, f32[8,2,72,128]{3,2,1,0:T(8,128)S(1)}, u32[]{:S(2)}, u32[]{:S(2)}) collective-permute-start(f32[8,2,72,128]{3,2,1,0:T(8,128)S(1)} %get-tuple-element.41), channel_id=1, source_target_pairs={{0,1},{1,0},{2,3},{3,2},{4,5},{5,4},{6,7},{7,6},{8,9},{9,8},{10,11... | collective-permute-start | bytes 1769480 | tf_op jit(solution)/shard_map/ppermute | solution.py:281
  142.7 22.9 %all-to-all-start.1 = ((f32[8,2,72,128]{3,2,1,0:T(8,128)}), f32[8,2,72,128]{3,2,1,0:T(8,128)S(1)}, u32[]{:S(2)}, u32[]{:S(2)}) async-start(f32[8,2,72,128]{3,2,1,0:T(8,128)} %add.47), calls=%async_computation.1 | async-start | bytes 1179648 | tf_op jit(solution)/shard_map/all_to_all | solution.py:282
  (8 other events, 21.0 us)

commit v8 on v6

--- a/solution.py
+++ b/solution.py
@@ -71,17 +71,13 @@
     )(place, cotangent)
 
 
-def features_kernel(place, kept, came, gate, own, cross):
+def features_kernel(place, kept, came, gate, out):
     for top, bottom, yh in ((kept, came, 0), (came, kept, 1)):
 
         @pl.when(place[9] == yh)
         def _():
-            for ref, hops, sign in ((own, range(5), 1), (cross, range(1, 4), -1)):
-                for at, count in enumerate(hops):
-                    start = pl.multiple_of(place[1 + (sign * count) % NX] * CHUNK, CHUNK)
-                    here = slice(at * CHUNK, (at + 1) * CHUNK)
-                    ref[:HB, here] = top[:, pl.ds(start, CHUNK)]
-                    ref[HB:FEAT, here] = bottom[:, pl.ds(start, CHUNK)]
+            out[:HB] = top[...]
+            out[HB:FEAT] = bottom[...]
 
     rest = jnp.concatenate([gate[:, z * GROUP : (z + 1) * GROUP] for z in range(8)], axis=0)
     rows = []
@@ -89,24 +85,18 @@
         part = rest.astype(jnp.bfloat16)
         rest = rest - part.astype(jnp.float32)
         rows.append(part)
-    rows = jnp.concatenate(rows + [jnp.zeros_like(rows[0])], axis=0)
-    for ref in (own, cross):
-        ref[FEAT:, :GROUP] = rows
-        if ref.shape[1] > GROUP:
-            ref[FEAT:, GROUP:] = jnp.zeros((32, ref.shape[1] - GROUP), jnp.bfloat16)
+    out[FEAT:, :GROUP] = jnp.concatenate(rows + [jnp.zeros_like(rows[0])], axis=0)
+    out[FEAT:, GROUP:] = jnp.zeros((32, TOK - GROUP), jnp.bfloat16)
 
 
 def features_of(place, kept, came, gate):
-    def shape(hops):
-        return jax.ShapeDtypeStruct((FEAT + 32, hops * CHUNK), jnp.bfloat16)
-
     def whole(array):
         return pl.BlockSpec(array.shape, lambda: (0, 0))
 
     return pl.pallas_call(
         features_kernel,
         in_specs=[pl.BlockSpec(memory_space=pltpu.SMEM), whole(kept), whole(came), whole(gate)],
-        out_shape=[shape(5), shape(3)],
+        out_shape=jax.ShapeDtypeStruct((FEAT + 32, TOK), jnp.bfloat16),
         name="features",
     )(place, kept, came, gate)
 
@@ -114,10 +104,7 @@
 def product_kernel(
     piece,
     place,
-    att_own,
-    att_beside,
-    att_cross,
-    att_across,
+    atts,
     own,
     beside,
     hop_one,
@@ -129,22 +116,31 @@
 ):
     group = 2 * (2 * piece + pl.program_id(0)) + place[10]
 
+    def att(clip, *hops):
+        parts = []
+        for at in hops:
+            columns = pl.ds(pl.multiple_of(place[1 + at] * CHUNK, CHUNK), CHUNK)
+            parts.append(atts[clip, :FEAT, columns])
+        return parts[0] if len(parts) == 1 else jnp.concatenate(parts, axis=1)
+
     def dot(left, *blocks):
         right = blocks[0] if len(blocks) == 1 else jnp.concatenate(blocks, axis=0)
         return jnp.dot(left, right, preferred_element_type=jnp.float32)
 
     total = jnp.zeros((FEAT, GROUP), jnp.float32)
-    for which, att in enumerate((att_own, att_beside, att_cross, att_across)):
+    for which in range(4):
+        z = place[10] if which % 2 == 0 else 1 - place[10]
+        at = 2 * z + (place[0] if which < 2 else 1 - place[0])
         one, two, three = hop_one[which], hop_two[which], hop_three[which]
         if which < 2:
             near = (own, beside)[which][0]
-            clip = dot(att[:FEAT, : 2 * CHUNK], near, one)
-            clip += dot(att[:FEAT, 2 * CHUNK : 4 * CHUNK], two, three)
-            clip += dot(att[:FEAT, 4 * CHUNK :], last[which])
+            clip = dot(att(at, 0, 1), near, one)
+            clip += dot(att(at, 2, 3), two, three)
+            clip += dot(att(at, 4), last[which])
         else:
-            clip = dot(att[:FEAT, : 2 * CHUNK], one, two)
-            clip += dot(att[:FEAT, 2 * CHUNK :], three)
-        parts = att[FEAT:, :GROUP].astype(jnp.float32)
+            clip = dot(att(at, 1, 2), one, two)
+            clip += dot(att(at, 3), three)
+        parts = atts[at, FEAT:, :GROUP].astype(jnp.float32)
         rows = lax.broadcasted_iota(jnp.int32, parts.shape, 0)
         mine = (rows & 7 == group) & (rows < 24)
         gate = jnp.sum(jnp.where(mine, parts, 0.0), axis=0, keepdims=True)
@@ -173,7 +169,7 @@
 
 def product(piece, place, atts, own, beside, blocks):
     count = blocks[0].shape[2] // GROUP
-    attn = [pl.BlockSpec(att.shape, lambda z: (0, 0)) for att in atts]
+    attn = pl.BlockSpec(atts.shape, lambda z: (0, 0, 0))
     near = pl.BlockSpec((1, CHUNK, GROUP), lambda z: (piece, 0, z))
     four = pl.BlockSpec((4, CHUNK, GROUP), lambda z: (0, 0, z))
     pair = pl.BlockSpec((2, CHUNK, GROUP), lambda z: (0, 0, z))
@@ -183,15 +179,14 @@
     return pl.pallas_call(
         functools.partial(product_kernel, piece),
         grid=(count,),
-        in_specs=[pl.BlockSpec(memory_space=pltpu.SMEM)]
-        + attn
+        in_specs=[pl.BlockSpec(memory_space=pltpu.SMEM), attn]
         + [near, near, four, four, four, pair],
         out_specs=[out, out],
         out_shape=[shape, shape],
         cost_estimate=pl.CostEstimate(flops=flops, bytes_accessed=8 << 20, transcendentals=0),
         compiler_params=pltpu.CompilerParams(vmem_limit_bytes=32 << 20),
         name="product",
-    )(place, *atts, own, beside, *blocks)
+    )(place, atts, own, beside, *blocks)
 
 
 def update_kernel(
@@ -262,25 +257,21 @@
 
     mine, other = split(place, cotangent)
     parts = [hop(mine), hop(other, 1, 0), hop(mine, 0, 1), hop(other, 1, 1)]
+    swapped = after(came, *parts)
     parts = [after(part, came) for part in parts]
     first_one = jnp.stack([part[0] for part in parts])
     first_two = jnp.stack([part[1] for part in parts])
+
+    att_own = features_of(place, kept, swapped, gate)
+    atts = lax.all_gather(att_own, ("zl", "c"))
+    beside = lax.ppermute(other, "zl", SWAP)
+
     second_one = hop(first_one)
-    second_two = hop(first_two)
-
-    att_own, att_swap = features_of(place, kept, after(came, first_two), gate)
-    atts = (
-        att_own,
-        lax.ppermute(att_own, "zl", SWAP),
-        lax.ppermute(att_swap, "c", SWAP),
-        lax.ppermute(att_swap, ("zl", "c"), [(0, 3), (1, 2), (2, 1), (3, 0)]),
-    )
-
-    beside = lax.ppermute(after(other, first_two), "zl", SWAP)
-    third_one = hop(after(second_one, first_two, att_own))
-    third_two = hop(after(second_two, third_one, atts[1]))
-    last_one = after(hop(after(third_one, second_two, beside)[:2]), third_two)
-    last_two = hop(third_two[:2])
+    second_two = hop(after(first_two, att_own))
+    third_one = hop(after(second_one, first_two))
+    third_two = hop(after(second_two, third_one))
+    last_one = after(hop(after(third_one, second_two)[:2]), third_two)
+    last_two = after(hop(after(third_two, beside)[:2]), last_one)
     rings = (
         (first_one, second_one, third_one, last_one),
         (first_two, second_two, third_two, last_two),

time: 187 us -> 219 us (1.17)
  local copies, waits for them, and re-layouts: 8.52 us -> 24.2 us
  between operations: 1 us -> 14.4 us
  waiting for transfers between devices: 61.3 us -> 74.3 us
  starting transfers between devices: 74.6 us -> 68.1 us
  blocking collectives: 20.6 us -> 17.5 us
    ppermute x10, waiting for transfers between devices: 17.2 us -> 33.7 us  [hop(): return lax.ppermute(block, ('x', 'zl', 'c'), ring(other_z, other_core))]
    unnamed x26 -> x52, local copies, waits for them, and re-layouts: 5.08 us -> 21.5 us
    ppermute x4 -> x1, starting transfers between devices: 11.4 us -> 1.91 us  [local(): beside = lax.ppermute(other, 'zl', SWAP)]
    ppermute x4 -> x1, waiting for transfers between devices: 18.2 us -> 14.8 us  [local(): beside = lax.ppermute(other, 'zl', SWAP)]
    all_to_all x1, blocking collectives: 20.6 us -> 17.5 us  [local(): parts = lax.all_to_all(jnp.concatenate(by_z, axis=0), 'zh', 0, 0)]
    ppermute x10, starting transfers between devices: 38.3 us -> 40.6 us  [hop(): return lax.ppermute(block, ('x', 'zl', 'c'), ring(other_z, other_core))]
  transfers between devices with their start and end apart: 19 -> 17, of which waited for: 11 -> 12; matrix products, arithmetic and copies ran while one was open for 2% -> 1% of each run, Pallas kernels for 5% -> 3%
where the time goes in v8:
time: 219 us; the launch traced here: 216 us
  waiting for transfers between devices  74.3 us (34%)
  starting transfers between devices  68.1 us (31%)
  local copies, waits for them, and re-layouts  24.2 us (11%)
  blocking collectives  17.5 us (8%)
  Pallas kernels  14.9 us (7%)
  between operations  14.4 us (7%)
  other arithmetic  3.09 us (1%)
    ppermute x10, starting transfers between devices, hop(): return lax.ppermute(block, ('x', 'zl', 'c'), ring(other_z, other_core))  40.6 us
    ppermute x10, waiting for transfers between devices, hop(): return lax.ppermute(block, ('x', 'zl', 'c'), ring(other_z, other_core))  33.7 us
    all_to_all x2, waiting for transfers between devices, local(): by_z.append(jnp.sum(lax.all_to_all(paired, Y, 0, 0), axis=0))  22.5 us
    unnamed x52, local copies, waits for them, and re-layouts  21.5 us
    all_to_all x1, blocking collectives, local(): parts = lax.all_to_all(jnp.concatenate(by_z, axis=0), 'zh', 0, 0)  17.5 us
    ppermute x1, waiting for transfers between devices, local(): beside = lax.ppermute(other, 'zl', SWAP)  14.8 us
    ppermute x1, starting transfers between devices, local(): came = lax.ppermute(away, 'yh', SWAP)  8.73 us
    ppermute x2, starting transfers between devices, local(): paired = keep + lax.ppermute(send, 'c', SWAP)  8.52 us
  transfers between devices with their start and end apart: 17, of which 12 were waited for; matrix products, arithmetic and copies ran while one was open for 1% of the time, Pallas kernels for 3%

profile of v8, /device:TPU:1, one launch (start us, length us, event | category | flops | bytes accessed | tf_op | source)
XLA Modules:
  0.0 216.5 jit_solution(6492775079402419811)
XLA Ops:
  7.2 1.9 dynamic-slice_bitcast_fusion
  9.1 8.7 %collective-permute-start = (bf16[192,1024]{1,0:T(8,128)(2,1)S(1)}, bf16[192,1024]{1,0:T(8,128)(2,1)S(1)}, u32[]{:S(2)}, u32[]{:S(2)}) collective-permute-start(bf16[192,1024]{1,0:T(8,128)(2,1)S(1)} %get-tuple-element.42), channel_id=1, source_target_pairs={{0,512},{512,0},{1,513},{513,1},{2,514},{514,2},{3,515},{515,3},{4... | collective-permute-start | bytes 1179656 | tf_op jit(solution)/shard_map/ppermute | solution.py:256
  18.6 2.1 split.1
  20.7 6.7 %collective-permute-start.4 = (bf16[2,128,768]{2,1,0:T(8,128)(2,1)}, bf16[2,128,768]{2,1,0:T(8,128)(2,1)S(1)}, u32[]{:S(2)}, u32[]{:S(2)}) collective-permute-start(bf16[2,128,768]{2,1,0:T(8,128)(2,1)} %get-tuple-element.25), channel_id=1, source_target_pairs={{0,457},{1,72},{8,449},{9,64},{64,9},{65,136},{72,1},{73,128},{128... | collective-permute-start | bytes 1179656 | tf_op jit(solution)/shard_map/ppermute | solution.py:49
  27.3 7.9 %collective-permute-start.2 = (bf16[2,128,768]{2,1,0:T(8,128)(2,1)}, bf16[2,128,768]{2,1,0:T(8,128)(2,1)S(1)}, u32[]{:S(2)}, u32[]{:S(2)}) collective-permute-start(bf16[2,128,768]{2,1,0:T(8,128)(2,1)} %get-tuple-element.25), channel_id=1, source_target_pairs={{0,72},{1,457},{8,64},{9,449},{64,136},{65,9},{72,128},{73,1},{128... | collective-permute-start | bytes 1179656 | tf_op jit(solution)/shard_map/ppermute | solution.py:49
  35.3 1.9 collective-permute-start.3
  37.2 1.9 collective-permute-start.1
  39.2 5.7 %collective-permute-done.2 = bf16[2,128,768]{2,1,0:T(8,128)(2,1)S(1)} collective-permute-done((bf16[2,128,768]{2,1,0:T(8,128)(2,1)}, bf16[2,128,768]{2,1,0:T(8,128)(2,1)S(1)}, u32[]{:S(2)}, u32[]{:S(2)}) %collective-permute-start.2) | collective-permute-done | bytes 393248 | tf_op jit(solution)/shard_map/ppermute | solution.py:49
  44.9 4.8 %collective-permute-done.3 = bf16[2,128,768]{2,1,0:T(8,128)(2,1)S(1)} collective-permute-done((bf16[2,128,768]{2,1,0:T(8,128)(2,1)}, bf16[2,128,768]{2,1,0:T(8,128)(2,1)S(1)}, u32[]{:S(2)}, u32[]{:S(2)}) %collective-permute-start.3) | collective-permute-done | bytes 393248 | tf_op jit(solution)/shard_map/ppermute | solution.py:49
  51.4 2.1 features.1
  53.8 3.6 %collective-permute-start.6 = (bf16[4,128,768]{2,1,0:T(8,128)(2,1)S(1)}, bf16[4,128,768]{2,1,0:T(8,128)(2,1)S(1)}, u32[]{:S(2)}, u32[]{:S(2)}) collective-permute-start(bf16[4,128,768]{2,1,0:T(8,128)(2,1)S(1)} %pad_maximum_fusion.hop_one), channel_id=1, source_target_pairs={{0,64},{1,449},{8,72},{9,457},{64,128},{65,1},{72,136},{73,9},{128... | collective-permute-start | bytes 2359304 | tf_op jit(solution)/shard_map/ppermute | solution.py:49
  58.3 4.0 %collective-permute-start.8 = (bf16[4,128,768]{2,1,0:T(8,128)(2,1)S(1)}, bf16[4,128,768]{2,1,0:T(8,128)(2,1)S(1)}, u32[]{:S(2)}, u32[]{:S(2)}) collective-permute-start(bf16[4,128,768]{2,1,0:T(8,128)(2,1)S(1)} %pad_maximum_fusion.1.hop_one), channel_id=1, source_target_pairs={{0,64},{1,449},{8,72},{9,457},{64,128},{65,1},{72,136},{73,9},{128... | collective-permute-start | bytes 2359304 | tf_op jit(solution)/shard_map/ppermute | solution.py:49
  63.2 3.6 %collective-permute-done.6.hop_two = bf16[4,128,768]{2,1,0:T(8,128)(2,1)S(1)} collective-permute-done((bf16[4,128,768]{2,1,0:T(8,128)(2,1)S(1)}, bf16[4,128,768]{2,1,0:T(8,128)(2,1)S(1)}, u32[]{:S(2)}, u32[]{:S(2)}) %collective-permute-start.6) | collective-permute-done | bytes 786464 | tf_op jit(solution)/shard_map/ppermute | solution.py:49
  66.8 4.5 %collective-permute-start.7 = (bf16[4,128,768]{2,1,0:T(8,128)(2,1)S(1)}, bf16[4,128,768]{2,1,0:T(8,128)(2,1)S(1)}, u32[]{:S(2)}, u32[]{:S(2)}) collective-permute-start(bf16[4,128,768]{2,1,0:T(8,128)(2,1)S(1)} %collective-permute-done.6.hop_two), channel_id=1, source_target_pairs={{0,64},{1,449},{8,72},{9,457},{64,128},{65,1},{72,136},{73,9},{128... | collective-permute-start | bytes 2359304 | tf_op jit(solution)/shard_map/ppermute | solution.py:49
  71.3 4.0 %collective-permute-done.8.hop_two = bf16[4,128,768]{2,1,0:T(8,128)(2,1)S(1)} collective-permute-done((bf16[4,128,768]{2,1,0:T(8,128)(2,1)S(1)}, bf16[4,128,768]{2,1,0:T(8,128)(2,1)S(1)}, u32[]{:S(2)}, u32[]{:S(2)}) %collective-permute-start.8) | collective-permute-done | bytes 786464 | tf_op jit(solution)/shard_map/ppermute | solution.py:49
  75.2 8.5 %collective-permute-done.7.hop_three = bf16[4,128,768]{2,1,0:T(8,128)(2,1)S(1)} collective-permute-done((bf16[4,128,768]{2,1,0:T(8,128)(2,1)S(1)}, bf16[4,128,768]{2,1,0:T(8,128)(2,1)S(1)}, u32[]{:S(2)}, u32[]{:S(2)}) %collective-permute-start.7) | collective-permute-done | bytes 786464 | tf_op jit(solution)/shard_map/ppermute | solution.py:49
  83.8 4.4 %collective-permute-start.10 = (bf16[4,128,768]{2,1,0:T(8,128)(2,1)S(1)}, bf16[4,128,768]{2,1,0:T(8,128)(2,1)S(1)}, u32[]{:S(2)}, u32[]{:S(2)}) collective-permute-start(bf16[4,128,768]{2,1,0:T(8,128)(2,1)S(1)} %collective-permute-done.8.hop_two), channel_id=1, source_target_pairs={{0,64},{1,449},{8,72},{9,457},{64,128},{65,1},{72,136},{73,9},{128... | collective-permute-start | bytes 2359304 | tf_op jit(solution)/shard_map/ppermute | solution.py:49
  91.9 3.2 %collective-permute-start.9 = (bf16[2,128,768]{2,1,0:T(8,128)(2,1)S(1)}, bf16[2,128,768]{2,1,0:T(8,128)(2,1)S(1)}, u32[]{:S(2)}, u32[]{:S(2)}) collective-permute-start(bf16[2,128,768]{2,1,0:T(8,128)(2,1)S(1)} %slice.38), channel_id=1, source_target_pairs={{0,64},{1,449},{8,72},{9,457},{64,128},{65,1},{72,136},{73,9},{128... | collective-permute-start | bytes 1179656 | tf_op jit(solution)/shard_map/ppermute | solution.py:49
  95.1 14.8 %collective-permute-done.5.beside = bf16[2,128,768]{2,1,0:T(8,128)(2,1)S(1)} collective-permute-done((bf16[2,128,768]{2,1,0:T(8,128)(2,1)S(1)}, bf16[2,128,768]{2,1,0:T(8,128)(2,1)S(1)}, u32[]{:S(2)}, u32[]{:S(2)}) %collective-permute-start.5) | collective-permute-done | bytes 393248 | tf_op jit(solution)/shard_map/ppermute | solution.py:267
  111.7 2.6 %collective-permute-start.12 = (bf16[2,128,768]{2,1,0:T(8,128)(2,1)S(1)}, bf16[2,128,768]{2,1,0:T(8,128)(2,1)S(1)}, u32[]{:S(2)}, u32[]{:S(2)}) collective-permute-start(bf16[2,128,768]{2,1,0:T(8,128)(2,1)S(1)} %slice.39), channel_id=1, source_target_pairs={{0,64},{1,449},{8,72},{9,457},{64,128},{65,1},{72,136},{73,9},{128... | collective-permute-start | bytes 1179656 | tf_op jit(solution)/shard_map/ppermute | solution.py:49
  115.1 5.4 %collective-permute-done.12.last = bf16[2,128,768]{2,1,0:T(8,128)(2,1)S(1)} collective-permute-done((bf16[2,128,768]{2,1,0:T(8,128)(2,1)S(1)}, bf16[2,128,768]{2,1,0:T(8,128)(2,1)S(1)}, u32[]{:S(2)}, u32[]{:S(2)}) %collective-permute-start.12) | collective-permute-done | bytes 393248 | tf_op jit(solution)/shard_map/ppermute | solution.py:49
  121.2 2.0 copy-done
  129.6 3.8 %product.3 = (f32[8,2,72,128]{3,2,1,0:T(8,128)S(1)}, f32[8,2,72,128]{3,2,1,0:T(8,128)S(1)}) custom-call(s32[11]{0:T(128)S(1)} %copy-done.23, bf16[4,416,1024]{2,1,0:T(8,128)(2,1)S(1)} %bitcast.16, bf16[2,128,768]{2,1,0:T(8,128)(2,1)S(1)} %copy-done.10, bf16[2,128,768]{2,1,0:T(8,128)(2,1)S(1)} %copy-done.13, bf16[4,128,768]{2,1,0:T(8,128)(2,1)S(1)} %copy-done.5, ...), custom_call_target="tpu_custom_call" | custom-call | flops 1207959552 | bytes 8388608 | tf_op jit(solution)/shard_map/product/pallas_call | solution.py:179
  133.4 6.0 %collective-permute-start.13 = (f32[8,2,72,128]{3,2,1,0:T(8,128)S(1)}, f32[8,2,72,128]{3,2,1,0:T(8,128)S(1)}, u32[]{:S(2)}, u32[]{:S(2)}) collective-permute-start(f32[8,2,72,128]{3,2,1,0:T(8,128)S(1)} %get-tuple-element.41), channel_id=1, source_target_pairs={{0,1},{1,0},{2,3},{3,2},{4,5},{5,4},{6,7},{7,6},{8,9},{9,8},{10,11... | collective-permute-start | bytes 1769480 | tf_op jit(solution)/shard_map/ppermute | solution.py:283
  141.9 4.7 %all-to-all-start.1 = ((f32[8,2,72,128]{3,2,1,0:T(8,128)}), f32[8,2,72,128]{3,2,1,0:T(8,128)}, u32[]{:S(2)}, u32[]{:S(2)}) async-start(f32[8,2,72,128]{3,2,1,0:T(8,128)} %add.47), calls=%async_computation.1 | async-start | bytes 1179648 | tf_op jit(solution)/shard_map/all_to_all | solution.py:284
  153.0 3.8 %product.2 = (f32[8,2,72,128]{3,2,1,0:T(8,128)S(1)}, f32[8,2,72,128]{3,2,1,0:T(8,128)S(1)}) custom-call(s32[11]{0:T(128)S(1)} %copy-done.23, bf16[4,416,1024]{2,1,0:T(8,128)(2,1)S(1)} %bitcast.17, bf16[2,128,768]{2,1,0:T(8,128)(2,1)S(1)} %copy-done.11, bf16[2,128,768]{2,1,0:T(8,128)(2,1)S(1)} %copy-done.14, bf16[4,128,768]{2,1,0:T(8,128)(2,1)S(1)} %copy-done.3, ...), custom_call_target="tpu_custom_call" | custom-call | flops 1207959552 | bytes 8388608 | tf_op jit(solution)/shard_map/product/pallas_call | solution.py:179
  156.7 2.5 %collective-permute-start.11 = (f32[8,2,72,128]{3,2,1,0:T(8,128)S(1)}, f32[8,2,72,128]{3,2,1,0:T(8,128)S(1)}, u32[]{:S(2)}, u32[]{:S(2)}) collective-permute-start(f32[8,2,72,128]{3,2,1,0:T(8,128)S(1)} %get-tuple-element.37), channel_id=1, source_target_pairs={{0,1},{1,0},{2,3},{3,2},{4,5},{5,4},{6,7},{7,6},{8,9},{9,8},{10,11... | collective-permute-start | bytes 1769480 | tf_op jit(solution)/shard_map/ppermute | solution.py:283
  161.7 4.3 %all-to-all-done.1 = f32[8,2,72,128]{3,2,1,0:T(8,128)} async-done(((f32[8,2,72,128]{3,2,1,0:T(8,128)}), f32[8,2,72,128]{3,2,1,0:T(8,128)}, u32[]{:S(2)}, u32[]{:S(2)}) %all-to-all-start.1) | async-done | bytes 589856 | tf_op jit(solution)/shard_map/all_to_all | solution.py:284
  166.0 3.5 %all-to-all-start = ((f32[8,2,72,128]{3,2,1,0:T(8,128)}), f32[8,2,72,128]{3,2,1,0:T(8,128)S(1)}, u32[]{:S(2)}, u32[]{:S(2)}) async-start(f32[8,2,72,128]{3,2,1,0:T(8,128)} %add.46), calls=%async_computation | async-start | bytes 1179648 | tf_op jit(solution)/shard_map/all_to_all | solution.py:284
  170.7 18.2 %all-to-all-done = f32[8,2,72,128]{3,2,1,0:T(8,128)S(1)} async-done(((f32[8,2,72,128]{3,2,1,0:T(8,128)}), f32[8,2,72,128]{3,2,1,0:T(8,128)S(1)}, u32[]{:S(2)}, u32[]{:S(2)}) %all-to-all-start) | async-done | bytes 589856 | tf_op jit(solution)/shard_map/all_to_all | solution.py:284
  188.9 17.5 %all_to_all.15.parts = f32[4,72,128]{2,1,0:T(8,128)} all-to-all(f32[4,72,128]{2,1,0:T(8,128)S(1)} %pad_maximum_fusion.2), channel_id=1, replica_groups=mesh['yh'=2,'x'=8,'zh'=4,'zl'=2,'yl'=4,'c'=2] {'zh'}, dimensions={0} | all-to-all | bytes 294912 | tf_op jit(solution)/shard_map/all_to_all | solution.py:285
  206.5 3.2 %update.1 = (f32[48,192]{1,0:T(8,128)}, f32[48,192]{1,0:T(8,128)}, f32[48,192]{1,0:T(8,128)}, f32[48,192]{1,0:T(8,128)}, f32[48,48]{1,0:T(8,128)}, /*index=5*/f32[192,192]{1,0:T(8,128)}) custom-call(f32[4,72,128]{2,1,0:T(8,128)} %all_to_all.15.parts, f32[48,192]{1,0:T(8,128)} %weight.1, f32[48,192]{1,0:T(8,128)} %exp_avg.1, f32[48,192]{1,0:T(8,128)} %exp_avg_sq.1, ...), custom_call_target="tpu_custom_call" | custom-call | tf_op jit(solution)/shard_map/update/pallas_call | solution.py:288
  (74 shorter events, 30.3 us)
Async XLA Ops:
  7.2 114.1 %all-gather.3.cloned.1.call-start = ((), (), s32[]{:S(2)}) async-start(), calls=%async_computation.3 | async-start | bytes 4259840 | tf_op jit(solution)/shard_map/all_gather | solution.py:266
  9.1 30.0 %collective-permute-start = (bf16[192,1024]{1,0:T(8,128)(2,1)S(1)}, bf16[192,1024]{1,0:T(8,128)(2,1)S(1)}, u32[]{:S(2)}, u32[]{:S(2)}) collective-permute-start(bf16[192,1024]{1,0:T(8,128)(2,1)S(1)} %get-tuple-element.42), channel_id=1, source_target_pairs={{0,512},{512,0},{1,513},{513,1},{2,514},{514,2},{3,515},{515,3},{4... | collective-permute-start | bytes 1179656 | tf_op jit(solution)/shard_map/ppermute | solution.py:256
  20.7 18.5 %collective-permute-start.4 = (bf16[2,128,768]{2,1,0:T(8,128)(2,1)}, bf16[2,128,768]{2,1,0:T(8,128)(2,1)S(1)}, u32[]{:S(2)}, u32[]{:S(2)}) collective-permute-start(bf16[2,128,768]{2,1,0:T(8,128)(2,1)} %get-tuple-element.25), channel_id=1, source_target_pairs={{0,457},{1,72},{8,449},{9,64},{64,9},{65,136},{72,1},{73,128},{128... | collective-permute-start | bytes 1179656 | tf_op jit(solution)/shard_map/ppermute | solution.py:49
  27.3 17.6 %collective-permute-start.2 = (bf16[2,128,768]{2,1,0:T(8,128)(2,1)}, bf16[2,128,768]{2,1,0:T(8,128)(2,1)S(1)}, u32[]{:S(2)}, u32[]{:S(2)}) collective-permute-start(bf16[2,128,768]{2,1,0:T(8,128)(2,1)} %get-tuple-element.25), channel_id=1, source_target_pairs={{0,72},{1,457},{8,64},{9,449},{64,136},{65,9},{72,128},{73,1},{128... | collective-permute-start | bytes 1179656 | tf_op jit(solution)/shard_map/ppermute | solution.py:49
  35.3 14.4 %collective-permute-start.3 = (bf16[2,128,768]{2,1,0:T(8,128)(2,1)}, bf16[2,128,768]{2,1,0:T(8,128)(2,1)S(1)}, u32[]{:S(2)}, u32[]{:S(2)}) collective-permute-start(bf16[2,128,768]{2,1,0:T(8,128)(2,1)} %get-tuple-element.24.own), channel_id=1, source_target_pairs={{0,449},{1,64},{8,457},{9,72},{64,1},{65,128},{72,9},{73,136},{128... | collective-permute-start | bytes 1179656 | tf_op jit(solution)/shard_map/ppermute | solution.py:49
  37.2 14.2 %collective-permute-start.1 = (bf16[2,128,768]{2,1,0:T(8,128)(2,1)}, bf16[2,128,768]{2,1,0:T(8,128)(2,1)S(1)}, u32[]{:S(2)}, u32[]{:S(2)}) collective-permute-start(bf16[2,128,768]{2,1,0:T(8,128)(2,1)} %get-tuple-element.24.own), channel_id=1, source_target_pairs={{0,64},{1,449},{8,72},{9,457},{64,128},{65,1},{72,136},{73,9},{128... | collective-permute-start | bytes 1179656 | tf_op jit(solution)/shard_map/ppermute | solution.py:49
  39.1 12.3 %copy-start.24 = (bf16[192,1024]{1,0:T(8,128)(2,1)}, bf16[192,1024]{1,0:T(8,128)(2,1)S(1)}, u32[]{:S(2)}) copy-start(bf16[192,1024]{1,0:T(8,128)(2,1)S(1)} %collective-permute-done.came) | copy-start | bytes 1179652
  53.5 35.6 %copy-start.25 = (bf16[2,128,768]{2,1,0:T(8,128)(2,1)S(1)}, bf16[2,128,768]{2,1,0:T(8,128)(2,1)}, u32[]{:S(2)}) copy-start(bf16[2,128,768]{2,1,0:T(8,128)(2,1)} %get-tuple-element.25) | copy-start | bytes 1179652
  53.6 67.6 %copy-start.23 = (s32[11]{0:T(128)S(1)}, s32[11]{0:T(128)}, u32[]{:S(2)}) copy-start(s32[11]{0:T(128)} %stack.53.place) | copy-start | bytes 136
  53.8 13.0 %collective-permute-start.6 = (bf16[4,128,768]{2,1,0:T(8,128)(2,1)S(1)}, bf16[4,128,768]{2,1,0:T(8,128)(2,1)S(1)}, u32[]{:S(2)}, u32[]{:S(2)}) collective-permute-start(bf16[4,128,768]{2,1,0:T(8,128)(2,1)S(1)} %pad_maximum_fusion.hop_one), channel_id=1, source_target_pairs={{0,64},{1,449},{8,72},{9,457},{64,128},{65,1},{72,136},{73,9},{128... | collective-permute-start | bytes 2359304 | tf_op jit(solution)/shard_map/ppermute | solution.py:49
  58.3 16.9 %collective-permute-start.8 = (bf16[4,128,768]{2,1,0:T(8,128)(2,1)S(1)}, bf16[4,128,768]{2,1,0:T(8,128)(2,1)S(1)}, u32[]{:S(2)}, u32[]{:S(2)}) collective-permute-start(bf16[4,128,768]{2,1,0:T(8,128)(2,1)S(1)} %pad_maximum_fusion.1.hop_one), channel_id=1, source_target_pairs={{0,64},{1,449},{8,72},{9,457},{64,128},{65,1},{72,136},{73,9},{128... | collective-permute-start | bytes 2359304 | tf_op jit(solution)/shard_map/ppermute | solution.py:49
  66.8 47.5 %copy-start.15 = (bf16[4,128,768]{2,1,0:T(8,128)(2,1)}, bf16[4,128,768]{2,1,0:T(8,128)(2,1)S(1)}, u32[]{:S(2)}) copy-start(bf16[4,128,768]{2,1,0:T(8,128)(2,1)S(1)} %collective-permute-done.6.hop_two) | copy-start | bytes 2359300
  66.8 17.0 %collective-permute-start.7 = (bf16[4,128,768]{2,1,0:T(8,128)(2,1)S(1)}, bf16[4,128,768]{2,1,0:T(8,128)(2,1)S(1)}, u32[]{:S(2)}, u32[]{:S(2)}) collective-permute-start(bf16[4,128,768]{2,1,0:T(8,128)(2,1)S(1)} %collective-permute-done.6.hop_two), channel_id=1, source_target_pairs={{0,64},{1,449},{8,72},{9,457},{64,128},{65,1},{72,136},{73,9},{128... | collective-permute-start | bytes 2359304 | tf_op jit(solution)/shard_map/ppermute | solution.py:49
  83.8 26.2 %collective-permute-start.10 = (bf16[4,128,768]{2,1,0:T(8,128)(2,1)S(1)}, bf16[4,128,768]{2,1,0:T(8,128)(2,1)S(1)}, u32[]{:S(2)}, u32[]{:S(2)}) collective-permute-start(bf16[4,128,768]{2,1,0:T(8,128)(2,1)S(1)} %collective-permute-done.8.hop_two), channel_id=1, source_target_pairs={{0,64},{1,449},{8,72},{9,457},{64,128},{65,1},{72,136},{73,9},{128... | collective-permute-start | bytes 2359304 | tf_op jit(solution)/shard_map/ppermute | solution.py:49
  89.1 20.9 %collective-permute-start.5 = (bf16[2,128,768]{2,1,0:T(8,128)(2,1)S(1)}, bf16[2,128,768]{2,1,0:T(8,128)(2,1)S(1)}, u32[]{:S(2)}, u32[]{:S(2)}) collective-permute-start(bf16[2,128,768]{2,1,0:T(8,128)(2,1)S(1)} %copy-done.25), channel_id=1, source_target_pairs={{0,8},{8,0},{1,9},{9,1},{2,10},{10,2},{3,11},{11,3},{4,12},{12,4},... | collective-permute-start | bytes 1179656 | tf_op jit(solution)/shard_map/ppermute | solution.py:267
  91.9 22.4 %collective-permute-start.9 = (bf16[2,128,768]{2,1,0:T(8,128)(2,1)S(1)}, bf16[2,128,768]{2,1,0:T(8,128)(2,1)S(1)}, u32[]{:S(2)}, u32[]{:S(2)}) collective-permute-start(bf16[2,128,768]{2,1,0:T(8,128)(2,1)S(1)} %slice.38), channel_id=1, source_target_pairs={{0,64},{1,449},{8,72},{9,457},{64,128},{65,1},{72,136},{73,9},{128... | collective-permute-start | bytes 1179656 | tf_op jit(solution)/shard_map/ppermute | solution.py:49
  111.7 8.8 %collective-permute-start.12 = (bf16[2,128,768]{2,1,0:T(8,128)(2,1)S(1)}, bf16[2,128,768]{2,1,0:T(8,128)(2,1)S(1)}, u32[]{:S(2)}, u32[]{:S(2)}) collective-permute-start(bf16[2,128,768]{2,1,0:T(8,128)(2,1)S(1)} %slice.39), channel_id=1, source_target_pairs={{0,64},{1,449},{8,72},{9,457},{64,128},{65,1},{72,136},{73,9},{128... | collective-permute-start | bytes 1179656 | tf_op jit(solution)/shard_map/ppermute | solution.py:49
  121.2 2.0 copy-start
  123.2 1.1 copy-start.5
  124.3 1.1 copy-start.9
  125.5 1.0 copy-start.10
  126.5 1.0 copy-start.13
  127.5 1.1 copy-start.18
  128.6 1.0 copy-start.22
  129.6 17.0 %copy-start.1 = (bf16[1664,1024]{1,0:T(8,128)(2,1)S(1)}, bf16[1664,1024]{1,0:T(8,128)(2,1)}, u32[]{:S(2)}) copy-start(bf16[1664,1024]{1,0:T(8,128)(2,1)} %all-gather.3.cloned.1.call-done) | copy-start | bytes 10223620
  133.4 7.6 %collective-permute-start.13 = (f32[8,2,72,128]{3,2,1,0:T(8,128)S(1)}, f32[8,2,72,128]{3,2,1,0:T(8,128)S(1)}, u32[]{:S(2)}, u32[]{:S(2)}) collective-permute-start(f32[8,2,72,128]{3,2,1,0:T(8,128)S(1)} %get-tuple-element.41), channel_id=1, source_target_pairs={{0,1},{1,0},{2,3},{3,2},{4,5},{5,4},{6,7},{7,6},{8,9},{9,8},{10,11... | collective-permute-start | bytes 1769480 | tf_op jit(solution)/shard_map/ppermute | solution.py:283
  141.9 24.2 %all-to-all-start.1 = ((f32[8,2,72,128]{3,2,1,0:T(8,128)}), f32[8,2,72,128]{3,2,1,0:T(8,128)}, u32[]{:S(2)}, u32[]{:S(2)}) async-start(f32[8,2,72,128]{3,2,1,0:T(8,128)} %add.47), calls=%async_computation.1 | async-start | bytes 1179648 | tf_op jit(solution)/shard_map/all_to_all | solution.py:284
  146.6 1.1 copy-start.3
  147.7 1.1 copy-start.7
  150.8 1.1 copy-start.16
  156.7 4.1 %collective-permute-start.11 = (f32[8,2,72,128]{3,2,1,0:T(8,128)S(1)}, f32[8,2,72,128]{3,2,1,0:T(8,128)S(1)}, u32[]{:S(2)}, u32[]{:S(2)}) collective-permute-start(f32[8,2,72,128]{3,2,1,0:T(8,128)S(1)} %get-tuple-element.37), channel_id=1, source_target_pairs={{0,1},{1,0},{2,3},{3,2},{4,5},{5,4},{6,7},{7,6},{8,9},{9,8},{10,11... | collective-permute-start | bytes 1769480 | tf_op jit(solution)/shard_map/ppermute | solution.py:283
  166.0 22.9 %all-to-all-start = ((f32[8,2,72,128]{3,2,1,0:T(8,128)}), f32[8,2,72,128]{3,2,1,0:T(8,128)S(1)}, u32[]{:S(2)}, u32[]{:S(2)}) async-start(f32[8,2,72,128]{3,2,1,0:T(8,128)} %add.46), calls=%async_computation | async-start | bytes 1179648 | tf_op jit(solution)/shard_map/all_to_all | solution.py:284
  (11 other events, 9.8 us)
Sparse Core Ops, SparseCore 0:
  53.6 61.4 all-gather.2

commit v9 on v6

--- a/solution.py
+++ b/solution.py
@@ -71,17 +71,16 @@
     )(place, cotangent)
 
 
-def features_kernel(place, kept, came, gate, own, cross):
+def features_kernel(place, kept, came, gate, out):
     for top, bottom, yh in ((kept, came, 0), (came, kept, 1)):
 
         @pl.when(place[9] == yh)
         def _():
-            for ref, hops, sign in ((own, range(5), 1), (cross, range(1, 4), -1)):
-                for at, count in enumerate(hops):
-                    start = pl.multiple_of(place[1 + (sign * count) % NX] * CHUNK, CHUNK)
-                    here = slice(at * CHUNK, (at + 1) * CHUNK)
-                    ref[:HB, here] = top[:, pl.ds(start, CHUNK)]
-                    ref[HB:FEAT, here] = bottom[:, pl.ds(start, CHUNK)]
+            for at, hops in enumerate((0, 1, 2, 3, 4, 7, 6, 5)):
+                start = pl.multiple_of(place[1 + hops] * CHUNK, CHUNK)
+                here = slice(at * CHUNK, (at + 1) * CHUNK)
+                out[:HB, here] = top[:, pl.ds(start, CHUNK)]
+                out[HB:FEAT, here] = bottom[:, pl.ds(start, CHUNK)]
 
     rest = jnp.concatenate([gate[:, z * GROUP : (z + 1) * GROUP] for z in range(8)], axis=0)
     rows = []
@@ -90,23 +89,19 @@
         rest = rest - part.astype(jnp.float32)
         rows.append(part)
     rows = jnp.concatenate(rows + [jnp.zeros_like(rows[0])], axis=0)
-    for ref in (own, cross):
-        ref[FEAT:, :GROUP] = rows
-        if ref.shape[1] > GROUP:
-            ref[FEAT:, GROUP:] = jnp.zeros((32, ref.shape[1] - GROUP), jnp.bfloat16)
+    out[FEAT:, :GROUP] = rows
+    out[FEAT:, GROUP : 5 * CHUNK] = jnp.zeros((32, 5 * CHUNK - GROUP), jnp.bfloat16)
+    out[FEAT:, 5 * CHUNK :] = rows
 
 
 def features_of(place, kept, came, gate):
-    def shape(hops):
-        return jax.ShapeDtypeStruct((FEAT + 32, hops * CHUNK), jnp.bfloat16)
-
     def whole(array):
         return pl.BlockSpec(array.shape, lambda: (0, 0))
 
     return pl.pallas_call(
         features_kernel,
         in_specs=[pl.BlockSpec(memory_space=pltpu.SMEM), whole(kept), whole(came), whole(gate)],
-        out_shape=[shape(5), shape(3)],
+        out_shape=jax.ShapeDtypeStruct((FEAT + 32, TOK), jnp.bfloat16),
         name="features",
     )(place, kept, came, gate)
 
@@ -117,7 +112,6 @@
     att_own,
     att_beside,
     att_cross,
-    att_across,
     own,
     beside,
     hop_one,
@@ -134,13 +128,13 @@
         return jnp.dot(left, right, preferred_element_type=jnp.float32)
 
     total = jnp.zeros((FEAT, GROUP), jnp.float32)
-    for which, att in enumerate((att_own, att_beside, att_cross, att_across)):
+    for which, att in enumerate((att_own, att_beside, att_cross.at[0], att_cross.at[1])):
         one, two, three = hop_one[which], hop_two[which], hop_three[which]
         if which < 2:
             near = (own, beside)[which][0]
             clip = dot(att[:FEAT, : 2 * CHUNK], near, one)
             clip += dot(att[:FEAT, 2 * CHUNK : 4 * CHUNK], two, three)
-            clip += dot(att[:FEAT, 4 * CHUNK :], last[which])
+            clip += dot(att[:FEAT, 4 * CHUNK : 5 * CHUNK], last[which])
         else:
             clip = dot(att[:FEAT, : 2 * CHUNK], one, two)
             clip += dot(att[:FEAT, 2 * CHUNK :], three)
@@ -173,7 +167,7 @@
 
 def product(piece, place, atts, own, beside, blocks):
     count = blocks[0].shape[2] // GROUP
-    attn = [pl.BlockSpec(att.shape, lambda z: (0, 0)) for att in atts]
+    attn = [pl.BlockSpec(att.shape, lambda z, rank=att.ndim: (0,) * rank) for att in atts]
     near = pl.BlockSpec((1, CHUNK, GROUP), lambda z: (piece, 0, z))
     four = pl.BlockSpec((4, CHUNK, GROUP), lambda z: (0, 0, z))
     pair = pl.BlockSpec((2, CHUNK, GROUP), lambda z: (0, 0, z))
@@ -262,25 +256,23 @@
 
     mine, other = split(place, cotangent)
     parts = [hop(mine), hop(other, 1, 0), hop(mine, 0, 1), hop(other, 1, 1)]
-    parts = [after(part, came) for part in parts]
+    beside = lax.ppermute(other, "zl", SWAP)
+    parts = [after(part, came, beside) for part in parts]
     first_one = jnp.stack([part[0] for part in parts])
     first_two = jnp.stack([part[1] for part in parts])
+
+    att_own = features_of(place, kept, after(came, first_two), gate)
+    att_beside = lax.ppermute(att_own, "zl", SWAP)
+    crossing = jnp.stack([att_own[:, 5 * CHUNK :], att_beside[:, 5 * CHUNK :]])
+    att_cross = lax.ppermute(crossing, "c", SWAP)
+    atts = att_own, att_beside, att_cross
+
     second_one = hop(first_one)
     second_two = hop(first_two)
-
-    att_own, att_swap = features_of(place, kept, after(came, first_two), gate)
-    atts = (
-        att_own,
-        lax.ppermute(att_own, "zl", SWAP),
-        lax.ppermute(att_swap, "c", SWAP),
-        lax.ppermute(att_swap, ("zl", "c"), [(0, 3), (1, 2), (2, 1), (3, 0)]),
-    )
-
-    beside = lax.ppermute(after(other, first_two), "zl", SWAP)
-    third_one = hop(after(second_one, first_two, att_own))
-    third_two = hop(after(second_two, third_one, atts[1]))
-    last_one = after(hop(after(third_one, second_two, beside)[:2]), third_two)
-    last_two = hop(third_two[:2])
+    third_one = hop(after(second_one, first_two))
+    third_two = hop(after(second_two, first_one))
+    last_one = after(hop(after(third_one, second_two)[:2]), third_two)
+    last_two = after(hop(after(third_two, second_one)[:2]), third_one)
     rings = (
         (first_one, second_one, third_one, last_one),
         (first_two, second_two, third_two, last_two),

time: 187 us -> 176 us (0.941)
  waiting for transfers between devices: 61.3 us -> 48.1 us
  starting transfers between devices: 74.6 us -> 79.4 us
    ppermute x4 -> x3, waiting for transfers between devices: 18.2 us -> 0.42 us  [the longest x1 0.42 us: local(): att_beside = lax.ppermute(att_own, 'zl', SWAP)]
    ppermute x1, waiting for transfers between devices: 0.01 us -> 3.77 us  [local(): came = lax.ppermute(away, 'yh', SWAP)]
    ppermute x2, starting transfers between devices: 7.17 us -> 10.2 us  [local(): paired = keep + lax.ppermute(send, 'c', SWAP)]
    ppermute x10, starting transfers between devices: 38.3 us -> 40.7 us  [hop(): return lax.ppermute(block, ('x', 'zl', 'c'), ring(other_z, other_core))]
    ppermute x10, waiting for transfers between devices: 17.2 us -> 19.3 us  [hop(): return lax.ppermute(block, ('x', 'zl', 'c'), ring(other_z, other_core))]
    unnamed x26 -> x34, local copies, waits for them, and re-layouts: 5.08 us -> 3.31 us
    ppermute x4 -> x3, starting transfers between devices: 11.4 us -> 11.6 us  [the longest x1 4.91 us: local(): beside = lax.ppermute(other, 'zl', SWAP)]
  transfers between devices with their start and end apart: 19 -> 18, of which waited for: 11 -> 10; matrix products, arithmetic and copies ran while one was open for 2% -> 3% of each run, Pallas kernels for 5% -> 4%
where the time goes in v9:
time: 176 us; the launch traced here: 174 us
  starting transfers between devices  79.4 us (45%)
  waiting for transfers between devices  48.1 us (27%)
  blocking collectives  19.9 us (11%)
  Pallas kernels  15.8 us (9%)
  local copies, waits for them, and re-layouts  6.65 us (4%)
  other arithmetic  3.19 us (2%)
    ppermute x10, starting transfers between devices, hop(): return lax.ppermute(block, ('x', 'zl', 'c'), ring(other_z, other_core))  40.7 us
    all_to_all x2, waiting for transfers between devices, local(): by_z.append(jnp.sum(lax.all_to_all(paired, Y, 0, 0), axis=0))  22.9 us
    all_to_all x1, blocking collectives, local(): parts = lax.all_to_all(jnp.concatenate(by_z, axis=0), 'zh', 0, 0)  19.9 us
    ppermute x10, waiting for transfers between devices, hop(): return lax.ppermute(block, ('x', 'zl', 'c'), ring(other_z, other_core))  19.3 us
    ppermute x2, starting transfers between devices, local(): paired = keep + lax.ppermute(send, 'c', SWAP)  10.2 us
    all_to_all x2, starting transfers between devices, local(): by_z.append(jnp.sum(lax.all_to_all(paired, Y, 0, 0), axis=0))  9.03 us
    pallas_call x2, Pallas kernels, product(): pl.pallas_call(functools.partial(product_kernel, piece), grid=(count,), i...  8.3 us
    ppermute x1, starting transfers between devices, local(): came = lax.ppermute(away, 'yh', SWAP)  7.9 us
  transfers between devices with their start and end apart: 18, of which 10 were waited for; matrix products, arithmetic and copies ran while one was open for 3% of the time, Pallas kernels for 4%

profile of v9, /device:TPU:1, one launch (start us, length us, event | category | flops | bytes accessed | tf_op | source)
XLA Modules:
  0.0 174.1 jit_solution(15960551980155655279)
XLA Ops:
  1.2 2.1 %split.1 = (bf16[2,128,768]{2,1,0:T(8,128)(2,1)}, bf16[2,128,768]{2,1,0:T(8,128)(2,1)}) custom-call(s32[11]{0:T(128)} %stack.62.place, bf16[128,3072]{1,0:T(8,128)(2,1)} %cotangent.1), custom_call_target="tpu_custom_call" | custom-call | tf_op jit(solution)/shard_map/split/pallas_call | solution.py:66
  3.3 5.3 %collective-permute-start.1 = (bf16[2,128,768]{2,1,0:T(8,128)(2,1)}, bf16[2,128,768]{2,1,0:T(8,128)(2,1)S(1)}, u32[]{:S(2)}, u32[]{:S(2)}) collective-permute-start(bf16[2,128,768]{2,1,0:T(8,128)(2,1)} %get-tuple-element.23.own), channel_id=1, source_target_pairs={{0,64},{1,449},{8,72},{9,457},{64,128},{65,1},{72,136},{73,9},{128... | collective-permute-start | bytes 1179656 | tf_op jit(solution)/shard_map/ppermute | solution.py:49
  8.7 4.9 %collective-permute-start.2 = (bf16[2,128,768]{2,1,0:T(8,128)(2,1)}, bf16[2,128,768]{2,1,0:T(8,128)(2,1)S(1)}, u32[]{:S(2)}, u32[]{:S(2)}) collective-permute-start(bf16[2,128,768]{2,1,0:T(8,128)(2,1)} %get-tuple-element.24), channel_id=1, source_target_pairs={{0,8},{8,0},{1,9},{9,1},{2,10},{10,2},{3,11},{11,3},{4,12},{12,4},... | collective-permute-start | bytes 1179656 | tf_op jit(solution)/shard_map/ppermute | solution.py:259
  14.5 7.9 %collective-permute-start = (bf16[192,1024]{1,0:T(8,128)(2,1)S(1)}, bf16[192,1024]{1,0:T(8,128)(2,1)S(1)}, u32[]{:S(2)}, u32[]{:S(2)}) collective-permute-start(bf16[192,1024]{1,0:T(8,128)(2,1)S(1)} %get-tuple-element.40), channel_id=1, source_target_pairs={{0,512},{512,0},{1,513},{513,1},{2,514},{514,2},{3,515},{515,3},{4... | collective-permute-start | bytes 1179656 | tf_op jit(solution)/shard_map/ppermute | solution.py:255
  22.4 2.8 %collective-permute-start.3 = (bf16[2,128,768]{2,1,0:T(8,128)(2,1)S(1)}, bf16[2,128,768]{2,1,0:T(8,128)(2,1)S(1)}, u32[]{:S(2)}, u32[]{:S(2)}) collective-permute-start(bf16[2,128,768]{2,1,0:T(8,128)(2,1)S(1)} %copy-done.16), channel_id=1, source_target_pairs={{0,72},{1,457},{8,64},{9,449},{64,136},{65,9},{72,128},{73,1},{128... | collective-permute-start | bytes 1179656 | tf_op jit(solution)/shard_map/ppermute | solution.py:49
  25.2 4.6 %collective-permute-start.5 = (bf16[2,128,768]{2,1,0:T(8,128)(2,1)S(1)}, bf16[2,128,768]{2,1,0:T(8,128)(2,1)S(1)}, u32[]{:S(2)}, u32[]{:S(2)}) collective-permute-start(bf16[2,128,768]{2,1,0:T(8,128)(2,1)S(1)} %copy-done.16), channel_id=1, source_target_pairs={{0,457},{1,72},{8,449},{9,64},{64,9},{65,136},{72,1},{73,128},{128... | collective-permute-start | bytes 1179656 | tf_op jit(solution)/shard_map/ppermute | solution.py:49
  29.8 2.1 %collective-permute-start.4 = (bf16[2,128,768]{2,1,0:T(8,128)(2,1)S(1)}, bf16[2,128,768]{2,1,0:T(8,128)(2,1)S(1)}, u32[]{:S(2)}, u32[]{:S(2)}) collective-permute-start(bf16[2,128,768]{2,1,0:T(8,128)(2,1)S(1)} %copy-done.5), channel_id=1, source_target_pairs={{0,449},{1,64},{8,457},{9,72},{64,1},{65,128},{72,9},{73,136},{128... | collective-permute-start | bytes 1179656 | tf_op jit(solution)/shard_map/ppermute | solution.py:49
  32.0 3.8 %collective-permute-done.came = bf16[192,1024]{1,0:T(8,128)(2,1)S(1)} collective-permute-done((bf16[192,1024]{1,0:T(8,128)(2,1)S(1)}, bf16[192,1024]{1,0:T(8,128)(2,1)S(1)}, u32[]{:S(2)}, u32[]{:S(2)}) %collective-permute-start) | collective-permute-done | bytes 393248 | tf_op jit(solution)/shard_map/ppermute | solution.py:255
  35.7 6.8 %collective-permute-done.5 = bf16[2,128,768]{2,1,0:T(8,128)(2,1)S(1)} collective-permute-done((bf16[2,128,768]{2,1,0:T(8,128)(2,1)S(1)}, bf16[2,128,768]{2,1,0:T(8,128)(2,1)S(1)}, u32[]{:S(2)}, u32[]{:S(2)}) %collective-permute-start.5) | collective-permute-done | bytes 393248 | tf_op jit(solution)/shard_map/ppermute | solution.py:49
  42.6 1.9 %collective-permute-done.4 = bf16[2,128,768]{2,1,0:T(8,128)(2,1)S(1)} collective-permute-done((bf16[2,128,768]{2,1,0:T(8,128)(2,1)S(1)}, bf16[2,128,768]{2,1,0:T(8,128)(2,1)S(1)}, u32[]{:S(2)}, u32[]{:S(2)}) %collective-permute-start.4) | collective-permute-done | bytes 393248 | tf_op jit(solution)/shard_map/ppermute | solution.py:49
  44.7 5.2 %collective-permute-start.8 = (bf16[4,128,768]{2,1,0:T(8,128)(2,1)S(1)}, bf16[4,128,768]{2,1,0:T(8,128)(2,1)}, u32[]{:S(2)}, u32[]{:S(2)}) collective-permute-start(bf16[4,128,768]{2,1,0:T(8,128)(2,1)S(1)} %pad_maximum_fusion.1.hop_one), channel_id=1, source_target_pairs={{0,64},{1,449},{8,72},{9,457},{64,128},{65,1},{72,136},{73,9},{128... | collective-permute-start | bytes 2359304 | tf_op jit(solution)/shard_map/ppermute | solution.py:49
  50.0 2.3 %features.1.att_own = bf16[416,1024]{1,0:T(8,128)(2,1)} custom-call(s32[11]{0:T(128)} %stack.62.place, bf16[192,1024]{1,0:T(8,128)(2,1)} %get-tuple-element.41.kept, bf16[192,1024]{1,0:T(8,128)(2,1)} %copy-done.15, f32[1,3072]{1,0:T(1,128)} %gate.1), custom_call_target="tpu_custom_call" | custom-call | tf_op jit(solution)/shard_map/features/pallas_call | solution.py:101
  52.2 2.6 %collective-permute-start.6 = (bf16[416,1024]{1,0:T(8,128)(2,1)}, bf16[416,1024]{1,0:T(8,128)(2,1)S(1)}, u32[]{:S(2)}, u32[]{:S(2)}) collective-permute-start(bf16[416,1024]{1,0:T(8,128)(2,1)} %features.1.att_own), channel_id=1, source_target_pairs={{0,8},{8,0},{1,9},{9,1},{2,10},{10,2},{3,11},{11,3},{4,12},{12,4},... | collective-permute-start | bytes 2555912 | tf_op jit(solution)/shard_map/ppermute | solution.py:265
  54.8 4.4 %collective-permute-start.10 = (bf16[4,128,768]{2,1,0:T(8,128)(2,1)S(1)}, bf16[4,128,768]{2,1,0:T(8,128)(2,1)S(1)}, u32[]{:S(2)}, u32[]{:S(2)}) collective-permute-start(bf16[4,128,768]{2,1,0:T(8,128)(2,1)S(1)} %pad_maximum_fusion.hop_one), channel_id=1, source_target_pairs={{0,64},{1,449},{8,72},{9,457},{64,128},{65,1},{72,136},{73,9},{128... | collective-permute-start | bytes 2359304 | tf_op jit(solution)/shard_map/ppermute | solution.py:49
  59.3 4.6 %collective-permute-start.9 = (bf16[4,128,768]{2,1,0:T(8,128)(2,1)}, bf16[4,128,768]{2,1,0:T(8,128)(2,1)S(1)}, u32[]{:S(2)}, u32[]{:S(2)}) collective-permute-start(bf16[4,128,768]{2,1,0:T(8,128)(2,1)} %collective-permute-done.8.hop_two), channel_id=1, source_target_pairs={{0,64},{1,449},{8,72},{9,457},{64,128},{65,1},{72,136},{73,9},{128... | collective-permute-start | bytes 2359304 | tf_op jit(solution)/shard_map/ppermute | solution.py:49
  64.9 3.3 %collective-permute-done.10.hop_two = bf16[4,128,768]{2,1,0:T(8,128)(2,1)S(1)} collective-permute-done((bf16[4,128,768]{2,1,0:T(8,128)(2,1)S(1)}, bf16[4,128,768]{2,1,0:T(8,128)(2,1)S(1)}, u32[]{:S(2)}, u32[]{:S(2)}) %collective-permute-start.10) | collective-permute-done | bytes 786464 | tf_op jit(solution)/shard_map/ppermute | solution.py:49
  68.2 5.0 %collective-permute-start.12 = (bf16[4,128,768]{2,1,0:T(8,128)(2,1)S(1)}, bf16[4,128,768]{2,1,0:T(8,128)(2,1)S(1)}, u32[]{:S(2)}, u32[]{:S(2)}) collective-permute-start(bf16[4,128,768]{2,1,0:T(8,128)(2,1)S(1)} %collective-permute-done.10.hop_two), channel_id=1, source_target_pairs={{0,64},{1,449},{8,72},{9,457},{64,128},{65,1},{72,136},{73,9},{128... | collective-permute-start | bytes 2359304 | tf_op jit(solution)/shard_map/ppermute | solution.py:49
  73.8 4.1 %collective-permute-start.7 = (bf16[2,416,384]{2,1,0:T(8,128)(2,1)S(1)}, bf16[2,416,384]{2,1,0:T(8,128)(2,1)S(1)}, u32[]{:S(2)}, u32[]{:S(2)}) collective-permute-start(bf16[2,416,384]{2,1,0:T(8,128)(2,1)S(1)} %pad_maximum_fusion.2), channel_id=1, source_target_pairs={{0,1},{1,0},{2,3},{3,2},{4,5},{5,4},{6,7},{7,6},{8,9},{9,8},{10,11... | collective-permute-start | bytes 1916936 | tf_op jit(solution)/shard_map/ppermute | solution.py:267
  77.9 3.9 %collective-permute-start.11 = (bf16[2,128,768]{2,1,0:T(8,128)(2,1)S(1)}, bf16[2,128,768]{2,1,0:T(8,128)(2,1)S(1)}, u32[]{:S(2)}, u32[]{:S(2)}) collective-permute-start(bf16[2,128,768]{2,1,0:T(8,128)(2,1)S(1)} %slice.46), channel_id=1, source_target_pairs={{0,64},{1,449},{8,72},{9,457},{64,128},{65,1},{72,136},{73,9},{128... | collective-permute-start | bytes 1179656 | tf_op jit(solution)/shard_map/ppermute | solution.py:49
  81.8 3.2 %collective-permute-done.12.hop_three = bf16[4,128,768]{2,1,0:T(8,128)(2,1)S(1)} collective-permute-done((bf16[4,128,768]{2,1,0:T(8,128)(2,1)S(1)}, bf16[4,128,768]{2,1,0:T(8,128)(2,1)S(1)}, u32[]{:S(2)}, u32[]{:S(2)}) %collective-permute-start.12) | collective-permute-done | bytes 786464 | tf_op jit(solution)/shard_map/ppermute | solution.py:49
  85.0 4.2 %collective-permute-done.11.last = bf16[2,128,768]{2,1,0:T(8,128)(2,1)S(1)} collective-permute-done((bf16[2,128,768]{2,1,0:T(8,128)(2,1)S(1)}, bf16[2,128,768]{2,1,0:T(8,128)(2,1)S(1)}, u32[]{:S(2)}, u32[]{:S(2)}) %collective-permute-start.11) | collective-permute-done | bytes 393248 | tf_op jit(solution)/shard_map/ppermute | solution.py:49
  89.3 4.2 %product.2 = (f32[8,2,72,128]{3,2,1,0:T(8,128)S(1)}, f32[8,2,72,128]{3,2,1,0:T(8,128)S(1)}) custom-call(s32[11]{0:T(128)S(1)} %copy-done.13, bf16[416,1024]{1,0:T(8,128)(2,1)S(1)} %copy-done, bf16[416,1024]{1,0:T(8,128)(2,1)S(1)} %collective-permute-done.6.att_beside, bf16[2,416,384]{2,1,0:T(8,128)(2,1)S(1)} %collective-permute-done.7.att_cross, ...), custom_call_target="tpu_custom_call" | custom-call | flops 1207959552 | bytes 8388608 | tf_op jit(solution)/shard_map/product/pallas_call | solution.py:177
  93.5 6.3 %collective-permute-start.13 = (f32[8,2,72,128]{3,2,1,0:T(8,128)S(1)}, f32[8,2,72,128]{3,2,1,0:T(8,128)S(1)}, u32[]{:S(2)}, u32[]{:S(2)}) collective-permute-start(f32[8,2,72,128]{3,2,1,0:T(8,128)S(1)} %get-tuple-element.35), channel_id=1, source_target_pairs={{0,1},{1,0},{2,3},{3,2},{4,5},{5,4},{6,7},{7,6},{8,9},{9,8},{10,11... | collective-permute-start | bytes 1769480 | tf_op jit(solution)/shard_map/ppermute | solution.py:284
  100.6 2.7 %collective-permute-start.14 = (bf16[2,128,768]{2,1,0:T(8,128)(2,1)}, bf16[2,128,768]{2,1,0:T(8,128)(2,1)}, u32[]{:S(2)}, u32[]{:S(2)}) collective-permute-start(bf16[2,128,768]{2,1,0:T(8,128)(2,1)} %slice.47), channel_id=1, source_target_pairs={{0,64},{1,449},{8,72},{9,457},{64,128},{65,1},{72,136},{73,9},{128... | collective-permute-start | bytes 1179656 | tf_op jit(solution)/shard_map/ppermute | solution.py:49
  104.2 5.5 %all-to-all-start = ((f32[8,2,72,128]{3,2,1,0:T(8,128)}), f32[8,2,72,128]{3,2,1,0:T(8,128)}, u32[]{:S(2)}, u32[]{:S(2)}) async-start(f32[8,2,72,128]{3,2,1,0:T(8,128)} %add.46), calls=%async_computation | async-start | bytes 1179648 | tf_op jit(solution)/shard_map/all_to_all | solution.py:285
  113.0 4.1 %product.3 = (f32[8,2,72,128]{3,2,1,0:T(8,128)S(1)}, f32[8,2,72,128]{3,2,1,0:T(8,128)S(1)}) custom-call(s32[11]{0:T(128)S(1)} %copy-done.13, bf16[416,1024]{1,0:T(8,128)(2,1)S(1)} %copy-done, bf16[416,1024]{1,0:T(8,128)(2,1)S(1)} %collective-permute-done.6.att_beside, bf16[2,416,384]{2,1,0:T(8,128)(2,1)S(1)} %copy-done.2, ...), custom_call_target="tpu_custom_call" | custom-call | flops 1207959552 | bytes 8388608 | tf_op jit(solution)/shard_map/product/pallas_call | solution.py:177
  117.1 3.9 %collective-permute-start.15 = (f32[8,2,72,128]{3,2,1,0:T(8,128)S(1)}, f32[8,2,72,128]{3,2,1,0:T(8,128)S(1)}, u32[]{:S(2)}, u32[]{:S(2)}) collective-permute-start(f32[8,2,72,128]{3,2,1,0:T(8,128)S(1)} %get-tuple-element.39), channel_id=1, source_target_pairs={{0,1},{1,0},{2,3},{3,2},{4,5},{5,4},{6,7},{7,6},{8,9},{9,8},{10,11... | collective-permute-start | bytes 1769480 | tf_op jit(solution)/shard_map/ppermute | solution.py:284
  123.5 4.7 %all-to-all-done = f32[8,2,72,128]{3,2,1,0:T(8,128)} async-done(((f32[8,2,72,128]{3,2,1,0:T(8,128)}), f32[8,2,72,128]{3,2,1,0:T(8,128)}, u32[]{:S(2)}, u32[]{:S(2)}) %all-to-all-start) | async-done | bytes 589856 | tf_op jit(solution)/shard_map/all_to_all | solution.py:285
  128.2 3.5 %all-to-all-start.1 = ((f32[8,2,72,128]{3,2,1,0:T(8,128)}), f32[8,2,72,128]{3,2,1,0:T(8,128)S(1)}, u32[]{:S(2)}, u32[]{:S(2)}) async-start(f32[8,2,72,128]{3,2,1,0:T(8,128)} %add.47), calls=%async_computation.1 | async-start | bytes 1179648 | tf_op jit(solution)/shard_map/all_to_all | solution.py:285
  132.8 18.2 %all-to-all-done.1 = f32[8,2,72,128]{3,2,1,0:T(8,128)S(1)} async-done(((f32[8,2,72,128]{3,2,1,0:T(8,128)}), f32[8,2,72,128]{3,2,1,0:T(8,128)S(1)}, u32[]{:S(2)}, u32[]{:S(2)}) %all-to-all-start.1) | async-done | bytes 589856 | tf_op jit(solution)/shard_map/all_to_all | solution.py:285
  151.1 19.9 %all_to_all.15.parts = f32[4,72,128]{2,1,0:T(8,128)} all-to-all(f32[4,72,128]{2,1,0:T(8,128)S(1)} %pad_maximum_fusion.3), channel_id=1, replica_groups=mesh['yh'=2,'x'=8,'zh'=4,'zl'=2,'yl'=4,'c'=2] {'zh'}, dimensions={0} | all-to-all | bytes 294912 | tf_op jit(solution)/shard_map/all_to_all | solution.py:286
  171.0 3.2 %update.1 = (f32[48,192]{1,0:T(8,128)}, f32[48,192]{1,0:T(8,128)}, f32[48,192]{1,0:T(8,128)}, f32[48,192]{1,0:T(8,128)}, f32[48,48]{1,0:T(8,128)}, /*index=5*/f32[192,192]{1,0:T(8,128)}) custom-call(f32[4,72,128]{2,1,0:T(8,128)} %all_to_all.15.parts, f32[48,192]{1,0:T(8,128)} %weight.1, f32[48,192]{1,0:T(8,128)} %exp_avg.1, f32[48,192]{1,0:T(8,128)} %exp_avg_sq.1, ...), custom_call_target="tpu_custom_call" | custom-call | tf_op jit(solution)/shard_map/update/pallas_call | solution.py:289
  (60 shorter events, 11.9 us)
Async XLA Ops:
  0.6 13.0 %copy-start.14 = (bf16[2048,192]{0,1:T(8,128)(2,1)S(1)}, bf16[2048,192]{0,1:T(8,128)(2,1)}, u32[]{:S(2)}) copy-start(bf16[2048,192]{0,1:T(8,128)(2,1)} %param.10) | copy-start | bytes 2359300
  3.3 26.5 %collective-permute-start.1 = (bf16[2,128,768]{2,1,0:T(8,128)(2,1)}, bf16[2,128,768]{2,1,0:T(8,128)(2,1)S(1)}, u32[]{:S(2)}, u32[]{:S(2)}) collective-permute-start(bf16[2,128,768]{2,1,0:T(8,128)(2,1)} %get-tuple-element.23.own), channel_id=1, source_target_pairs={{0,64},{1,449},{8,72},{9,457},{64,128},{65,1},{72,136},{73,9},{128... | collective-permute-start | bytes 1179656 | tf_op jit(solution)/shard_map/ppermute | solution.py:49
  8.7 23.3 %collective-permute-start.2 = (bf16[2,128,768]{2,1,0:T(8,128)(2,1)}, bf16[2,128,768]{2,1,0:T(8,128)(2,1)S(1)}, u32[]{:S(2)}, u32[]{:S(2)}) collective-permute-start(bf16[2,128,768]{2,1,0:T(8,128)(2,1)} %get-tuple-element.24), channel_id=1, source_target_pairs={{0,8},{8,0},{1,9},{9,1},{2,10},{10,2},{3,11},{11,3},{4,12},{12,4},... | collective-permute-start | bytes 1179656 | tf_op jit(solution)/shard_map/ppermute | solution.py:259
  13.6 8.8 %copy-start.16 = (bf16[2,128,768]{2,1,0:T(8,128)(2,1)S(1)}, bf16[2,128,768]{2,1,0:T(8,128)(2,1)}, u32[]{:S(2)}) copy-start(bf16[2,128,768]{2,1,0:T(8,128)(2,1)} %get-tuple-element.24) | copy-start | bytes 1179652
  13.6 16.2 %copy-start.5 = (bf16[2,128,768]{2,1,0:T(8,128)(2,1)S(1)}, bf16[2,128,768]{2,1,0:T(8,128)(2,1)}, u32[]{:S(2)}) copy-start(bf16[2,128,768]{2,1,0:T(8,128)(2,1)} %get-tuple-element.23.own) | copy-start | bytes 1179652
  14.5 21.3 %collective-permute-start = (bf16[192,1024]{1,0:T(8,128)(2,1)S(1)}, bf16[192,1024]{1,0:T(8,128)(2,1)S(1)}, u32[]{:S(2)}, u32[]{:S(2)}) collective-permute-start(bf16[192,1024]{1,0:T(8,128)(2,1)S(1)} %get-tuple-element.40), channel_id=1, source_target_pairs={{0,512},{512,0},{1,513},{513,1},{2,514},{514,2},{3,515},{515,3},{4... | collective-permute-start | bytes 1179656 | tf_op jit(solution)/shard_map/ppermute | solution.py:255
  22.4 13.4 %collective-permute-start.3 = (bf16[2,128,768]{2,1,0:T(8,128)(2,1)S(1)}, bf16[2,128,768]{2,1,0:T(8,128)(2,1)S(1)}, u32[]{:S(2)}, u32[]{:S(2)}) collective-permute-start(bf16[2,128,768]{2,1,0:T(8,128)(2,1)S(1)} %copy-done.16), channel_id=1, source_target_pairs={{0,72},{1,457},{8,64},{9,449},{64,136},{65,9},{72,128},{73,1},{128... | collective-permute-start | bytes 1179656 | tf_op jit(solution)/shard_map/ppermute | solution.py:49
  25.2 17.4 %collective-permute-start.5 = (bf16[2,128,768]{2,1,0:T(8,128)(2,1)S(1)}, bf16[2,128,768]{2,1,0:T(8,128)(2,1)S(1)}, u32[]{:S(2)}, u32[]{:S(2)}) collective-permute-start(bf16[2,128,768]{2,1,0:T(8,128)(2,1)S(1)} %copy-done.16), channel_id=1, source_target_pairs={{0,457},{1,72},{8,449},{9,64},{64,9},{65,136},{72,1},{73,128},{128... | collective-permute-start | bytes 1179656 | tf_op jit(solution)/shard_map/ppermute | solution.py:49
  29.8 14.6 %collective-permute-start.4 = (bf16[2,128,768]{2,1,0:T(8,128)(2,1)S(1)}, bf16[2,128,768]{2,1,0:T(8,128)(2,1)S(1)}, u32[]{:S(2)}, u32[]{:S(2)}) collective-permute-start(bf16[2,128,768]{2,1,0:T(8,128)(2,1)S(1)} %copy-done.5), channel_id=1, source_target_pairs={{0,449},{1,64},{8,457},{9,72},{64,1},{65,128},{72,9},{73,136},{128... | collective-permute-start | bytes 1179656 | tf_op jit(solution)/shard_map/ppermute | solution.py:49
  32.0 12.5 %copy-start.8 = (bf16[2,128,768]{2,1,0:T(8,128)(2,1)}, bf16[2,128,768]{2,1,0:T(8,128)(2,1)S(1)}, u32[]{:S(2)}) copy-start(bf16[2,128,768]{2,1,0:T(8,128)(2,1)S(1)} %collective-permute-done.2.beside) | copy-start | bytes 1179652
  35.7 6.8 %copy-start.15 = (bf16[192,1024]{1,0:T(8,128)(2,1)}, bf16[192,1024]{1,0:T(8,128)(2,1)S(1)}, u32[]{:S(2)}) copy-start(bf16[192,1024]{1,0:T(8,128)(2,1)S(1)} %collective-permute-done.came) | copy-start | bytes 1179652
  44.7 14.6 %collective-permute-start.8 = (bf16[4,128,768]{2,1,0:T(8,128)(2,1)S(1)}, bf16[4,128,768]{2,1,0:T(8,128)(2,1)}, u32[]{:S(2)}, u32[]{:S(2)}) collective-permute-start(bf16[4,128,768]{2,1,0:T(8,128)(2,1)S(1)} %pad_maximum_fusion.1.hop_one), channel_id=1, source_target_pairs={{0,64},{1,449},{8,72},{9,457},{64,128},{65,1},{72,136},{73,9},{128... | collective-permute-start | bytes 2359304 | tf_op jit(solution)/shard_map/ppermute | solution.py:49
  52.2 21.4 %collective-permute-start.6 = (bf16[416,1024]{1,0:T(8,128)(2,1)}, bf16[416,1024]{1,0:T(8,128)(2,1)S(1)}, u32[]{:S(2)}, u32[]{:S(2)}) collective-permute-start(bf16[416,1024]{1,0:T(8,128)(2,1)} %features.1.att_own), channel_id=1, source_target_pairs={{0,8},{8,0},{1,9},{9,1},{2,10},{10,2},{3,11},{11,3},{4,12},{12,4},... | collective-permute-start | bytes 2555912 | tf_op jit(solution)/shard_map/ppermute | solution.py:265
  54.8 13.3 %collective-permute-start.10 = (bf16[4,128,768]{2,1,0:T(8,128)(2,1)S(1)}, bf16[4,128,768]{2,1,0:T(8,128)(2,1)S(1)}, u32[]{:S(2)}, u32[]{:S(2)}) collective-permute-start(bf16[4,128,768]{2,1,0:T(8,128)(2,1)S(1)} %pad_maximum_fusion.hop_one), channel_id=1, source_target_pairs={{0,64},{1,449},{8,72},{9,457},{64,128},{65,1},{72,136},{73,9},{128... | collective-permute-start | bytes 2359304 | tf_op jit(solution)/shard_map/ppermute | solution.py:49
  59.3 18.6 %collective-permute-start.9 = (bf16[4,128,768]{2,1,0:T(8,128)(2,1)}, bf16[4,128,768]{2,1,0:T(8,128)(2,1)S(1)}, u32[]{:S(2)}, u32[]{:S(2)}) collective-permute-start(bf16[4,128,768]{2,1,0:T(8,128)(2,1)} %collective-permute-done.8.hop_two), channel_id=1, source_target_pairs={{0,64},{1,449},{8,72},{9,457},{64,128},{65,1},{72,136},{73,9},{128... | collective-permute-start | bytes 2359304 | tf_op jit(solution)/shard_map/ppermute | solution.py:49
  68.2 5.6 %copy-start.11 = (bf16[4,128,768]{2,1,0:T(8,128)(2,1)}, bf16[4,128,768]{2,1,0:T(8,128)(2,1)S(1)}, u32[]{:S(2)}) copy-start(bf16[4,128,768]{2,1,0:T(8,128)(2,1)S(1)} %collective-permute-done.10.hop_two) | copy-start | bytes 2359300
  68.2 16.9 %collective-permute-start.12 = (bf16[4,128,768]{2,1,0:T(8,128)(2,1)S(1)}, bf16[4,128,768]{2,1,0:T(8,128)(2,1)S(1)}, u32[]{:S(2)}, u32[]{:S(2)}) collective-permute-start(bf16[4,128,768]{2,1,0:T(8,128)(2,1)S(1)} %collective-permute-done.10.hop_two), channel_id=1, source_target_pairs={{0,64},{1,449},{8,72},{9,457},{64,128},{65,1},{72,136},{73,9},{128... | collective-permute-start | bytes 2359304 | tf_op jit(solution)/shard_map/ppermute | solution.py:49
  73.6 15.6 %copy-start = (bf16[416,1024]{1,0:T(8,128)(2,1)S(1)}, bf16[416,1024]{1,0:T(8,128)(2,1)}, u32[]{:S(2)}) copy-start(bf16[416,1024]{1,0:T(8,128)(2,1)} %features.1.att_own) | copy-start | bytes 2555908
  73.6 15.6 %copy-start.13 = (s32[11]{0:T(128)S(1)}, s32[11]{0:T(128)}, u32[]{:S(2)}) copy-start(s32[11]{0:T(128)} %stack.62.place) | copy-start | bytes 136
  73.7 15.5 %copy-start.6 = (bf16[2,128,768]{2,1,0:T(8,128)(2,1)S(1)}, bf16[2,128,768]{2,1,0:T(8,128)(2,1)}, u32[]{:S(2)}) copy-start(bf16[2,128,768]{2,1,0:T(8,128)(2,1)} %get-tuple-element.23.own) | copy-start | bytes 1179652
  73.8 15.5 %copy-start.9 = (bf16[2,128,768]{2,1,0:T(8,128)(2,1)S(1)}, bf16[2,128,768]{2,1,0:T(8,128)(2,1)}, u32[]{:S(2)}) copy-start(bf16[2,128,768]{2,1,0:T(8,128)(2,1)} %copy-done.8) | copy-start | bytes 1179652
  73.8 15.5 %collective-permute-start.7 = (bf16[2,416,384]{2,1,0:T(8,128)(2,1)S(1)}, bf16[2,416,384]{2,1,0:T(8,128)(2,1)S(1)}, u32[]{:S(2)}, u32[]{:S(2)}) collective-permute-start(bf16[2,416,384]{2,1,0:T(8,128)(2,1)S(1)} %pad_maximum_fusion.2), channel_id=1, source_target_pairs={{0,1},{1,0},{2,3},{3,2},{4,5},{5,4},{6,7},{7,6},{8,9},{9,8},{10,11... | collective-permute-start | bytes 1916936 | tf_op jit(solution)/shard_map/ppermute | solution.py:267
  77.9 11.3 %collective-permute-start.11 = (bf16[2,128,768]{2,1,0:T(8,128)(2,1)S(1)}, bf16[2,128,768]{2,1,0:T(8,128)(2,1)S(1)}, u32[]{:S(2)}, u32[]{:S(2)}) collective-permute-start(bf16[2,128,768]{2,1,0:T(8,128)(2,1)S(1)} %slice.46), channel_id=1, source_target_pairs={{0,64},{1,449},{8,72},{9,457},{64,128},{65,1},{72,136},{73,9},{128... | collective-permute-start | bytes 1179656 | tf_op jit(solution)/shard_map/ppermute | solution.py:49
  85.0 14.8 %copy-start.3 = (bf16[4,128,768]{2,1,0:T(8,128)(2,1)}, bf16[4,128,768]{2,1,0:T(8,128)(2,1)S(1)}, u32[]{:S(2)}) copy-start(bf16[4,128,768]{2,1,0:T(8,128)(2,1)S(1)} %collective-permute-done.12.hop_three) | copy-start | bytes 2359300
  89.2 4.3 %copy-start.1 = (bf16[2,416,384]{2,1,0:T(8,128)(2,1)}, bf16[2,416,384]{2,1,0:T(8,128)(2,1)S(1)}, u32[]{:S(2)}) copy-start(bf16[2,416,384]{2,1,0:T(8,128)(2,1)S(1)} %collective-permute-done.7.att_cross) | copy-start | bytes 1916932
  93.5 9.8 %collective-permute-start.13 = (f32[8,2,72,128]{3,2,1,0:T(8,128)S(1)}, f32[8,2,72,128]{3,2,1,0:T(8,128)S(1)}, u32[]{:S(2)}, u32[]{:S(2)}) collective-permute-start(f32[8,2,72,128]{3,2,1,0:T(8,128)S(1)} %get-tuple-element.35), channel_id=1, source_target_pairs={{0,1},{1,0},{2,3},{3,2},{4,5},{5,4},{6,7},{7,6},{8,9},{9,8},{10,11... | collective-permute-start | bytes 1769480 | tf_op jit(solution)/shard_map/ppermute | solution.py:284
  100.6 9.1 %collective-permute-start.14 = (bf16[2,128,768]{2,1,0:T(8,128)(2,1)}, bf16[2,128,768]{2,1,0:T(8,128)(2,1)}, u32[]{:S(2)}, u32[]{:S(2)}) collective-permute-start(bf16[2,128,768]{2,1,0:T(8,128)(2,1)} %slice.47), channel_id=1, source_target_pairs={{0,64},{1,449},{8,72},{9,457},{64,128},{65,1},{72,136},{73,9},{128... | collective-permute-start | bytes 1179656 | tf_op jit(solution)/shard_map/ppermute | solution.py:49
  104.2 5.5 %copy-start.2 = (bf16[2,416,384]{2,1,0:T(8,128)(2,1)S(1)}, bf16[2,416,384]{2,1,0:T(8,128)(2,1)}, u32[]{:S(2)}) copy-start(bf16[2,416,384]{2,1,0:T(8,128)(2,1)} %copy-done.1) | copy-start | bytes 1916932
  104.2 5.5 %copy-start.7 = (bf16[2,128,768]{2,1,0:T(8,128)(2,1)S(1)}, bf16[2,128,768]{2,1,0:T(8,128)(2,1)}, u32[]{:S(2)}) copy-start(bf16[2,128,768]{2,1,0:T(8,128)(2,1)} %get-tuple-element.23.own) | copy-start | bytes 1179652
  104.2 24.0 %all-to-all-start = ((f32[8,2,72,128]{3,2,1,0:T(8,128)}), f32[8,2,72,128]{3,2,1,0:T(8,128)}, u32[]{:S(2)}, u32[]{:S(2)}) async-start(f32[8,2,72,128]{3,2,1,0:T(8,128)} %add.46), calls=%async_computation | async-start | bytes 1179648 | tf_op jit(solution)/shard_map/all_to_all | solution.py:285
  117.1 5.5 %collective-permute-start.15 = (f32[8,2,72,128]{3,2,1,0:T(8,128)S(1)}, f32[8,2,72,128]{3,2,1,0:T(8,128)S(1)}, u32[]{:S(2)}, u32[]{:S(2)}) collective-permute-start(f32[8,2,72,128]{3,2,1,0:T(8,128)S(1)} %get-tuple-element.39), channel_id=1, source_target_pairs={{0,1},{1,0},{2,3},{3,2},{4,5},{5,4},{6,7},{7,6},{8,9},{9,8},{10,11... | collective-permute-start | bytes 1769480 | tf_op jit(solution)/shard_map/ppermute | solution.py:284
  128.2 22.9 %all-to-all-start.1 = ((f32[8,2,72,128]{3,2,1,0:T(8,128)}), f32[8,2,72,128]{3,2,1,0:T(8,128)S(1)}, u32[]{:S(2)}, u32[]{:S(2)}) async-start(f32[8,2,72,128]{3,2,1,0:T(8,128)} %add.47), calls=%async_computation.1 | async-start | bytes 1179648 | tf_op jit(solution)/shard_map/all_to_all | solution.py:285
  (3 other events, 3.3 us)

commit v10 on v9

--- a/solution.py
+++ b/solution.py
@@ -183,7 +183,7 @@
         out_specs=[out, out],
         out_shape=[shape, shape],
         cost_estimate=pl.CostEstimate(flops=flops, bytes_accessed=8 << 20, transcendentals=0),
-        compiler_params=pltpu.CompilerParams(vmem_limit_bytes=32 << 20),
+        compiler_params=pltpu.CompilerParams(vmem_limit_bytes=16 << 20),
         name="product",
     )(place, *atts, own, beside, *blocks)
 
@@ -257,14 +257,14 @@
     mine, other = split(place, cotangent)
     parts = [hop(mine), hop(other, 1, 0), hop(mine, 0, 1), hop(other, 1, 1)]
     beside = lax.ppermute(other, "zl", SWAP)
-    parts = [after(part, came, beside) for part in parts]
+    parts = [after(part, came) for part in parts]
     first_one = jnp.stack([part[0] for part in parts])
     first_two = jnp.stack([part[1] for part in parts])
 
     att_own = features_of(place, kept, after(came, first_two), gate)
     att_beside = lax.ppermute(att_own, "zl", SWAP)
     crossing = jnp.stack([att_own[:, 5 * CHUNK :], att_beside[:, 5 * CHUNK :]])
-    att_cross = lax.ppermute(crossing, "c", SWAP)
+    att_cross = lax.ppermute(after(crossing, beside), "c", SWAP)
     atts = att_own, att_beside, att_cross
 
     second_one = hop(first_one)

time: 176 us -> 178 us (1.011)
  starting transfers between devices: 79.4 us -> 71 us
  waiting for transfers between devices: 48.1 us -> 56.2 us
  blocking collectives: 19.9 us -> 22.6 us
    ppermute x1, waiting for transfers between devices: 0.01 us -> 8.27 us  [local(): beside = lax.ppermute(other, 'zl', SWAP)]
    ppermute x10, waiting for transfers between devices: 19.3 us -> 23 us  [hop(): return lax.ppermute(block, ('x', 'zl', 'c'), ring(other_z, other_core))]
    ppermute x1, waiting for transfers between devices: 3.77 us -> 0.35 us  [local(): came = lax.ppermute(away, 'yh', SWAP)]
    ppermute x10, starting transfers between devices: 40.7 us -> 37.5 us  [hop(): return lax.ppermute(block, ('x', 'zl', 'c'), ring(other_z, other_core))]
    all_to_all x1, blocking collectives: 19.9 us -> 22.6 us  [local(): parts = lax.all_to_all(jnp.concatenate(by_z, axis=0), 'zh', 0, 0)]
    ppermute x2, starting transfers between devices: 10.2 us -> 7.46 us  [local(): paired = keep + lax.ppermute(send, 'c', SWAP)]
    ppermute x1, starting transfers between devices: 4.91 us -> 2.74 us  [local(): beside = lax.ppermute(other, 'zl', SWAP)]
  transfers between devices with their start and end apart: 18 -> 18, of which waited for: 10 -> 12; matrix products, arithmetic and copies ran while one was open for 3% -> 3% of each run, Pallas kernels for 4% -> 4%
where the time goes in v10:
time: 178 us; the launch traced here: 177 us
  starting transfers between devices  71 us (40%)
  waiting for transfers between devices  56.2 us (32%)
  blocking collectives  22.6 us (13%)
  Pallas kernels  15.8 us (9%)
  local copies, waits for them, and re-layouts  6.74 us (4%)
  other arithmetic  3.19 us (2%)
    ppermute x10, starting transfers between devices, hop(): return lax.ppermute(block, ('x', 'zl', 'c'), ring(other_z, other_core))  37.5 us
    ppermute x10, waiting for transfers between devices, hop(): return lax.ppermute(block, ('x', 'zl', 'c'), ring(other_z, other_core))  23 us
    all_to_all x1, blocking collectives, local(): parts = lax.all_to_all(jnp.concatenate(by_z, axis=0), 'zh', 0, 0)  22.6 us
    all_to_all x2, waiting for transfers between devices, local(): by_z.append(jnp.sum(lax.all_to_all(paired, Y, 0, 0), axis=0))  22.6 us
    pallas_call x2, Pallas kernels, product(): pl.pallas_call(functools.partial(product_kernel, piece), grid=(count,), i...  8.3 us
    ppermute x1, waiting for transfers between devices, local(): beside = lax.ppermute(other, 'zl', SWAP)  8.27 us
    ppermute x1, starting transfers between devices, local(): came = lax.ppermute(away, 'yh', SWAP)  7.9 us
    all_to_all x2, starting transfers between devices, local(): by_z.append(jnp.sum(lax.all_to_all(paired, Y, 0, 0), axis=0))  7.87 us
  transfers between devices with their start and end apart: 18, of which 12 were waited for; matrix products, arithmetic and copies ran while one was open for 3% of the time, Pallas kernels for 4%

profile of v10, /device:TPU:1, one launch (start us, length us, event | category | flops | bytes accessed | tf_op | source)
XLA Modules:
  0.0 176.7 jit_solution(148771724738565988)
XLA Ops:
  1.3 2.1 %split.1 = (bf16[2,128,768]{2,1,0:T(8,128)(2,1)}, bf16[2,128,768]{2,1,0:T(8,128)(2,1)}) custom-call(s32[11]{0:T(128)} %stack.62.place, bf16[128,3072]{1,0:T(8,128)(2,1)} %cotangent.1), custom_call_target="tpu_custom_call" | custom-call | tf_op jit(solution)/shard_map/split/pallas_call | solution.py:66
  3.4 5.3 %collective-permute-start.1 = (bf16[2,128,768]{2,1,0:T(8,128)(2,1)}, bf16[2,128,768]{2,1,0:T(8,128)(2,1)S(1)}, u32[]{:S(2)}, u32[]{:S(2)}) collective-permute-start(bf16[2,128,768]{2,1,0:T(8,128)(2,1)} %get-tuple-element.24.own), channel_id=1, source_target_pairs={{0,64},{1,449},{8,72},{9,457},{64,128},{65,1},{72,136},{73,9},{128... | collective-permute-start | bytes 1179656 | tf_op jit(solution)/shard_map/ppermute | solution.py:49
  9.6 7.9 %collective-permute-start = (bf16[192,1024]{1,0:T(8,128)(2,1)S(1)}, bf16[192,1024]{1,0:T(8,128)(2,1)S(1)}, u32[]{:S(2)}, u32[]{:S(2)}) collective-permute-start(bf16[192,1024]{1,0:T(8,128)(2,1)S(1)} %get-tuple-element.42), channel_id=1, source_target_pairs={{0,512},{512,0},{1,513},{513,1},{2,514},{514,2},{3,515},{515,3},{4... | collective-permute-start | bytes 1179656 | tf_op jit(solution)/shard_map/ppermute | solution.py:255
  17.5 5.8 %collective-permute-start.2 = (bf16[2,128,768]{2,1,0:T(8,128)(2,1)}, bf16[2,128,768]{2,1,0:T(8,128)(2,1)S(1)}, u32[]{:S(2)}, u32[]{:S(2)}) collective-permute-start(bf16[2,128,768]{2,1,0:T(8,128)(2,1)} %get-tuple-element.26), channel_id=1, source_target_pairs={{0,72},{1,457},{8,64},{9,449},{64,136},{65,9},{72,128},{73,1},{128... | collective-permute-start | bytes 1179656 | tf_op jit(solution)/shard_map/ppermute | solution.py:49
  23.3 1.9 %collective-permute-start.4 = (bf16[2,128,768]{2,1,0:T(8,128)(2,1)}, bf16[2,128,768]{2,1,0:T(8,128)(2,1)S(1)}, u32[]{:S(2)}, u32[]{:S(2)}) collective-permute-start(bf16[2,128,768]{2,1,0:T(8,128)(2,1)} %get-tuple-element.26), channel_id=1, source_target_pairs={{0,457},{1,72},{8,449},{9,64},{64,9},{65,136},{72,1},{73,128},{128... | collective-permute-start | bytes 1179656 | tf_op jit(solution)/shard_map/ppermute | solution.py:49
  25.2 3.2 %collective-permute-start.3 = (bf16[2,128,768]{2,1,0:T(8,128)(2,1)S(1)}, bf16[2,128,768]{2,1,0:T(8,128)(2,1)S(1)}, u32[]{:S(2)}, u32[]{:S(2)}) collective-permute-start(bf16[2,128,768]{2,1,0:T(8,128)(2,1)S(1)} %copy-done.5), channel_id=1, source_target_pairs={{0,449},{1,64},{8,457},{9,72},{64,1},{65,128},{72,9},{73,136},{128... | collective-permute-start | bytes 1179656 | tf_op jit(solution)/shard_map/ppermute | solution.py:49
  28.8 3.6 %collective-permute-done.2 = bf16[2,128,768]{2,1,0:T(8,128)(2,1)S(1)} collective-permute-done((bf16[2,128,768]{2,1,0:T(8,128)(2,1)}, bf16[2,128,768]{2,1,0:T(8,128)(2,1)S(1)}, u32[]{:S(2)}, u32[]{:S(2)}) %collective-permute-start.2) | collective-permute-done | bytes 393248 | tf_op jit(solution)/shard_map/ppermute | solution.py:49
  32.3 7.1 %collective-permute-done.4 = bf16[2,128,768]{2,1,0:T(8,128)(2,1)S(1)} collective-permute-done((bf16[2,128,768]{2,1,0:T(8,128)(2,1)}, bf16[2,128,768]{2,1,0:T(8,128)(2,1)S(1)}, u32[]{:S(2)}, u32[]{:S(2)}) %collective-permute-start.4) | collective-permute-done | bytes 393248 | tf_op jit(solution)/shard_map/ppermute | solution.py:49
  39.4 4.3 %collective-permute-done.3 = bf16[2,128,768]{2,1,0:T(8,128)(2,1)S(1)} collective-permute-done((bf16[2,128,768]{2,1,0:T(8,128)(2,1)S(1)}, bf16[2,128,768]{2,1,0:T(8,128)(2,1)S(1)}, u32[]{:S(2)}, u32[]{:S(2)}) %collective-permute-start.3) | collective-permute-done | bytes 393248 | tf_op jit(solution)/shard_map/ppermute | solution.py:49
  43.9 2.4 %collective-permute-start.8 = (bf16[4,128,768]{2,1,0:T(8,128)(2,1)S(1)}, bf16[4,128,768]{2,1,0:T(8,128)(2,1)}, u32[]{:S(2)}, u32[]{:S(2)}) collective-permute-start(bf16[4,128,768]{2,1,0:T(8,128)(2,1)S(1)} %pad_maximum_fusion.1.hop_one), channel_id=1, source_target_pairs={{0,64},{1,449},{8,72},{9,457},{64,128},{65,1},{72,136},{73,9},{128... | collective-permute-start | bytes 2359304 | tf_op jit(solution)/shard_map/ppermute | solution.py:49
  46.4 2.3 %features.1.att_own = bf16[416,1024]{1,0:T(8,128)(2,1)} custom-call(s32[11]{0:T(128)} %stack.62.place, bf16[192,1024]{1,0:T(8,128)(2,1)} %get-tuple-element.43.kept, bf16[192,1024]{1,0:T(8,128)(2,1)} %copy-done.14, f32[1,3072]{1,0:T(1,128)} %gate.1), custom_call_target="tpu_custom_call" | custom-call | tf_op jit(solution)/shard_map/features/pallas_call | solution.py:101
  48.7 3.6 %collective-permute-start.5 = (bf16[416,1024]{1,0:T(8,128)(2,1)}, bf16[416,1024]{1,0:T(8,128)(2,1)S(1)}, u32[]{:S(2)}, u32[]{:S(2)}) collective-permute-start(bf16[416,1024]{1,0:T(8,128)(2,1)} %features.1.att_own), channel_id=1, source_target_pairs={{0,8},{8,0},{1,9},{9,1},{2,10},{10,2},{3,11},{11,3},{4,12},{12,4},... | collective-permute-start | bytes 2555912 | tf_op jit(solution)/shard_map/ppermute | solution.py:265
  52.3 3.7 %collective-permute-start.10 = (bf16[4,128,768]{2,1,0:T(8,128)(2,1)S(1)}, bf16[4,128,768]{2,1,0:T(8,128)(2,1)S(1)}, u32[]{:S(2)}, u32[]{:S(2)}) collective-permute-start(bf16[4,128,768]{2,1,0:T(8,128)(2,1)S(1)} %pad_maximum_fusion.hop_one), channel_id=1, source_target_pairs={{0,64},{1,449},{8,72},{9,457},{64,128},{65,1},{72,136},{73,9},{128... | collective-permute-start | bytes 2359304 | tf_op jit(solution)/shard_map/ppermute | solution.py:49
  56.1 2.7 %collective-permute-start.6 = (bf16[2,128,768]{2,1,0:T(8,128)(2,1)}, bf16[2,128,768]{2,1,0:T(8,128)(2,1)S(1)}, u32[]{:S(2)}, u32[]{:S(2)}) collective-permute-start(bf16[2,128,768]{2,1,0:T(8,128)(2,1)} %get-tuple-element.26), channel_id=1, source_target_pairs={{0,8},{8,0},{1,9},{9,1},{2,10},{10,2},{3,11},{11,3},{4,12},{12,4},... | collective-permute-start | bytes 1179656 | tf_op jit(solution)/shard_map/ppermute | solution.py:259
  58.8 2.6 %collective-permute-start.9 = (bf16[4,128,768]{2,1,0:T(8,128)(2,1)}, bf16[4,128,768]{2,1,0:T(8,128)(2,1)S(1)}, u32[]{:S(2)}, u32[]{:S(2)}) collective-permute-start(bf16[4,128,768]{2,1,0:T(8,128)(2,1)} %collective-permute-done.8.hop_two), channel_id=1, source_target_pairs={{0,64},{1,449},{8,72},{9,457},{64,128},{65,1},{72,136},{73,9},{128... | collective-permute-start | bytes 2359304 | tf_op jit(solution)/shard_map/ppermute | solution.py:49
  62.4 3.0 %collective-permute-done.10.hop_two = bf16[4,128,768]{2,1,0:T(8,128)(2,1)S(1)} collective-permute-done((bf16[4,128,768]{2,1,0:T(8,128)(2,1)S(1)}, bf16[4,128,768]{2,1,0:T(8,128)(2,1)S(1)}, u32[]{:S(2)}, u32[]{:S(2)}) %collective-permute-start.10) | collective-permute-done | bytes 786464 | tf_op jit(solution)/shard_map/ppermute | solution.py:49
  65.4 4.6 %collective-permute-start.12 = (bf16[4,128,768]{2,1,0:T(8,128)(2,1)S(1)}, bf16[4,128,768]{2,1,0:T(8,128)(2,1)S(1)}, u32[]{:S(2)}, u32[]{:S(2)}) collective-permute-start(bf16[4,128,768]{2,1,0:T(8,128)(2,1)S(1)} %collective-permute-done.10.hop_two), channel_id=1, source_target_pairs={{0,64},{1,449},{8,72},{9,457},{64,128},{65,1},{72,136},{73,9},{128... | collective-permute-start | bytes 2359304 | tf_op jit(solution)/shard_map/ppermute | solution.py:49
  70.5 8.3 %collective-permute-done.6.beside = bf16[2,128,768]{2,1,0:T(8,128)(2,1)S(1)} collective-permute-done((bf16[2,128,768]{2,1,0:T(8,128)(2,1)}, bf16[2,128,768]{2,1,0:T(8,128)(2,1)S(1)}, u32[]{:S(2)}, u32[]{:S(2)}) %collective-permute-start.6) | collective-permute-done | bytes 393248 | tf_op jit(solution)/shard_map/ppermute | solution.py:259
  78.8 3.9 %collective-permute-start.7 = (bf16[2,416,384]{2,1,0:T(8,128)(2,1)S(1)}, bf16[2,416,384]{2,1,0:T(8,128)(2,1)S(1)}, u32[]{:S(2)}, u32[]{:S(2)}) collective-permute-start(bf16[2,416,384]{2,1,0:T(8,128)(2,1)S(1)} %pad_maximum_fusion.2), channel_id=1, source_target_pairs={{0,1},{1,0},{2,3},{3,2},{4,5},{5,4},{6,7},{7,6},{8,9},{9,8},{10,11... | collective-permute-start | bytes 1916936 | tf_op jit(solution)/shard_map/ppermute | solution.py:267
  82.8 4.5 %collective-permute-start.11 = (bf16[2,128,768]{2,1,0:T(8,128)(2,1)S(1)}, bf16[2,128,768]{2,1,0:T(8,128)(2,1)S(1)}, u32[]{:S(2)}, u32[]{:S(2)}) collective-permute-start(bf16[2,128,768]{2,1,0:T(8,128)(2,1)S(1)} %slice.46), channel_id=1, source_target_pairs={{0,64},{1,449},{8,72},{9,457},{64,128},{65,1},{72,136},{73,9},{128... | collective-permute-start | bytes 1179656 | tf_op jit(solution)/shard_map/ppermute | solution.py:49
  87.4 4.7 %collective-permute-done.11.last = bf16[2,128,768]{2,1,0:T(8,128)(2,1)S(1)} collective-permute-done((bf16[2,128,768]{2,1,0:T(8,128)(2,1)S(1)}, bf16[2,128,768]{2,1,0:T(8,128)(2,1)S(1)}, u32[]{:S(2)}, u32[]{:S(2)}) %collective-permute-start.11) | collective-permute-done | bytes 393248 | tf_op jit(solution)/shard_map/ppermute | solution.py:49
  92.1 4.2 %product.2 = (f32[8,2,72,128]{3,2,1,0:T(8,128)S(1)}, f32[8,2,72,128]{3,2,1,0:T(8,128)S(1)}) custom-call(s32[11]{0:T(128)S(1)} %copy-done.12, bf16[416,1024]{1,0:T(8,128)(2,1)S(1)} %copy-done, bf16[416,1024]{1,0:T(8,128)(2,1)S(1)} %collective-permute-done.5.att_beside, bf16[2,416,384]{2,1,0:T(8,128)(2,1)S(1)} %collective-permute-done.7.att_cross, ...), custom_call_target="tpu_custom_call" | custom-call | flops 1207959552 | bytes 8388608 | tf_op jit(solution)/shard_map/product/pallas_call | solution.py:177
  96.3 3.5 %collective-permute-start.13 = (f32[8,2,72,128]{3,2,1,0:T(8,128)S(1)}, f32[8,2,72,128]{3,2,1,0:T(8,128)S(1)}, u32[]{:S(2)}, u32[]{:S(2)}) collective-permute-start(f32[8,2,72,128]{3,2,1,0:T(8,128)S(1)} %get-tuple-element.37), channel_id=1, source_target_pairs={{0,1},{1,0},{2,3},{3,2},{4,5},{5,4},{6,7},{7,6},{8,9},{9,8},{10,11... | collective-permute-start | bytes 1769480 | tf_op jit(solution)/shard_map/ppermute | solution.py:284
  100.7 3.4 %collective-permute-start.14 = (bf16[2,128,768]{2,1,0:T(8,128)(2,1)}, bf16[2,128,768]{2,1,0:T(8,128)(2,1)}, u32[]{:S(2)}, u32[]{:S(2)}) collective-permute-start(bf16[2,128,768]{2,1,0:T(8,128)(2,1)} %slice.47), channel_id=1, source_target_pairs={{0,64},{1,449},{8,72},{9,457},{64,128},{65,1},{72,136},{73,9},{128... | collective-permute-start | bytes 1179656 | tf_op jit(solution)/shard_map/ppermute | solution.py:49
  105.0 4.3 %all-to-all-start = ((f32[8,2,72,128]{3,2,1,0:T(8,128)}), f32[8,2,72,128]{3,2,1,0:T(8,128)}, u32[]{:S(2)}, u32[]{:S(2)}) async-start(f32[8,2,72,128]{3,2,1,0:T(8,128)} %add.46), calls=%async_computation | async-start | bytes 1179648 | tf_op jit(solution)/shard_map/all_to_all | solution.py:285
  113.1 4.1 %product.3 = (f32[8,2,72,128]{3,2,1,0:T(8,128)S(1)}, f32[8,2,72,128]{3,2,1,0:T(8,128)S(1)}) custom-call(s32[11]{0:T(128)S(1)} %copy-done.12, bf16[416,1024]{1,0:T(8,128)(2,1)S(1)} %copy-done, bf16[416,1024]{1,0:T(8,128)(2,1)S(1)} %collective-permute-done.5.att_beside, bf16[2,416,384]{2,1,0:T(8,128)(2,1)S(1)} %copy-done.2, ...), custom_call_target="tpu_custom_call" | custom-call | flops 1207959552 | bytes 8388608 | tf_op jit(solution)/shard_map/product/pallas_call | solution.py:177
  117.1 3.9 %collective-permute-start.15 = (f32[8,2,72,128]{3,2,1,0:T(8,128)S(1)}, f32[8,2,72,128]{3,2,1,0:T(8,128)S(1)}, u32[]{:S(2)}, u32[]{:S(2)}) collective-permute-start(f32[8,2,72,128]{3,2,1,0:T(8,128)S(1)} %get-tuple-element.41), channel_id=1, source_target_pairs={{0,1},{1,0},{2,3},{3,2},{4,5},{5,4},{6,7},{7,6},{8,9},{9,8},{10,11... | collective-permute-start | bytes 1769480 | tf_op jit(solution)/shard_map/ppermute | solution.py:284
  123.6 4.4 %all-to-all-done = f32[8,2,72,128]{3,2,1,0:T(8,128)} async-done(((f32[8,2,72,128]{3,2,1,0:T(8,128)}), f32[8,2,72,128]{3,2,1,0:T(8,128)}, u32[]{:S(2)}, u32[]{:S(2)}) %all-to-all-start) | async-done | bytes 589856 | tf_op jit(solution)/shard_map/all_to_all | solution.py:285
  128.0 3.5 %all-to-all-start.1 = ((f32[8,2,72,128]{3,2,1,0:T(8,128)}), f32[8,2,72,128]{3,2,1,0:T(8,128)S(1)}, u32[]{:S(2)}, u32[]{:S(2)}) async-start(f32[8,2,72,128]{3,2,1,0:T(8,128)} %add.47), calls=%async_computation.1 | async-start | bytes 1179648 | tf_op jit(solution)/shard_map/all_to_all | solution.py:285
  132.6 18.2 %all-to-all-done.1 = f32[8,2,72,128]{3,2,1,0:T(8,128)S(1)} async-done(((f32[8,2,72,128]{3,2,1,0:T(8,128)}), f32[8,2,72,128]{3,2,1,0:T(8,128)S(1)}, u32[]{:S(2)}, u32[]{:S(2)}) %all-to-all-start.1) | async-done | bytes 589856 | tf_op jit(solution)/shard_map/all_to_all | solution.py:285
  150.9 22.6 %all_to_all.15.parts = f32[4,72,128]{2,1,0:T(8,128)} all-to-all(f32[4,72,128]{2,1,0:T(8,128)S(1)} %pad_maximum_fusion.3), channel_id=1, replica_groups=mesh['yh'=2,'x'=8,'zh'=4,'zl'=2,'yl'=4,'c'=2] {'zh'}, dimensions={0} | all-to-all | bytes 294912 | tf_op jit(solution)/shard_map/all_to_all | solution.py:286
  173.5 3.2 %update.1 = (f32[48,192]{1,0:T(8,128)}, f32[48,192]{1,0:T(8,128)}, f32[48,192]{1,0:T(8,128)}, f32[48,192]{1,0:T(8,128)}, f32[48,48]{1,0:T(8,128)}, /*index=5*/f32[192,192]{1,0:T(8,128)}) custom-call(f32[4,72,128]{2,1,0:T(8,128)} %all_to_all.15.parts, f32[48,192]{1,0:T(8,128)} %weight.1, f32[48,192]{1,0:T(8,128)} %exp_avg.1, f32[48,192]{1,0:T(8,128)} %exp_avg_sq.1, ...), custom_call_target="tpu_custom_call" | custom-call | tf_op jit(solution)/shard_map/update/pallas_call | solution.py:289
  (56 shorter events, 12.7 us)
Async XLA Ops:
  0.6 8.1 %copy-start.13 = (bf16[2048,192]{0,1:T(8,128)(2,1)S(1)}, bf16[2048,192]{0,1:T(8,128)(2,1)}, u32[]{:S(2)}) copy-start(bf16[2048,192]{0,1:T(8,128)(2,1)} %param.10) | copy-start | bytes 2359300
  3.4 25.0 %collective-permute-start.1 = (bf16[2,128,768]{2,1,0:T(8,128)(2,1)}, bf16[2,128,768]{2,1,0:T(8,128)(2,1)S(1)}, u32[]{:S(2)}, u32[]{:S(2)}) collective-permute-start(bf16[2,128,768]{2,1,0:T(8,128)(2,1)} %get-tuple-element.24.own), channel_id=1, source_target_pairs={{0,64},{1,449},{8,72},{9,457},{64,128},{65,1},{72,136},{73,9},{128... | collective-permute-start | bytes 1179656 | tf_op jit(solution)/shard_map/ppermute | solution.py:49
  8.8 16.4 %copy-start.5 = (bf16[2,128,768]{2,1,0:T(8,128)(2,1)S(1)}, bf16[2,128,768]{2,1,0:T(8,128)(2,1)}, u32[]{:S(2)}) copy-start(bf16[2,128,768]{2,1,0:T(8,128)(2,1)} %get-tuple-element.24.own) | copy-start | bytes 1179652
  9.6 19.2 %collective-permute-start = (bf16[192,1024]{1,0:T(8,128)(2,1)S(1)}, bf16[192,1024]{1,0:T(8,128)(2,1)S(1)}, u32[]{:S(2)}, u32[]{:S(2)}) collective-permute-start(bf16[192,1024]{1,0:T(8,128)(2,1)S(1)} %get-tuple-element.42), channel_id=1, source_target_pairs={{0,512},{512,0},{1,513},{513,1},{2,514},{514,2},{3,515},{515,3},{4... | collective-permute-start | bytes 1179656 | tf_op jit(solution)/shard_map/ppermute | solution.py:255
  17.5 14.8 %collective-permute-start.2 = (bf16[2,128,768]{2,1,0:T(8,128)(2,1)}, bf16[2,128,768]{2,1,0:T(8,128)(2,1)S(1)}, u32[]{:S(2)}, u32[]{:S(2)}) collective-permute-start(bf16[2,128,768]{2,1,0:T(8,128)(2,1)} %get-tuple-element.26), channel_id=1, source_target_pairs={{0,72},{1,457},{8,64},{9,449},{64,136},{65,9},{72,128},{73,1},{128... | collective-permute-start | bytes 1179656 | tf_op jit(solution)/shard_map/ppermute | solution.py:49
  23.3 16.1 %collective-permute-start.4 = (bf16[2,128,768]{2,1,0:T(8,128)(2,1)}, bf16[2,128,768]{2,1,0:T(8,128)(2,1)S(1)}, u32[]{:S(2)}, u32[]{:S(2)}) collective-permute-start(bf16[2,128,768]{2,1,0:T(8,128)(2,1)} %get-tuple-element.26), channel_id=1, source_target_pairs={{0,457},{1,72},{8,449},{9,64},{64,9},{65,136},{72,1},{73,128},{128... | collective-permute-start | bytes 1179656 | tf_op jit(solution)/shard_map/ppermute | solution.py:49
  25.2 18.4 %collective-permute-start.3 = (bf16[2,128,768]{2,1,0:T(8,128)(2,1)S(1)}, bf16[2,128,768]{2,1,0:T(8,128)(2,1)S(1)}, u32[]{:S(2)}, u32[]{:S(2)}) collective-permute-start(bf16[2,128,768]{2,1,0:T(8,128)(2,1)S(1)} %copy-done.5), channel_id=1, source_target_pairs={{0,449},{1,64},{8,457},{9,72},{64,1},{65,128},{72,9},{73,136},{128... | collective-permute-start | bytes 1179656 | tf_op jit(solution)/shard_map/ppermute | solution.py:49
  28.8 14.9 %copy-start.14 = (bf16[192,1024]{1,0:T(8,128)(2,1)}, bf16[192,1024]{1,0:T(8,128)(2,1)S(1)}, u32[]{:S(2)}) copy-start(bf16[192,1024]{1,0:T(8,128)(2,1)S(1)} %collective-permute-done.came) | copy-start | bytes 1179652
  43.9 14.9 %collective-permute-start.8 = (bf16[4,128,768]{2,1,0:T(8,128)(2,1)S(1)}, bf16[4,128,768]{2,1,0:T(8,128)(2,1)}, u32[]{:S(2)}, u32[]{:S(2)}) collective-permute-start(bf16[4,128,768]{2,1,0:T(8,128)(2,1)S(1)} %pad_maximum_fusion.1.hop_one), channel_id=1, source_target_pairs={{0,64},{1,449},{8,72},{9,457},{64,128},{65,1},{72,136},{73,9},{128... | collective-permute-start | bytes 2359304 | tf_op jit(solution)/shard_map/ppermute | solution.py:49
  48.7 21.7 %collective-permute-start.5 = (bf16[416,1024]{1,0:T(8,128)(2,1)}, bf16[416,1024]{1,0:T(8,128)(2,1)S(1)}, u32[]{:S(2)}, u32[]{:S(2)}) collective-permute-start(bf16[416,1024]{1,0:T(8,128)(2,1)} %features.1.att_own), channel_id=1, source_target_pairs={{0,8},{8,0},{1,9},{9,1},{2,10},{10,2},{3,11},{11,3},{4,12},{12,4},... | collective-permute-start | bytes 2555912 | tf_op jit(solution)/shard_map/ppermute | solution.py:265
  52.3 13.0 %collective-permute-start.10 = (bf16[4,128,768]{2,1,0:T(8,128)(2,1)S(1)}, bf16[4,128,768]{2,1,0:T(8,128)(2,1)S(1)}, u32[]{:S(2)}, u32[]{:S(2)}) collective-permute-start(bf16[4,128,768]{2,1,0:T(8,128)(2,1)S(1)} %pad_maximum_fusion.hop_one), channel_id=1, source_target_pairs={{0,64},{1,449},{8,72},{9,457},{64,128},{65,1},{72,136},{73,9},{128... | collective-permute-start | bytes 2359304 | tf_op jit(solution)/shard_map/ppermute | solution.py:49
  56.1 22.8 %collective-permute-start.6 = (bf16[2,128,768]{2,1,0:T(8,128)(2,1)}, bf16[2,128,768]{2,1,0:T(8,128)(2,1)S(1)}, u32[]{:S(2)}, u32[]{:S(2)}) collective-permute-start(bf16[2,128,768]{2,1,0:T(8,128)(2,1)} %get-tuple-element.26), channel_id=1, source_target_pairs={{0,8},{8,0},{1,9},{9,1},{2,10},{10,2},{3,11},{11,3},{4,12},{12,4},... | collective-permute-start | bytes 1179656 | tf_op jit(solution)/shard_map/ppermute | solution.py:259
  58.8 24.0 %collective-permute-start.9 = (bf16[4,128,768]{2,1,0:T(8,128)(2,1)}, bf16[4,128,768]{2,1,0:T(8,128)(2,1)S(1)}, u32[]{:S(2)}, u32[]{:S(2)}) collective-permute-start(bf16[4,128,768]{2,1,0:T(8,128)(2,1)} %collective-permute-done.8.hop_two), channel_id=1, source_target_pairs={{0,64},{1,449},{8,72},{9,457},{64,128},{65,1},{72,136},{73,9},{128... | collective-permute-start | bytes 2359304 | tf_op jit(solution)/shard_map/ppermute | solution.py:49
  65.4 5.1 %copy-start.10 = (bf16[4,128,768]{2,1,0:T(8,128)(2,1)}, bf16[4,128,768]{2,1,0:T(8,128)(2,1)S(1)}, u32[]{:S(2)}) copy-start(bf16[4,128,768]{2,1,0:T(8,128)(2,1)S(1)} %collective-permute-done.10.hop_two) | copy-start | bytes 2359300
  65.4 22.0 %collective-permute-start.12 = (bf16[4,128,768]{2,1,0:T(8,128)(2,1)S(1)}, bf16[4,128,768]{2,1,0:T(8,128)(2,1)S(1)}, u32[]{:S(2)}, u32[]{:S(2)}) collective-permute-start(bf16[4,128,768]{2,1,0:T(8,128)(2,1)S(1)} %collective-permute-done.10.hop_two), channel_id=1, source_target_pairs={{0,64},{1,449},{8,72},{9,457},{64,128},{65,1},{72,136},{73,9},{128... | collective-permute-start | bytes 2359304 | tf_op jit(solution)/shard_map/ppermute | solution.py:49
  70.4 21.6 %copy-start = (bf16[416,1024]{1,0:T(8,128)(2,1)S(1)}, bf16[416,1024]{1,0:T(8,128)(2,1)}, u32[]{:S(2)}) copy-start(bf16[416,1024]{1,0:T(8,128)(2,1)} %features.1.att_own) | copy-start | bytes 2555908
  70.5 21.5 %copy-start.6 = (bf16[2,128,768]{2,1,0:T(8,128)(2,1)S(1)}, bf16[2,128,768]{2,1,0:T(8,128)(2,1)}, u32[]{:S(2)}) copy-start(bf16[2,128,768]{2,1,0:T(8,128)(2,1)} %get-tuple-element.24.own) | copy-start | bytes 1179652
  70.5 21.5 %copy-start.12 = (s32[11]{0:T(128)S(1)}, s32[11]{0:T(128)}, u32[]{:S(2)}) copy-start(s32[11]{0:T(128)} %stack.62.place) | copy-start | bytes 136
  78.8 13.2 %copy-start.8 = (bf16[2,128,768]{2,1,0:T(8,128)(2,1)}, bf16[2,128,768]{2,1,0:T(8,128)(2,1)S(1)}, u32[]{:S(2)}) copy-start(bf16[2,128,768]{2,1,0:T(8,128)(2,1)S(1)} %collective-permute-done.6.beside) | copy-start | bytes 1179652
  78.8 13.2 %collective-permute-start.7 = (bf16[2,416,384]{2,1,0:T(8,128)(2,1)S(1)}, bf16[2,416,384]{2,1,0:T(8,128)(2,1)S(1)}, u32[]{:S(2)}, u32[]{:S(2)}) collective-permute-start(bf16[2,416,384]{2,1,0:T(8,128)(2,1)S(1)} %pad_maximum_fusion.2), channel_id=1, source_target_pairs={{0,1},{1,0},{2,3},{3,2},{4,5},{5,4},{6,7},{7,6},{8,9},{9,8},{10,11... | collective-permute-start | bytes 1916936 | tf_op jit(solution)/shard_map/ppermute | solution.py:267
  82.8 9.2 %collective-permute-start.11 = (bf16[2,128,768]{2,1,0:T(8,128)(2,1)S(1)}, bf16[2,128,768]{2,1,0:T(8,128)(2,1)S(1)}, u32[]{:S(2)}, u32[]{:S(2)}) collective-permute-start(bf16[2,128,768]{2,1,0:T(8,128)(2,1)S(1)} %slice.46), channel_id=1, source_target_pairs={{0,64},{1,449},{8,72},{9,457},{64,128},{65,1},{72,136},{73,9},{128... | collective-permute-start | bytes 1179656 | tf_op jit(solution)/shard_map/ppermute | solution.py:49
  87.4 12.5 %copy-start.3 = (bf16[4,128,768]{2,1,0:T(8,128)(2,1)}, bf16[4,128,768]{2,1,0:T(8,128)(2,1)S(1)}, u32[]{:S(2)}) copy-start(bf16[4,128,768]{2,1,0:T(8,128)(2,1)S(1)} %collective-permute-done.12.hop_three) | copy-start | bytes 2359300
  92.1 4.3 %copy-start.1 = (bf16[2,416,384]{2,1,0:T(8,128)(2,1)}, bf16[2,416,384]{2,1,0:T(8,128)(2,1)S(1)}, u32[]{:S(2)}) copy-start(bf16[2,416,384]{2,1,0:T(8,128)(2,1)S(1)} %collective-permute-done.7.att_cross) | copy-start | bytes 1916932
  96.3 7.7 %collective-permute-start.13 = (f32[8,2,72,128]{3,2,1,0:T(8,128)S(1)}, f32[8,2,72,128]{3,2,1,0:T(8,128)S(1)}, u32[]{:S(2)}, u32[]{:S(2)}) collective-permute-start(f32[8,2,72,128]{3,2,1,0:T(8,128)S(1)} %get-tuple-element.37), channel_id=1, source_target_pairs={{0,1},{1,0},{2,3},{3,2},{4,5},{5,4},{6,7},{7,6},{8,9},{9,8},{10,11... | collective-permute-start | bytes 1769480 | tf_op jit(solution)/shard_map/ppermute | solution.py:284
  100.7 9.1 %collective-permute-start.14 = (bf16[2,128,768]{2,1,0:T(8,128)(2,1)}, bf16[2,128,768]{2,1,0:T(8,128)(2,1)}, u32[]{:S(2)}, u32[]{:S(2)}) collective-permute-start(bf16[2,128,768]{2,1,0:T(8,128)(2,1)} %slice.47), channel_id=1, source_target_pairs={{0,64},{1,449},{8,72},{9,457},{64,128},{65,1},{72,136},{73,9},{128... | collective-permute-start | bytes 1179656 | tf_op jit(solution)/shard_map/ppermute | solution.py:49
  105.0 4.8 %copy-start.2 = (bf16[2,416,384]{2,1,0:T(8,128)(2,1)S(1)}, bf16[2,416,384]{2,1,0:T(8,128)(2,1)}, u32[]{:S(2)}) copy-start(bf16[2,416,384]{2,1,0:T(8,128)(2,1)} %copy-done.1) | copy-start | bytes 1916932
  105.0 4.8 %copy-start.7 = (bf16[2,128,768]{2,1,0:T(8,128)(2,1)S(1)}, bf16[2,128,768]{2,1,0:T(8,128)(2,1)}, u32[]{:S(2)}) copy-start(bf16[2,128,768]{2,1,0:T(8,128)(2,1)} %get-tuple-element.24.own) | copy-start | bytes 1179652
  105.0 23.0 %all-to-all-start = ((f32[8,2,72,128]{3,2,1,0:T(8,128)}), f32[8,2,72,128]{3,2,1,0:T(8,128)}, u32[]{:S(2)}, u32[]{:S(2)}) async-start(f32[8,2,72,128]{3,2,1,0:T(8,128)} %add.46), calls=%async_computation | async-start | bytes 1179648 | tf_op jit(solution)/shard_map/all_to_all | solution.py:285
  109.8 1.1 copy-start.4
  111.9 1.1 copy-start.11
  117.1 5.6 %collective-permute-start.15 = (f32[8,2,72,128]{3,2,1,0:T(8,128)S(1)}, f32[8,2,72,128]{3,2,1,0:T(8,128)S(1)}, u32[]{:S(2)}, u32[]{:S(2)}) collective-permute-start(f32[8,2,72,128]{3,2,1,0:T(8,128)S(1)} %get-tuple-element.41), channel_id=1, source_target_pairs={{0,1},{1,0},{2,3},{3,2},{4,5},{5,4},{6,7},{7,6},{8,9},{9,8},{10,11... | collective-permute-start | bytes 1769480 | tf_op jit(solution)/shard_map/ppermute | solution.py:284
  128.0 22.9 %all-to-all-start.1 = ((f32[8,2,72,128]{3,2,1,0:T(8,128)}), f32[8,2,72,128]{3,2,1,0:T(8,128)S(1)}, u32[]{:S(2)}, u32[]{:S(2)}) async-start(f32[8,2,72,128]{3,2,1,0:T(8,128)} %add.47), calls=%async_computation.1 | async-start | bytes 1179648 | tf_op jit(solution)/shard_map/all_to_all | solution.py:285
  (1 other events, 1.0 us)

commit v11 on v10

--- a/solution.py
+++ b/solution.py
@@ -255,21 +255,21 @@
     came = lax.ppermute(away, "yh", SWAP)
 
     mine, other = split(place, cotangent)
-    parts = [hop(mine), hop(other, 1, 0), hop(mine, 0, 1), hop(other, 1, 1)]
     beside = lax.ppermute(other, "zl", SWAP)
-    parts = [after(part, came) for part in parts]
-    first_one = jnp.stack([part[0] for part in parts])
-    first_two = jnp.stack([part[1] for part in parts])
-
-    att_own = features_of(place, kept, after(came, first_two), gate)
+    pair = jnp.stack([mine, beside], axis=1)
+    parts = [hop(pair), hop(pair, other_core=1)]
+    first_one = jnp.concatenate([part[0] for part in parts])
+    first_two = jnp.concatenate([part[1] for part in parts])
+
+    att_own = features_of(place, kept, after(came, first_one), gate)
     att_beside = lax.ppermute(att_own, "zl", SWAP)
     crossing = jnp.stack([att_own[:, 5 * CHUNK :], att_beside[:, 5 * CHUNK :]])
-    att_cross = lax.ppermute(after(crossing, beside), "c", SWAP)
+    att_cross = lax.ppermute(crossing, "c", SWAP)
     atts = att_own, att_beside, att_cross
 
     second_one = hop(first_one)
     second_two = hop(first_two)
-    third_one = hop(after(second_one, first_two))
+    third_one = hop(after(second_one, first_two, att_own))
     third_two = hop(after(second_two, first_one))
     last_one = after(hop(after(third_one, second_two)[:2]), third_two)
     last_two = after(hop(after(third_two, second_one)[:2]), third_one)

time: 178 us -> 185 us (1.039)
  starting transfers between devices: 71 us -> 79.9 us
  waiting for transfers between devices: 56.2 us -> 49.4 us
  other arithmetic: 3.19 us -> 6.17 us
    ppermute x10 -> x8, starting transfers between devices: 37.5 us -> 46.6 us  [hop(): return lax.ppermute(block, ('x', 'zl', 'c'), ring(other_z, other_core))]
    ppermute x10 -> x8, waiting for transfers between devices: 23 us -> 19.9 us  [hop(): return lax.ppermute(block, ('x', 'zl', 'c'), ring(other_z, other_core))]
    ppermute x1, starting transfers between devices: 2.74 us -> 5.73 us  [local(): beside = lax.ppermute(other, 'zl', SWAP)]
    ppermute x1, waiting for transfers between devices: 8.27 us -> 5.36 us  [local(): beside = lax.ppermute(other, 'zl', SWAP)]
    concatenate x0 -> x2, other arithmetic: none -> 2.03 us  [the longest x1 1.07 us: local(): first_two = jnp.concatenate([part[1] for part in parts])]
    squeeze x0 -> x2, local copies, waits for them, and re-layouts: none -> 1.98 us  [local(): first_two = jnp.concatenate([part[1] for part in parts])]
    ppermute x1, starting transfers between devices: 3.94 us -> 2.05 us  [local(): att_cross = lax.ppermute(crossing, 'c', SWAP)]
    unnamed x30 -> x22, local copies, waits for them, and re-layouts: 3.31 us -> 4.11 us
  transfers between devices with their start and end apart: 18 -> 16, of which waited for: 12 -> 10; matrix products, arithmetic and copies ran while one was open for 3% -> 5% of each run, Pallas kernels for 4% -> 3%
where the time goes in v11:
time: 185 us; the launch traced here: 182 us
  starting transfers between devices  79.9 us (43%)
  waiting for transfers between devices  49.4 us (27%)
  blocking collectives  21.6 us (12%)
  Pallas kernels  16 us (9%)
  local copies, waits for them, and re-layouts  8.41 us (5%)
  other arithmetic  6.17 us (3%)
    ppermute x8, starting transfers between devices, hop(): return lax.ppermute(block, ('x', 'zl', 'c'), ring(other_z, other_core))  46.6 us
    all_to_all x2, waiting for transfers between devices, local(): by_z.append(jnp.sum(lax.all_to_all(paired, Y, 0, 0), axis=0))  22.5 us
    all_to_all x1, blocking collectives, local(): parts = lax.all_to_all(jnp.concatenate(by_z, axis=0), 'zh', 0, 0)  21.6 us
    ppermute x8, waiting for transfers between devices, hop(): return lax.ppermute(block, ('x', 'zl', 'c'), ring(other_z, other_core))  19.9 us
    pallas_call x2, Pallas kernels, product(): pl.pallas_call(functools.partial(product_kernel, piece), grid=(count,), i...  8.44 us
    ppermute x1, starting transfers between devices, local(): came = lax.ppermute(away, 'yh', SWAP)  7.9 us
    ppermute x2, starting transfers between devices, local(): paired = keep + lax.ppermute(send, 'c', SWAP)  7.88 us
    all_to_all x2, starting transfers between devices, local(): by_z.append(jnp.sum(lax.all_to_all(paired, Y, 0, 0), axis=0))  7.72 us
  transfers between devices with their start and end apart: 16, of which 10 were waited for; matrix products, arithmetic and copies ran while one was open for 5% of the time, Pallas kernels for 3%

profile of v11, /device:TPU:1, one launch (start us, length us, event | category | flops | bytes accessed | tf_op | source)
XLA Modules:
  0.0 182.5 jit_solution(12464080965278225354)
XLA Ops:
  1.3 2.1 %split.1 = (bf16[2,128,768]{2,1,0:T(8,128)(2,1)}, bf16[2,128,768]{2,1,0:T(8,128)(2,1)}) custom-call(s32[11]{0:T(128)} %stack.65.place, bf16[128,3072]{1,0:T(8,128)(2,1)} %cotangent.1), custom_call_target="tpu_custom_call" | custom-call | tf_op jit(solution)/shard_map/split/pallas_call | solution.py:66
  3.4 5.7 %collective-permute-start.1 = (bf16[2,128,768]{2,1,0:T(8,128)(2,1)}, bf16[2,128,768]{2,1,0:T(8,128)(2,1)S(1)}, u32[]{:S(2)}, u32[]{:S(2)}) collective-permute-start(bf16[2,128,768]{2,1,0:T(8,128)(2,1)} %get-tuple-element.20), channel_id=1, source_target_pairs={{0,8},{8,0},{1,9},{9,1},{2,10},{10,2},{3,11},{11,3},{4,12},{12,4},... | collective-permute-start | bytes 1179656 | tf_op jit(solution)/shard_map/ppermute | solution.py:258
  9.1 5.4 %collective-permute-done.1.beside = bf16[2,128,768]{2,1,0:T(8,128)(2,1)S(1)} collective-permute-done((bf16[2,128,768]{2,1,0:T(8,128)(2,1)}, bf16[2,128,768]{2,1,0:T(8,128)(2,1)S(1)}, u32[]{:S(2)}, u32[]{:S(2)}) %collective-permute-start.1) | collective-permute-done | bytes 393248 | tf_op jit(solution)/shard_map/ppermute | solution.py:258
  15.6 8.2 %collective-permute-start.2 = (bf16[2,2,128,768]{3,2,1,0:T(8,128)(2,1)S(1)}, bf16[2,2,128,768]{3,2,1,0:T(8,128)(2,1)}, u32[]{:S(2)}, u32[]{:S(2)}) collective-permute-start(bf16[2,2,128,768]{3,2,1,0:T(8,128)(2,1)S(1)} %pad_maximum_fusion), channel_id=1, source_target_pairs={{0,64},{1,449},{8,72},{9,457},{64,128},{65,1},{72,136},{73,9},{128... | collective-permute-start | bytes 2359304 | tf_op jit(solution)/shard_map/ppermute | solution.py:49
  23.8 3.1 %collective-permute-start.3 = (bf16[2,2,128,768]{3,2,1,0:T(8,128)(2,1)S(1)}, bf16[2,2,128,768]{3,2,1,0:T(8,128)(2,1)S(1)}, u32[]{:S(2)}, u32[]{:S(2)}) collective-permute-start(bf16[2,2,128,768]{3,2,1,0:T(8,128)(2,1)S(1)} %pad_maximum_fusion), channel_id=1, source_target_pairs={{0,449},{1,64},{8,457},{9,72},{64,1},{65,128},{72,9},{73,136},{128... | collective-permute-start | bytes 2359304 | tf_op jit(solution)/shard_map/ppermute | solution.py:49
  27.8 7.9 %collective-permute-start = (bf16[192,1024]{1,0:T(8,128)(2,1)S(1)}, bf16[192,1024]{1,0:T(8,128)(2,1)S(1)}, u32[]{:S(2)}, u32[]{:S(2)}) collective-permute-start(bf16[192,1024]{1,0:T(8,128)(2,1)S(1)} %get-tuple-element.36), channel_id=1, source_target_pairs={{0,512},{512,0},{1,513},{513,1},{2,514},{514,2},{3,515},{515,3},{4... | collective-permute-start | bytes 1179656 | tf_op jit(solution)/shard_map/ppermute | solution.py:255
  35.7 1.2 slice_bitcast_fusion.1
  36.9 3.7 %collective-permute-done.3 = bf16[2,2,128,768]{3,2,1,0:T(8,128)(2,1)S(1)} collective-permute-done((bf16[2,2,128,768]{3,2,1,0:T(8,128)(2,1)S(1)}, bf16[2,2,128,768]{3,2,1,0:T(8,128)(2,1)S(1)}, u32[]{:S(2)}, u32[]{:S(2)}) %collective-permute-start.3) | collective-permute-done | bytes 786464 | tf_op jit(solution)/shard_map/ppermute | solution.py:49
  42.4 12.2 %collective-permute-start.6 = (bf16[4,128,768]{2,1,0:T(8,128)(2,1)}, bf16[4,128,768]{2,1,0:T(8,128)(2,1)}, u32[]{:S(2)}, u32[]{:S(2)}) collective-permute-start(bf16[4,128,768]{2,1,0:T(8,128)(2,1)} %pad_maximum_fusion.1.hop_one), channel_id=1, source_target_pairs={{0,64},{1,449},{8,72},{9,457},{64,128},{65,1},{72,136},{73,9},{128... | collective-permute-start | bytes 2359304 | tf_op jit(solution)/shard_map/ppermute | solution.py:49
  55.4 2.3 %features.1.att_own = bf16[416,1024]{1,0:T(8,128)(2,1)} custom-call(s32[11]{0:T(128)} %stack.65.place, bf16[192,1024]{1,0:T(8,128)(2,1)} %get-tuple-element.37.kept, bf16[192,1024]{1,0:T(8,128)(2,1)} %copy-done.10, f32[1,3072]{1,0:T(1,128)} %gate.1), custom_call_target="tpu_custom_call" | custom-call | tf_op jit(solution)/shard_map/features/pallas_call | solution.py:101
  57.7 2.0 %collective-permute-start.4 = (bf16[416,1024]{1,0:T(8,128)(2,1)}, bf16[416,1024]{1,0:T(8,128)(2,1)S(1)}, u32[]{:S(2)}, u32[]{:S(2)}) collective-permute-start(bf16[416,1024]{1,0:T(8,128)(2,1)} %features.1.att_own), channel_id=1, source_target_pairs={{0,8},{8,0},{1,9},{9,1},{2,10},{10,2},{3,11},{11,3},{4,12},{12,4},... | collective-permute-start | bytes 2555912 | tf_op jit(solution)/shard_map/ppermute | solution.py:265
  60.8 7.6 %collective-permute-start.8 = (bf16[4,128,768]{2,1,0:T(8,128)(2,1)S(1)}, bf16[4,128,768]{2,1,0:T(8,128)(2,1)S(1)}, u32[]{:S(2)}, u32[]{:S(2)}) collective-permute-start(bf16[4,128,768]{2,1,0:T(8,128)(2,1)S(1)} %pad_maximum_fusion.2.hop_one), channel_id=1, source_target_pairs={{0,64},{1,449},{8,72},{9,457},{64,128},{65,1},{72,136},{73,9},{128... | collective-permute-start | bytes 2359304 | tf_op jit(solution)/shard_map/ppermute | solution.py:49
  68.4 1.9 %collective-permute-start.7 = (bf16[4,128,768]{2,1,0:T(8,128)(2,1)}, bf16[4,128,768]{2,1,0:T(8,128)(2,1)S(1)}, u32[]{:S(2)}, u32[]{:S(2)}) collective-permute-start(bf16[4,128,768]{2,1,0:T(8,128)(2,1)} %collective-permute-done.6.hop_two), channel_id=1, source_target_pairs={{0,64},{1,449},{8,72},{9,457},{64,128},{65,1},{72,136},{73,9},{128... | collective-permute-start | bytes 2359304 | tf_op jit(solution)/shard_map/ppermute | solution.py:49
  70.4 6.9 %collective-permute-done.8.hop_two = bf16[4,128,768]{2,1,0:T(8,128)(2,1)S(1)} collective-permute-done((bf16[4,128,768]{2,1,0:T(8,128)(2,1)S(1)}, bf16[4,128,768]{2,1,0:T(8,128)(2,1)S(1)}, u32[]{:S(2)}, u32[]{:S(2)}) %collective-permute-start.8) | collective-permute-done | bytes 786464 | tf_op jit(solution)/shard_map/ppermute | solution.py:49
  77.3 5.0 %collective-permute-start.10 = (bf16[4,128,768]{2,1,0:T(8,128)(2,1)S(1)}, bf16[4,128,768]{2,1,0:T(8,128)(2,1)S(1)}, u32[]{:S(2)}, u32[]{:S(2)}) collective-permute-start(bf16[4,128,768]{2,1,0:T(8,128)(2,1)S(1)} %collective-permute-done.8.hop_two), channel_id=1, source_target_pairs={{0,64},{1,449},{8,72},{9,457},{64,128},{65,1},{72,136},{73,9},{128... | collective-permute-start | bytes 2359304 | tf_op jit(solution)/shard_map/ppermute | solution.py:49
  82.5 2.1 %collective-permute-start.5 = (bf16[2,416,384]{2,1,0:T(8,128)(2,1)S(1)}, bf16[2,416,384]{2,1,0:T(8,128)(2,1)S(1)}, u32[]{:S(2)}, u32[]{:S(2)}) collective-permute-start(bf16[2,416,384]{2,1,0:T(8,128)(2,1)S(1)} %pad_maximum_fusion.3), channel_id=1, source_target_pairs={{0,1},{1,0},{2,3},{3,2},{4,5},{5,4},{6,7},{7,6},{8,9},{9,8},{10,11... | collective-permute-start | bytes 1916936 | tf_op jit(solution)/shard_map/ppermute | solution.py:267
  84.6 1.3 collective-permute-done.7.hop_three
  85.9 4.9 %collective-permute-start.9 = (bf16[2,128,768]{2,1,0:T(8,128)(2,1)S(1)}, bf16[2,128,768]{2,1,0:T(8,128)(2,1)S(1)}, u32[]{:S(2)}, u32[]{:S(2)}) collective-permute-start(bf16[2,128,768]{2,1,0:T(8,128)(2,1)S(1)} %slice.30), channel_id=1, source_target_pairs={{0,64},{1,449},{8,72},{9,457},{64,128},{65,1},{72,136},{73,9},{128... | collective-permute-start | bytes 1179656 | tf_op jit(solution)/shard_map/ppermute | solution.py:49
  90.8 3.4 %collective-permute-done.10.hop_three = bf16[4,128,768]{2,1,0:T(8,128)(2,1)S(1)} collective-permute-done((bf16[4,128,768]{2,1,0:T(8,128)(2,1)S(1)}, bf16[4,128,768]{2,1,0:T(8,128)(2,1)S(1)}, u32[]{:S(2)}, u32[]{:S(2)}) %collective-permute-start.10) | collective-permute-done | bytes 786464 | tf_op jit(solution)/shard_map/ppermute | solution.py:49
  94.2 4.2 %collective-permute-done.9.last = bf16[2,128,768]{2,1,0:T(8,128)(2,1)S(1)} collective-permute-done((bf16[2,128,768]{2,1,0:T(8,128)(2,1)S(1)}, bf16[2,128,768]{2,1,0:T(8,128)(2,1)S(1)}, u32[]{:S(2)}, u32[]{:S(2)}) %collective-permute-start.9) | collective-permute-done | bytes 393248 | tf_op jit(solution)/shard_map/ppermute | solution.py:49
  98.4 4.4 %product.2 = (f32[8,2,72,128]{3,2,1,0:T(8,128)S(1)}, f32[8,2,72,128]{3,2,1,0:T(8,128)S(1)}) custom-call(s32[11]{0:T(128)S(1)} %copy-done.8, bf16[416,1024]{1,0:T(8,128)(2,1)S(1)} %copy-done, bf16[416,1024]{1,0:T(8,128)(2,1)S(1)} %collective-permute-done.4.att_beside, bf16[2,416,384]{2,1,0:T(8,128)(2,1)S(1)} %collective-permute-done.5.att_cross, ...), custom_call_target="tpu_custom_call" | custom-call | flops 1207959552 | bytes 8388608 | tf_op jit(solution)/shard_map/product/pallas_call | solution.py:177
  102.8 3.9 %collective-permute-start.11 = (f32[8,2,72,128]{3,2,1,0:T(8,128)S(1)}, f32[8,2,72,128]{3,2,1,0:T(8,128)S(1)}, u32[]{:S(2)}, u32[]{:S(2)}) collective-permute-start(f32[8,2,72,128]{3,2,1,0:T(8,128)S(1)} %get-tuple-element.27), channel_id=1, source_target_pairs={{0,1},{1,0},{2,3},{3,2},{4,5},{5,4},{6,7},{7,6},{8,9},{9,8},{10,11... | collective-permute-start | bytes 1769480 | tf_op jit(solution)/shard_map/ppermute | solution.py:284
  107.5 3.6 %collective-permute-start.12 = (bf16[2,128,768]{2,1,0:T(8,128)(2,1)}, bf16[2,128,768]{2,1,0:T(8,128)(2,1)}, u32[]{:S(2)}, u32[]{:S(2)}) collective-permute-start(bf16[2,128,768]{2,1,0:T(8,128)(2,1)} %slice.31), channel_id=1, source_target_pairs={{0,64},{1,449},{8,72},{9,457},{64,128},{65,1},{72,136},{73,9},{128... | collective-permute-start | bytes 1179656 | tf_op jit(solution)/shard_map/ppermute | solution.py:49
  112.1 4.2 %all-to-all-start = ((f32[8,2,72,128]{3,2,1,0:T(8,128)}), f32[8,2,72,128]{3,2,1,0:T(8,128)}, u32[]{:S(2)}, u32[]{:S(2)}) async-start(f32[8,2,72,128]{3,2,1,0:T(8,128)} %add.46), calls=%async_computation | async-start | bytes 1179648 | tf_op jit(solution)/shard_map/all_to_all | solution.py:285
  120.0 4.1 %product.3 = (f32[8,2,72,128]{3,2,1,0:T(8,128)S(1)}, f32[8,2,72,128]{3,2,1,0:T(8,128)S(1)}) custom-call(s32[11]{0:T(128)S(1)} %copy-done.8, bf16[416,1024]{1,0:T(8,128)(2,1)S(1)} %copy-done, bf16[416,1024]{1,0:T(8,128)(2,1)S(1)} %collective-permute-done.4.att_beside, bf16[2,416,384]{2,1,0:T(8,128)(2,1)S(1)} %copy-done.3, bf16[2,128,768]{2,1,0:T(8,128)(2,1)S(1)} %copy-done.1, ...), custom_call_target="tpu_custom_call" | custom-call | flops 1207959552 | bytes 8388608 | tf_op jit(solution)/shard_map/product/pallas_call | solution.py:177
  124.1 3.9 %collective-permute-start.13 = (f32[8,2,72,128]{3,2,1,0:T(8,128)S(1)}, f32[8,2,72,128]{3,2,1,0:T(8,128)S(1)}, u32[]{:S(2)}, u32[]{:S(2)}) collective-permute-start(f32[8,2,72,128]{3,2,1,0:T(8,128)S(1)} %get-tuple-element.31), channel_id=1, source_target_pairs={{0,1},{1,0},{2,3},{3,2},{4,5},{5,4},{6,7},{7,6},{8,9},{9,8},{10,11... | collective-permute-start | bytes 1769480 | tf_op jit(solution)/shard_map/ppermute | solution.py:284
  128.0 1.6 collective-permute-done.13
  130.5 4.2 %all-to-all-done = f32[8,2,72,128]{3,2,1,0:T(8,128)} async-done(((f32[8,2,72,128]{3,2,1,0:T(8,128)}), f32[8,2,72,128]{3,2,1,0:T(8,128)}, u32[]{:S(2)}, u32[]{:S(2)}) %all-to-all-start) | async-done | bytes 589856 | tf_op jit(solution)/shard_map/all_to_all | solution.py:285
  134.8 3.5 %all-to-all-start.1 = ((f32[8,2,72,128]{3,2,1,0:T(8,128)}), f32[8,2,72,128]{3,2,1,0:T(8,128)S(1)}, u32[]{:S(2)}, u32[]{:S(2)}) async-start(f32[8,2,72,128]{3,2,1,0:T(8,128)} %add.47), calls=%async_computation.1 | async-start | bytes 1179648 | tf_op jit(solution)/shard_map/all_to_all | solution.py:285
  139.4 18.2 %all-to-all-done.1 = f32[8,2,72,128]{3,2,1,0:T(8,128)S(1)} async-done(((f32[8,2,72,128]{3,2,1,0:T(8,128)}), f32[8,2,72,128]{3,2,1,0:T(8,128)S(1)}, u32[]{:S(2)}, u32[]{:S(2)}) %all-to-all-start.1) | async-done | bytes 589856 | tf_op jit(solution)/shard_map/all_to_all | solution.py:285
  157.7 21.6 %all_to_all.15.parts = f32[4,72,128]{2,1,0:T(8,128)} all-to-all(f32[4,72,128]{2,1,0:T(8,128)S(1)} %pad_maximum_fusion.4), channel_id=1, replica_groups=mesh['yh'=2,'x'=8,'zh'=4,'zl'=2,'yl'=4,'c'=2] {'zh'}, dimensions={0} | all-to-all | bytes 294912 | tf_op jit(solution)/shard_map/all_to_all | solution.py:286
  179.3 3.2 %update.1 = (f32[48,192]{1,0:T(8,128)}, f32[48,192]{1,0:T(8,128)}, f32[48,192]{1,0:T(8,128)}, f32[48,192]{1,0:T(8,128)}, f32[48,48]{1,0:T(8,128)}, /*index=5*/f32[192,192]{1,0:T(8,128)}) custom-call(f32[4,72,128]{2,1,0:T(8,128)} %all_to_all.15.parts, f32[48,192]{1,0:T(8,128)} %weight.1, f32[48,192]{1,0:T(8,128)} %exp_avg.1, f32[48,192]{1,0:T(8,128)} %exp_avg_sq.1, ...), custom_call_target="tpu_custom_call" | custom-call | tf_op jit(solution)/shard_map/update/pallas_call | solution.py:289
  (45 shorter events, 13.8 us)
Async XLA Ops:
  3.4 11.1 %collective-permute-start.1 = (bf16[2,128,768]{2,1,0:T(8,128)(2,1)}, bf16[2,128,768]{2,1,0:T(8,128)(2,1)S(1)}, u32[]{:S(2)}, u32[]{:S(2)}) collective-permute-start(bf16[2,128,768]{2,1,0:T(8,128)(2,1)} %get-tuple-element.20), channel_id=1, source_target_pairs={{0,8},{8,0},{1,9},{9,1},{2,10},{10,2},{3,11},{11,3},{4,12},{12,4},... | collective-permute-start | bytes 1179656 | tf_op jit(solution)/shard_map/ppermute | solution.py:258
  14.5 12.5 %copy-start.9 = (bf16[2048,192]{0,1:T(8,128)(2,1)S(1)}, bf16[2048,192]{0,1:T(8,128)(2,1)}, u32[]{:S(2)}) copy-start(bf16[2048,192]{0,1:T(8,128)(2,1)} %param.10) | copy-start | bytes 2359300
  15.6 20.1 %collective-permute-start.2 = (bf16[2,2,128,768]{3,2,1,0:T(8,128)(2,1)S(1)}, bf16[2,2,128,768]{3,2,1,0:T(8,128)(2,1)}, u32[]{:S(2)}, u32[]{:S(2)}) collective-permute-start(bf16[2,2,128,768]{3,2,1,0:T(8,128)(2,1)S(1)} %pad_maximum_fusion), channel_id=1, source_target_pairs={{0,64},{1,449},{8,72},{9,457},{64,128},{65,1},{72,136},{73,9},{128... | collective-permute-start | bytes 2359304 | tf_op jit(solution)/shard_map/ppermute | solution.py:49
  23.8 16.8 %collective-permute-start.3 = (bf16[2,2,128,768]{3,2,1,0:T(8,128)(2,1)S(1)}, bf16[2,2,128,768]{3,2,1,0:T(8,128)(2,1)S(1)}, u32[]{:S(2)}, u32[]{:S(2)}) collective-permute-start(bf16[2,2,128,768]{3,2,1,0:T(8,128)(2,1)S(1)} %pad_maximum_fusion), channel_id=1, source_target_pairs={{0,449},{1,64},{8,457},{9,72},{64,1},{65,128},{72,9},{73,136},{128... | collective-permute-start | bytes 2359304 | tf_op jit(solution)/shard_map/ppermute | solution.py:49
  27.8 26.8 %collective-permute-start = (bf16[192,1024]{1,0:T(8,128)(2,1)S(1)}, bf16[192,1024]{1,0:T(8,128)(2,1)S(1)}, u32[]{:S(2)}, u32[]{:S(2)}) collective-permute-start(bf16[192,1024]{1,0:T(8,128)(2,1)S(1)} %get-tuple-element.36), channel_id=1, source_target_pairs={{0,512},{512,0},{1,513},{513,1},{2,514},{514,2},{3,515},{515,3},{4... | collective-permute-start | bytes 1179656 | tf_op jit(solution)/shard_map/ppermute | solution.py:255
  42.4 26.0 %collective-permute-start.6 = (bf16[4,128,768]{2,1,0:T(8,128)(2,1)}, bf16[4,128,768]{2,1,0:T(8,128)(2,1)}, u32[]{:S(2)}, u32[]{:S(2)}) collective-permute-start(bf16[4,128,768]{2,1,0:T(8,128)(2,1)} %pad_maximum_fusion.1.hop_one), channel_id=1, source_target_pairs={{0,64},{1,449},{8,72},{9,457},{64,128},{65,1},{72,136},{73,9},{128... | collective-permute-start | bytes 2359304 | tf_op jit(solution)/shard_map/ppermute | solution.py:49
  54.7 0.7 copy-start.10
  57.7 12.7 %copy-start = (bf16[416,1024]{1,0:T(8,128)(2,1)S(1)}, bf16[416,1024]{1,0:T(8,128)(2,1)}, u32[]{:S(2)}) copy-start(bf16[416,1024]{1,0:T(8,128)(2,1)} %features.1.att_own) | copy-start | bytes 2555908
  57.7 24.7 %collective-permute-start.4 = (bf16[416,1024]{1,0:T(8,128)(2,1)}, bf16[416,1024]{1,0:T(8,128)(2,1)S(1)}, u32[]{:S(2)}, u32[]{:S(2)}) collective-permute-start(bf16[416,1024]{1,0:T(8,128)(2,1)} %features.1.att_own), channel_id=1, source_target_pairs={{0,8},{8,0},{1,9},{9,1},{2,10},{10,2},{3,11},{11,3},{4,12},{12,4},... | collective-permute-start | bytes 2555912 | tf_op jit(solution)/shard_map/ppermute | solution.py:265
  60.8 16.5 %collective-permute-start.8 = (bf16[4,128,768]{2,1,0:T(8,128)(2,1)S(1)}, bf16[4,128,768]{2,1,0:T(8,128)(2,1)S(1)}, u32[]{:S(2)}, u32[]{:S(2)}) collective-permute-start(bf16[4,128,768]{2,1,0:T(8,128)(2,1)S(1)} %pad_maximum_fusion.2.hop_one), channel_id=1, source_target_pairs={{0,64},{1,449},{8,72},{9,457},{64,128},{65,1},{72,136},{73,9},{128... | collective-permute-start | bytes 2359304 | tf_op jit(solution)/shard_map/ppermute | solution.py:49
  68.4 17.4 %collective-permute-start.7 = (bf16[4,128,768]{2,1,0:T(8,128)(2,1)}, bf16[4,128,768]{2,1,0:T(8,128)(2,1)S(1)}, u32[]{:S(2)}, u32[]{:S(2)}) collective-permute-start(bf16[4,128,768]{2,1,0:T(8,128)(2,1)} %collective-permute-done.6.hop_two), channel_id=1, source_target_pairs={{0,64},{1,449},{8,72},{9,457},{64,128},{65,1},{72,136},{73,9},{128... | collective-permute-start | bytes 2359304 | tf_op jit(solution)/shard_map/ppermute | solution.py:49
  77.3 5.2 %copy-start.6 = (bf16[4,128,768]{2,1,0:T(8,128)(2,1)}, bf16[4,128,768]{2,1,0:T(8,128)(2,1)S(1)}, u32[]{:S(2)}) copy-start(bf16[4,128,768]{2,1,0:T(8,128)(2,1)S(1)} %collective-permute-done.8.hop_two) | copy-start | bytes 2359300
  77.3 16.9 %collective-permute-start.10 = (bf16[4,128,768]{2,1,0:T(8,128)(2,1)S(1)}, bf16[4,128,768]{2,1,0:T(8,128)(2,1)S(1)}, u32[]{:S(2)}, u32[]{:S(2)}) collective-permute-start(bf16[4,128,768]{2,1,0:T(8,128)(2,1)S(1)} %collective-permute-done.8.hop_two), channel_id=1, source_target_pairs={{0,64},{1,449},{8,72},{9,457},{64,128},{65,1},{72,136},{73,9},{128... | collective-permute-start | bytes 2359304 | tf_op jit(solution)/shard_map/ppermute | solution.py:49
  82.5 15.9 %copy-start.1 = (bf16[2,128,768]{2,1,0:T(8,128)(2,1)S(1)}, bf16[2,128,768]{2,1,0:T(8,128)(2,1)}, u32[]{:S(2)}) copy-start(bf16[2,128,768]{2,1,0:T(8,128)(2,1)} %get-tuple-element.19.own) | copy-start | bytes 1179652
  82.5 15.9 %copy-start.8 = (s32[11]{0:T(128)S(1)}, s32[11]{0:T(128)}, u32[]{:S(2)}) copy-start(s32[11]{0:T(128)} %stack.65.place) | copy-start | bytes 136
  82.5 15.9 %collective-permute-start.5 = (bf16[2,416,384]{2,1,0:T(8,128)(2,1)S(1)}, bf16[2,416,384]{2,1,0:T(8,128)(2,1)S(1)}, u32[]{:S(2)}, u32[]{:S(2)}) collective-permute-start(bf16[2,416,384]{2,1,0:T(8,128)(2,1)S(1)} %pad_maximum_fusion.3), channel_id=1, source_target_pairs={{0,1},{1,0},{2,3},{3,2},{4,5},{5,4},{6,7},{7,6},{8,9},{9,8},{10,11... | collective-permute-start | bytes 1916936 | tf_op jit(solution)/shard_map/ppermute | solution.py:267
  85.9 12.5 %collective-permute-start.9 = (bf16[2,128,768]{2,1,0:T(8,128)(2,1)S(1)}, bf16[2,128,768]{2,1,0:T(8,128)(2,1)S(1)}, u32[]{:S(2)}, u32[]{:S(2)}) collective-permute-start(bf16[2,128,768]{2,1,0:T(8,128)(2,1)S(1)} %slice.30), channel_id=1, source_target_pairs={{0,64},{1,449},{8,72},{9,457},{64,128},{65,1},{72,136},{73,9},{128... | collective-permute-start | bytes 1179656 | tf_op jit(solution)/shard_map/ppermute | solution.py:49
  94.2 12.6 %copy-start.4 = (bf16[4,128,768]{2,1,0:T(8,128)(2,1)}, bf16[4,128,768]{2,1,0:T(8,128)(2,1)S(1)}, u32[]{:S(2)}) copy-start(bf16[4,128,768]{2,1,0:T(8,128)(2,1)S(1)} %collective-permute-done.10.hop_three) | copy-start | bytes 2359300
  98.4 4.4 %copy-start.2 = (bf16[2,416,384]{2,1,0:T(8,128)(2,1)}, bf16[2,416,384]{2,1,0:T(8,128)(2,1)S(1)}, u32[]{:S(2)}) copy-start(bf16[2,416,384]{2,1,0:T(8,128)(2,1)S(1)} %collective-permute-done.5.att_cross) | copy-start | bytes 1916932
  102.8 8.4 %collective-permute-start.11 = (f32[8,2,72,128]{3,2,1,0:T(8,128)S(1)}, f32[8,2,72,128]{3,2,1,0:T(8,128)S(1)}, u32[]{:S(2)}, u32[]{:S(2)}) collective-permute-start(f32[8,2,72,128]{3,2,1,0:T(8,128)S(1)} %get-tuple-element.27), channel_id=1, source_target_pairs={{0,1},{1,0},{2,3},{3,2},{4,5},{5,4},{6,7},{7,6},{8,9},{9,8},{10,11... | collective-permute-start | bytes 1769480 | tf_op jit(solution)/shard_map/ppermute | solution.py:284
  107.5 9.1 %collective-permute-start.12 = (bf16[2,128,768]{2,1,0:T(8,128)(2,1)}, bf16[2,128,768]{2,1,0:T(8,128)(2,1)}, u32[]{:S(2)}, u32[]{:S(2)}) collective-permute-start(bf16[2,128,768]{2,1,0:T(8,128)(2,1)} %slice.31), channel_id=1, source_target_pairs={{0,64},{1,449},{8,72},{9,457},{64,128},{65,1},{72,136},{73,9},{128... | collective-permute-start | bytes 1179656 | tf_op jit(solution)/shard_map/ppermute | solution.py:49
  112.1 22.7 %all-to-all-start = ((f32[8,2,72,128]{3,2,1,0:T(8,128)}), f32[8,2,72,128]{3,2,1,0:T(8,128)}, u32[]{:S(2)}, u32[]{:S(2)}) async-start(f32[8,2,72,128]{3,2,1,0:T(8,128)} %add.46), calls=%async_computation | async-start | bytes 1179648 | tf_op jit(solution)/shard_map/all_to_all | solution.py:285
  116.7 1.1 copy-start.3
  117.7 1.1 copy-start.5
  118.9 1.1 copy-start.7
  124.1 5.6 %collective-permute-start.13 = (f32[8,2,72,128]{3,2,1,0:T(8,128)S(1)}, f32[8,2,72,128]{3,2,1,0:T(8,128)S(1)}, u32[]{:S(2)}, u32[]{:S(2)}) collective-permute-start(f32[8,2,72,128]{3,2,1,0:T(8,128)S(1)} %get-tuple-element.31), channel_id=1, source_target_pairs={{0,1},{1,0},{2,3},{3,2},{4,5},{5,4},{6,7},{7,6},{8,9},{9,8},{10,11... | collective-permute-start | bytes 1769480 | tf_op jit(solution)/shard_map/ppermute | solution.py:284
  134.8 22.9 %all-to-all-start.1 = ((f32[8,2,72,128]{3,2,1,0:T(8,128)}), f32[8,2,72,128]{3,2,1,0:T(8,128)S(1)}, u32[]{:S(2)}, u32[]{:S(2)}) async-start(f32[8,2,72,128]{3,2,1,0:T(8,128)} %add.47), calls=%async_computation.1 | async-start | bytes 1179648 | tf_op jit(solution)/shard_map/all_to_all | solution.py:285
